TPU v7x, 32 devices: a whole 2x2x4 slice. The times are simulated.
32 devices in a mesh: gx: 16 (over z, y, core), gy: 2 (over x).
Axes of the slice: x: 2, y: 2, z: 4, core: 2. Of those that a mesh axis runs over, the one named last changes fastest.
Arguments:
- velocity: float32 [3, 512, 256, 128], P(None, 'gx', 'gy'), may hold values from -6 to 6
- stress: float32 [6, 512, 256, 128], P(None, 'gx', 'gy'), may hold values from -6 to 6
- lame_lambda: bfloat16 [512, 256, 128], P('gx', 'gy'), may hold values from 0.5 to 1.5
- shear_modulus: bfloat16 [512, 256, 128], P('gx', 'gy'), may hold values from 0.29882812 to 1
- buoyancy: bfloat16 [512, 256, 128], P('gx', 'gy'), may hold values from 0.5 to 1.5
- source_p: bfloat16 [3, 512, 256, 128], P(None, 'gx', 'gy'), may hold values from -6 to 6
- source_s: bfloat16 [3, 512, 256, 128], P(None, 'gx', 'gy'), may hold values from -6 to 6
Outputs:
- image_p: float32 [512, 256, 128], P('gx', 'gy')
- image_s: float32 [512, 256, 128], P('gx', 'gy')
All inputs are finite; a program needn't handle non-finite values.
Results may differ from a plain program's by a relative error of at most 0.0003.
Values sent between devices are 32-bit elements; how exact they have to be, the bound alone decides.
No kernel may reach another device: no remote copies, remote signals or barrier semaphores. Data moves between devices by JAX's collectives and lax.ppermute only.
A program may use at most 128 MiB of HBM per device.

v0:
```python
import math

import jax
import jax.numpy as jnp
from jax import lax
from jax.sharding import PartitionSpec as P

STEPS = 2


time_step = 0.2


def passed_along(block, axis, distance):
    devices = range(lax.axis_size(axis))
    route = [(i - distance, i) for i in devices if i - distance in devices]
    return lax.ppermute(block, axis, route)


def x_rims(planes, offset):
    return passed_along(planes, "gx", offset)


def y_rims(planes, offset):
    return passed_along(planes, "gy", offset)


def with_next(field, rim, which):
    length = field.shape[which]
    return jnp.concatenate([lax.slice_in_dim(field, 1, length, axis=which), rim], axis=which)


def with_prior(field, rim, which):
    length = field.shape[which]
    return jnp.concatenate([rim, lax.slice_in_dim(field, 0, length - 1, axis=which)], axis=which)


def zero_rim(field, which):
    return jnp.zeros_like(lax.slice_in_dim(field, 0, 1, axis=which))


def stress_step(velocity, stress, lame_value, shear_value):
    x_speed, y_speed, z_speed = (velocity[0], velocity[1], velocity[2])
    prior_x = x_rims(x_speed[None, -1:], 1)
    next_x = x_rims(jnp.stack([y_speed[:1], z_speed[:1]]), -1)
    prior_y = y_rims(y_speed[None, :, -1:], 1)
    next_y = y_rims(jnp.stack([x_speed[:, :1], z_speed[:, :1]]), -1)
    strain_x = x_speed - with_prior(x_speed, prior_x[0], 0)
    strain_y = y_speed - with_prior(y_speed, prior_y[0], 1)
    strain_z = z_speed - with_prior(z_speed, zero_rim(z_speed, 2), 2)
    volume = strain_x + strain_y + strain_z
    normal_x = stress[0] + time_step * (lame_value * volume + 2.0 * shear_value * strain_x)
    normal_y = stress[1] + time_step * (lame_value * volume + 2.0 * shear_value * strain_y)
    normal_z = stress[2] + time_step * (lame_value * volume + 2.0 * shear_value * strain_z)
    shear_xy = stress[3] + time_step * shear_value * (
        with_next(x_speed, next_y[0], 1) - x_speed + (with_next(y_speed, next_x[0], 0) - y_speed)
    )
    shear_xz = stress[4] + time_step * shear_value * (
        with_next(x_speed, zero_rim(x_speed, 2), 2)
        - x_speed
        + (with_next(z_speed, next_x[1], 0) - z_speed)
    )
    shear_yz = stress[5] + time_step * shear_value * (
        with_next(y_speed, zero_rim(y_speed, 2), 2)
        - y_speed
        + (with_next(z_speed, next_y[1], 1) - z_speed)
    )
    return jnp.stack([normal_x, normal_y, normal_z, shear_xy, shear_xz, shear_yz])


def velocity_step(velocity, stress, buoy_value):
    normal_x, normal_y, normal_z = (stress[0], stress[1], stress[2])
    shear_xy, shear_xz, shear_yz = (stress[3], stress[4], stress[5])
    next_x = x_rims(normal_x[None, :1], -1)
    prior_x = x_rims(jnp.stack([shear_xy[-1:], shear_xz[-1:]]), 1)
    next_y = y_rims(normal_y[None, :, :1], -1)
    prior_y = y_rims(jnp.stack([shear_xy[:, -1:], shear_yz[:, -1:]]), 1)
    x_speed = velocity[0] + time_step * buoy_value * (
        with_next(normal_x, next_x[0], 0)
        - normal_x
        + (shear_xy - with_prior(shear_xy, prior_y[0], 1))
        + (shear_xz - with_prior(shear_xz, zero_rim(shear_xz, 2), 2))
    )
    y_speed = velocity[1] + time_step * buoy_value * (
        shear_xy
        - with_prior(shear_xy, prior_x[0], 0)
        + (with_next(normal_y, next_y[0], 1) - normal_y)
        + (shear_yz - with_prior(shear_yz, zero_rim(shear_yz, 2), 2))
    )
    z_speed = velocity[2] + time_step * buoy_value * (
        shear_xz
        - with_prior(shear_xz, prior_x[1], 0)
        + (shear_yz - with_prior(shear_yz, prior_y[1], 1))
        + (with_next(normal_z, zero_rim(normal_z, 2), 2) - normal_z)
    )
    return jnp.stack([x_speed, y_speed, z_speed])


def phase_tables(length):
    positions = jnp.arange(length, dtype=jnp.int32)
    product = positions[:, None] * positions[None, :] % length
    phases = product.astype(jnp.float32) * (2.0 * math.pi / length)
    return (jnp.cos(phases), jnp.sin(phases))


def z_tables(z_cells, gy_count):
    quarter = z_cells // (2 * gy_count)
    width = gy_count * (quarter + 1)
    column = jnp.arange(width, dtype=jnp.int32)
    block = column // (quarter + 1)
    slot = column % (quarter + 1)
    waves = jnp.where(slot < quarter, block * quarter + slot, z_cells // 2)
    weight = jnp.where(
        slot < quarter, jnp.where(waves == 0, 1.0, 2.0), jnp.where(block == gy_count - 1, 1.0, 0.0)
    ).astype(jnp.float32)
    positions = jnp.arange(z_cells, dtype=jnp.int32)
    product = positions[:, None] * waves[None, :] % z_cells
    phases = product.astype(jnp.float32) * (2.0 * math.pi / z_cells)
    cos_fwd = jnp.cos(phases)
    sin_fwd = jnp.sin(phases)
    cos_back = jnp.transpose(cos_fwd) * weight[:, None]
    sin_back = jnp.transpose(sin_fwd) * weight[:, None]
    return (cos_fwd, sin_fwd, cos_back, sin_back, waves)


def contract(pattern, left, right):
    return jnp.einsum(pattern, left, right, precision=lax.Precision.HIGHEST)


def complex_sum(real_in, imag_in, cosine, sine, pattern, forward_sign):
    cos_real = contract(pattern, real_in, cosine)
    sin_imag = contract(pattern, imag_in, sine)
    cos_imag = contract(pattern, imag_in, cosine)
    sin_real = contract(pattern, real_in, sine)
    if forward_sign:
        return (cos_real + sin_imag, cos_imag - sin_real)
    return (cos_real - sin_imag, cos_imag + sin_real)


def signed_index(positions, length):
    half_length = length // 2
    signed = jnp.where(
        positions < half_length,
        positions,
        jnp.where(positions == half_length, 0, positions - length),
    )
    return signed.astype(jnp.float32)


def forward(velocity, cos_fwd, sin_fwd):
    x_cells, y_cells = (velocity.shape[1], velocity.shape[2])
    gx_count = lax.axis_size("gx")
    gy_count = lax.axis_size("gy")
    x_total = gx_count * x_cells
    y_total = gy_count * y_cells
    kept = cos_fwd.shape[1]
    z_part = kept // gy_count
    y_part = y_total // gx_count
    real_part = contract("cxyn,nk->ckxy", velocity, cos_fwd)
    imag_part = -contract("cxyn,nk->ckxy", velocity, sin_fwd)
    packed = jnp.stack([real_part, imag_part]).reshape(2, 3, 1, kept, x_cells * y_cells)
    arrived = lax.all_to_all(packed, "gy", split_axis=3, concat_axis=2, tiled=True)
    comp_count = arrived.shape[1]
    pieces = arrived.reshape(2, comp_count, gy_count, z_part, x_cells, y_cells)
    cos_y, sin_y = phase_tables(y_total)
    cos_y = cos_y.reshape(gy_count, y_cells, y_total)
    sin_y = sin_y.reshape(gy_count, y_cells, y_total)
    real_out, imag_out = complex_sum(pieces[0], pieces[1], cos_y, sin_y, "cgzxl,glk->ckzx", True)
    after_y = jnp.stack([real_out, imag_out]).reshape(2, comp_count, 1, y_total, z_part * x_cells)
    arrived = lax.all_to_all(after_y, "gx", split_axis=3, concat_axis=2, tiled=True)
    comp_count = arrived.shape[1]
    pieces = arrived.reshape(2, comp_count, gx_count, y_part, z_part, x_cells)
    cos_x, sin_x = phase_tables(x_total)
    cos_x = cos_x.reshape(gx_count, x_cells, x_total)
    sin_x = sin_x.reshape(gx_count, x_cells, x_total)
    real_out, imag_out = complex_sum(pieces[0], pieces[1], cos_x, sin_x, "cgazl,glk->cazk", True)
    return jnp.stack([real_out, imag_out])


def project(spectra, waves, z_total):
    y_part, z_part, x_total = (spectra.shape[2], spectra.shape[3], spectra.shape[4])
    gy_count = lax.axis_size("gy")
    y_total = y_part * lax.axis_size("gx")
    y_index = lax.axis_index("gx") * y_part + jnp.arange(y_part, dtype=jnp.int32)
    z_index = lax.dynamic_slice_in_dim(waves.reshape(gy_count, z_part), lax.axis_index("gy"), 1, 0)[
        0
    ]
    wave_x = signed_index(jnp.arange(x_total, dtype=jnp.int32), x_total)[None, None, :]
    wave_y = signed_index(y_index, y_total)[:, None, None]
    wave_z = signed_index(z_index, z_total)[None, :, None]
    inverse_norm = 1.0 / jnp.maximum(wave_x * wave_x + wave_y * wave_y + wave_z * wave_z, 1.0)
    radial = (
        wave_x * spectra[:, 0] + wave_y * spectra[:, 1] + wave_z * spectra[:, 2]
    ) * inverse_norm
    return jnp.stack([wave_x * radial, wave_y * radial, wave_z * radial], axis=1)


def inverse_fields(spectrum, x_cells, y_cells, z_cells, cos_back, sin_back):
    comp_count, y_part, z_part, x_total = (
        spectrum.shape[1],
        spectrum.shape[2],
        spectrum.shape[3],
        spectrum.shape[4],
    )
    gx_count = lax.axis_size("gx")
    gy_count = lax.axis_size("gy")
    y_total = y_part * gx_count
    norm_factor = 1.0 / (x_total * y_total * z_cells)
    cos_x, sin_x = phase_tables(x_total)
    real_part, imag_part = complex_sum(
        spectrum[0], spectrum[1], cos_x, sin_x, "cazk,kx->cxaz", False
    )
    packed = jnp.stack([real_part, imag_part]).reshape(2, comp_count, 1, x_total, y_part * z_part)
    arrived = lax.all_to_all(packed, "gx", split_axis=3, concat_axis=2, tiled=True)
    count_here = arrived.shape[1]
    pieces = arrived.reshape(2, count_here, gx_count, x_cells, y_part, z_part)
    cos_y, sin_y = phase_tables(y_total)
    cos_y = cos_y.reshape(gx_count, y_part, y_total)
    sin_y = sin_y.reshape(gx_count, y_part, y_total)
    real_out, imag_out = complex_sum(pieces[0], pieces[1], cos_y, sin_y, "cgxaz,gay->cyzx", False)
    middle = jnp.stack([real_out, imag_out]).reshape(2, count_here, 1, y_total, z_part * x_cells)
    arrived = lax.all_to_all(middle, "gy", split_axis=3, concat_axis=2, tiled=True)
    count_here = arrived.shape[1]
    pieces = arrived.reshape(2, count_here, gy_count, y_cells, z_part, x_cells)
    cos_z = cos_back.reshape(gy_count, z_part, z_cells)
    sin_z = sin_back.reshape(gy_count, z_part, z_cells)
    cos_real = contract("cgybx,gbn->cxyn", pieces[0], cos_z)
    sin_imag = contract("cgybx,gbn->cxyn", pieces[1], sin_z)
    return (cos_real - sin_imag) * norm_factor


def shards(velocity, stress, lame_lambda, shear_modulus, buoyancy, source_p, source_s):
    lame_value = lame_lambda.astype(jnp.float32)
    shear_value = shear_modulus.astype(jnp.float32)
    buoy_value = buoyancy.astype(jnp.float32)
    for step_index in range(STEPS):
        stress = stress_step(velocity, stress, lame_value, shear_value)
        velocity = velocity_step(velocity, stress, buoy_value)
    x_cells, y_cells, z_cells = (velocity.shape[1], velocity.shape[2], velocity.shape[3])
    gy_count = lax.axis_size("gy")
    cos_fwd, sin_fwd, cos_back, sin_back, waves = z_tables(z_cells, gy_count)
    spectra = forward(velocity, cos_fwd, sin_fwd)
    compression = project(spectra, waves, z_cells)
    p_field = inverse_fields(compression, x_cells, y_cells, z_cells, cos_back, sin_back)
    s_field = velocity - p_field
    image_p = jnp.sum(source_p.astype(jnp.float32) * p_field, axis=0)
    image_s = jnp.sum(source_s.astype(jnp.float32) * s_field, axis=0)
    return (image_p, image_s)


def solution(mesh):
    in_specs = (
        P(None, "gx", "gy", None),
        P(None, "gx", "gy", None),
        P("gx", "gy", None),
        P("gx", "gy", None),
        P("gx", "gy", None),
        P(None, "gx", "gy", None),
        P(None, "gx", "gy", None),
    )
    out_specs = (P("gx", "gy", None), P("gx", "gy", None))
    return jax.shard_map(shards, mesh=mesh, in_specs=in_specs, out_specs=out_specs, check_vma=False)
```

profile of v0, /device:TPU:12, one launch (start us, length us, event | category | flops | bytes accessed | tf_op | source)
XLA Modules:
  0.0 1248.2 jit_solution(2979467968352895398)
XLA Ops:
  188.9 71.9 %all-to-all-done = f32[2,3,1,66,4096]{4,0,2,1,3:T(2,128)} async-done(((f32[2,3,1,66,4096]{4,0,2,1,3:T(2,128)}), f32[2,3,1,66,4096]{4,0,2,1,3:T(2,128)}, u32[]{:S(2)}, u32[]{:S(2)}) %all-to-all-start) | async-done | bytes 6488096 | tf_op jit(solution)/shard_map/all_to_all | solution.py:162
  303.3 16.8 %copy.144 = f32[2,3,1,256,1056]{4,2,1,0,3:T(1,128)} copy(f32[2,3,1,256,1056]{3,4,2,1,0:T(8,128)} %pad_maximum_fusion.2) | data formatting | bytes 12976128 | tf_op jit(solution)/shard_map/stack | solution.py:169
  329.4 153.1 %all-to-all-done.1 = f32[2,3,1,256,1056]{4,2,1,0,3:T(1,128)} async-done(((f32[2,3,1,256,1056]{4,2,1,0,3:T(1,128)}), f32[2,3,1,256,1056]{4,2,1,0,3:T(1,128)}, u32[]{:S(2)}, u32[]{:S(2)}) %all-to-all-start.1) | async-done | bytes 6488096 | tf_op jit(solution)/shard_map/all_to_all | solution.py:170
  482.4 26.2 %slice_reduce_fusion.3 = (f32[3,256,1056]{2,0,1:T(4,128)}, f32[3,256,1056]{2,0,1:T(4,128)}) fusion(f32[2,3,1,256,1056]{4,2,1,0,3:T(1,128)} %all-to-all-done.1), kind=kLoop, calls=%fused_computation.68 | loop fusion | bytes 12976128 | tf_op jit(solution)/shard_map/slice | solution.py:176
  508.6 12.5 reshape.520
  521.1 29.4 %fusion.2 = f32[3,16,33,512,1]{3,2,4,1,0:T(8,128)} fusion(f32[3,16,16,33,32]{4,3,0,2,1:T(8,128)} %reshape.520, s32[16,32]{1,0:T(8,128)S(1)} %multiply_add_fusion), kind=kOutput, calls=%fused_computation.2 | convolution fusion | flops 4986503168 | bytes 6490112 | tf_op jit(solution)/shard_map/cgazl,glk->cazk/dot_general | solution.py:127
  550.5 27.3 %fusion = f32[3,16,33,512,1]{3,2,4,1,0:T(8,128)} fusion(f32[3,16,16,33,32]{4,3,0,2,1:T(8,128)S(1)} %copy-done.22, s32[16,32]{1,0:T(8,128)S(1)} %multiply_add_fusion), kind=kOutput, calls=%fused_computation | convolution fusion | flops 4986503168 | bytes 6490112 | tf_op jit(solution)/shard_map/cgazl,glk->cazk/dot_general | solution.py:127
  577.8 12.5 reshape.519
  590.3 29.0 %fusion.31 = f32[1,3,16,33,512]{4,3,2,1,0:T(8,128)S(1)} fusion(f32[3,16,33,512,1]{3,2,4,1,0:T(8,128)} %fusion.2, f32[3,16,16,33,32]{4,3,0,2,1:T(8,128)} %reshape.519, s32[16,32]{1,0:T(8,128)S(1)} %multiply_add_fusion), kind=kOutput, calls=%fused_computation.52 | convolution fusion | flops 4987314176 | bytes 9734144 | tf_op jit(solution)/shard_map/cgazl,glk->cazk/dot_general | solution.py:127
  619.3 25.6 %fusion.30 = f32[1,3,16,33,512]{4,3,2,1,0:T(8,128)S(1)} fusion(f32[3,16,33,512,1]{3,2,4,1,0:T(8,128)S(1)} %copy-done.33, f32[3,16,16,33,32]{4,3,0,2,1:T(8,128)S(1)} %copy-done.21, s32[16,32]{1,0:T(8,128)S(1)} %multiply_add_fusion), kind=kOutput, calls=%fused_computation.50 | convolution fusion | flops 4987314176 | bytes 9734144 | tf_op jit(solution)/shard_map/cgazl,glk->cazk/dot_general | solution.py:127
  685.1 14.7 %add_bitcast_fusion = f32[3,512,16,33]{1,3,2,0:T(8,128)} fusion(f32[512,3,16,33]{0,3,2,1:T(8,128)} %fusion.38, f32[2,3,16,33,512]{4,3,2,1,0:T(8,128)} %copy-done.24), kind=kOutput, calls=%fused_computation.61 | convolution fusion | flops 4987314176 | bytes 11108352 | tf_op jit(solution)/shard_map/cazk,kx->cxaz/dot_general | solution.py:127
  710.3 12.1 copy.151
  727.5 171.0 %all-to-all-done.2 = f32[2,3,1,512,528]{4,0,2,1,3:T(2,128)} async-done(((f32[2,3,1,512,528]{4,0,2,1,3:T(2,128)}), f32[2,3,1,512,528]{4,0,2,1,3:T(2,128)}, u32[]{:S(2)}, u32[]{:S(2)}) %all-to-all-start.2) | async-done | bytes 6488096 | tf_op jit(solution)/shard_map/all_to_all | solution.py:214
  898.4 29.6 %slice_reduce_fusion.1 = (f32[3,512,528]{2,0,1:T(4,128)}, f32[3,512,528]{2,0,1:T(4,128)}) fusion(f32[2,3,1,512,528]{4,0,2,1,3:T(2,128)} %all-to-all-done.2), kind=kLoop, calls=%fused_computation.42 | loop fusion | bytes 12976128 | tf_op jit(solution)/shard_map/slice | solution.py:220
  928.0 14.7 %reshape.522 = f32[3,16,32,16,33]{4,3,0,2,1:T(8,128)} reshape(f32[3,512,528]{2,0,1:T(4,128)} %get-tuple-element.3) | data formatting | bytes 6488064 | tf_op jit(solution)/shard_map/squeeze | solution.py:220
  942.7 31.7 %fusion.10 = f32[256,3,32,33,1]{0,3,4,2,1:T(8,128)} fusion(f32[3,16,32,16,33]{4,3,0,2,1:T(8,128)} %reshape.522, s32[16,16]{0,1:T(8,128)S(1)} %multiply_add_fusion.1), kind=kOutput, calls=%fused_computation.10 | convolution fusion | flops 2492334080 | bytes 6489088 | tf_op jit(solution)/shard_map/cgxaz,gay->cyzx/dot_general | solution.py:127
  974.5 27.4 %fusion.8 = f32[256,3,32,33,1]{0,3,4,2,1:T(8,128)} fusion(f32[3,16,32,16,33]{4,3,0,2,1:T(8,128)S(1)} %copy-done.2, s32[16,16]{0,1:T(8,128)S(1)} %multiply_add_fusion.1), kind=kOutput, calls=%fused_computation.8 | convolution fusion | flops 2492334080 | bytes 6489088 | tf_op jit(solution)/shard_map/cgxaz,gay->cyzx/dot_general | solution.py:127
  1001.9 14.8 %reshape.521 = f32[3,16,32,16,33]{4,3,0,2,1:T(8,128)} reshape(f32[3,512,528]{2,0,1:T(4,128)} %get-tuple-element.2) | data formatting | bytes 6488064 | tf_op jit(solution)/shard_map/squeeze | solution.py:220
  1016.7 31.4 %fusion.29 = f32[3,256,33,32]{1,2,3,0:T(8,128)S(1)} fusion(f32[256,3,32,33,1]{0,3,4,2,1:T(8,128)} %fusion.10, f32[3,16,32,16,33]{4,3,0,2,1:T(8,128)} %reshape.521, s32[16,16]{0,1:T(8,128)S(1)} %multiply_add_fusion.1), kind=kOutput, calls=%fused_computation.48 | convolution fusion | flops 2493145088 | bytes 9733120 | tf_op jit(solution)/shard_map/cgxaz,gay->cyzx/dot_general | solution.py:127
  1050.7 25.7 %fusion.28 = f32[3,256,33,32]{1,2,3,0:T(8,128)S(1)} fusion(f32[256,3,32,33,1]{0,3,4,2,1:T(8,128)S(1)} %copy-done.20, f32[3,16,32,16,33]{4,3,0,2,1:T(8,128)S(1)} %copy-done.1, s32[16,16]{0,1:T(8,128)S(1)} %multiply_add_fusion.1), kind=kOutput, calls=%fused_computation.46 | convolution fusion | flops 2493145088 | bytes 9733120 | tf_op jit(solution)/shard_map/cgxaz,gay->cyzx/dot_general | solution.py:127
  1081.5 16.8 %copy.160 = f32[2,3,1,256,1056]{4,2,1,0,3:T(1,128)} copy(f32[2,3,1,256,1056]{3,4,2,1,0:T(8,128)} %pad_maximum_fusion.4) | data formatting | bytes 12976128 | tf_op jit(solution)/shard_map/stack | solution.py:221
  1105.2 79.0 %all-to-all-done.3 = f32[2,3,1,256,1056]{4,2,1,0,3:T(1,128)} async-done(((f32[2,3,1,256,1056]{4,2,1,0,3:T(1,128)}), f32[2,3,1,256,1056]{4,2,1,0,3:T(1,128)}, u32[]{:S(2)}, u32[]{:S(2)}) %all-to-all-start.3) | async-done | bytes 6488096 | tf_op jit(solution)/shard_map/all_to_all | solution.py:222
  1218.0 13.0 %fusion.34 = f32[128,3,128,32,1]{0,2,4,3,1:T(8,128)S(1)} fusion(f32[3,2,128,33,32]{2,1,4,3,0:T(2,128)} %squeeze.181, f32[2,33]{1,0:T(2,128)S(1)} %fusion.230, s32[2,33]{1,0:T(2,128)S(1)} %copy-done.32), kind=kOutput, calls=%fused_computation.57 | convolution fusion | flops 1245835008 | bytes 9536016 | tf_op jit(solution)/shard_map/cgybx,gbn->cxyn/dot_general | solution.py:127
  1231.1 16.9 %fusion.18 = (f32[32,128,128]{2,1,0:T(8,128)}, f32[32,128,128]{2,1,0:T(8,128)}) fusion(bf16[3,32,128,128]{3,2,1,0:T(8,128)(2,1)S(1)} %copy-done.26, f32[1,32,128,128]{3,2,1,0:T(8,128)S(1)} %copy-done.11, f32[1,32,128,128]{3,2,1,0:T(8,128)S(1)} %copy-done.7, f32[1,32,128,128]{3,2,1,0:T(8,128)S(1)} %copy-done.9, bf16[3,32,128,128]{3,2,1,0:T(8,128)(2,1)} %param.12, ...), kind=kOutput, calls=%fused_computation.30 | convolution fusion | flops 1262087936 | bytes 26313232 | tf_op jit(solution)/shard_map/cgybx,gbn->cxyn/dot_general | solution.py:127
  (220 shorter events, 343.3 us)
Async XLA Ops:
  4.1 19.1 %collective-permute-start.1 = (f32[1,32,1,128]{3,1,2,0:T(8,128)S(1)}, f32[1,32,1,128]{3,1,2,0:T(8,128)S(1)}, u32[]{:S(2)}, u32[]{:S(2)}) collective-permute-start(f32[1,32,1,128]{3,1,2,0:T(8,128)S(1)} %bitcast.437), channel_id=1, source_target_pairs={{0,1},{2,3},{4,5},{6,7},{8,9},{10,11},{12,13},{14,15},{16,17},{18,... | collective-permute-start | bytes 49160 | tf_op jit(solution)/shard_map/ppermute | solution.py:17
  7.7 10.9 collective-permute-start.4
  9.6 13.6 %collective-permute-start = (f32[1,1,128,128]{3,2,1,0:T(8,128)S(1)}, f32[1,1,128,128]{3,2,1,0:T(8,128)S(1)}, u32[]{:S(2)}, u32[]{:S(2)}) collective-permute-start(f32[1,1,128,128]{3,2,1,0:T(8,128)S(1)} %slice.326), channel_id=1, source_target_pairs={{0,2},{2,4},{4,6},{6,8},{8,10},{10,12},{12,14},{14,16},{16,18},{18... | collective-permute-start | bytes 196616 | tf_op jit(solution)/shard_map/ppermute | solution.py:17
  12.1 6.4 collective-permute-start.3
  34.5 18.9 %collective-permute-start.5 = (f32[2,32,1,128]{3,1,2,0:T(8,128)S(1)}, f32[2,32,1,128]{3,1,2,0:T(8,128)S(1)}, u32[]{:S(2)}, u32[]{:S(2)}) collective-permute-start(f32[2,32,1,128]{3,1,2,0:T(8,128)S(1)} %pad_maximum_fusion.17), channel_id=1, source_target_pairs={{0,1},{2,3},{4,5},{6,7},{8,9},{10,11},{12,13},{14,15},{16,17},{18,... | collective-permute-start | bytes 98312 | tf_op jit(solution)/shard_map/ppermute | solution.py:17
  46.5 6.9 collective-permute-start.7
  49.5 4.5 collective-permute-start.2
  52.0 11.4 collective-permute-start.8
  62.0 24.6 %collective-permute-start.11 = (f32[2,32,1,128]{3,1,2,0:T(8,128)}, f32[2,32,1,128]{3,1,2,0:T(8,128)S(1)}, u32[]{:S(2)}, u32[]{:S(2)}) collective-permute-start(f32[2,32,1,128]{3,1,2,0:T(8,128)} %pad_maximum_fusion.18), channel_id=1, source_target_pairs={{1,0},{3,2},{5,4},{7,6},{9,8},{11,10},{13,12},{15,14},{17,16},{19,... | collective-permute-start | bytes 98312 | tf_op jit(solution)/shard_map/ppermute | solution.py:17
  76.1 10.5 collective-permute-start.12
  79.8 6.8 collective-permute-start.9
  84.1 5.6 collective-permute-start.6
  104.6 20.5 %collective-permute-start.13 = (f32[2,32,1,128]{3,1,2,0:T(8,128)S(1)}, f32[2,32,1,128]{3,1,2,0:T(8,128)S(1)}, u32[]{:S(2)}, u32[]{:S(2)}) collective-permute-start(f32[2,32,1,128]{3,1,2,0:T(8,128)S(1)} %pad_maximum_fusion.19), channel_id=1, source_target_pairs={{0,1},{2,3},{4,5},{6,7},{8,9},{10,11},{12,13},{14,15},{16,17},{18,... | collective-permute-start | bytes 98312 | tf_op jit(solution)/shard_map/ppermute | solution.py:17
  116.4 8.8 collective-permute-start.14
  119.3 5.9 collective-permute-start.15
  122.5 6.6 collective-permute-start.10
  182.6 78.2 %all-to-all-start = ((f32[2,3,1,66,4096]{4,0,2,1,3:T(2,128)}), f32[2,3,1,66,4096]{4,0,2,1,3:T(2,128)}, u32[]{:S(2)}, u32[]{:S(2)}) async-start(f32[2,3,1,66,4096]{4,0,2,1,3:T(2,128)} %copy.135), calls=%async_computation | async-start | bytes 12976128 | tf_op jit(solution)/shard_map/all_to_all | solution.py:162
  320.1 162.3 %all-to-all-start.1 = ((f32[2,3,1,256,1056]{4,2,1,0,3:T(1,128)}), f32[2,3,1,256,1056]{4,2,1,0,3:T(1,128)}, u32[]{:S(2)}, u32[]{:S(2)}) async-start(f32[2,3,1,256,1056]{4,2,1,0,3:T(1,128)} %copy.144), calls=%async_computation.1 | async-start | bytes 14155776 | tf_op jit(solution)/shard_map/all_to_all | solution.py:170
  521.1 29.4 %copy-start.22 = (f32[3,16,16,33,32]{4,3,0,2,1:T(8,128)S(1)}, f32[3,16,16,33,32]{4,3,0,2,1:T(8,128)}, u32[]{:S(2)}) copy-start(f32[3,16,16,33,32]{4,3,0,2,1:T(8,128)} %reshape.520) | copy-start | bytes 9732100
  590.3 29.1 %copy-start.33 = (f32[3,16,33,512,1]{3,2,4,1,0:T(8,128)S(1)}, f32[3,16,33,512,1]{3,2,4,1,0:T(8,128)}, u32[]{:S(2)}) copy-start(f32[3,16,33,512,1]{3,2,4,1,0:T(8,128)} %fusion) | copy-start | bytes 9732100
  722.4 176.0 %all-to-all-start.2 = ((f32[2,3,1,512,528]{4,0,2,1,3:T(2,128)}), f32[2,3,1,512,528]{4,0,2,1,3:T(2,128)}, u32[]{:S(2)}, u32[]{:S(2)}) async-start(f32[2,3,1,512,528]{4,0,2,1,3:T(2,128)} %copy.151), calls=%async_computation.2 | async-start | bytes 15728640 | tf_op jit(solution)/shard_map/all_to_all | solution.py:214
  942.7 31.7 %copy-start.2 = (f32[3,16,32,16,33]{4,3,0,2,1:T(8,128)S(1)}, f32[3,16,32,16,33]{4,3,0,2,1:T(8,128)}, u32[]{:S(2)}) copy-start(f32[3,16,32,16,33]{4,3,0,2,1:T(8,128)} %reshape.522) | copy-start | bytes 9732100
  1016.7 34.0 %copy-start.1 = (f32[3,16,32,16,33]{4,3,0,2,1:T(8,128)S(1)}, f32[3,16,32,16,33]{4,3,0,2,1:T(8,128)}, u32[]{:S(2)}) copy-start(f32[3,16,32,16,33]{4,3,0,2,1:T(8,128)} %reshape.521) | copy-start | bytes 9732100
  1098.3 85.9 %all-to-all-start.3 = ((f32[2,3,1,256,1056]{4,2,1,0,3:T(1,128)}), f32[2,3,1,256,1056]{4,2,1,0,3:T(1,128)}, u32[]{:S(2)}, u32[]{:S(2)}) async-start(f32[2,3,1,256,1056]{4,2,1,0,3:T(1,128)} %copy.160), calls=%async_computation.3 | async-start | bytes 14155776 | tf_op jit(solution)/shard_map/all_to_all | solution.py:222
  (30 other events, 269.5 us)
where the time goes:
time: 1260 us; the launch traced here: 1250 us
  waiting for transfers between devices  478 us (38%)
  matrix products  349 us (28%)
  local copies, waits for them, and re-layouts  282 us (22%)
  other arithmetic  70.3 us (6%)
  starting transfers between devices  67.2 us (5%)
    dot_general x20, matrix products, contract(): return jnp.einsum(pattern, left, right, precision=lax.Precision.HIGHEST)  349 us
    all_to_all x1, waiting for transfers between devices, inverse_fields(): lax.all_to_all(packed, 'gx', split_axis=3, concat_axis=2, tiled=True)  171 us
    all_to_all x1, waiting for transfers between devices, forward(): lax.all_to_all(after_y, 'gx', split_axis=3, concat_axis=2, tiled=True)  153 us
    all_to_all x1, waiting for transfers between devices, inverse_fields(): lax.all_to_all(middle, 'gy', split_axis=3, concat_axis=2, tiled=True)  79 us
    all_to_all x1, waiting for transfers between devices, forward(): lax.all_to_all(packed, 'gy', split_axis=3, concat_axis=2, tiled=True)  71.9 us
    ppermute x16, starting transfers between devices, passed_along(): return lax.ppermute(block, axis, route)  40.7 us
    slice x2, local copies, waits for them, and re-layouts, forward(): pieces[0]  36.9 us
    slice x1, local copies, waits for them, and re-layouts, inverse_fields(): pieces[0]  29.6 us
  transfers between devices with their start and end apart: 20, of which 5 were waited for; matrix products, arithmetic and copies ran while one was open for 4% of the time, Pallas kernels for 0%

commit v1 on v0

v1 whole, which is shorter than its diff:
```python
import numpy as np
import ml_dtypes
import jax
import jax.numpy as jnp
from jax import lax
from jax.experimental import pallas as pl
from jax.experimental.pallas import tpu as pltpu
from jax.sharding import PartitionSpec as P

STEPS = 2
MOST_CHUNKS = 2
VMEM_BYTES = 56 * 2**20

time_step = 0.2


def passed_along(block, axis, distance):
    devices = range(lax.axis_size(axis))
    route = [(i - distance, i) for i in devices if i - distance in devices]
    return lax.ppermute(block, axis, route)


def x_rims(planes, offset):
    return passed_along(planes, "gx", offset)


def y_rims(planes, offset):
    return passed_along(planes, "gy", offset)


def with_next(field, rim, which):
    length = field.shape[which]
    return jnp.concatenate([lax.slice_in_dim(field, 1, length, axis=which), rim], axis=which)


def with_prior(field, rim, which):
    length = field.shape[which]
    return jnp.concatenate([rim, lax.slice_in_dim(field, 0, length - 1, axis=which)], axis=which)


def zero_rim(field, which):
    return jnp.zeros_like(lax.slice_in_dim(field, 0, 1, axis=which))


def stress_step(velocity, stress, lame_value, shear_value):
    x_speed, y_speed, z_speed = (velocity[0], velocity[1], velocity[2])
    prior_x = x_rims(x_speed[None, -1:], 1)
    next_x = x_rims(jnp.stack([y_speed[:1], z_speed[:1]]), -1)
    prior_y = y_rims(y_speed[None, :, -1:], 1)
    next_y = y_rims(jnp.stack([x_speed[:, :1], z_speed[:, :1]]), -1)
    strain_x = x_speed - with_prior(x_speed, prior_x[0], 0)
    strain_y = y_speed - with_prior(y_speed, prior_y[0], 1)
    strain_z = z_speed - with_prior(z_speed, zero_rim(z_speed, 2), 2)
    volume = strain_x + strain_y + strain_z
    normal_x = stress[0] + time_step * (lame_value * volume + 2.0 * shear_value * strain_x)
    normal_y = stress[1] + time_step * (lame_value * volume + 2.0 * shear_value * strain_y)
    normal_z = stress[2] + time_step * (lame_value * volume + 2.0 * shear_value * strain_z)
    shear_xy = stress[3] + time_step * shear_value * (
        with_next(x_speed, next_y[0], 1) - x_speed + (with_next(y_speed, next_x[0], 0) - y_speed)
    )
    shear_xz = stress[4] + time_step * shear_value * (
        with_next(x_speed, zero_rim(x_speed, 2), 2)
        - x_speed
        + (with_next(z_speed, next_x[1], 0) - z_speed)
    )
    shear_yz = stress[5] + time_step * shear_value * (
        with_next(y_speed, zero_rim(y_speed, 2), 2)
        - y_speed
        + (with_next(z_speed, next_y[1], 1) - z_speed)
    )
    return jnp.stack([normal_x, normal_y, normal_z, shear_xy, shear_xz, shear_yz])


def velocity_step(velocity, stress, buoy_value):
    normal_x, normal_y, normal_z = (stress[0], stress[1], stress[2])
    shear_xy, shear_xz, shear_yz = (stress[3], stress[4], stress[5])
    next_x = x_rims(normal_x[None, :1], -1)
    prior_x = x_rims(jnp.stack([shear_xy[-1:], shear_xz[-1:]]), 1)
    next_y = y_rims(normal_y[None, :, :1], -1)
    prior_y = y_rims(jnp.stack([shear_xy[:, -1:], shear_yz[:, -1:]]), 1)
    x_speed = velocity[0] + time_step * buoy_value * (
        with_next(normal_x, next_x[0], 0)
        - normal_x
        + (shear_xy - with_prior(shear_xy, prior_y[0], 1))
        + (shear_xz - with_prior(shear_xz, zero_rim(shear_xz, 2), 2))
    )
    y_speed = velocity[1] + time_step * buoy_value * (
        shear_xy
        - with_prior(shear_xy, prior_x[0], 0)
        + (with_next(normal_y, next_y[0], 1) - normal_y)
        + (shear_yz - with_prior(shear_yz, zero_rim(shear_yz, 2), 2))
    )
    z_speed = velocity[2] + time_step * buoy_value * (
        shear_xz
        - with_prior(shear_xz, prior_x[1], 0)
        + (shear_yz - with_prior(shear_yz, prior_y[1], 1))
        + (with_next(normal_z, zero_rim(normal_z, 2), 2) - normal_z)
    )
    return jnp.stack([x_speed, y_speed, z_speed])


def basis(length):
    half = length // 2
    wave = np.arange(half)
    place = np.arange(length)
    angle = (wave[:, None] * place[None, :] % length) * (2.0 * np.pi / length)
    cosine, sine = np.cos(angle), np.sin(angle)
    sine[0] = 1.0 - 2.0 * (place % 2)
    return np.concatenate([cosine, sine])


def waves_of(length):
    return np.tile(np.arange(length // 2, dtype=np.float64), 2)


def inverse_basis(length):
    weight = np.where(waves_of(length) == 0, 1.0, 2.0) / length
    return basis(length) * weight[:, None]


def turned(table):
    half = table.shape[0] // 2
    return np.concatenate([table[half:], -table[:half]]) * waves_of(table.shape[0])[:, None]


def halves(table):
    high = table.astype(ml_dtypes.bfloat16)
    low = (table - high.astype(np.float64)).astype(ml_dtypes.bfloat16)
    return np.stack([high, low])


def split(value):
    high = value.astype(jnp.bfloat16)
    return high, (value - high.astype(jnp.float32)).astype(jnp.bfloat16)


def times(left, right, dims=((1,), (0,))):
    def one(a, b):
        return lax.dot_general(a, b, (dims, ((), ())), preferred_element_type=jnp.float32)

    return one(left[0], right[0]) + (one(left[1], right[0]) + one(left[0], right[1]))


def joined(pieces, axis):
    return pieces[0] if len(pieces) == 1 else jnp.concatenate(pieces, axis=axis)


def fit(length, most):
    size = min(length, most)
    while length % size:
        size -= 1
    return size


def params():
    return pltpu.CompilerParams(vmem_limit_bytes=VMEM_BYTES)


def whole_block(shape):
    return pl.BlockSpec(shape, lambda *_: (0,) * len(shape))


def scalars():
    return pl.BlockSpec(memory_space=pltpu.SMEM)


class Plan:
    def __init__(self, brick):
        self.x, self.y, self.z = brick
        self.gx, self.gy = lax.axis_size("gx"), lax.axis_size("gy")
        self.nx, self.ny = self.x * self.gx, self.y * self.gy
        chunks = MOST_CHUNKS
        while chunks > 1 and self.z % (chunks * self.gy * self.gx):
            chunks -= 1
        self.chunks = chunks
        self.kz = self.z // (chunks * self.gy)
        self.parts = max(1, self.gx // self.kz)
        self.per = max(1, self.kz // self.gx)
        self.ky = self.ny // self.parts


def source(me, step, count):
    return lax.rem(me - step + count, count)


def z_forward(plan, place, velocity):
    x, y, z, kz = plan.x, plan.y, plan.z, plan.kz
    table = np.stack([halves(basis(z)), halves(turned(basis(z)))])
    table = table.reshape(2, 2, plan.chunks, plan.gy, kz, z)
    count = plan.chunks * plan.gy

    def kernel(place_ref, table_ref, v_ref, *outs):
        at = pl.program_id(0)
        me = place_ref[1]
        for comp in range(3):
            kind = 1 if comp == 2 else 0
            field = split(v_ref[comp, 0])
            for chunk in range(plan.chunks):
                for step in range(plan.gy):
                    group = lax.rem(me + step, plan.gy)
                    rows = (table_ref[kind, 0, chunk, group], table_ref[kind, 1, chunk, group])
                    value = times(rows, field, ((1,), (1,)))
                    outs[chunk * plan.gy + step][comp, pl.ds(at, kz, stride=x), :] = value

    outs = pl.pallas_call(
        kernel,
        grid=(x,),
        in_specs=[
            scalars(),
            whole_block(table.shape),
            pl.BlockSpec((3, 1, y, z), lambda i: (0, i, 0, 0)),
        ],
        out_specs=[whole_block((3, kz * x, y))] * count,
        out_shape=[jax.ShapeDtypeStruct((3, kz * x, y), jnp.float32)] * count,
        compiler_params=params(),
        cost_estimate=pl.CostEstimate(
            flops=18 * x * y * z * z, bytes_accessed=24 * x * y * z, transcendentals=0
        ),
        name="z_forward",
    )(place, jnp.asarray(table), velocity)
    outs = [out.reshape(3, kz, x, y) for out in outs]
    return [outs[c * plan.gy : (c + 1) * plan.gy] for c in range(plan.chunks)]


def swap_gy(blocks):
    count = len(blocks)
    moved = [blocks[0]]
    for step in range(1, count):
        route = [(i, (i + step) % count) for i in range(count)]
        moved.append(lax.ppermute(blocks[step], "gy", route))
    return moved


def y_forward(plan, place, blocks):
    x, y, ny, kz = plan.x, plan.y, plan.ny, plan.kz
    table = halves(basis(ny).T).reshape(2, plan.gy, y, ny)
    deep = fit(kz, 8)
    rows = deep * x
    half = ny // 2
    aligned = y % 128 == 0

    def kernel(place_ref, table_ref, *refs):
        ins, out = refs[:-1], refs[-1]
        me = place_ref[1]
        groups = [source(me, step, plan.gy) for step in range(plan.gy)]
        tables = [(table_ref[0, g], table_ref[1, g]) for g in groups]
        if aligned:
            tables = [tuple(joined([t[i] for t in tables], 0) for i in range(2))]

        def moved(comp):
            fields = [ref[comp].reshape(rows, y) for ref in ins]
            if aligned:
                fields = [joined(fields, 1)]
            return sum(times(split(f), t) for f, t in zip(fields, tables))

        wave = lax.broadcasted_iota(jnp.int32, (1, half), 1).astype(jnp.float32)
        out[:, 0] = moved(0).reshape(deep, x, ny)
        along, rest = moved(1), moved(2)
        out[:, 1, :, :half] = (rest[:, :half] + wave * along[:, half:]).reshape(deep, x, half)
        out[:, 1, :, half:] = (rest[:, half:] - wave * along[:, :half]).reshape(deep, x, half)

    return pl.pallas_call(
        kernel,
        grid=(kz // deep,),
        in_specs=[scalars(), whole_block(table.shape)]
        + [pl.BlockSpec((3, deep, x, y), lambda i: (0, i, 0, 0))] * plan.gy,
        out_specs=pl.BlockSpec((deep, 2, x, ny), lambda i: (i, 0, 0, 0)),
        out_shape=jax.ShapeDtypeStruct((kz, 2, x, ny), jnp.float32),
        compiler_params=params(),
        cost_estimate=pl.CostEstimate(
            flops=18 * kz * x * ny * ny, bytes_accessed=20 * kz * x * ny, transcendentals=0
        ),
        name="y_forward",
    )(place, jnp.asarray(table), *blocks)


def to_lines(plan, planes):
    if plan.parts > 1:
        planes = planes.reshape(plan.kz, 2, plan.x, plan.parts, plan.ky).transpose(0, 3, 1, 2, 4)
    planes = planes.reshape(plan.gx, plan.per, 2, plan.x, plan.ky)
    return lax.all_to_all(planes, "gx", 0, 0, tiled=True)


def to_planes(plan, lines):
    planes = lax.all_to_all(lines, "gx", 0, 0, tiled=True)
    if plan.parts > 1:
        planes = planes.reshape(plan.kz, plan.parts, 2, plan.x, plan.ky).transpose(0, 2, 3, 1, 4)
    return planes.reshape(plan.kz, 2, plan.x, plan.ny)


def x_lines(plan, place, lines, chunk):
    x, nx, ny, ky, gx = plan.x, plan.nx, plan.ny, plan.ky, plan.gx
    forth = halves(basis(nx))
    back = halves(-inverse_basis(nx).T)
    lanes = 128 if ky % 128 == 0 else ky
    half = nx // 2
    aligned = lanes % 128 == 0

    def kernel(place_ref, forth_ref, back_ref, in_ref, out_ref):
        me_x, me_y = place_ref[0], place_ref[1]
        which, lane = pl.program_id(0), pl.program_id(1)

        def through(table_ref, pair):
            table = (table_ref[0], table_ref[1])
            if aligned:
                both = times(table, split(jnp.concatenate(pair, axis=1)))
                return both[:, :lanes], both[:, lanes:]
            return tuple(times(table, split(value)) for value in pair)

        pair = [in_ref[:, 0, i].reshape(nx, lanes) for i in range(2)]
        along, rest = through(forth_ref, pair)
        wave_x = lax.broadcasted_iota(jnp.int32, (half, lanes), 0).astype(jnp.float32)
        slot_y = lax.broadcasted_iota(jnp.int32, (1, lanes), 1) + (
            lane * lanes + lax.rem(me_x, plan.parts) * ky
        )
        wave_y = lax.rem(slot_y, ny // 2).astype(jnp.float32)
        slot_z = (chunk * plan.gy + me_y) * plan.kz + me_x // plan.parts * plan.per + which
        wave_z = lax.rem(slot_z, plan.z // 2).astype(jnp.float32)
        scale = 1.0 / jnp.maximum(wave_x * wave_x + (wave_y * wave_y + wave_z * wave_z), 1.0)
        cosine = (rest[:half] + wave_x * along[half:]) * scale
        sine = (rest[half:] - wave_x * along[:half]) * scale
        plain = jnp.concatenate([cosine, sine], axis=0)
        slope = jnp.concatenate([wave_x * sine, -wave_x * cosine], axis=0)
        for i, value in enumerate(through(back_ref, [slope, plain])):
            out_ref[:, 0, i] = value.reshape(gx, x, lanes)

    block = pl.BlockSpec((gx, 1, 2, x, lanes), lambda i, j: (0, i, 0, 0, j))
    return pl.pallas_call(
        kernel,
        grid=(plan.per, ky // lanes),
        in_specs=[scalars(), whole_block(forth.shape), whole_block(back.shape), block],
        out_specs=block,
        out_shape=jax.ShapeDtypeStruct(lines.shape, jnp.float32),
        compiler_params=params(),
        cost_estimate=pl.CostEstimate(
            flops=24 * plan.per * ky * nx * nx,
            bytes_accessed=16 * plan.per * ky * nx,
            transcendentals=0,
        ),
        name="x_lines",
    )(place, jnp.asarray(forth), jnp.asarray(back), lines)


def y_inverse(plan, place, planes):
    x, y, ny, kz = plan.x, plan.y, plan.ny, plan.kz
    table = np.stack(np.split(inverse_basis(ny), plan.gy, axis=1))
    table = halves(table)
    deep = fit(kz, 8)
    rows = deep * x
    half = ny // 2
    aligned = y % 128 == 0

    def kernel(place_ref, table_ref, in_ref, *outs):
        me = place_ref[1]
        groups = [lax.rem(me + step, plan.gy) for step in range(plan.gy)]
        tables = [(table_ref[0, g], table_ref[1, g]) for g in groups]
        slope = in_ref[:, 0].reshape(rows, ny)
        plain = in_ref[:, 1].reshape(rows, ny)
        wave = lax.broadcasted_iota(jnp.int32, (1, half), 1).astype(jnp.float32)
        along = jnp.concatenate([wave * plain[:, half:], -wave * plain[:, :half]], axis=1)
        for comp, value in enumerate((slope, along, plain)):
            parts = split(value)
            if aligned:
                table = tuple(joined([t[i] for t in tables], 1) for i in range(2))
                found = times(parts, table)
                pieces = [found[:, s * y : (s + 1) * y] for s in range(plan.gy)]
            else:
                pieces = [times(parts, t) for t in tables]
            for out, piece in zip(outs, pieces):
                out[comp] = piece.reshape(deep, x, y)

    return pl.pallas_call(
        kernel,
        grid=(kz // deep,),
        in_specs=[
            scalars(),
            whole_block(table.shape),
            pl.BlockSpec((deep, 2, x, ny), lambda i: (i, 0, 0, 0)),
        ],
        out_specs=[pl.BlockSpec((3, deep, x, y), lambda i: (0, i, 0, 0))] * plan.gy,
        out_shape=[jax.ShapeDtypeStruct((3, kz, x, y), jnp.float32)] * plan.gy,
        compiler_params=params(),
        cost_estimate=pl.CostEstimate(
            flops=18 * kz * x * ny * ny, bytes_accessed=20 * kz * x * ny, transcendentals=0
        ),
        name="y_inverse",
    )(place, jnp.asarray(table), planes)


def images(plan, place, blocks, velocity, source_p, source_s):
    x, y, z, kz = plan.x, plan.y, plan.z, plan.kz
    table = np.stack([halves(inverse_basis(z)), halves(-turned(inverse_basis(z)))])
    table = table.reshape(2, 2, plan.chunks, plan.gy, kz, z)
    blocks = [block.reshape(3, kz * x, y) for group in blocks for block in group]

    def kernel(place_ref, table_ref, v_ref, p_ref, s_ref, *refs):
        ins, (image_p, image_s) = refs[:-2], refs[-2:]
        at = pl.program_id(0)
        me = place_ref[1]
        order = [
            (chunk, source(me, step, plan.gy))
            for chunk in range(plan.chunks)
            for step in range(plan.gy)
        ]
        total_p = total_s = 0.0
        for comp in range(3):
            kind = 1 if comp == 2 else 0
            value = joined([ref[comp, pl.ds(at, kz, stride=x), :] for ref in ins], 0)
            back = tuple(joined([table_ref[kind, i, c, g] for c, g in order], 0) for i in range(2))
            field = times(split(value), back, ((0,), (0,)))
            total_p += p_ref[comp, 0].astype(jnp.float32) * field
            total_s += s_ref[comp, 0].astype(jnp.float32) * (v_ref[comp, 0] - field)
        image_p[0] = total_p
        image_s[0] = total_s

    plane = pl.BlockSpec((3, 1, y, z), lambda i: (0, i, 0, 0))
    image = pl.BlockSpec((1, y, z), lambda i: (i, 0, 0))
    return pl.pallas_call(
        kernel,
        grid=(x,),
        in_specs=[scalars(), whole_block(table.shape), plane, plane, plane]
        + [whole_block((3, kz * x, y))] * len(blocks),
        out_specs=[image, image],
        out_shape=[jax.ShapeDtypeStruct((x, y, z), jnp.float32)] * 2,
        compiler_params=params(),
        cost_estimate=pl.CostEstimate(
            flops=18 * x * y * z * z, bytes_accessed=44 * x * y * z, transcendentals=0
        ),
        name="images",
    )(place, jnp.asarray(table), velocity, source_p, source_s, *blocks)


def shards(velocity, stress, lame_lambda, shear_modulus, buoyancy, source_p, source_s):
    lame_value = lame_lambda.astype(jnp.float32)
    shear_value = shear_modulus.astype(jnp.float32)
    buoy_value = buoyancy.astype(jnp.float32)
    for step_index in range(STEPS):
        stress = stress_step(velocity, stress, lame_value, shear_value)
        velocity = velocity_step(velocity, stress, buoy_value)
    plan = Plan(velocity.shape[1:])
    place = jnp.stack([lax.axis_index("gx"), lax.axis_index("gy")]).astype(jnp.int32)
    blocks = z_forward(plan, place, velocity)
    lines = [to_lines(plan, y_forward(plan, place, swap_gy(group))) for group in blocks]
    lines = [x_lines(plan, place, part, chunk) for chunk, part in enumerate(lines)]
    blocks = [swap_gy(y_inverse(plan, place, to_planes(plan, part))) for part in lines]
    return tuple(images(plan, place, blocks, velocity, source_p, source_s))


def solution(mesh):
    in_specs = (
        P(None, "gx", "gy", None),
        P(None, "gx", "gy", None),
        P("gx", "gy", None),
        P("gx", "gy", None),
        P("gx", "gy", None),
        P(None, "gx", "gy", None),
        P(None, "gx", "gy", None),
    )
    out_specs = (P("gx", "gy", None), P("gx", "gy", None))
    return jax.shard_map(shards, mesh=mesh, in_specs=in_specs, out_specs=out_specs, check_vma=False)
```

time: 1260 us -> 512 us (0.41)
  matrix products: 349 us -> 0 us
  waiting for transfers between devices: 478 us -> 226 us
  local copies, waits for them, and re-layouts: 282 us -> 55.7 us
  Pallas kernels: 0 us -> 100 us
  other arithmetic: 70.3 us -> 53.9 us
    all_to_all x4, waiting for transfers between devices: 475 us -> 119 us  [the longest x2 77.6 us: to_planes(): planes = lax.all_to_all(lines, 'gx', 0, 0, tiled=True)]
    dot_general x20 -> x0, matrix products: 349 us -> none  [contract(): return jnp.einsum(pattern, left, right, precision=lax.Precision.HIGHEST)]
    ppermute x0 -> x4, waiting for transfers between devices: none -> 104 us  [swap_gy(): moved.append(lax.ppermute(blocks[step], 'gy', route))]
    pallas_call x0 -> x8, Pallas kernels: none -> 100 us  [the longest x1 31.7 us: z_forward(): pl.pallas_call(kernel, grid=(x,), in_specs=[scalars(), whole_block(table....]
    slice x6 -> x0, local copies, waits for them, and re-layouts: 91.2 us -> none  [the longest x2 36.9 us: forward(): pieces[0]]
    another operation x8 -> x0, local copies, waits for them, and re-layouts: 72.3 us -> none  [the longest x3 20 us: inverse_fields(): jnp.stack([real_part, imag_part])]
    squeeze x6 -> x0, local copies, waits for them, and re-layouts: 63.4 us -> none  [the longest x1 14.8 us: inverse_fields(): pieces[0]]
    another operation x5 -> x1, other arithmetic: 18.7 us -> 0.59 us  [shards(): jnp.stack([lax.axis_index('gx'), lax.axis_index('gy')]).astype(jnp.int32)]
  transfers between devices with their start and end apart: 20 -> 24, of which waited for: 5 -> 8; matrix products, arithmetic and copies ran while one was open for 4% -> 12% of each run, Pallas kernels for 0% -> 7%
where the time goes in v1:
time: 512 us; the launch traced here: 509 us
  waiting for transfers between devices  226 us (44%)
  Pallas kernels  100 us (20%)
  starting transfers between devices  71.9 us (14%)
  local copies, waits for them, and re-layouts  55.7 us (11%)
  other arithmetic  53.9 us (11%)
    ppermute x4, waiting for transfers between devices, swap_gy(): moved.append(lax.ppermute(blocks[step], 'gy', route))  104 us
    all_to_all x2, waiting for transfers between devices, to_planes(): planes = lax.all_to_all(lines, 'gx', 0, 0, tiled=True)  77.6 us
    all_to_all x2, waiting for transfers between devices, to_lines(): return lax.all_to_all(planes, 'gx', 0, 0, tiled=True)  41.6 us
    ppermute x16, starting transfers between devices, passed_along(): return lax.ppermute(block, axis, route)  40.9 us
    pallas_call x1, Pallas kernels, z_forward(): pl.pallas_call(kernel, grid=(x,), in_specs=[scalars(), whole_block(table....  31.7 us
    pallas_call x1, Pallas kernels, images(): pl.pallas_call(kernel, grid=(x,), in_specs=[scalars(), whole_block(table....  28.2 us
    slice x16, local copies, waits for them, and re-layouts, with_next(): lax.slice_in_dim(field, 1, length, axis=which)  25.3 us
    pallas_call x2, Pallas kernels, x_lines(): pl.pallas_call(kernel, grid=(plan.per, ky // lanes), in_specs=[scalars(),...  20.5 us
  transfers between devices with their start and end apart: 24, of which 8 were waited for; matrix products, arithmetic and copies ran while one was open for 12% of the time, Pallas kernels for 7%

profile of v1, /device:TPU:12, one launch (start us, length us, event | category | flops | bytes accessed | tf_op | source)
XLA Modules:
  0.0 508.9 jit_solution(719314995639863058)
XLA Ops:
  35.9 6.7 %fusion.23 = (f32[32,128,128]{2,1,0:T(8,128)S(1)}, f32[32,128,128]{2,1,0:T(8,128)S(1)}, f32[32,128,128]{2,1,0:T(8,128)S(1)}) fusion(f32[32,128,128]{2,1,0:T(8,128)S(1)} %get-tuple-element.21, bf16[32,128,128]{2,1,0:T(8,128)(2,1)S(1)} %copy-done.8, f32[6,32,128,128]{3,2,1,0:T(8,128)} %param.18, f32[32,127,128]{2,1,0:T(8,128)} %bitcast.197, ...), kind=kLoop, calls=%fused_computation.28 | loop fusion | flops 10485760 | bytes 28278784 | tf_op jit(solution)/shard_map/add | solution.py:56
  64.0 5.4 %fusion.39 = (f32[32,128,128]{2,1,0:T(8,128)S(1)}, f32[32,128,128]{2,1,0:T(8,128)S(1)}) fusion(f32[32,128,128]{2,1,0:T(8,128)S(1)} %get-tuple-element.20, f32[1,128,128]{2,1,0:T(8,128)} %bitcast.212, f32[31,128,128]{2,1,0:T(8,128)} %slice.362, f32[32,128,128]{2,1,0:T(8,128)S(1)} %fusion.12, f32[32,127,128]{2,1,0:T(8,128)S(1)} %bitcast.189, ...), kind=kLoop, calls=%fused_computation.47 | loop fusion | flops 10485760 | bytes 32473088 | tf_op jit(solution)/shard_map/add | solution.py:81
  99.2 5.3 %fusion.29 = (f32[32,128,128]{2,1,0:T(8,128)}, f32[32,128,128]{2,1,0:T(8,128)}, f32[32,128,128]{2,1,0:T(8,128)S(1)}) fusion(f32[32,128,128]{2,1,0:T(8,128)S(1)} %copy-done.5, bf16[32,128,128]{2,1,0:T(8,128)(2,1)S(1)} %copy-done.9, f32[32,128,128]{2,1,0:T(8,128)S(1)} %get-tuple-element.26, f32[31,128,128]{2,1,0:T(8,128)S(1)} %slice.380, ...), kind=kLoop, calls=%fused_computation.34 | loop fusion | flops 12058624 | bytes 29343744 | tf_op jit(solution)/shard_map/add | solution.py:55
  104.5 8.7 %fusion.32 = (f32[32,128,128]{2,1,0:T(8,128)}, f32[32,128,128]{2,1,0:T(8,128)S(1)}, f32[32,128,128]{2,1,0:T(8,128)}, f32[32,128,128]{2,1,0:T(8,128)}) fusion(f32[32,128,128]{2,1,0:T(8,128)S(1)} %get-tuple-element.22, f32[32,128,128]{2,1,0:T(8,128)} %get-tuple-element.19, bf16[32,128,128]{2,1,0:T(8,128)(2,1)} %param.20, f32[32,128,128]{2,1,0:T(8,128)S(1)} %fusion.46, ...), kind=kLoop, calls=%fused_computation.37 | loop fusion | flops 13631488 | bytes 38748160 | tf_op jit(solution)/shard_map/add | solution.py:56
  134.9 5.2 %fusion.63 = f32[1,32,128,128]{3,2,1,0:T(8,128)} fusion(f32[32,128,128]{2,1,0:T(8,128)S(1)} %fusion.46, f32[32,128,128]{2,1,0:T(8,128)S(1)} %get-tuple-element.34, f32[31,128,128]{2,1,0:T(8,128)} %slice.420, f32[1,128,128]{2,1,0:T(8,128)S(1)} %get-tuple-element.41, f32[32,128,128]{2,1,0:T(8,128)S(1)} %copy-done.10, f32[32,1,128]{2,1,0:T(1,128)S(1)} %bitcast.233, ...), kind=kLoop, calls=%fused_computation.89 | loop fusion | flops 5767168 | bytes 17809408 | tf_op jit(solution)/shard_map/stack | solution.py:99
  140.2 5.4 %fusion.55 = (f32[1,32,128,128]{3,2,1,0:T(8,128)S(1)}, f32[1,32,128,128]{3,2,1,0:T(8,128)S(1)}) fusion(f32[32,128,128]{2,1,0:T(8,128)S(1)} %get-tuple-element.26, f32[32,128,128]{2,1,0:T(8,128)S(1)} %copy-done.13, f32[1,128,128]{2,1,0:T(8,128)S(1)} %bitcast.210, f32[31,128,128]{2,1,0:T(8,128)} %slice.396, f32[32,128,128]{2,1,0:T(8,128)S(1)} %get-tuple-element.34, ...), kind=kLoop, calls=%fused_computation.75 | loop fusion | flops 10485760 | bytes 32473088 | tf_op jit(solution)/shard_map/stack | solution.py:99
  148.7 31.7 %z_forward.1 = (f32[3,1024,128]{2,1,0:T(8,128)}, f32[3,1024,128]{2,1,0:T(8,128)}, f32[3,1024,128]{2,1,0:T(8,128)}, f32[3,1024,128]{2,1,0:T(8,128)}) custom-call(s32[2]{0:T(128)} %pad_add_fusion.place_ref, bf16[2,2,2,2,32,128]{5,4,3,2,1,0:T(8,128)(2,1)} %constant.26.clone.table_ref, f32[3,32,128,128]{3,2,1,0:T(8,128)} %pad_maximum_fusion.v_ref), custom_call_target="tpu_custom_call" | custom-call | flops 1207959552 | bytes 12582912 | tf_op jit(solution)/shard_map/z_forward/pallas_call | solution.py:205
  182.8 33.5 %collective-permute-done.18.refs_1_ = f32[3,32,32,128]{3,2,1,0:T(8,128)S(1)} collective-permute-done((f32[3,32,32,128]{3,2,1,0:T(8,128)}, f32[3,32,32,128]{3,2,1,0:T(8,128)S(1)}, u32[]{:S(2)}, u32[]{:S(2)}) %collective-permute-start.18) | collective-permute-done | bytes 1572896 | tf_op jit(solution)/shard_map/ppermute | solution.py:230
  217.5 4.9 y_forward.3
  222.4 8.2 %all-to-all-start.2 = ((f32[16,2,2,32,256]{4,3,2,1,0:T(8,128)}), f32[16,2,2,32,256]{4,3,2,1,0:T(8,128)S(1)}, u32[]{:S(2)}, u32[]{:S(2)}) async-start(f32[16,2,2,32,256]{4,3,2,1,0:T(8,128)} %bitcast.201), calls=%async_computation.2 | async-start | bytes 4194304 | tf_op jit(solution)/shard_map/all_to_all | solution.py:281
  232.4 34.9 %collective-permute-done.16.refs_1_ = f32[3,32,32,128]{3,2,1,0:T(8,128)S(1)} collective-permute-done((f32[3,32,32,128]{3,2,1,0:T(8,128)}, f32[3,32,32,128]{3,2,1,0:T(8,128)S(1)}, u32[]{:S(2)}, u32[]{:S(2)}) %collective-permute-start.16) | collective-permute-done | bytes 1572896 | tf_op jit(solution)/shard_map/ppermute | solution.py:230
  268.4 4.9 y_forward.2
  279.2 5.1 all-to-all-start
  284.3 10.3 %x_lines.3 = f32[16,2,2,32,256]{4,3,2,1,0:T(8,128)} custom-call(s32[2]{0:T(128)} %pad_add_fusion.place_ref, bf16[2,512,512]{2,1,0:T(8,128)(2,1)} %constant.28.clone.forth_ref, bf16[2,512,512]{2,1,0:T(8,128)(2,1)} %constant.29.clone.back_ref, f32[16,2,2,32,256]{4,3,2,1,0:T(8,128)} %copy-done.21), custom_call_target="tpu_custom_call" | custom-call | flops 3221225472 | bytes 4194304 | tf_op jit(solution)/shard_map/x_lines/pallas_call | solution.py:328
  294.6 37.1 %all-to-all-done.in_ref = f32[16,2,2,32,256]{4,3,2,1,0:T(8,128)} async-done(((f32[16,2,2,32,256]{4,3,2,1,0:T(8,128)}), f32[16,2,2,32,256]{4,3,2,1,0:T(8,128)}, u32[]{:S(2)}, u32[]{:S(2)}) %all-to-all-start) | async-done | bytes 2097184 | tf_op jit(solution)/shard_map/all_to_all | solution.py:281
  331.7 5.1 all-to-all-start.3
  336.7 10.3 %x_lines.2 = f32[16,2,2,32,256]{4,3,2,1,0:T(8,128)} custom-call(s32[2]{0:T(128)} %pad_add_fusion.place_ref, bf16[2,512,512]{2,1,0:T(8,128)(2,1)} %constant.28.clone.forth_ref, bf16[2,512,512]{2,1,0:T(8,128)(2,1)} %constant.29.clone.back_ref, f32[16,2,2,32,256]{4,3,2,1,0:T(8,128)} %all-to-all-done.in_ref), custom_call_target="tpu_custom_call" | custom-call | flops 3221225472 | bytes 4194304 | tf_op jit(solution)/shard_map/x_lines/pallas_call | solution.py:328
  347.0 37.0 %all-to-all-done.3 = f32[16,2,2,32,256]{4,3,2,1,0:T(8,128)S(1)} async-done(((f32[16,2,2,32,256]{4,3,2,1,0:T(8,128)}), f32[16,2,2,32,256]{4,3,2,1,0:T(8,128)S(1)}, u32[]{:S(2)}, u32[]{:S(2)}) %all-to-all-start.3) | async-done | bytes 2097184 | tf_op jit(solution)/shard_map/all_to_all | solution.py:285
  385.3 5.1 all-to-all-start.1
  390.4 5.0 y_inverse.3
  397.1 40.6 %all-to-all-done.1 = f32[16,2,2,32,256]{4,3,2,1,0:T(8,128)} async-done(((f32[16,2,2,32,256]{4,3,2,1,0:T(8,128)}), f32[16,2,2,32,256]{4,3,2,1,0:T(8,128)}, u32[]{:S(2)}, u32[]{:S(2)}) %all-to-all-start.1) | async-done | bytes 2097184 | tf_op jit(solution)/shard_map/all_to_all | solution.py:285
  437.7 4.9 y_inverse.2
  444.4 35.1 %collective-permute-done.17 = f32[3,32,32,128]{3,2,1,0:T(8,128)S(1)} collective-permute-done((f32[3,32,32,128]{3,2,1,0:T(8,128)}, f32[3,32,32,128]{3,2,1,0:T(8,128)S(1)}, u32[]{:S(2)}, u32[]{:S(2)}) %collective-permute-start.17) | collective-permute-done | bytes 1572896 | tf_op jit(solution)/shard_map/ppermute | solution.py:230
  480.7 28.2 %images.1 = (f32[32,128,128]{2,1,0:T(8,128)}, f32[32,128,128]{2,1,0:T(8,128)}) custom-call(s32[2]{0:T(128)} %pad_add_fusion.place_ref, bf16[2,2,2,2,32,128]{5,4,3,2,1,0:T(8,128)(2,1)} %constant.31.clone.table_ref, f32[3,32,128,128]{3,2,1,0:T(8,128)} %pad_maximum_fusion.v_ref, bf16[3,32,128,128]{3,2,1,0:T(8,128)(2,1)} %p_ref.1, ...), custom_call_target="tpu_custom_call" | custom-call | flops 1207959552 | bytes 23068672 | tf_op jit(solution)/shard_map/images/pallas_call | solution.py:418
  (169 shorter events, 128.9 us)
Async XLA Ops:
  4.7 26.4 %collective-permute-start.1 = (f32[1,32,1,128]{3,1,2,0:T(8,128)}, f32[1,32,1,128]{3,1,2,0:T(8,128)S(1)}, u32[]{:S(2)}, u32[]{:S(2)}) collective-permute-start(f32[1,32,1,128]{3,1,2,0:T(8,128)} %bitcast.7), channel_id=1, source_target_pairs={{0,1},{2,3},{4,5},{6,7},{8,9},{10,11},{12,13},{14,15},{16,17},{18,... | collective-permute-start | bytes 49160 | tf_op jit(solution)/shard_map/ppermute | solution.py:20
  8.9 16.6 %collective-permute-start.4 = (f32[2,1,128,128]{3,2,1,0:T(8,128)}, f32[2,1,128,128]{3,2,1,0:T(8,128)}, u32[]{:S(2)}, u32[]{:S(2)}) collective-permute-start(f32[2,1,128,128]{3,2,1,0:T(8,128)} %stack.95), channel_id=1, source_target_pairs={{2,0},{4,2},{6,4},{8,6},{10,8},{12,10},{14,12},{16,14},{18,16},{20... | collective-permute-start | bytes 393224 | tf_op jit(solution)/shard_map/ppermute | solution.py:20
  11.5 19.7 %collective-permute-start = (f32[1,1,128,128]{3,2,1,0:T(8,128)}, f32[1,1,128,128]{3,2,1,0:T(8,128)}, u32[]{:S(2)}, u32[]{:S(2)}) collective-permute-start(f32[1,1,128,128]{3,2,1,0:T(8,128)} %slice.275), channel_id=1, source_target_pairs={{0,2},{2,4},{4,6},{6,8},{8,10},{10,12},{12,14},{14,16},{16,18},{18... | collective-permute-start | bytes 196616 | tf_op jit(solution)/shard_map/ppermute | solution.py:20
  14.0 11.6 %collective-permute-start.3 = (f32[2,32,1,128]{3,1,2,0:T(8,128)S(1)}, f32[2,32,1,128]{3,1,2,0:T(8,128)S(1)}, u32[]{:S(2)}, u32[]{:S(2)}) collective-permute-start(f32[2,32,1,128]{3,1,2,0:T(8,128)S(1)} %pad_maximum_fusion.4), channel_id=1, source_target_pairs={{1,0},{3,2},{5,4},{7,6},{9,8},{11,10},{13,12},{15,14},{17,16},{19,... | collective-permute-start | bytes 98312 | tf_op jit(solution)/shard_map/ppermute | solution.py:20
  42.7 20.1 %collective-permute-start.5 = (f32[2,32,1,128]{3,1,2,0:T(8,128)S(1)}, f32[2,32,1,128]{3,1,2,0:T(8,128)S(1)}, u32[]{:S(2)}, u32[]{:S(2)}) collective-permute-start(f32[2,32,1,128]{3,1,2,0:T(8,128)S(1)} %pad_maximum_fusion.5), channel_id=1, source_target_pairs={{0,1},{2,3},{4,5},{6,7},{8,9},{10,11},{12,13},{14,15},{16,17},{18,... | collective-permute-start | bytes 98312 | tf_op jit(solution)/shard_map/ppermute | solution.py:20
  55.8 6.9 %collective-permute-start.7 = (f32[2,1,128,128]{3,2,1,0:T(8,128)S(1)}, f32[2,1,128,128]{3,2,1,0:T(8,128)S(1)}, u32[]{:S(2)}, u32[]{:S(2)}) collective-permute-start(f32[2,1,128,128]{3,2,1,0:T(8,128)S(1)} %pad_maximum_fusion.1), channel_id=1, source_target_pairs={{0,2},{2,4},{4,6},{6,8},{8,10},{10,12},{12,14},{14,16},{16,18},{18... | collective-permute-start | bytes 393224 | tf_op jit(solution)/shard_map/ppermute | solution.py:20
  58.9 4.5 collective-permute-start.2
  61.4 11.4 %collective-permute-start.8 = (f32[1,32,1,128]{3,1,2,0:T(8,128)}, f32[1,32,1,128]{3,1,2,0:T(8,128)}, u32[]{:S(2)}, u32[]{:S(2)}) collective-permute-start(f32[1,32,1,128]{3,1,2,0:T(8,128)} %bitcast.33), channel_id=1, source_target_pairs={{1,0},{3,2},{5,4},{7,6},{9,8},{11,10},{13,12},{15,14},{17,16},{19,... | collective-permute-start | bytes 49160 | tf_op jit(solution)/shard_map/ppermute | solution.py:20
  71.4 24.7 %collective-permute-start.11 = (f32[2,32,1,128]{3,1,2,0:T(8,128)}, f32[2,32,1,128]{3,1,2,0:T(8,128)S(1)}, u32[]{:S(2)}, u32[]{:S(2)}) collective-permute-start(f32[2,32,1,128]{3,1,2,0:T(8,128)} %pad_maximum_fusion.6), channel_id=1, source_target_pairs={{1,0},{3,2},{5,4},{7,6},{9,8},{11,10},{13,12},{15,14},{17,16},{19,... | collective-permute-start | bytes 98312 | tf_op jit(solution)/shard_map/ppermute | solution.py:20
  85.6 10.5 %collective-permute-start.12 = (f32[2,1,128,128]{3,2,1,0:T(8,128)S(1)}, f32[2,1,128,128]{3,2,1,0:T(8,128)S(1)}, u32[]{:S(2)}, u32[]{:S(2)}) collective-permute-start(f32[2,1,128,128]{3,2,1,0:T(8,128)S(1)} %pad_maximum_fusion.2), channel_id=1, source_target_pairs={{2,0},{4,2},{6,4},{8,6},{10,8},{12,10},{14,12},{16,14},{18,16},{20... | collective-permute-start | bytes 393224 | tf_op jit(solution)/shard_map/ppermute | solution.py:20
  89.3 6.8 %collective-permute-start.9 = (f32[1,32,1,128]{3,1,2,0:T(8,128)S(1)}, f32[1,32,1,128]{3,1,2,0:T(8,128)S(1)}, u32[]{:S(2)}, u32[]{:S(2)}) collective-permute-start(f32[1,32,1,128]{3,1,2,0:T(8,128)S(1)} %bitcast.234), channel_id=1, source_target_pairs={{0,1},{2,3},{4,5},{6,7},{8,9},{10,11},{12,13},{14,15},{16,17},{18,... | collective-permute-start | bytes 49160 | tf_op jit(solution)/shard_map/ppermute | solution.py:20
  93.6 5.6 %collective-permute-start.6 = (f32[1,1,128,128]{3,2,1,0:T(8,128)S(1)}, f32[1,1,128,128]{3,2,1,0:T(8,128)S(1)}, u32[]{:S(2)}, u32[]{:S(2)}) collective-permute-start(f32[1,1,128,128]{3,2,1,0:T(8,128)S(1)} %copy-done.29), channel_id=1, source_target_pairs={{0,2},{2,4},{4,6},{6,8},{8,10},{10,12},{12,14},{14,16},{16,18},{18... | collective-permute-start | bytes 196616 | tf_op jit(solution)/shard_map/ppermute | solution.py:20
  114.1 20.7 %collective-permute-start.13 = (f32[2,32,1,128]{3,1,2,0:T(8,128)S(1)}, f32[2,32,1,128]{3,1,2,0:T(8,128)S(1)}, u32[]{:S(2)}, u32[]{:S(2)}) collective-permute-start(f32[2,32,1,128]{3,1,2,0:T(8,128)S(1)} %pad_maximum_fusion.7), channel_id=1, source_target_pairs={{0,1},{2,3},{4,5},{6,7},{8,9},{10,11},{12,13},{14,15},{16,17},{18,... | collective-permute-start | bytes 98312 | tf_op jit(solution)/shard_map/ppermute | solution.py:20
  125.8 9.1 %collective-permute-start.14 = (f32[2,1,128,128]{3,2,1,0:T(8,128)S(1)}, f32[2,1,128,128]{3,2,1,0:T(8,128)S(1)}, u32[]{:S(2)}, u32[]{:S(2)}) collective-permute-start(f32[2,1,128,128]{3,2,1,0:T(8,128)S(1)} %pad_maximum_fusion.3), channel_id=1, source_target_pairs={{0,2},{2,4},{4,6},{6,8},{8,10},{10,12},{12,14},{14,16},{16,18},{18... | collective-permute-start | bytes 393224 | tf_op jit(solution)/shard_map/ppermute | solution.py:20
  128.7 6.1 %collective-permute-start.15 = (f32[1,32,1,128]{3,1,2,0:T(8,128)S(1)}, f32[1,32,1,128]{3,1,2,0:T(8,128)S(1)}, u32[]{:S(2)}, u32[]{:S(2)}) collective-permute-start(f32[1,32,1,128]{3,1,2,0:T(8,128)S(1)} %bitcast.235), channel_id=1, source_target_pairs={{1,0},{3,2},{5,4},{7,6},{9,8},{11,10},{13,12},{15,14},{17,16},{19,... | collective-permute-start | bytes 49160 | tf_op jit(solution)/shard_map/ppermute | solution.py:20
  132.0 8.2 %collective-permute-start.10 = (f32[1,1,128,128]{3,2,1,0:T(8,128)S(1)}, f32[1,1,128,128]{3,2,1,0:T(8,128)S(1)}, u32[]{:S(2)}, u32[]{:S(2)}) collective-permute-start(f32[1,1,128,128]{3,2,1,0:T(8,128)S(1)} %slice_bitcast_fusion.14), channel_id=1, source_target_pairs={{2,0},{4,2},{6,4},{8,6},{10,8},{12,10},{14,12},{16,14},{18,16},{20... | collective-permute-start | bytes 196616 | tf_op jit(solution)/shard_map/ppermute | solution.py:20
  180.4 35.9 %collective-permute-start.18 = (f32[3,32,32,128]{3,2,1,0:T(8,128)}, f32[3,32,32,128]{3,2,1,0:T(8,128)S(1)}, u32[]{:S(2)}, u32[]{:S(2)}) collective-permute-start(f32[3,32,32,128]{3,2,1,0:T(8,128)} %bitcast.237), channel_id=1, source_target_pairs={{0,1},{1,0},{2,3},{3,2},{4,5},{5,4},{6,7},{7,6},{8,9},{9,8},{10,11... | collective-permute-start | bytes 4718600 | tf_op jit(solution)/shard_map/ppermute | solution.py:230
  222.4 55.5 %all-to-all-start.2 = ((f32[16,2,2,32,256]{4,3,2,1,0:T(8,128)}), f32[16,2,2,32,256]{4,3,2,1,0:T(8,128)S(1)}, u32[]{:S(2)}, u32[]{:S(2)}) async-start(f32[16,2,2,32,256]{4,3,2,1,0:T(8,128)} %bitcast.201), calls=%async_computation.2 | async-start | bytes 4194304 | tf_op jit(solution)/shard_map/all_to_all | solution.py:281
  230.6 36.7 %collective-permute-start.16 = (f32[3,32,32,128]{3,2,1,0:T(8,128)}, f32[3,32,32,128]{3,2,1,0:T(8,128)S(1)}, u32[]{:S(2)}, u32[]{:S(2)}) collective-permute-start(f32[3,32,32,128]{3,2,1,0:T(8,128)} %bitcast.236), channel_id=1, source_target_pairs={{0,1},{1,0},{2,3},{3,2},{4,5},{5,4},{6,7},{7,6},{8,9},{9,8},{10,11... | collective-permute-start | bytes 4718600 | tf_op jit(solution)/shard_map/ppermute | solution.py:230
  279.2 52.4 %all-to-all-start = ((f32[16,2,2,32,256]{4,3,2,1,0:T(8,128)}), f32[16,2,2,32,256]{4,3,2,1,0:T(8,128)}, u32[]{:S(2)}, u32[]{:S(2)}) async-start(f32[16,2,2,32,256]{4,3,2,1,0:T(8,128)} %bitcast.202), calls=%async_computation | async-start | bytes 4194304 | tf_op jit(solution)/shard_map/all_to_all | solution.py:281
  331.7 52.3 %all-to-all-start.3 = ((f32[16,2,2,32,256]{4,3,2,1,0:T(8,128)}), f32[16,2,2,32,256]{4,3,2,1,0:T(8,128)S(1)}, u32[]{:S(2)}, u32[]{:S(2)}) async-start(f32[16,2,2,32,256]{4,3,2,1,0:T(8,128)} %x_lines.3), calls=%async_computation.3 | async-start | bytes 4194304 | tf_op jit(solution)/shard_map/all_to_all | solution.py:285
  385.3 52.4 %all-to-all-start.1 = ((f32[16,2,2,32,256]{4,3,2,1,0:T(8,128)}), f32[16,2,2,32,256]{4,3,2,1,0:T(8,128)}, u32[]{:S(2)}, u32[]{:S(2)}) async-start(f32[16,2,2,32,256]{4,3,2,1,0:T(8,128)} %x_lines.2), calls=%async_computation.1 | async-start | bytes 4194304 | tf_op jit(solution)/shard_map/all_to_all | solution.py:285
  395.4 49.0 %collective-permute-start.19 = (f32[3,32,32,128]{3,2,1,0:T(8,128)}, f32[3,32,32,128]{3,2,1,0:T(8,128)S(1)}, u32[]{:S(2)}, u32[]{:S(2)}) collective-permute-start(f32[3,32,32,128]{3,2,1,0:T(8,128)} %get-tuple-element.17), channel_id=1, source_target_pairs={{0,1},{1,0},{2,3},{3,2},{4,5},{5,4},{6,7},{7,6},{8,9},{9,8},{10,11... | collective-permute-start | bytes 4718600 | tf_op jit(solution)/shard_map/ppermute | solution.py:230
  442.7 36.8 %collective-permute-start.17 = (f32[3,32,32,128]{3,2,1,0:T(8,128)}, f32[3,32,32,128]{3,2,1,0:T(8,128)S(1)}, u32[]{:S(2)}, u32[]{:S(2)}) collective-permute-start(f32[3,32,32,128]{3,2,1,0:T(8,128)} %get-tuple-element.13), channel_id=1, source_target_pairs={{0,1},{1,0},{2,3},{3,2},{4,5},{5,4},{6,7},{7,6},{8,9},{9,8},{10,11... | collective-permute-start | bytes 4718600 | tf_op jit(solution)/shard_map/ppermute | solution.py:230
  (32 other events, 265.7 us)

commit v2 on v1

--- a/solution.py
+++ b/solution.py
@@ -20,83 +20,241 @@
     return lax.ppermute(block, axis, route)
 
 
-def x_rims(planes, offset):
-    return passed_along(planes, "gx", offset)
-
-
-def y_rims(planes, offset):
-    return passed_along(planes, "gy", offset)
-
-
-def with_next(field, rim, which):
-    length = field.shape[which]
-    return jnp.concatenate([lax.slice_in_dim(field, 1, length, axis=which), rim], axis=which)
-
-
-def with_prior(field, rim, which):
-    length = field.shape[which]
-    return jnp.concatenate([rim, lax.slice_in_dim(field, 0, length - 1, axis=which)], axis=which)
-
-
-def zero_rim(field, which):
-    return jnp.zeros_like(lax.slice_in_dim(field, 0, 1, axis=which))
-
-
-def stress_step(velocity, stress, lame_value, shear_value):
-    x_speed, y_speed, z_speed = (velocity[0], velocity[1], velocity[2])
-    prior_x = x_rims(x_speed[None, -1:], 1)
-    next_x = x_rims(jnp.stack([y_speed[:1], z_speed[:1]]), -1)
-    prior_y = y_rims(y_speed[None, :, -1:], 1)
-    next_y = y_rims(jnp.stack([x_speed[:, :1], z_speed[:, :1]]), -1)
-    strain_x = x_speed - with_prior(x_speed, prior_x[0], 0)
-    strain_y = y_speed - with_prior(y_speed, prior_y[0], 1)
-    strain_z = z_speed - with_prior(z_speed, zero_rim(z_speed, 2), 2)
-    volume = strain_x + strain_y + strain_z
-    normal_x = stress[0] + time_step * (lame_value * volume + 2.0 * shear_value * strain_x)
-    normal_y = stress[1] + time_step * (lame_value * volume + 2.0 * shear_value * strain_y)
-    normal_z = stress[2] + time_step * (lame_value * volume + 2.0 * shear_value * strain_z)
-    shear_xy = stress[3] + time_step * shear_value * (
-        with_next(x_speed, next_y[0], 1) - x_speed + (with_next(y_speed, next_x[0], 0) - y_speed)
+def across_corner(row, x_way, y_way):
+    x_count, y_count = lax.axis_size("gx"), lax.axis_size("gy")
+    route = [
+        ((i - x_way) * y_count + j - y_way, i * y_count + j)
+        for i in range(x_count)
+        for j in range(y_count)
+        if 0 <= i - x_way < x_count and 0 <= j - y_way < y_count
+    ]
+    return lax.ppermute(row, ("gx", "gy"), route)
+
+
+def exchange(x_last, x_first, y_last, y_first):
+    return (
+        passed_along(x_last, "gx", 1),
+        passed_along(x_first, "gx", -1),
+        passed_along(y_last, "gy", 1),
+        passed_along(y_first, "gy", -1),
+        across_corner(y_last[1, :1], -1, 1),
+        across_corner(y_first[0, -1:], 1, -1),
     )
-    shear_xz = stress[4] + time_step * shear_value * (
-        with_next(x_speed, zero_rim(x_speed, 2), 2)
-        - x_speed
-        + (with_next(z_speed, next_x[1], 0) - z_speed)
+
+
+def stencil(brick, velocity, stress, lame, shear, buoyancy, rims, medium, last):
+    x, y, z = brick
+    group = fit(x, 4)
+    steps = x // group
+
+    def kernel(*refs):
+        (v_ref, s_ref, lame_ref, shear_ref, buoy_ref, v_next_ref, xx_next_ref) = refs[:7]
+        (lame_next_ref, shear_next_ref, xl, xr, yl, yr, edge_y, edge_x) = refs[7:15]
+        (xl_medium, xr_medium, yl_medium, yr_medium) = refs[15:19]
+        carried = refs[-1]
+        outs = refs[19:-1]
+        step = pl.program_id(0)
+        at = step * group
+        row = lax.broadcasted_iota(jnp.int32, (y, z), 0)
+        lane = lax.broadcasted_iota(jnp.int32, (y, z), 1)
+        first_row, last_row = row == 0, row == y - 1
+        first_lane, last_lane = lane == 0, lane == z - 1
+
+        def next_z(field):
+            edge = last_lane if field.shape[0] == y else last_lane[:1]
+            return jnp.where(edge, 0.0, pltpu.roll(field, z - 1, 1))
+
+        def prior_z(field):
+            edge = first_lane if field.shape[0] == y else first_lane[:1]
+            return jnp.where(edge, 0.0, pltpu.roll(field, 1, 1))
+
+        def next_y(field, rim):
+            return jnp.where(last_row, rim, pltpu.roll(field, y - 1, 0))
+
+        def prior_y(field, rim):
+            return jnp.where(first_row, rim, pltpu.roll(field, 1, 0))
+
+        def wide(value):
+            return value.astype(jnp.float32)
+
+        def line(ref, which, place):
+            return ref[which, pl.ds(place, 1), :]
+
+        def line_after(place):
+            inside = line(yl, 1, jnp.minimum(place, x - 1))
+            return jnp.where(place == x, edge_y[...], inside)
+
+        @pl.when(step == 0)
+        def _():
+            shear_rim = xl_medium[5]
+            vx, vy, vz = xl[0], xl[1], xl[2]
+            carried[0] = vx
+            carried[1] = xl[3] + time_step * shear_rim * (
+                (next_y(vx, edge_x[...]) - vx) + (v_ref[1, 0] - vy)
+            )
+            carried[2] = xl[4] + time_step * shear_rim * ((next_z(vx) - vx) + (v_ref[2, 0] - vz))
+
+        end = step == steps - 1
+        after = [jnp.where(end, xr[i], v_next_ref[i, 0]) for i in range(3)]
+        stresses = []
+        vx_prior = carried[0]
+        for k in range(group):
+            vx, vy, vz = v_ref[0, k], v_ref[1, k], v_ref[2, k]
+            vy_next = after[1] if k == group - 1 else v_ref[1, k + 1]
+            vz_next = after[2] if k == group - 1 else v_ref[2, k + 1]
+            lame_value, shear_value = wide(lame_ref[k]), wide(shear_ref[k])
+            ex = vx - vx_prior
+            ey = vy - prior_y(vy, line(yl, 1, at + k))
+            ez = vz - prior_z(vz)
+            swell = lame_value * (ex + ey + ez)
+            double = 2.0 * shear_value
+            xx = s_ref[0, k] + time_step * (swell + double * ex)
+            yy = s_ref[1, k] + time_step * (swell + double * ey)
+            zz = s_ref[2, k] + time_step * (swell + double * ez)
+            pull = time_step * shear_value
+            xy = s_ref[3, k] + pull * ((next_y(vx, line(yr, 0, at + k)) - vx) + (vy_next - vy))
+            xz = s_ref[4, k] + pull * ((next_z(vx) - vx) + (vz_next - vz))
+            yz = s_ref[5, k] + pull * (
+                (next_z(vy) - vy) + (next_y(vz, line(yr, 2, at + k)) - vz)
+            )
+            stresses.append((xx, yy, zz, xy, xz, yz))
+            vx_prior = vx
+
+        ex = after[0] - vx_prior
+        ey = after[1] - prior_y(after[1], line_after(at + group))
+        ez = after[2] - prior_z(after[2])
+        lame_value = jnp.where(end, xr_medium[4], wide(lame_next_ref[0]))
+        shear_value = jnp.where(end, xr_medium[5], wide(shear_next_ref[0]))
+        xx_after = jnp.where(end, xr[3], xx_next_ref[0, 0]) + time_step * (
+            lame_value * (ex + ey + ez) + 2.0 * shear_value * ex
+        )
+
+        xy_prior, xz_prior = carried[1], carried[2]
+        new = outs[0]
+        for k in range(group):
+            xx, yy, zz, xy, xz, yz = stresses[k]
+            xx_next = xx_after if k == group - 1 else stresses[k + 1][0]
+            here = at + k
+            vx, vy, vz = v_ref[0, k], v_ref[1, k], v_ref[2, k]
+            pull = time_step * line(yl_medium, 5, here)
+            vy_rim, vz_rim = line(yl, 1, here), line(yl, 2, here)
+            xy_rim = line(yl, 3, here) + pull * (
+                (vx[:1] - line(yl, 0, here)) + (line_after(here + 1) - vy_rim)
+            )
+            yz_rim = line(yl, 4, here) + pull * ((next_z(vy_rim) - vy_rim) + (vz[:1] - vz_rim))
+            vx_rim, vz_rim = line(yr, 0, here), line(yr, 2, here)
+            vx_before = jnp.where(here == 0, edge_x[...], line(yr, 0, jnp.maximum(here - 1, 0)))
+            ex = vx_rim - vx_before
+            ey = line(yr, 1, here) - vy[-1:]
+            ez = vz_rim - prior_z(vz_rim)
+            yy_rim = line(yr, 3, here) + time_step * (
+                line(yr_medium, 4, here) * (ex + ey + ez) + 2.0 * line(yr_medium, 5, here) * ey
+            )
+            push = time_step * wide(buoy_ref[k])
+            vx = vx + push * (
+                (xx_next - xx) + (xy - prior_y(xy, xy_rim)) + (xz - prior_z(xz))
+            )
+            vy = vy + push * ((xy - xy_prior) + (next_y(yy, yy_rim) - yy) + (yz - prior_z(yz)))
+            vz = vz + push * ((xz - xz_prior) + (yz - prior_y(yz, yz_rim)) + (next_z(zz) - zz))
+            xy_prior, xz_prior = xy, xz
+            for i, value in enumerate((vx, vy, vz)):
+                new[i, k] = value
+            if not last:
+                s_out, x_last, x_first, y_last, y_first = outs[1:]
+                for i, value in enumerate((xx, yy, zz, xy, xz, yz)):
+                    s_out[i, k] = value
+                for i, value in enumerate((vx, vy, vz, xy, yz)):
+                    y_last[i, pl.ds(here, 1), :] = value[-1:]
+                for i, value in enumerate((vx, vy, vz, yy)):
+                    y_first[i, pl.ds(here, 1), :] = value[:1]
+                if k == 0:
+
+                    @pl.when(step == 0)
+                    def _():
+                        for i, value in enumerate((vx, vy, vz, xx)):
+                            x_first[i] = value
+
+                if k == group - 1:
+
+                    @pl.when(end)
+                    def _():
+                        for i, value in enumerate((vx, vy, vz, xy, xz)):
+                            x_last[i] = value
+
+        carried[0] = v_ref[0, group - 1]
+        carried[1] = stresses[-1][3]
+        carried[2] = stresses[-1][4]
+
+    def after(i):
+        return jnp.minimum((i + 1) * group, x - 1)
+
+    def planes(count, depth):
+        return pl.BlockSpec((count, depth, y, z), lambda i: (0, i, 0, 0))
+
+    medium_block = pl.BlockSpec((group, y, z), lambda i: (i, 0, 0))
+    medium_next = pl.BlockSpec((1, y, z), lambda i: (after(i), 0, 0))
+    rim_blocks = [whole_block(rim.shape) for rim in (*rims, *medium)]
+    f32 = jnp.float32
+    out_shape = [jax.ShapeDtypeStruct((3, x, y, z), f32)]
+    out_specs = [planes(3, group)]
+    if not last:
+        edges = [(5, y, z), (4, y, z), (5, x, z), (4, x, z)]
+        out_shape += [jax.ShapeDtypeStruct((6, x, y, z), f32)]
+        out_shape += [jax.ShapeDtypeStruct(edge, f32) for edge in edges]
+        out_specs += [planes(6, group)] + [whole_block(edge) for edge in edges]
+    return pl.pallas_call(
+        kernel,
+        grid=(steps,),
+        in_specs=[
+            planes(3, group),
+            planes(6, group),
+            medium_block,
+            medium_block,
+            medium_block,
+            pl.BlockSpec((3, 1, y, z), lambda i: (0, after(i), 0, 0)),
+            pl.BlockSpec((1, 1, y, z), lambda i: (0, after(i), 0, 0)),
+            medium_next,
+            medium_next,
+        ]
+        + rim_blocks,
+        out_specs=out_specs,
+        out_shape=out_shape,
+        scratch_shapes=[pltpu.VMEM((3, y, z), f32)],
+        compiler_params=params(),
+        cost_estimate=pl.CostEstimate(
+            flops=80 * x * y * z, bytes_accessed=(54 if last else 78) * x * y * z, transcendentals=0
+        ),
+        name="stencil",
+    )(
+        velocity, stress, lame, shear, buoyancy, velocity, stress, lame, shear, *rims, *medium
     )
-    shear_yz = stress[5] + time_step * shear_value * (
-        with_next(y_speed, zero_rim(y_speed, 2), 2)
-        - y_speed
-        + (with_next(z_speed, next_y[1], 1) - z_speed)
+
+
+def propagate(velocity, stress, lame, shear, buoyancy):
+    brick = velocity.shape[1:]
+    lame_wide, shear_wide = lame.astype(jnp.float32), shear.astype(jnp.float32)
+
+    def side(which, at, chosen, mediums):
+        index = (at,) if which == 0 else (slice(None), at)
+        fields = [velocity[(i, *index)] for i in range(3)]
+        fields += [stress[(i, *index)] for i in chosen]
+        return jnp.stack(fields + [medium[index] for medium in mediums])
+
+    rims = exchange(
+        side(0, -1, (3, 4), (shear_wide,)),
+        side(0, 0, (0,), (lame_wide, shear_wide)),
+        side(1, -1, (3, 5), (shear_wide,)),
+        side(1, 0, (1,), (lame_wide, shear_wide)),
     )
-    return jnp.stack([normal_x, normal_y, normal_z, shear_xy, shear_xz, shear_yz])
-
-
-def velocity_step(velocity, stress, buoy_value):
-    normal_x, normal_y, normal_z = (stress[0], stress[1], stress[2])
-    shear_xy, shear_xz, shear_yz = (stress[3], stress[4], stress[5])
-    next_x = x_rims(normal_x[None, :1], -1)
-    prior_x = x_rims(jnp.stack([shear_xy[-1:], shear_xz[-1:]]), 1)
-    next_y = y_rims(normal_y[None, :, :1], -1)
-    prior_y = y_rims(jnp.stack([shear_xy[:, -1:], shear_yz[:, -1:]]), 1)
-    x_speed = velocity[0] + time_step * buoy_value * (
-        with_next(normal_x, next_x[0], 0)
-        - normal_x
-        + (shear_xy - with_prior(shear_xy, prior_y[0], 1))
-        + (shear_xz - with_prior(shear_xz, zero_rim(shear_xz, 2), 2))
-    )
-    y_speed = velocity[1] + time_step * buoy_value * (
-        shear_xy
-        - with_prior(shear_xy, prior_x[0], 0)
-        + (with_next(normal_y, next_y[0], 1) - normal_y)
-        + (shear_yz - with_prior(shear_yz, zero_rim(shear_yz, 2), 2))
-    )
-    z_speed = velocity[2] + time_step * buoy_value * (
-        shear_xz
-        - with_prior(shear_xz, prior_x[1], 0)
-        + (shear_yz - with_prior(shear_yz, prior_y[1], 1))
-        + (with_next(normal_z, zero_rim(normal_z, 2), 2) - normal_z)
-    )
-    return jnp.stack([x_speed, y_speed, z_speed])
+    medium = rims[:4]
+    for step_index in range(STEPS):
+        last = step_index == STEPS - 1
+        found = stencil(brick, velocity, stress, lame, shear, buoyancy, rims, medium, last)
+        velocity = found[0]
+        if not last:
+            stress = found[1]
+            rims = exchange(*found[2:])
+    return velocity
 
 
 def basis(length):
@@ -134,11 +292,12 @@
     return high, (value - high.astype(jnp.float32)).astype(jnp.bfloat16)
 
 
-def times(left, right, dims=((1,), (0,))):
-    def one(a, b):
-        return lax.dot_general(a, b, (dims, ((), ())), preferred_element_type=jnp.float32)
-
-    return one(left[0], right[0]) + (one(left[1], right[0]) + one(left[0], right[1]))
+def dot(left, right, dims=((1,), (0,))):
+    return lax.dot_general(left, right, (dims, ((), ())), preferred_element_type=jnp.float32)
+
+
+def times(left, right):
+    return dot(left[0], right[0]) + (dot(left[1], right[0]) + dot(left[0], right[1]))
 
 
 def joined(pieces, axis):
@@ -189,26 +348,35 @@
     table = table.reshape(2, 2, plan.chunks, plan.gy, kz, z)
     count = plan.chunks * plan.gy
 
+    group = fit(x, 8)
+    deep = fit(group, 2)
+
     def kernel(place_ref, table_ref, v_ref, *outs):
-        at = pl.program_id(0)
+        at = pl.program_id(0) * group
         me = place_ref[1]
+        order = [(c, lax.rem(me + s, plan.gy)) for c in range(plan.chunks) for s in range(plan.gy)]
+        tables = []
+        for kind in range(2):
+            high, low = (joined([table_ref[kind, i, c, g] for c, g in order], 0) for i in range(2))
+            tables.append((jnp.concatenate([high, high], axis=1), low))
         for comp in range(3):
-            kind = 1 if comp == 2 else 0
-            field = split(v_ref[comp, 0])
-            for chunk in range(plan.chunks):
-                for step in range(plan.gy):
-                    group = lax.rem(me + step, plan.gy)
-                    rows = (table_ref[kind, 0, chunk, group], table_ref[kind, 1, chunk, group])
-                    value = times(rows, field, ((1,), (1,)))
-                    outs[chunk * plan.gy + step][comp, pl.ds(at, kz, stride=x), :] = value
+            twice, low = tables[1 if comp == 2 else 0]
+            for plane in range(0, group, deep):
+                field = split(v_ref[comp, plane : plane + deep].reshape(deep * y, z))
+                value = dot(twice, jnp.concatenate(field, axis=1), ((1,), (1,)))
+                value += dot(low, field[0], ((1,), (1,)))
+                for i, out in enumerate(outs):
+                    for k in range(deep):
+                        part = value[i * kz : (i + 1) * kz, k * y : (k + 1) * y]
+                        out[comp, pl.ds(at + plane + k, kz, stride=x), :] = part
 
     outs = pl.pallas_call(
         kernel,
-        grid=(x,),
+        grid=(x // group,),
         in_specs=[
             scalars(),
             whole_block(table.shape),
-            pl.BlockSpec((3, 1, y, z), lambda i: (0, i, 0, 0)),
+            pl.BlockSpec((3, group, y, z), lambda i: (0, i, 0, 0)),
         ],
         out_specs=[whole_block((3, kz * x, y))] * count,
         out_shape=[jax.ShapeDtypeStruct((3, kz * x, y), jnp.float32)] * count,
@@ -393,31 +561,45 @@
     table = table.reshape(2, 2, plan.chunks, plan.gy, kz, z)
     blocks = [block.reshape(3, kz * x, y) for group in blocks for block in group]
 
+    group = fit(x, 8)
+    deep = fit(group, 2)
+
     def kernel(place_ref, table_ref, v_ref, p_ref, s_ref, *refs):
         ins, (image_p, image_s) = refs[:-2], refs[-2:]
-        at = pl.program_id(0)
+        at = pl.program_id(0) * group
         me = place_ref[1]
         order = [
             (chunk, source(me, step, plan.gy))
             for chunk in range(plan.chunks)
             for step in range(plan.gy)
         ]
-        total_p = total_s = 0.0
-        for comp in range(3):
-            kind = 1 if comp == 2 else 0
-            value = joined([ref[comp, pl.ds(at, kz, stride=x), :] for ref in ins], 0)
-            back = tuple(joined([table_ref[kind, i, c, g] for c, g in order], 0) for i in range(2))
-            field = times(split(value), back, ((0,), (0,)))
-            total_p += p_ref[comp, 0].astype(jnp.float32) * field
-            total_s += s_ref[comp, 0].astype(jnp.float32) * (v_ref[comp, 0] - field)
-        image_p[0] = total_p
-        image_s[0] = total_s
-
-    plane = pl.BlockSpec((3, 1, y, z), lambda i: (0, i, 0, 0))
-    image = pl.BlockSpec((1, y, z), lambda i: (i, 0, 0))
+        tables = []
+        for kind in range(2):
+            high, low = (joined([table_ref[kind, i, c, g] for c, g in order], 0) for i in range(2))
+            high, low = (part.astype(jnp.float32).T.astype(jnp.bfloat16) for part in (high, low))
+            tables.append((jnp.concatenate([high, high], axis=1), low))
+        for plane in range(0, group, deep):
+            here = slice(plane, plane + deep)
+            total_p = total_s = 0.0
+            for comp in range(3):
+                twice, low = tables[1 if comp == 2 else 0]
+                columns = [
+                    joined([ref[comp, pl.ds(at + plane + k, kz, stride=x), :] for ref in ins], 0)
+                    for k in range(deep)
+                ]
+                high, rest = split(joined(columns, 1))
+                field = dot(twice, jnp.concatenate([high, rest], axis=0)) + dot(low, high)
+                field = field.T.reshape(deep, y, z)
+                total_p += p_ref[comp, here].astype(jnp.float32) * field
+                total_s += s_ref[comp, here].astype(jnp.float32) * (v_ref[comp, here] - field)
+            image_p[here] = total_p
+            image_s[here] = total_s
+
+    plane = pl.BlockSpec((3, group, y, z), lambda i: (0, i, 0, 0))
+    image = pl.BlockSpec((group, y, z), lambda i: (i, 0, 0))
     return pl.pallas_call(
         kernel,
-        grid=(x,),
+        grid=(x // group,),
         in_specs=[scalars(), whole_block(table.shape), plane, plane, plane]
         + [whole_block((3, kz * x, y))] * len(blocks),
         out_specs=[image, image],
@@ -431,12 +613,7 @@
 
 
 def shards(velocity, stress, lame_lambda, shear_modulus, buoyancy, source_p, source_s):
-    lame_value = lame_lambda.astype(jnp.float32)
-    shear_value = shear_modulus.astype(jnp.float32)
-    buoy_value = buoyancy.astype(jnp.float32)
-    for step_index in range(STEPS):
-        stress = stress_step(velocity, stress, lame_value, shear_value)
-        velocity = velocity_step(velocity, stress, buoy_value)
+    velocity = propagate(velocity, stress, lame_lambda, shear_modulus, buoyancy)
     plan = Plan(velocity.shape[1:])
     place = jnp.stack([lax.axis_index("gx"), lax.axis_index("gy")]).astype(jnp.int32)
     blocks = z_forward(plan, place, velocity)

time: 512 us -> 421 us (0.82)
  other arithmetic: 53.9 us -> 3.11 us
  local copies, waits for them, and re-layouts: 55.7 us -> 27 us
  starting transfers between devices: 71.9 us -> 53.1 us
  waiting for transfers between devices: 226 us -> 237 us
    add x7 -> x0, other arithmetic: 38.1 us -> none  [the longest x2 15.4 us: stress_step(): stress[1] + time_step * (lame_value * volume + 2.0 * shear_value * strain_y)]
    slice x39 -> x6, local copies, waits for them, and re-layouts: 36.1 us -> 6.42 us  [the longest x2 2.62 us: side(): fields += [stress[i, *index] for i in chosen]]
    ppermute x16 -> x8, starting transfers between devices: 40.9 us -> 19.4 us  [passed_along(): return lax.ppermute(block, axis, route)]
    another operation x10 -> x0, other arithmetic: 15.3 us -> none  [the longest x3 13.8 us: velocity_step(): return jnp.stack([x_speed, y_speed, z_speed])]
    ppermute x0 -> x4, starting transfers between devices: none -> 11.9 us  [across_corner(): return lax.ppermute(row, ('gx', 'gy'), route)]
    ppermute x4, starting transfers between devices: 7.6 us -> 0.91 us  [swap_gy(): moved.append(lax.ppermute(blocks[step], 'gy', route))]
    ppermute x4, waiting for transfers between devices: 104 us -> 110 us  [swap_gy(): moved.append(lax.ppermute(blocks[step], 'gy', route))]
    ppermute x0 -> x4, waiting for transfers between devices: none -> 6.06 us  [across_corner(): return lax.ppermute(row, ('gx', 'gy'), route)]
  transfers between devices with their start and end apart: 24 -> 20, of which waited for: 8 -> 10; matrix products, arithmetic and copies ran while one was open for 12% -> 2% of each run, Pallas kernels for 7% -> 8%
where the time goes in v2:
time: 421 us; the launch traced here: 419 us
  waiting for transfers between devices  237 us (56%)
  Pallas kernels  97.5 us (23%)
  starting transfers between devices  53.1 us (13%)
  local copies, waits for them, and re-layouts  27 us (6%)
    ppermute x4, waiting for transfers between devices, swap_gy(): moved.append(lax.ppermute(blocks[step], 'gy', route))  110 us
    all_to_all x2, waiting for transfers between devices, to_planes(): planes = lax.all_to_all(lines, 'gx', 0, 0, tiled=True)  79.1 us
    all_to_all x2, waiting for transfers between devices, to_lines(): return lax.all_to_all(planes, 'gx', 0, 0, tiled=True)  41.6 us
    pallas_call x2, Pallas kernels, stencil(): pl.pallas_call(kernel, grid=(steps,), in_specs=[planes(3, group), planes(...  35.4 us
    pallas_call x2, Pallas kernels, x_lines(): pl.pallas_call(kernel, grid=(plan.per, ky // lanes), in_specs=[scalars(),...  20.5 us
    ppermute x8, starting transfers between devices, passed_along(): return lax.ppermute(block, axis, route)  19.4 us
    unnamed x46, local copies, waits for them, and re-layouts  14.3 us
    ppermute x4, starting transfers between devices, across_corner(): return lax.ppermute(row, ('gx', 'gy'), route)  11.9 us
  transfers between devices with their start and end apart: 20, of which 10 were waited for; matrix products, arithmetic and copies ran while one was open for 2% of the time, Pallas kernels for 8%

profile of v2, /device:TPU:12, one launch (start us, length us, event | category | flops | bytes accessed | tf_op | source)
XLA Modules:
  0.0 419.0 jit_solution(411206918656467055)
XLA Ops:
  29.2 4.0 collective-permute-start.4
  40.2 20.4 %stencil.2 = (f32[3,32,128,128]{3,2,1,0:T(8,128)}, f32[6,32,128,128]{3,2,1,0:T(8,128)}, f32[5,128,128]{2,1,0:T(8,128)}, f32[4,128,128]{2,1,0:T(8,128)}, f32[5,32,128]{2,1,0:T(8,128)}, /*index=5*/f32[4,32,128]{2,1,0:T(8,128)}) custom-call(f32[3,32,128,128]{3,2,1,0:T(8,128)} %refs_5_.1, f32[6,32,128,128]{3,2,1,0:T(8,128)} %refs_6_.1, ...), custom_call_target="tpu_custom_call" | custom-call | flops 41943040 | bytes 40894464 | tf_op jit(solution)/shard_map/stencil/pallas_call | solution.py:205
  64.9 5.3 %collective-permute-start.10 = (f32[1,128]{1,0:T(1,128)S(1)}, f32[1,128]{1,0:T(1,128)S(1)}, u32[]{:S(2)}, u32[]{:S(2)}) collective-permute-start(f32[1,128]{1,0:T(1,128)S(1)} %slice_bitcast_fusion.6), channel_id=1, source_target_pairs={{2,1},{4,3},{6,5},{8,7},{10,9},{12,11},{14,13},{16,15},{18,17},{20... | collective-permute-start | bytes 1544 | tf_op jit(solution)/shard_map/ppermute | solution.py:31
  78.5 3.8 collective-permute-done.11.refs_14_
  83.2 15.0 %stencil.3.v_ref = f32[3,32,128,128]{3,2,1,0:T(8,128)} custom-call(f32[3,32,128,128]{3,2,1,0:T(8,128)} %get-tuple-element.16.refs_0_.refs_5_, f32[6,32,128,128]{3,2,1,0:T(8,128)} %get-tuple-element.17.refs_1_.refs_6_, bf16[32,128,128]{2,1,0:T(8,128)(2,1)} %refs_7_.3, bf16[32,128,128]{2,1,0:T(8,128)(2,1)} %refs_8_.3, bf16[32,128,128]{2,1,0:T(8,128)(2,1)} %refs_4_.3, ...), custom_call_target="tpu_custom_call" | custom-call | flops 41943040 | bytes 28311552 | tf_op jit(solution)/shard_map/stencil/pallas_call | solution.py:205
  98.2 9.9 %z_forward.1 = (f32[3,1024,128]{2,1,0:T(8,128)}, f32[3,1024,128]{2,1,0:T(8,128)}, f32[3,1024,128]{2,1,0:T(8,128)}, f32[3,1024,128]{2,1,0:T(8,128)}) custom-call(s32[2]{0:T(128)} %pad_add_fusion.place_ref, bf16[2,2,2,2,32,128]{5,4,3,2,1,0:T(8,128)(2,1)} %constant.20.clone.table_ref, f32[3,32,128,128]{3,2,1,0:T(8,128)} %stencil.3.v_ref), custom_call_target="tpu_custom_call" | custom-call | flops 1207959552 | bytes 12582912 | tf_op jit(solution)/shard_map/z_forward/pallas_call | solution.py:373
  108.2 37.1 %collective-permute-done.14.refs_1_ = f32[3,32,32,128]{3,2,1,0:T(8,128)S(1)} collective-permute-done((f32[3,32,32,128]{3,2,1,0:T(8,128)}, f32[3,32,32,128]{3,2,1,0:T(8,128)S(1)}, u32[]{:S(2)}, u32[]{:S(2)}) %collective-permute-start.14) | collective-permute-done | bytes 1572896 | tf_op jit(solution)/shard_map/ppermute | solution.py:398
  146.4 4.9 %y_forward.3 = f32[32,2,32,256]{3,2,1,0:T(8,128)} custom-call(s32[2]{0:T(128)} %pad_add_fusion.place_ref, bf16[2,2,128,256]{3,2,1,0:T(8,128)(2,1)} %constant.21.clone.table_ref, f32[3,32,32,128]{3,2,1,0:T(8,128)} %bitcast.74, f32[3,32,32,128]{3,2,1,0:T(8,128)} %copy-done.4), custom_call_target="tpu_custom_call" | custom-call | flops 1207959552 | bytes 5242880 | tf_op jit(solution)/shard_map/y_forward/pallas_call | solution.py:430
  151.4 5.8 %all-to-all-start.2 = ((f32[16,2,2,32,256]{4,3,2,1,0:T(8,128)}), f32[16,2,2,32,256]{4,3,2,1,0:T(8,128)S(1)}, u32[]{:S(2)}, u32[]{:S(2)}) async-start(f32[16,2,2,32,256]{4,3,2,1,0:T(8,128)} %bitcast.70), calls=%async_computation.2 | async-start | bytes 4194304 | tf_op jit(solution)/shard_map/all_to_all | solution.py:449
  157.4 36.4 %collective-permute-done.12.refs_1_ = f32[3,32,32,128]{3,2,1,0:T(8,128)S(1)} collective-permute-done((f32[3,32,32,128]{3,2,1,0:T(8,128)}, f32[3,32,32,128]{3,2,1,0:T(8,128)S(1)}, u32[]{:S(2)}, u32[]{:S(2)}) %collective-permute-start.12) | collective-permute-done | bytes 1572896 | tf_op jit(solution)/shard_map/ppermute | solution.py:398
  194.9 4.9 %y_forward.2 = f32[32,2,32,256]{3,2,1,0:T(8,128)} custom-call(s32[2]{0:T(128)} %pad_add_fusion.place_ref, bf16[2,2,128,256]{3,2,1,0:T(8,128)(2,1)} %constant.21.clone.table_ref, f32[3,32,32,128]{3,2,1,0:T(8,128)} %bitcast.73, f32[3,32,32,128]{3,2,1,0:T(8,128)} %copy-done.3), custom_call_target="tpu_custom_call" | custom-call | flops 1207959552 | bytes 5242880 | tf_op jit(solution)/shard_map/y_forward/pallas_call | solution.py:430
  199.9 4.5 %all-to-all-done.2.in_ref = f32[16,2,2,32,256]{4,3,2,1,0:T(8,128)S(1)} async-done(((f32[16,2,2,32,256]{4,3,2,1,0:T(8,128)}), f32[16,2,2,32,256]{4,3,2,1,0:T(8,128)S(1)}, u32[]{:S(2)}, u32[]{:S(2)}) %all-to-all-start.2) | async-done | bytes 2097184 | tf_op jit(solution)/shard_map/all_to_all | solution.py:449
  205.7 5.1 %all-to-all-start = ((f32[16,2,2,32,256]{4,3,2,1,0:T(8,128)}), f32[16,2,2,32,256]{4,3,2,1,0:T(8,128)}, u32[]{:S(2)}, u32[]{:S(2)}) async-start(f32[16,2,2,32,256]{4,3,2,1,0:T(8,128)} %bitcast.71), calls=%async_computation | async-start | bytes 4194304 | tf_op jit(solution)/shard_map/all_to_all | solution.py:449
  210.8 10.3 %x_lines.3 = f32[16,2,2,32,256]{4,3,2,1,0:T(8,128)} custom-call(s32[2]{0:T(128)} %pad_add_fusion.place_ref, bf16[2,512,512]{2,1,0:T(8,128)(2,1)} %constant.22.clone.forth_ref, bf16[2,512,512]{2,1,0:T(8,128)(2,1)} %constant.23.clone.back_ref, f32[16,2,2,32,256]{4,3,2,1,0:T(8,128)} %copy-done.1), custom_call_target="tpu_custom_call" | custom-call | flops 3221225472 | bytes 4194304 | tf_op jit(solution)/shard_map/x_lines/pallas_call | solution.py:496
  221.1 37.1 %all-to-all-done.in_ref = f32[16,2,2,32,256]{4,3,2,1,0:T(8,128)} async-done(((f32[16,2,2,32,256]{4,3,2,1,0:T(8,128)}), f32[16,2,2,32,256]{4,3,2,1,0:T(8,128)}, u32[]{:S(2)}, u32[]{:S(2)}) %all-to-all-start) | async-done | bytes 2097184 | tf_op jit(solution)/shard_map/all_to_all | solution.py:449
  258.2 5.1 %all-to-all-start.3 = ((f32[16,2,2,32,256]{4,3,2,1,0:T(8,128)}), f32[16,2,2,32,256]{4,3,2,1,0:T(8,128)S(1)}, u32[]{:S(2)}, u32[]{:S(2)}) async-start(f32[16,2,2,32,256]{4,3,2,1,0:T(8,128)} %x_lines.3), calls=%async_computation.3 | async-start | bytes 4194304 | tf_op jit(solution)/shard_map/all_to_all | solution.py:453
  263.2 10.2 %x_lines.2 = f32[16,2,2,32,256]{4,3,2,1,0:T(8,128)} custom-call(s32[2]{0:T(128)} %pad_add_fusion.place_ref, bf16[2,512,512]{2,1,0:T(8,128)(2,1)} %constant.22.clone.forth_ref, bf16[2,512,512]{2,1,0:T(8,128)(2,1)} %constant.23.clone.back_ref, f32[16,2,2,32,256]{4,3,2,1,0:T(8,128)} %all-to-all-done.in_ref), custom_call_target="tpu_custom_call" | custom-call | flops 3221225472 | bytes 4194304 | tf_op jit(solution)/shard_map/x_lines/pallas_call | solution.py:496
  273.5 37.0 %all-to-all-done.3 = f32[16,2,2,32,256]{4,3,2,1,0:T(8,128)S(1)} async-done(((f32[16,2,2,32,256]{4,3,2,1,0:T(8,128)}), f32[16,2,2,32,256]{4,3,2,1,0:T(8,128)S(1)}, u32[]{:S(2)}, u32[]{:S(2)}) %all-to-all-start.3) | async-done | bytes 2097184 | tf_op jit(solution)/shard_map/all_to_all | solution.py:453
  311.8 5.1 %all-to-all-start.1 = ((f32[16,2,2,32,256]{4,3,2,1,0:T(8,128)}), f32[16,2,2,32,256]{4,3,2,1,0:T(8,128)}, u32[]{:S(2)}, u32[]{:S(2)}) async-start(f32[16,2,2,32,256]{4,3,2,1,0:T(8,128)} %x_lines.2), calls=%async_computation.1 | async-start | bytes 4194304 | tf_op jit(solution)/shard_map/all_to_all | solution.py:453
  316.9 5.0 %y_inverse.3 = (f32[3,32,32,128]{3,2,1,0:T(8,128)}, f32[3,32,32,128]{3,2,1,0:T(8,128)}) custom-call(s32[2]{0:T(128)} %pad_add_fusion.place_ref, bf16[2,2,256,128]{3,2,1,0:T(8,128)(2,1)} %constant.24.clone.table_ref, f32[32,2,32,256]{3,2,1,0:T(8,128)} %bitcast.72), custom_call_target="tpu_custom_call" | custom-call | flops 1207959552 | bytes 5242880 | tf_op jit(solution)/shard_map/y_inverse/pallas_call | solution.py:540
  322.1 42.1 %all-to-all-done.1 = f32[16,2,2,32,256]{4,3,2,1,0:T(8,128)} async-done(((f32[16,2,2,32,256]{4,3,2,1,0:T(8,128)}), f32[16,2,2,32,256]{4,3,2,1,0:T(8,128)}, u32[]{:S(2)}, u32[]{:S(2)}) %all-to-all-start.1) | async-done | bytes 2097184 | tf_op jit(solution)/shard_map/all_to_all | solution.py:453
  364.2 4.9 %y_inverse.2 = (f32[3,32,32,128]{3,2,1,0:T(8,128)}, f32[3,32,32,128]{3,2,1,0:T(8,128)}) custom-call(s32[2]{0:T(128)} %pad_add_fusion.place_ref, bf16[2,2,256,128]{3,2,1,0:T(8,128)(2,1)} %constant.24.clone.table_ref, f32[32,2,32,256]{3,2,1,0:T(8,128)} %bitcast.30.in_ref), custom_call_target="tpu_custom_call" | custom-call | flops 1207959552 | bytes 5242880 | tf_op jit(solution)/shard_map/y_inverse/pallas_call | solution.py:540
  369.5 36.5 %collective-permute-done.13 = f32[3,32,32,128]{3,2,1,0:T(8,128)S(1)} collective-permute-done((f32[3,32,32,128]{3,2,1,0:T(8,128)}, f32[3,32,32,128]{3,2,1,0:T(8,128)S(1)}, u32[]{:S(2)}, u32[]{:S(2)}) %collective-permute-start.13) | collective-permute-done | bytes 1572896 | tf_op jit(solution)/shard_map/ppermute | solution.py:398
  407.2 11.8 %images.1 = (f32[32,128,128]{2,1,0:T(8,128)}, f32[32,128,128]{2,1,0:T(8,128)}) custom-call(s32[2]{0:T(128)} %pad_add_fusion.place_ref, bf16[2,2,2,2,32,128]{5,4,3,2,1,0:T(8,128)(2,1)} %constant.25.clone.table_ref, f32[3,32,128,128]{3,2,1,0:T(8,128)} %stencil.3.v_ref, bf16[3,32,128,128]{3,2,1,0:T(8,128)(2,1)} %p_ref.1, bf16[3,32,128,128]{3,2,1,0:T(8,128)(2,1)} %s_ref.1, ...), custom_call_target="tpu_custom_call" | custom-call | flops 1207959552 | bytes 23068672 | tf_op jit(solution)/shard_map/images/pallas_call | solution.py:600
  (90 shorter events, 55.8 us)
Async XLA Ops:
  0.6 5.5 %copy-start = (bf16[32,128,128]{2,1,0:T(8,128)(2,1)S(1)}, bf16[32,128,128]{2,1,0:T(8,128)(2,1)}, u32[]{:S(2)}) copy-start(bf16[32,128,128]{2,1,0:T(8,128)(2,1)} %refs_8_.3) | copy-start | bytes 3145732
  2.0 4.8 %copy-start.13 = (f32[1,32,1,128]{3,2,1,0:T(1,128)}, f32[1,32,1,128]{3,2,1,0:T(1,128)S(1)}, u32[]{:S(2)}) copy-start(f32[1,32,1,128]{3,2,1,0:T(1,128)S(1)} %get-tuple-element.40) | copy-start | bytes 49156
  12.2 26.7 %collective-permute-start.2 = (f32[6,32,128]{2,1,0:T(8,128)}, f32[6,32,128]{2,1,0:T(8,128)S(1)}, u32[]{:S(2)}, u32[]{:S(2)}) collective-permute-start(f32[6,32,128]{2,1,0:T(8,128)} %get-tuple-element.49), channel_id=1, source_target_pairs={{0,1},{2,3},{4,5},{6,7},{8,9},{10,11},{12,13},{14,15},{16,17},{18,... | collective-permute-start | bytes 294920 | tf_op jit(solution)/shard_map/ppermute | solution.py:20
  15.6 23.4 %collective-permute-start.3 = (f32[6,32,128]{2,1,0:T(8,128)}, f32[6,32,128]{2,1,0:T(8,128)S(1)}, u32[]{:S(2)}, u32[]{:S(2)}) collective-permute-start(f32[6,32,128]{2,1,0:T(8,128)} %get-tuple-element.48), channel_id=1, source_target_pairs={{1,0},{3,2},{5,4},{7,6},{9,8},{11,10},{13,12},{15,14},{17,16},{19,... | collective-permute-start | bytes 294920 | tf_op jit(solution)/shard_map/ppermute | solution.py:20
  20.8 12.3 %collective-permute-start = (f32[6,128,128]{2,0,1:T(8,128)S(1)}, f32[6,128,128]{2,0,1:T(8,128)S(1)}, u32[]{:S(2)}, u32[]{:S(2)}) collective-permute-start(f32[6,128,128]{2,0,1:T(8,128)S(1)} %stack.24), channel_id=1, source_target_pairs={{0,2},{2,4},{4,6},{6,8},{8,10},{10,12},{12,14},{14,16},{16,18},{18... | collective-permute-start | bytes 1179656 | tf_op jit(solution)/shard_map/ppermute | solution.py:20
  24.9 11.0 %collective-permute-start.1 = (f32[6,128,128]{2,0,1:T(8,128)S(1)}, f32[6,128,128]{2,0,1:T(8,128)S(1)}, u32[]{:S(2)}, u32[]{:S(2)}) collective-permute-start(f32[6,128,128]{2,0,1:T(8,128)S(1)} %stack.25), channel_id=1, source_target_pairs={{2,0},{4,2},{6,4},{8,6},{10,8},{12,10},{14,12},{16,14},{18,16},{20... | collective-permute-start | bytes 1179656 | tf_op jit(solution)/shard_map/ppermute | solution.py:20
  29.2 7.5 %collective-permute-start.4 = (f32[1,128]{1,0:T(1,128)S(1)}, f32[1,128]{1,0:T(1,128)S(1)}, u32[]{:S(2)}, u32[]{:S(2)}) collective-permute-start(f32[1,128]{1,0:T(1,128)S(1)} %slice_bitcast_fusion.4), channel_id=1, source_target_pairs={{2,1},{4,3},{6,5},{8,7},{10,9},{12,11},{14,13},{16,15},{18,17},{20... | collective-permute-start | bytes 1544 | tf_op jit(solution)/shard_map/ppermute | solution.py:31
  33.2 5.8 %collective-permute-start.5 = (f32[1,128]{1,0:T(1,128)S(1)}, f32[1,128]{1,0:T(1,128)S(1)}, u32[]{:S(2)}, u32[]{:S(2)}) collective-permute-start(f32[1,128]{1,0:T(1,128)S(1)} %slice_bitcast_fusion.3), channel_id=1, source_target_pairs={{1,2},{3,4},{5,6},{7,8},{9,10},{11,12},{13,14},{15,16},{17,18},{19... | collective-permute-start | bytes 1544 | tf_op jit(solution)/shard_map/ppermute | solution.py:31
  60.6 21.7 %collective-permute-start.8 = (f32[5,32,128]{2,1,0:T(8,128)}, f32[5,32,128]{2,1,0:T(8,128)S(1)}, u32[]{:S(2)}, u32[]{:S(2)}) collective-permute-start(f32[5,32,128]{2,1,0:T(8,128)} %get-tuple-element.20), channel_id=1, source_target_pairs={{0,1},{2,3},{4,5},{6,7},{8,9},{10,11},{12,13},{14,15},{16,17},{18,... | collective-permute-start | bytes 245768 | tf_op jit(solution)/shard_map/ppermute | solution.py:20
  63.6 18.6 %collective-permute-start.9 = (f32[4,32,128]{2,1,0:T(8,128)}, f32[4,32,128]{2,1,0:T(8,128)S(1)}, u32[]{:S(2)}, u32[]{:S(2)}) collective-permute-start(f32[4,32,128]{2,1,0:T(8,128)} %get-tuple-element.21), channel_id=1, source_target_pairs={{1,0},{3,2},{5,4},{7,6},{9,8},{11,10},{13,12},{15,14},{17,16},{19,... | collective-permute-start | bytes 196616 | tf_op jit(solution)/shard_map/ppermute | solution.py:20
  64.9 11.6 %collective-permute-start.10 = (f32[1,128]{1,0:T(1,128)S(1)}, f32[1,128]{1,0:T(1,128)S(1)}, u32[]{:S(2)}, u32[]{:S(2)}) collective-permute-start(f32[1,128]{1,0:T(1,128)S(1)} %slice_bitcast_fusion.6), channel_id=1, source_target_pairs={{2,1},{4,3},{6,5},{8,7},{10,9},{12,11},{14,13},{16,15},{18,17},{20... | collective-permute-start | bytes 1544 | tf_op jit(solution)/shard_map/ppermute | solution.py:31
  70.2 12.1 %collective-permute-start.6 = (f32[5,128,128]{2,1,0:T(8,128)}, f32[5,128,128]{2,1,0:T(8,128)S(1)}, u32[]{:S(2)}, u32[]{:S(2)}) collective-permute-start(f32[5,128,128]{2,1,0:T(8,128)} %get-tuple-element.18), channel_id=1, source_target_pairs={{0,2},{2,4},{4,6},{6,8},{8,10},{10,12},{12,14},{14,16},{16,18},{18... | collective-permute-start | bytes 983048 | tf_op jit(solution)/shard_map/ppermute | solution.py:20
  72.2 10.1 %collective-permute-start.7 = (f32[4,128,128]{2,1,0:T(8,128)}, f32[4,128,128]{2,1,0:T(8,128)S(1)}, u32[]{:S(2)}, u32[]{:S(2)}) collective-permute-start(f32[4,128,128]{2,1,0:T(8,128)} %get-tuple-element.19), channel_id=1, source_target_pairs={{2,0},{4,2},{6,4},{8,6},{10,8},{12,10},{14,12},{16,14},{18,16},{20... | collective-permute-start | bytes 786440 | tf_op jit(solution)/shard_map/ppermute | solution.py:20
  76.5 5.8 %copy-start.16 = (f32[1,128]{1,0:T(1,128)}, f32[1,128]{1,0:T(1,128)S(1)}, u32[]{:S(2)}) copy-start(f32[1,128]{1,0:T(1,128)S(1)} %collective-permute-done.10.refs_13_) | copy-start | bytes 1540
  76.5 5.8 %collective-permute-start.11 = (f32[1,128]{1,0:T(1,128)S(1)}, f32[1,128]{1,0:T(1,128)S(1)}, u32[]{:S(2)}, u32[]{:S(2)}) collective-permute-start(f32[1,128]{1,0:T(1,128)S(1)} %slice_bitcast_fusion.5), channel_id=1, source_target_pairs={{1,2},{3,4},{5,6},{7,8},{9,10},{11,12},{13,14},{15,16},{17,18},{19... | collective-permute-start | bytes 1544 | tf_op jit(solution)/shard_map/ppermute | solution.py:31
  108.1 37.2 %collective-permute-start.14 = (f32[3,32,32,128]{3,2,1,0:T(8,128)}, f32[3,32,32,128]{3,2,1,0:T(8,128)S(1)}, u32[]{:S(2)}, u32[]{:S(2)}) collective-permute-start(f32[3,32,32,128]{3,2,1,0:T(8,128)} %bitcast.100), channel_id=1, source_target_pairs={{0,1},{1,0},{2,3},{3,2},{4,5},{5,4},{6,7},{7,6},{8,9},{9,8},{10,11... | collective-permute-start | bytes 4718600 | tf_op jit(solution)/shard_map/ppermute | solution.py:398
  151.4 53.0 %all-to-all-start.2 = ((f32[16,2,2,32,256]{4,3,2,1,0:T(8,128)}), f32[16,2,2,32,256]{4,3,2,1,0:T(8,128)S(1)}, u32[]{:S(2)}, u32[]{:S(2)}) async-start(f32[16,2,2,32,256]{4,3,2,1,0:T(8,128)} %bitcast.70), calls=%async_computation.2 | async-start | bytes 4194304 | tf_op jit(solution)/shard_map/all_to_all | solution.py:449
  157.1 36.7 %collective-permute-start.12 = (f32[3,32,32,128]{3,2,1,0:T(8,128)}, f32[3,32,32,128]{3,2,1,0:T(8,128)S(1)}, u32[]{:S(2)}, u32[]{:S(2)}) collective-permute-start(f32[3,32,32,128]{3,2,1,0:T(8,128)} %bitcast.99), channel_id=1, source_target_pairs={{0,1},{1,0},{2,3},{3,2},{4,5},{5,4},{6,7},{7,6},{8,9},{9,8},{10,11... | collective-permute-start | bytes 4718600 | tf_op jit(solution)/shard_map/ppermute | solution.py:398
  205.7 52.4 %all-to-all-start = ((f32[16,2,2,32,256]{4,3,2,1,0:T(8,128)}), f32[16,2,2,32,256]{4,3,2,1,0:T(8,128)}, u32[]{:S(2)}, u32[]{:S(2)}) async-start(f32[16,2,2,32,256]{4,3,2,1,0:T(8,128)} %bitcast.71), calls=%async_computation | async-start | bytes 4194304 | tf_op jit(solution)/shard_map/all_to_all | solution.py:449
  258.2 52.3 %all-to-all-start.3 = ((f32[16,2,2,32,256]{4,3,2,1,0:T(8,128)}), f32[16,2,2,32,256]{4,3,2,1,0:T(8,128)S(1)}, u32[]{:S(2)}, u32[]{:S(2)}) async-start(f32[16,2,2,32,256]{4,3,2,1,0:T(8,128)} %x_lines.3), calls=%async_computation.3 | async-start | bytes 4194304 | tf_op jit(solution)/shard_map/all_to_all | solution.py:453
  311.8 52.4 %all-to-all-start.1 = ((f32[16,2,2,32,256]{4,3,2,1,0:T(8,128)}), f32[16,2,2,32,256]{4,3,2,1,0:T(8,128)}, u32[]{:S(2)}, u32[]{:S(2)}) async-start(f32[16,2,2,32,256]{4,3,2,1,0:T(8,128)} %x_lines.2), calls=%async_computation.1 | async-start | bytes 4194304 | tf_op jit(solution)/shard_map/all_to_all | solution.py:453
  321.9 47.6 %collective-permute-start.15 = (f32[3,32,32,128]{3,2,1,0:T(8,128)}, f32[3,32,32,128]{3,2,1,0:T(8,128)S(1)}, u32[]{:S(2)}, u32[]{:S(2)}) collective-permute-start(f32[3,32,32,128]{3,2,1,0:T(8,128)} %get-tuple-element.29), channel_id=1, source_target_pairs={{0,1},{1,0},{2,3},{3,2},{4,5},{5,4},{6,7},{7,6},{8,9},{9,8},{10,11... | collective-permute-start | bytes 4718600 | tf_op jit(solution)/shard_map/ppermute | solution.py:398
  369.2 36.8 %collective-permute-start.13 = (f32[3,32,32,128]{3,2,1,0:T(8,128)}, f32[3,32,32,128]{3,2,1,0:T(8,128)S(1)}, u32[]{:S(2)}, u32[]{:S(2)}) collective-permute-start(f32[3,32,32,128]{3,2,1,0:T(8,128)} %get-tuple-element.25), channel_id=1, source_target_pairs={{0,1},{1,0},{2,3},{3,2},{4,5},{5,4},{6,7},{7,6},{8,9},{9,8},{10,11... | collective-permute-start | bytes 4718600 | tf_op jit(solution)/shard_map/ppermute | solution.py:398
  369.5 36.5 %copy-start.5 = (f32[3,32,32,128]{3,2,1,0:T(8,128)}, f32[3,32,32,128]{3,2,1,0:T(8,128)S(1)}, u32[]{:S(2)}) copy-start(f32[3,32,32,128]{3,2,1,0:T(8,128)S(1)} %collective-permute-done.15) | copy-start | bytes 4718596
  (14 other events, 13.7 us)

commit v3 on v2

--- a/solution.py
+++ b/solution.py
@@ -8,7 +8,7 @@
 from jax.sharding import PartitionSpec as P
 
 STEPS = 2
-MOST_CHUNKS = 2
+MOST_CHUNKS = 1
 VMEM_BYTES = 56 * 2**20
 
 time_step = 0.2
@@ -31,30 +31,110 @@
     return lax.ppermute(row, ("gx", "gy"), route)
 
 
-def exchange(x_last, x_first, y_last, y_first):
-    return (
-        passed_along(x_last, "gx", 1),
-        passed_along(x_first, "gx", -1),
-        passed_along(y_last, "gy", 1),
-        passed_along(y_first, "gy", -1),
-        across_corner(y_last[1, :1], -1, 1),
-        across_corner(y_first[0, -1:], 1, -1),
+def exchange(x_last, x_first, y_last, y_first, corner_y, corner_x):
+    yl, yr = passed_along(y_last, "gy", 1), passed_along(y_first, "gy", -1)
+    xl, xr = passed_along(x_last, "gx", 1), passed_along(x_first, "gx", -1)
+    return (yl, yr), (xl, xr, across_corner(corner_y, -1, 1), across_corner(corner_x, 1, -1))
+
+
+def first_rims(brick, velocity, stress, lame, shear):
+    x, y, z = brick
+    some = fit(y, 8)
+    many = fit(y, 16)
+
+    def kernel(*refs):
+        (v_first, v_last, s_first, s_last, lame_first, shear_first, shear_last) = refs[:7]
+        (v_low, v_high, s_low, s_high, lame_low, shear_low, shear_high) = refs[7:14]
+        x_last, x_first, y_last, y_first, corner_y, corner_x = refs[14:]
+
+        def wide(value):
+            return value.astype(jnp.float32)
+
+        for i in range(3):
+            x_last[i], x_first[i] = v_last[i, 0], v_first[i, 0]
+            y_last[i], y_first[i] = v_high[i, :, some - 1], v_low[i, :, 0]
+        x_last[3], x_last[4], x_last[5] = s_last[3, 0], s_last[4, 0], wide(shear_last[0])
+        x_first[3], x_first[4], x_first[5] = s_first[0, 0], wide(lame_first[0]), wide(shear_first[0])
+        y_last[3], y_last[4] = s_high[3, :, some - 1], s_high[5, :, some - 1]
+        y_last[5] = wide(shear_high[...])[:, many - 1]
+        y_first[3], y_first[4] = s_low[1, :, 0], wide(lame_low[...])[:, 0]
+        y_first[5] = wide(shear_low[...])[:, 0]
+        corner_y[...] = v_first[1, 0, y - 1 :]
+        corner_x[...] = v_last[0, 0, :1]
+
+    def plane(count, at):
+        return pl.BlockSpec((count, 1, y, z), lambda i: (0, at, 0, 0))
+
+    def medium_plane(at):
+        return pl.BlockSpec((1, y, z), lambda i: (at, 0, 0))
+
+    def rows(count, at):
+        return pl.BlockSpec((count, x, some, z), lambda i: (0, 0, at, 0))
+
+    def medium_rows(at):
+        return pl.BlockSpec((x, many, z), lambda i: (0, at, 0))
+
+    shapes = [(6, y, z), (6, y, z), (6, x, z), (6, x, z), (1, z), (1, z)]
+    ends, highs, most = x - 1, y // some - 1, y // many - 1
+    return pl.pallas_call(
+        kernel,
+        grid=(1,),
+        in_specs=[plane(3, 0), plane(3, ends), plane(6, 0), plane(6, ends)]
+        + [medium_plane(0), medium_plane(0), medium_plane(ends)]
+        + [rows(3, 0), rows(3, highs), rows(6, 0), rows(6, highs)]
+        + [medium_rows(0), medium_rows(0), medium_rows(most)],
+        out_specs=[whole_block(shape) for shape in shapes],
+        out_shape=[jax.ShapeDtypeStruct(shape, jnp.float32) for shape in shapes],
+        compiler_params=params(),
+        cost_estimate=pl.CostEstimate(
+            flops=0, bytes_accessed=80 * (y + 8 * x) * z, transcendentals=0
+        ),
+        name="first_rims",
+    )(
+        *(velocity, velocity, stress, stress, lame, shear, shear),
+        *(velocity, velocity, stress, stress, lame, shear, shear),
     )
 
 
-def stencil(brick, velocity, stress, lame, shear, buoyancy, rims, medium, last):
+def stencil(brick, state, rims, medium, x_rims, x_medium, done, last):
     x, y, z = brick
+    velocity, stress, lame, shear, buoyancy = state
     group = fit(x, 4)
-    steps = x // group
+    groups = x // group
+    ends = x_rims is not None
+    if ends:
+        count, of = min(groups, 2), lambda i: i * (groups - 1)
+    else:
+        count, of = groups - 2, lambda i: i + 1
+    f32 = jnp.float32
 
     def kernel(*refs):
-        (v_ref, s_ref, lame_ref, shear_ref, buoy_ref, v_next_ref, xx_next_ref) = refs[:7]
-        (lame_next_ref, shear_next_ref, xl, xr, yl, yr, edge_y, edge_x) = refs[7:15]
-        (xl_medium, xr_medium, yl_medium, yr_medium) = refs[15:19]
-        carried = refs[-1]
-        outs = refs[19:-1]
-        step = pl.program_id(0)
-        at = step * group
+        refs = list(refs)
+
+        def take(number):
+            taken = refs[:number]
+            del refs[:number]
+            return taken
+
+        v_ref, s_ref, lame_ref, shear_ref, buoy_ref = take(5)
+        v_next_ref, xx_next_ref, lame_next_ref, shear_next_ref = take(4)
+        v_prior_ref, xy_prior_ref, xz_prior_ref, shear_prior_ref = take(4)
+        yl, yr = take(2)
+        yl_medium, yr_medium = take(2) if medium else (yl, yr)
+        if ends:
+            xl, xr, edge_y, edge_x = take(4)
+            xl_medium, xr_medium = take(2) if medium else (xl, xr)
+        given = take(len(done))
+        new = take(1)[0]
+        if not last:
+            s_out, y_last, y_first = take(3)
+            if ends:
+                x_last, x_first, corner_y, corner_x = take(4)
+        carried = take(1)[0]
+        turn = pl.program_id(0)
+        here_group = of(turn)
+        at = here_group * group
+        start, end = here_group == 0, here_group == groups - 1
         row = lax.broadcasted_iota(jnp.int32, (y, z), 0)
         lane = lax.broadcasted_iota(jnp.int32, (y, z), 1)
         first_row, last_row = row == 0, row == y - 1
@@ -75,27 +155,49 @@
             return jnp.where(first_row, rim, pltpu.roll(field, 1, 0))
 
         def wide(value):
-            return value.astype(jnp.float32)
+            return value.astype(f32)
 
         def line(ref, which, place):
             return ref[which, pl.ds(place, 1), :]
 
         def line_after(place):
-            inside = line(yl, 1, jnp.minimum(place, x - 1))
-            return jnp.where(place == x, edge_y[...], inside)
-
-        @pl.when(step == 0)
-        def _():
-            shear_rim = xl_medium[5]
-            vx, vy, vz = xl[0], xl[1], xl[2]
+            if not ends:
+                return line(yl, 1, place)
+            return jnp.where(place == x, edge_y[...], line(yl, 1, jnp.minimum(place, x - 1)))
+
+        def line_before(place):
+            if not ends:
+                return line(yr, 0, place)
+            return jnp.where(place < 0, edge_x[...], line(yr, 0, jnp.maximum(place, 0)))
+
+        def begin(value, rim):
+            return jnp.where(start, rim(), value) if ends else value
+
+        def finish(value, rim):
+            return jnp.where(end, rim(), value) if ends else value
+
+        def fresh():
+            shear_rim = begin(wide(shear_prior_ref[0]), lambda: xl_medium[5])
+            vx, vy, vz = (begin(v_prior_ref[i, 0], lambda: xl[i]) for i in range(3))
+            xy = begin(xy_prior_ref[0, 0], lambda: xl[3])
+            xz = begin(xz_prior_ref[0, 0], lambda: xl[4])
+            pull = time_step * shear_rim
             carried[0] = vx
-            carried[1] = xl[3] + time_step * shear_rim * (
-                (next_y(vx, edge_x[...]) - vx) + (v_ref[1, 0] - vy)
-            )
-            carried[2] = xl[4] + time_step * shear_rim * ((next_z(vx) - vx) + (v_ref[2, 0] - vz))
-
-        end = step == steps - 1
-        after = [jnp.where(end, xr[i], v_next_ref[i, 0]) for i in range(3)]
+            carried[1] = xy + pull * ((next_y(vx, line_before(at - 1)) - vx) + (v_ref[1, 0] - vy))
+            carried[2] = xz + pull * ((next_z(vx) - vx) + (v_ref[2, 0] - vz))
+
+        if ends:
+            fresh()
+        else:
+            pl.when(turn == 0)(fresh)
+        if not last and done:
+
+            @pl.when(turn == 0)
+            def _():
+                y_last[...] = given[2][...]
+                y_first[...] = given[3][...]
+
+        after = [finish(v_next_ref[i, 0], lambda: xr[i]) for i in range(3)]
         stresses = []
         vx_prior = carried[0]
         for k in range(group):
@@ -123,14 +225,13 @@
         ex = after[0] - vx_prior
         ey = after[1] - prior_y(after[1], line_after(at + group))
         ez = after[2] - prior_z(after[2])
-        lame_value = jnp.where(end, xr_medium[4], wide(lame_next_ref[0]))
-        shear_value = jnp.where(end, xr_medium[5], wide(shear_next_ref[0]))
-        xx_after = jnp.where(end, xr[3], xx_next_ref[0, 0]) + time_step * (
+        lame_value = finish(wide(lame_next_ref[0]), lambda: xr_medium[4])
+        shear_value = finish(wide(shear_next_ref[0]), lambda: xr_medium[5])
+        xx_after = finish(xx_next_ref[0, 0], lambda: xr[3]) + time_step * (
             lame_value * (ex + ey + ez) + 2.0 * shear_value * ex
         )
 
         xy_prior, xz_prior = carried[1], carried[2]
-        new = outs[0]
         for k in range(group):
             xx, yy, zz, xy, xz, yz = stresses[k]
             xx_next = xx_after if k == group - 1 else stresses[k + 1][0]
@@ -143,8 +244,7 @@
             )
             yz_rim = line(yl, 4, here) + pull * ((next_z(vy_rim) - vy_rim) + (vz[:1] - vz_rim))
             vx_rim, vz_rim = line(yr, 0, here), line(yr, 2, here)
-            vx_before = jnp.where(here == 0, edge_x[...], line(yr, 0, jnp.maximum(here - 1, 0)))
-            ex = vx_rim - vx_before
+            ex = vx_rim - line_before(here - 1)
             ey = line(yr, 1, here) - vy[-1:]
             ez = vz_rim - prior_z(vz_rim)
             yy_rim = line(yr, 3, here) + time_step * (
@@ -159,101 +259,110 @@
             xy_prior, xz_prior = xy, xz
             for i, value in enumerate((vx, vy, vz)):
                 new[i, k] = value
-            if not last:
-                s_out, x_last, x_first, y_last, y_first = outs[1:]
-                for i, value in enumerate((xx, yy, zz, xy, xz, yz)):
-                    s_out[i, k] = value
-                for i, value in enumerate((vx, vy, vz, xy, yz)):
-                    y_last[i, pl.ds(here, 1), :] = value[-1:]
-                for i, value in enumerate((vx, vy, vz, yy)):
-                    y_first[i, pl.ds(here, 1), :] = value[:1]
-                if k == 0:
-
-                    @pl.when(step == 0)
-                    def _():
-                        for i, value in enumerate((vx, vy, vz, xx)):
-                            x_first[i] = value
-
-                if k == group - 1:
-
-                    @pl.when(end)
-                    def _():
-                        for i, value in enumerate((vx, vy, vz, xy, xz)):
-                            x_last[i] = value
-
-        carried[0] = v_ref[0, group - 1]
-        carried[1] = stresses[-1][3]
-        carried[2] = stresses[-1][4]
-
-    def after(i):
-        return jnp.minimum((i + 1) * group, x - 1)
-
-    def planes(count, depth):
-        return pl.BlockSpec((count, depth, y, z), lambda i: (0, i, 0, 0))
-
-    medium_block = pl.BlockSpec((group, y, z), lambda i: (i, 0, 0))
-    medium_next = pl.BlockSpec((1, y, z), lambda i: (after(i), 0, 0))
-    rim_blocks = [whole_block(rim.shape) for rim in (*rims, *medium)]
-    f32 = jnp.float32
-    out_shape = [jax.ShapeDtypeStruct((3, x, y, z), f32)]
-    out_specs = [planes(3, group)]
+            if last:
+                continue
+            for i, value in enumerate((xx, yy, zz, xy, xz, yz)):
+                s_out[i, k] = value
+            for i, value in enumerate((vx, vy, vz, xy, yz)):
+                y_last[i, pl.ds(here, 1), :] = value[-1:]
+            for i, value in enumerate((vx, vy, vz, yy)):
+                y_first[i, pl.ds(here, 1), :] = value[:1]
+            if ends and k == 0:
+
+                @pl.when(start)
+                def _():
+                    for i, value in enumerate((vx, vy, vz, xx)):
+                        x_first[i] = value
+                    corner_y[...] = vy[-1:]
+
+            if ends and k == group - 1:
+
+                @pl.when(end)
+                def _():
+                    for i, value in enumerate((vx, vy, vz, xy, xz)):
+                        x_last[i] = value
+                    corner_x[...] = vx[:1]
+
+        if not ends:
+            carried[0] = v_ref[0, group - 1]
+            carried[1] = stresses[-1][3]
+            carried[2] = stresses[-1][4]
+
+    def next_plane(i):
+        return jnp.minimum((of(i) + 1) * group, x - 1)
+
+    def prior_plane(i):
+        return jnp.maximum(of(i) * group - 1, 0)
+
+    def planes(number):
+        return pl.BlockSpec((number, group, y, z), lambda i: (0, of(i), 0, 0))
+
+    def one(number, which, place):
+        return pl.BlockSpec((number, 1, y, z), lambda i: (which, place(i), 0, 0))
+
+    def medium_one(place):
+        return pl.BlockSpec((1, y, z), lambda i: (place(i), 0, 0))
+
+    medium_block = pl.BlockSpec((group, y, z), lambda i: (of(i), 0, 0))
+    args = [velocity, stress, lame, shear, buoyancy, velocity, stress, lame, shear]
+    args += [velocity, stress, stress, shear, *rims, *medium]
+    in_specs = [planes(3), planes(6), medium_block, medium_block, medium_block]
+    in_specs += [one(3, 0, next_plane), one(1, 0, next_plane)]
+    in_specs += [medium_one(next_plane), medium_one(next_plane)]
+    in_specs += [one(3, 0, prior_plane), one(1, 3, prior_plane), one(1, 4, prior_plane)]
+    in_specs += [medium_one(prior_plane)]
+    in_specs += [whole_block(rim.shape) for rim in (*rims, *medium)]
+    if ends:
+        args += [*x_rims, *x_medium]
+        in_specs += [whole_block(rim.shape) for rim in (*x_rims, *x_medium)]
+    aliases = {}
+    for i, value in enumerate(done):
+        if i < 2:
+            aliases[len(args)] = i
+        in_specs.append(unread() if i < 2 else whole_block(value.shape))
+        args.append(value)
+    out_shape = [(3, x, y, z)]
+    out_specs = [planes(3)]
     if not last:
-        edges = [(5, y, z), (4, y, z), (5, x, z), (4, x, z)]
-        out_shape += [jax.ShapeDtypeStruct((6, x, y, z), f32)]
-        out_shape += [jax.ShapeDtypeStruct(edge, f32) for edge in edges]
-        out_specs += [planes(6, group)] + [whole_block(edge) for edge in edges]
-    return pl.pallas_call(
-        kernel,
-        grid=(steps,),
-        in_specs=[
-            planes(3, group),
-            planes(6, group),
-            medium_block,
-            medium_block,
-            medium_block,
-            pl.BlockSpec((3, 1, y, z), lambda i: (0, after(i), 0, 0)),
-            pl.BlockSpec((1, 1, y, z), lambda i: (0, after(i), 0, 0)),
-            medium_next,
-            medium_next,
-        ]
-        + rim_blocks,
+        out_shape += [(6, x, y, z), (5, x, z), (4, x, z)]
+        out_specs += [planes(6)]
+        if ends:
+            out_shape += [(5, y, z), (4, y, z), (1, z), (1, z)]
+        out_specs += [whole_block(shape) for shape in out_shape[2:]]
+    part = count * group * y * z
+    return pl.pallas_call(
+        kernel,
+        grid=(count,),
+        in_specs=in_specs,
         out_specs=out_specs,
-        out_shape=out_shape,
+        out_shape=[jax.ShapeDtypeStruct(shape, f32) for shape in out_shape],
         scratch_shapes=[pltpu.VMEM((3, y, z), f32)],
+        input_output_aliases=aliases,
         compiler_params=params(),
         cost_estimate=pl.CostEstimate(
-            flops=80 * x * y * z, bytes_accessed=(54 if last else 78) * x * y * z, transcendentals=0
+            flops=80 * part, bytes_accessed=(54 if last else 78) * part, transcendentals=0
         ),
-        name="stencil",
-    )(
-        velocity, stress, lame, shear, buoyancy, velocity, stress, lame, shear, *rims, *medium
-    )
+        name="stencil_ends" if ends else "stencil_middle",
+    )(*args)
 
 
 def propagate(velocity, stress, lame, shear, buoyancy):
     brick = velocity.shape[1:]
-    lame_wide, shear_wide = lame.astype(jnp.float32), shear.astype(jnp.float32)
-
-    def side(which, at, chosen, mediums):
-        index = (at,) if which == 0 else (slice(None), at)
-        fields = [velocity[(i, *index)] for i in range(3)]
-        fields += [stress[(i, *index)] for i in chosen]
-        return jnp.stack(fields + [medium[index] for medium in mediums])
-
-    rims = exchange(
-        side(0, -1, (3, 4), (shear_wide,)),
-        side(0, 0, (0,), (lame_wide, shear_wide)),
-        side(1, -1, (3, 5), (shear_wide,)),
-        side(1, 0, (1,), (lame_wide, shear_wide)),
-    )
-    medium = rims[:4]
+    between = brick[0] // fit(brick[0], 4) > 2
+    rims, x_rims = exchange(*first_rims(brick, velocity, stress, lame, shear))
+    held, medium, x_medium = (rims, x_rims[:2]), (), ()
     for step_index in range(STEPS):
         last = step_index == STEPS - 1
-        found = stencil(brick, velocity, stress, lame, shear, buoyancy, rims, medium, last)
+        state = (velocity, stress, lame, shear, buoyancy)
+        done = []
+        if between:
+            done = stencil(brick, state, rims, medium, None, None, done, last)
+        found = stencil(brick, state, rims, medium, x_rims, x_medium, done, last)
         velocity = found[0]
         if not last:
-            stress = found[1]
-            rims = exchange(*found[2:])
+            stress, y_last, y_first, x_last, x_first, corner_y, corner_x = found[1:]
+            rims, x_rims = exchange(x_last, x_first, y_last, y_first, corner_y, corner_x)
+            medium, x_medium = held
     return velocity
 
 
@@ -612,10 +721,428 @@
     )(place, jnp.asarray(table), velocity, source_p, source_s, *blocks)
 
 
+def doubled(table, axis):
+    high, low = halves(table)
+    return np.concatenate([high, high], axis=axis), low
+
+
+def left_times(table, value):
+    high, low = split(value)
+    return dot(table[0], jnp.concatenate([high, low], axis=0)) + dot(table[1], high)
+
+
+def right_times(value, table):
+    high, low = split(value)
+    return dot(jnp.concatenate([high, low], axis=1), table[0]) + dot(high, table[1])
+
+
+def side_by_side(table, values):
+    width = values[0].shape[1]
+    if width % 128:
+        return [left_times(table, value) for value in values]
+    both = left_times(table, joined(values, 1))
+    return [both[:, i * width : (i + 1) * width] for i in range(len(values))]
+
+
+def cost(flops, values):
+    return pl.CostEstimate(flops=6 * flops, bytes_accessed=4 * values, transcendentals=0)
+
+
+WEIGHT = 1000
+
+
+def crossed(table, plan):
+    shape = (plan.gy, plan.gx, plan.per, table.shape[-1])
+    return table.reshape(shape).transpose(1, 0, 2, 3).reshape(table.shape)
+
+
+def unread():
+    return pl.BlockSpec(memory_space=pl.ANY)
+
+
+def along_z(plan, place, velocity, comps, tables, outs, ahead=()):
+    x, y, z = plan.x, plan.y, plan.z
+    table = np.stack([halves(table) for table in tables]).reshape(len(comps), 2, outs, z // outs, z)
+    group = fit(x, 8)
+    deep = fit(group, 2)
+    rows = z // outs
+
+    def kernel(place_ref, table_ref, *refs):
+        fields, found = refs[: len(comps)], refs[len(comps) + len(ahead) :]
+        at = pl.program_id(0) * group
+        me = place_ref[1]
+        order = [lax.rem(me + s, outs) if outs > 1 else 0 for s in range(outs)]
+        for comp, field in enumerate(fields):
+            high, low = (joined([table_ref[comp, i, g] for g in order], 0) for i in range(2))
+            twice = jnp.concatenate([high, high], axis=1)
+            for plane in range(0, group, deep):
+                parts = split(field[0, plane : plane + deep].reshape(deep * y, z))
+                value = dot(twice, jnp.concatenate(parts, axis=1), ((1,), (1,)))
+                value += dot(low, parts[0], ((1,), (1,)))
+                for i, out in enumerate(found):
+                    for k in range(deep):
+                        part = value[i * rows : (i + 1) * rows, k * y : (k + 1) * y]
+                        out[comp, pl.ds(at + plane + k, rows, stride=x), :] = part
+
+    def block(comp):
+        return pl.BlockSpec((1, group, y, z), lambda i: (comp, i, 0, 0))
+
+    shape = (len(comps), rows * x, y)
+    found = pl.pallas_call(
+        kernel,
+        grid=(x // group,),
+        in_specs=[scalars(), whole_block(table.shape)]
+        + [block(comp) for comp in comps]
+        + [unread()] * len(ahead),
+        out_specs=[whole_block(shape)] * outs,
+        out_shape=[jax.ShapeDtypeStruct(shape, jnp.float32)] * outs,
+        compiler_params=params(),
+        cost_estimate=cost(len(comps) * x * y * z * z, 2 * len(comps) * x * y * z),
+        name="along_z",
+    )(place, jnp.asarray(table), *[velocity] * len(comps), *ahead)
+    return [out.reshape(len(comps), rows, x, y) for out in found]
+
+
+def y_table(plan, table_ref, groups):
+    tables = [(table_ref[0, g], table_ref[1, g]) for g in groups]
+    if plan.y % 128 == 0:
+        high, low = (joined([table[i] for table in tables], 0) for i in range(2))
+        return [(jnp.concatenate([high, high], axis=0), low)]
+    return [(jnp.concatenate([high, high], axis=0), low) for high, low in tables]
+
+
+def over_y(fields, tables):
+    if len(tables) == 1:
+        fields = [joined(fields, 1)]
+    return sum(right_times(field, table) for field, table in zip(fields, tables))
+
+
+def pair_y_forward(plan, place, blocks):
+    x, y, ny = plan.x, plan.y, plan.ny
+    count = blocks[0].shape[1]
+    table = halves(basis(ny).T).reshape(2, plan.gy, y, ny)
+    deep = fit(count, 8)
+    rows = deep * x
+    half = ny // 2
+
+    def kernel(place_ref, table_ref, *refs):
+        ins, out = refs[:-1], refs[-1]
+        me = place_ref[1]
+        tables = y_table(plan, table_ref, [source(me, s, plan.gy) for s in range(plan.gy)])
+        along, rest = (
+            over_y([ref[comp].reshape(rows, y) for ref in ins], tables) for comp in range(2)
+        )
+        wave = lax.broadcasted_iota(jnp.int32, (1, half), 1).astype(jnp.float32)
+        out[:, :, :half] = (rest[:, :half] + wave * along[:, half:]).reshape(deep, x, half)
+        out[:, :, half:] = (rest[:, half:] - wave * along[:, :half]).reshape(deep, x, half)
+
+    return pl.pallas_call(
+        kernel,
+        grid=(count // deep,),
+        in_specs=[scalars(), whole_block(table.shape)]
+        + [pl.BlockSpec((2, deep, x, y), lambda i: (0, i, 0, 0))] * plan.gy,
+        out_specs=pl.BlockSpec((deep, x, ny), lambda i: (i, 0, 0)),
+        out_shape=jax.ShapeDtypeStruct((count, x, ny), jnp.float32),
+        compiler_params=params(),
+        cost_estimate=cost(2 * WEIGHT * count * x * ny * ny, 3 * WEIGHT * count * x * ny),
+        name="pair_y_forward",
+    )(place, jnp.asarray(table), *blocks)
+
+
+def first_x_forward(plan, place, lines):
+    x, y, nx = plan.x, plan.y, plan.nx
+    twice, low = doubled(basis(nx), 1)
+
+    def kernel(place_ref, twice_ref, low_ref, in_ref, *outs):
+        me = place_ref[1]
+        fields = [in_ref[:, lax.rem(me + s, plan.gy), 0].reshape(nx, y) for s in range(plan.gy)]
+        found = side_by_side((twice_ref[...], low_ref[...]), fields)
+        for out, value in zip(outs, found):
+            out[0] = value
+
+    return pl.pallas_call(
+        kernel,
+        grid=(plan.per,),
+        in_specs=[
+            scalars(),
+            whole_block(twice.shape),
+            whole_block(low.shape),
+            pl.BlockSpec((plan.gx, plan.gy, 1, x, y), lambda i: (0, 0, i, 0, 0)),
+        ],
+        out_specs=[pl.BlockSpec((1, nx, y), lambda i: (i, 0, 0))] * plan.gy,
+        out_shape=[jax.ShapeDtypeStruct((plan.per, nx, y), jnp.float32)] * plan.gy,
+        compiler_params=params(),
+        cost_estimate=cost(plan.per * plan.ny * nx * nx, 2 * plan.per * plan.ny * nx),
+        name="first_x_forward",
+    )(place, jnp.asarray(twice), jnp.asarray(low), lines)
+
+
+def slope_x(value):
+    half = value.shape[0] // 2
+    wave = lax.broadcasted_iota(jnp.int32, (half, 1), 0).astype(jnp.float32)
+    return wave * value[half:], -wave * value[:half]
+
+
+def first_y_forward(plan, place, blocks):
+    y, nx, ny = plan.y, plan.nx, plan.ny
+    table = halves(basis(ny).T).reshape(2, plan.gy, y, ny)
+    half = nx // 2
+
+    def kernel(place_ref, table_ref, *refs):
+        ins, out = refs[:-1], refs[-1]
+        me = place_ref[1]
+        tables = y_table(plan, table_ref, [source(me, s, plan.gy) for s in range(plan.gy)])
+        cosine, sine = slope_x(over_y([ref[0] for ref in ins], tables))
+        out[0, :half] = cosine
+        out[0, half:] = sine
+
+    return pl.pallas_call(
+        kernel,
+        grid=(plan.per,),
+        in_specs=[scalars(), whole_block(table.shape)]
+        + [pl.BlockSpec((1, nx, y), lambda i: (i, 0, 0))] * plan.gy,
+        out_specs=pl.BlockSpec((1, nx, ny), lambda i: (i, 0, 0)),
+        out_shape=jax.ShapeDtypeStruct((plan.per, nx, ny), jnp.float32),
+        compiler_params=params(),
+        cost_estimate=cost(plan.per * nx * ny * ny, 2 * plan.per * nx * ny),
+        name="first_y_forward",
+    )(place, jnp.asarray(table), *blocks)
+
+
+def potential(plan, place, first, lines):
+    x, nx, ny, gx = plan.x, plan.nx, plan.ny, plan.gx
+    forth_twice, forth_low = doubled(basis(nx), 1)
+    back_twice, back_low = doubled(-inverse_basis(nx).T, 1)
+    half = nx // 2
+
+    def kernel(place_ref, ft_ref, fl_ref, bt_ref, bl_ref, first_ref, in_ref, out_ref, slope_ref):
+        me_x, me_y = place_ref[0], place_ref[1]
+        total = left_times((ft_ref[...], fl_ref[...]), in_ref[:, 0].reshape(nx, ny))
+        wave_x = lax.broadcasted_iota(jnp.int32, (half, 1), 0).astype(jnp.float32)
+        slot_y = lax.broadcasted_iota(jnp.int32, (1, ny), 1)
+        wave_y = lax.rem(slot_y, ny // 2).astype(jnp.float32)
+        slot_z = (me_y * gx + me_x) * plan.per + pl.program_id(0)
+        wave_z = lax.rem(slot_z, plan.z // 2).astype(jnp.float32)
+        scale = 1.0 / jnp.maximum(wave_x * wave_x + (wave_y * wave_y + wave_z * wave_z), 1.0)
+        cosine = (total[:half] + first_ref[0, :half]) * scale
+        sine = (total[half:] + first_ref[0, half:]) * scale
+        found = jnp.concatenate([cosine, sine], axis=0)
+        out_ref[:, 0] = left_times((bt_ref[...], bl_ref[...]), found).reshape(gx, x, ny)
+        slope_ref[0, :half], slope_ref[0, half:] = slope_x(found)
+
+    tables = [forth_twice, forth_low, back_twice, back_low]
+    spectrum = pl.BlockSpec((1, nx, ny), lambda i: (i, 0, 0))
+    block = pl.BlockSpec((gx, 1, x, ny), lambda i: (0, i, 0, 0))
+    return pl.pallas_call(
+        kernel,
+        grid=(plan.per,),
+        in_specs=[scalars()] + [whole_block(t.shape) for t in tables] + [spectrum, block],
+        out_specs=[block, spectrum],
+        out_shape=[
+            jax.ShapeDtypeStruct(lines.shape, jnp.float32),
+            jax.ShapeDtypeStruct((plan.per, nx, ny), jnp.float32),
+        ],
+        compiler_params=params(),
+        cost_estimate=cost(2 * plan.per * ny * nx * nx, 4 * plan.per * ny * nx),
+        name="potential",
+    )(place, *[jnp.asarray(t) for t in tables], first, lines)
+
+
+def pieces_of_y(plan, table_ref, me, values):
+    groups = [lax.rem(me + s, plan.gy) for s in range(plan.gy)]
+    y = plan.y
+    tables = [(table_ref[0, g], table_ref[1, g]) for g in groups]
+    if y % 128 == 0:
+        tables = [tuple(joined([table[i] for table in tables], 1) for i in range(2))]
+    tables = [(jnp.concatenate([high, high], axis=0), low) for high, low in tables]
+    found = []
+    for value in values:
+        pieces = [right_times(value, table) for table in tables]
+        if y % 128 == 0:
+            pieces = [pieces[0][:, s * y : (s + 1) * y] for s in range(plan.gy)]
+        found.append(pieces)
+    return found
+
+
+def last_y_inverse(plan, place, slope):
+    y, nx, ny = plan.y, plan.nx, plan.ny
+    table = halves(np.stack(np.split(inverse_basis(ny), plan.gy, axis=1)))
+
+    def kernel(place_ref, table_ref, in_ref, *outs):
+        (pieces,) = pieces_of_y(plan, table_ref, place_ref[1], [in_ref[0]])
+        for out, piece in zip(outs, pieces):
+            out[0] = piece
+
+    return pl.pallas_call(
+        kernel,
+        grid=(plan.per,),
+        in_specs=[
+            scalars(),
+            whole_block(table.shape),
+            pl.BlockSpec((1, nx, ny), lambda i: (i, 0, 0)),
+        ],
+        out_specs=[pl.BlockSpec((1, nx, y), lambda i: (i, 0, 0))] * plan.gy,
+        out_shape=[jax.ShapeDtypeStruct((plan.per, nx, y), jnp.float32)] * plan.gy,
+        compiler_params=params(),
+        cost_estimate=cost(plan.per * nx * ny * ny, 2 * plan.per * nx * ny),
+        name="last_y_inverse",
+    )(place, jnp.asarray(table), slope)
+
+
+def last_x_inverse(plan, place, blocks):
+    x, y, nx, gx = plan.x, plan.y, plan.nx, plan.gx
+    twice, low = doubled(-inverse_basis(nx).T, 1)
+
+    def kernel(place_ref, twice_ref, low_ref, *refs):
+        ins, out = refs[:-1], refs[-1]
+        me = place_ref[1]
+        found = side_by_side((twice_ref[...], low_ref[...]), [ref[0] for ref in ins])
+        for s, value in enumerate(found):
+            out[:, source(me, s, plan.gy), 0] = value.reshape(gx, x, y)
+
+    return pl.pallas_call(
+        kernel,
+        grid=(plan.per,),
+        in_specs=[scalars(), whole_block(twice.shape), whole_block(low.shape)]
+        + [pl.BlockSpec((1, nx, y), lambda i: (i, 0, 0))] * plan.gy,
+        out_specs=pl.BlockSpec((gx, plan.gy, 1, x, y), lambda i: (0, 0, i, 0, 0)),
+        out_shape=jax.ShapeDtypeStruct((gx, plan.gy, plan.per, x, y), jnp.float32),
+        compiler_params=params(),
+        cost_estimate=cost(plan.per * plan.ny * nx * nx, 2 * plan.per * plan.ny * nx),
+        name="last_x_inverse",
+    )(place, jnp.asarray(twice), jnp.asarray(low), *blocks)
+
+
+def pair_y_inverse(plan, place, planes, behind):
+    x, y, ny = plan.x, plan.y, plan.ny
+    count = planes.shape[0]
+    table = halves(np.stack(np.split(inverse_basis(ny), plan.gy, axis=1)))
+    deep = fit(count, 8)
+    rows = deep * x
+    half = ny // 2
+
+    def kernel(place_ref, table_ref, in_ref, _, *outs):
+        plain = in_ref[...].reshape(rows, ny)
+        wave = lax.broadcasted_iota(jnp.int32, (1, half), 1).astype(jnp.float32)
+        along = jnp.concatenate([wave * plain[:, half:], -wave * plain[:, :half]], axis=1)
+        found = pieces_of_y(plan, table_ref, place_ref[1], [along, plain])
+        for comp, pieces in enumerate(found):
+            for out, piece in zip(outs[:-1], pieces):
+                out[comp] = piece.reshape(deep, x, y)
+
+    return pl.pallas_call(
+        kernel,
+        grid=(count // deep,),
+        in_specs=[
+            scalars(),
+            whole_block(table.shape),
+            pl.BlockSpec((deep, x, ny), lambda i: (i, 0, 0)),
+            unread(),
+        ],
+        out_specs=[pl.BlockSpec((2, deep, x, y), lambda i: (0, i, 0, 0))] * plan.gy + [unread()],
+        out_shape=[jax.ShapeDtypeStruct((2, count, x, y), jnp.float32)] * plan.gy
+        + [jax.ShapeDtypeStruct(behind.shape, behind.dtype)],
+        input_output_aliases={3: plan.gy},
+        compiler_params=params(),
+        cost_estimate=cost(2 * count * x * ny * ny, 3 * count * x * ny),
+        name="pair_y_inverse",
+    )(place, jnp.asarray(table), planes, behind)
+
+
+def image_part(plan, place, comps, tables, blocks, fields, before, weight):
+    x, y, z = plan.x, plan.y, plan.z
+    outs = len(blocks)
+    rows = z // outs
+    table = np.stack([halves(table) for table in tables]).reshape(len(comps), 2, outs, rows, z)
+    group = fit(x, 8)
+    deep = fit(group, 2)
+
+    def kernel(place_ref, table_ref, *refs):
+        refs = list(refs)
+        inputs = [[refs.pop(0) for _ in comps] for _ in range(3)]
+        started = [refs.pop(0) for _ in before]
+        *ins, image_p, image_s = refs
+        at = pl.program_id(0) * group
+        order = [source(place_ref[1], s, outs) if outs > 1 else 0 for s in range(outs)]
+        turned_tables = []
+        for comp in range(len(comps)):
+            parts = [joined([table_ref[comp, i, g] for g in order], 0) for i in range(2)]
+            high, low = (part.astype(jnp.float32).T.astype(jnp.bfloat16) for part in parts)
+            turned_tables.append((jnp.concatenate([high, high], axis=1), low))
+        for plane in range(0, group, deep):
+            here = slice(plane, plane + deep)
+            total_p, total_s = (ref[here] for ref in started) if before else (0.0, 0.0)
+            for comp, table in enumerate(turned_tables):
+                v_ref, p_ref, s_ref = (each[comp] for each in inputs)
+                columns = []
+                for k in range(deep):
+                    cut = pl.ds(at + plane + k, rows, stride=x)
+                    columns.append(joined([ref[comp, cut, :] for ref in ins], 0))
+                field = left_times(table, joined(columns, 1)).T.reshape(deep, y, z)
+                total_p += p_ref[0, here].astype(jnp.float32) * field
+                total_s += s_ref[0, here].astype(jnp.float32) * (v_ref[0, here] - field)
+            image_p[here] = total_p
+            image_s[here] = total_s
+
+    def block(comp):
+        return pl.BlockSpec((1, group, y, z), lambda i: (comp, i, 0, 0))
+
+    blocks = [part.reshape(len(comps), rows * x, y) for part in blocks]
+    image = pl.BlockSpec((group, y, z), lambda i: (i, 0, 0))
+    return pl.pallas_call(
+        kernel,
+        grid=(x // group,),
+        in_specs=[scalars(), whole_block(table.shape)]
+        + [block(comp) for _ in fields for comp in comps]
+        + [image] * len(before)
+        + [whole_block(part.shape) for part in blocks],
+        out_specs=[image, image],
+        out_shape=[jax.ShapeDtypeStruct((x, y, z), jnp.float32)] * 2,
+        compiler_params=params(),
+        cost_estimate=cost(
+            weight * len(comps) * x * y * z * z, weight * (2 + 3 * len(comps)) * x * y * z
+        ),
+        name="image_part",
+    )(
+        place,
+        jnp.asarray(table),
+        *[field for field in fields for _ in comps],
+        *before,
+        *blocks,
+    )
+
+
+def over_gx(blocks):
+    return lax.all_to_all(blocks, "gx", 0, 0, tiled=True)
+
+
+def separated(plan, place, velocity, source_p, source_s):
+    x, y, z, gx, gy, per = plan.x, plan.y, plan.z, plan.gx, plan.gy, plan.per
+    plain = basis(z)
+    pair = along_z(plan, place, velocity, (1, 2), (plain, turned(plain)), gy)
+    (first,) = along_z(plan, place, velocity, (0,), (crossed(plain, plan),), 1, pair[:1])
+    first = over_gx(first.reshape(gx, gy, per, x, y))
+    pair = pair_y_forward(plan, place, swap_gy(pair))
+    pair = over_gx(pair.reshape(gx, per, x, plan.ny))
+    first = first_y_forward(plan, place, swap_gy(first_x_forward(plan, place, first)))
+    lines, slope = potential(plan, place, first, pair)
+    pair = over_gx(lines)
+    last = last_x_inverse(plan, place, swap_gy(last_y_inverse(plan, place, slope)))
+    *pair, last = pair_y_inverse(plan, place, pair.reshape(gx * per, x, plan.ny), last)
+    pair = swap_gy(pair)
+    last = over_gx(last)
+    back = inverse_basis(z)
+    fields = (velocity, source_p, source_s)
+    found = image_part(plan, place, (1, 2), (back, -turned(back)), pair, fields, (), WEIGHT)
+    return image_part(plan, place, (0,), (crossed(back, plan),), [last], fields, found, 1)
+
+
 def shards(velocity, stress, lame_lambda, shear_modulus, buoyancy, source_p, source_s):
     velocity = propagate(velocity, stress, lame_lambda, shear_modulus, buoyancy)
     plan = Plan(velocity.shape[1:])
     place = jnp.stack([lax.axis_index("gx"), lax.axis_index("gy")]).astype(jnp.int32)
+    if plan.z % (plan.gx * plan.gy) == 0:
+        return tuple(separated(plan, place, velocity, source_p, source_s))
     blocks = z_forward(plan, place, velocity)
     lines = [to_lines(plan, y_forward(plan, place, swap_gy(group))) for group in blocks]
     lines = [x_lines(plan, place, part, chunk) for chunk, part in enumerate(lines)]

time: 421 us -> 344 us (0.82)
  waiting for transfers between devices: 237 us -> 155 us
  Pallas kernels: 97.5 us -> 118 us
  local copies, waits for them, and re-layouts: 27 us -> 10.7 us
    all_to_all x4, waiting for transfers between devices: 121 us -> 28.9 us  [over_gx(): return lax.all_to_all(blocks, 'gx', 0, 0, tiled=True)]
    pallas_call x10 -> x16, Pallas kernels: 97.5 us -> 118 us  [the longest x4 38.5 us: stencil(): pl.pallas_call(kernel, grid=(count,), in_specs=in_specs, out_specs=out_sp...]
    ppermute x4, waiting for transfers between devices: 110 us -> 124 us  [swap_gy(): moved.append(lax.ppermute(blocks[step], 'gy', route))]
    slice x6 -> x0, local copies, waits for them, and re-layouts: 6.42 us -> none  [the longest x2 2.62 us: side(): fields += [stress[i, *index] for i in chosen]]
    ppermute x4, waiting for transfers between devices: 6.06 us -> 0.01 us  [across_corner(): return lax.ppermute(row, ('gx', 'gy'), route)]
    unnamed x46 -> x36, local copies, waits for them, and re-layouts: 14.3 us -> 10.7 us
  transfers between devices with their start and end apart: 20 -> 20, of which waited for: 10 -> 9; matrix products, arithmetic and copies ran while one was open for 2% -> 0% of each run, Pallas kernels for 8% -> 20%
where the time goes in v3:
time: 344 us; the launch traced here: 342 us
  waiting for transfers between devices  155 us (45%)
  Pallas kernels  118 us (34%)
  starting transfers between devices  57.1 us (17%)
  local copies, waits for them, and re-layouts  10.7 us (3%)
    ppermute x4, waiting for transfers between devices, swap_gy(): moved.append(lax.ppermute(blocks[step], 'gy', route))  124 us
    pallas_call x4, Pallas kernels, stencil(): pl.pallas_call(kernel, grid=(count,), in_specs=in_specs, out_specs=out_sp...  38.5 us
    all_to_all x4, waiting for transfers between devices, over_gx(): return lax.all_to_all(blocks, 'gx', 0, 0, tiled=True)  28.9 us
    all_to_all x4, starting transfers between devices, over_gx(): return lax.all_to_all(blocks, 'gx', 0, 0, tiled=True)  22.7 us
    ppermute x8, starting transfers between devices, passed_along(): return lax.ppermute(block, axis, route)  21.8 us
    pallas_call x2, Pallas kernels, image_part(): pl.pallas_call(kernel, grid=(x // group,), in_specs=[scalars(), whole_blo...  17.3 us
    pallas_call x2, Pallas kernels, along_z(): pl.pallas_call(kernel, grid=(x // group,), in_specs=[scalars(), whole_blo...  12.8 us
    unnamed x36, local copies, waits for them, and re-layouts  10.7 us
  transfers between devices with their start and end apart: 20, of which 9 were waited for; matrix products, arithmetic and copies ran while one was open for 0% of the time, Pallas kernels for 20%

profile of v3, /device:TPU:12, one launch (start us, length us, event | category | flops | bytes accessed | tf_op | source)
XLA Modules:
  0.0 342.2 jit_solution(2135415356817269652)
XLA Ops:
  20.2 14.3 %stencil_middle.2 = (f32[3,32,128,128]{3,2,1,0:T(8,128)}, f32[6,32,128,128]{3,2,1,0:T(8,128)}, f32[5,32,128]{2,1,0:T(8,128)}, f32[4,32,128]{2,1,0:T(8,128)}) custom-call(f32[3,32,128,128]{3,2,1,0:T(8,128)} %refs_9_.5, f32[6,32,128,128]{3,2,1,0:T(8,128)} %refs_11_.5, bf16[32,128,128]{2,1,0:T(8,128)(2,1)} %refs_7_.9, bf16[32,128,128]{2,1,0:T(8,128)(2,1)} %refs_12_.9, ...), custom_call_target="tpu_custom_call" | custom-call | flops 31457280 | bytes 30670848 | tf_op jit(solution)/shard_map/stencil_middle/pallas_call | solution.py:333
  35.5 6.8 %stencil_ends.2 = (f32[3,32,128,128]{3,2,1,0:T(8,128)}, f32[6,32,128,128]{3,2,1,0:T(8,128)}, f32[5,32,128]{2,1,0:T(8,128)}, f32[4,32,128]{2,1,0:T(8,128)}, f32[5...) custom-call(f32[3,32,128,128]{3,2,1,0:T(8,128)} %refs_9_.5, ...), custom_call_target="tpu_custom_call", output_to_operand_aliasing={{0}: (19, {}), {1}: (20, {})} | custom-call | flops 10485760 | bytes 10223616 | tf_op jit(solution)/shard_map/stencil_ends/pallas_call | solution.py:333
  61.2 11.7 %stencil_middle.3.refs_23_ = f32[3,32,128,128]{3,2,1,0:T(8,128)} custom-call(f32[3,32,128,128]{3,2,1,0:T(8,128)} %get-tuple-element.43.refs_0_.refs_5_.refs_9_, f32[6,32,128,128]{3,2,1,0:T(8,128)} %get-tuple-element.44.refs_1_.refs_6_.refs_10_.refs_11_, bf16[32,128,128]{2,1,0:T(8,128)(2,1)} %refs_7_.9, bf16[32,128,128]{2,1,0:T(8,128)(2,1)} %refs_12_.9, ...), custom_call_target="tpu_custom_call" | custom-call | flops 31457280 | bytes 21233664 | tf_op jit(solution)/shard_map/stencil_middle/pallas_call | solution.py:333
  74.4 5.7 %stencil_ends.3.refs_0_.refs_1_ = f32[3,32,128,128]{3,2,1,0:T(8,128)} custom-call(f32[3,32,128,128]{3,2,1,0:T(8,128)} %get-tuple-element.43.refs_0_.refs_5_.refs_9_, f32[6,32,128,128]{3,2,1,0:T(8,128)} %get-tuple-element.44.refs_1_.refs_6_.refs_10_.refs_11_, bf16[32,128,128]{2,1,0:T(8,128)(2,1)} %refs_7_.9, ...), custom_call_target="tpu_custom_call", output_to_operand_aliasing={{}: (23, {})} | custom-call | flops 10485760 | bytes 7077888 | tf_op jit(solution)/shard_map/stencil_ends/pallas_call | solution.py:333
  80.1 7.5 %along_z.2 = (f32[2,2048,128]{2,1,0:T(8,128)}, f32[2,2048,128]{2,1,0:T(8,128)}) custom-call(s32[2]{0:T(128)} %pad_add_fusion.place_ref, bf16[2,2,2,64,128]{4,3,2,1,0:T(8,128)(2,1)} %constant.28.clone.table_ref, f32[3,32,128,128]{3,2,1,0:T(8,128)} %stencil_ends.3.refs_0_.refs_1_, f32[3,32,128,128]{3,2,1,0:T(8,128)} %stencil_ends.3.refs_0_.refs_1_), custom_call_target="tpu_custom_call" | custom-call | flops 805306368 | bytes 8388608 | tf_op jit(solution)/shard_map/along_z/pallas_call | solution.py:791
  89.9 5.3 %along_z.3 = f32[1,4096,128]{2,1,0:T(8,128)} custom-call(s32[2]{0:T(128)} %pad_add_fusion.place_ref, bf16[1,2,1,128,128]{4,3,2,1,0:T(8,128)(2,1)} %constant.29.clone.table_ref, f32[3,32,128,128]{3,2,1,0:T(8,128)} %stencil_ends.3.refs_0_.refs_1_, f32[2,64,32,128]{3,2,1,0:T(8,128)} %bitcast.13), custom_call_target="tpu_custom_call" | custom-call | flops 402653184 | bytes 4194304 | tf_op jit(solution)/shard_map/along_z/pallas_call | solution.py:791
  95.2 7.6 %all-to-all-start = ((f32[16,2,4,32,128]{4,3,2,1,0:T(8,128)}), f32[16,2,4,32,128]{4,3,2,1,0:T(8,128)}, u32[]{:S(2)}, u32[]{:S(2)}) async-start(f32[16,2,4,32,128]{4,3,2,1,0:T(8,128)} %bitcast.10), calls=%async_computation | async-start | bytes 4194304 | tf_op jit(solution)/shard_map/all_to_all | solution.py:1116
  102.7 31.4 %collective-permute-done.13.refs_1_ = f32[2,64,32,128]{3,2,1,0:T(8,128)S(1)} collective-permute-done((f32[2,64,32,128]{3,2,1,0:T(8,128)}, f32[2,64,32,128]{3,2,1,0:T(8,128)S(1)}, u32[]{:S(2)}, u32[]{:S(2)}) %collective-permute-start.13) | collective-permute-done | bytes 2097184 | tf_op jit(solution)/shard_map/ppermute | solution.py:507
  135.5 7.5 %pair_y_forward.1 = f32[64,32,256]{2,1,0:T(8,128)} custom-call(s32[2]{0:T(128)} %pad_add_fusion.place_ref, bf16[2,2,128,256]{3,2,1,0:T(8,128)(2,1)} %constant.30.clone.table_ref, f32[2,64,32,128]{3,2,1,0:T(8,128)} %bitcast.14, f32[2,64,32,128]{3,2,1,0:T(8,128)} %copy-done.16), custom_call_target="tpu_custom_call" | custom-call | flops 1610612736000 | bytes 6291456000 | tf_op jit(solution)/shard_map/pair_y_forward/pallas_call | solution.py:839
  143.0 7.1 %all-to-all-done.in_ref = f32[16,2,4,32,128]{4,3,2,1,0:T(8,128)} async-done(((f32[16,2,4,32,128]{4,3,2,1,0:T(8,128)}), f32[16,2,4,32,128]{4,3,2,1,0:T(8,128)}, u32[]{:S(2)}, u32[]{:S(2)}) %all-to-all-start) | async-done | bytes 2097184 | tf_op jit(solution)/shard_map/all_to_all | solution.py:1116
  150.1 5.1 %all-to-all-start.1 = ((f32[16,4,32,256]{3,2,1,0:T(8,128)}), f32[16,4,32,256]{3,2,1,0:T(8,128)S(1)}, u32[]{:S(2)}, u32[]{:S(2)}) async-start(f32[16,4,32,256]{3,2,1,0:T(8,128)} %bitcast.12), calls=%async_computation.1 | async-start | bytes 4194304 | tf_op jit(solution)/shard_map/all_to_all | solution.py:1116
  155.2 5.4 %first_x_forward.1 = (f32[4,512,128]{2,1,0:T(8,128)}, f32[4,512,128]{2,1,0:T(8,128)}) custom-call(s32[2]{0:T(128)} %pad_add_fusion.place_ref, bf16[512,1024]{1,0:T(8,128)(2,1)} %constant.31.clone.twice_ref.ft_ref, bf16[512,512]{1,0:T(8,128)(2,1)} %constant.32.clone.low_ref.fl_ref, f32[16,2,4,32,128]{4,3,2,1,0:T(8,128)} %all-to-all-done.in_ref), custom_call_target="tpu_custom_call" | custom-call | flops 1610612736 | bytes 4194304 | tf_op jit(solution)/shard_map/first_x_forward/pallas_call | solution.py:863
  160.9 25.1 %collective-permute-done.12.refs_1_ = f32[4,512,128]{2,1,0:T(8,128)S(1)} collective-permute-done((f32[4,512,128]{2,1,0:T(8,128)}, f32[4,512,128]{2,1,0:T(8,128)S(1)}, u32[]{:S(2)}, u32[]{:S(2)}) %collective-permute-start.12) | collective-permute-done | bytes 1048608 | tf_op jit(solution)/shard_map/ppermute | solution.py:507
  191.5 10.9 %all-to-all-done.1.in_ref = f32[16,4,32,256]{3,2,1,0:T(8,128)S(1)} async-done(((f32[16,4,32,256]{3,2,1,0:T(8,128)}), f32[16,4,32,256]{3,2,1,0:T(8,128)S(1)}, u32[]{:S(2)}, u32[]{:S(2)}) %all-to-all-start.1) | async-done | bytes 2097184 | tf_op jit(solution)/shard_map/all_to_all | solution.py:1116
  203.8 10.6 %potential.1 = (f32[16,4,32,256]{3,2,1,0:T(8,128)}, f32[4,512,256]{2,1,0:T(8,128)}) custom-call(s32[2]{0:T(128)} %pad_add_fusion.place_ref, bf16[512,1024]{1,0:T(8,128)(2,1)} %constant.31.clone.twice_ref.ft_ref, bf16[512,512]{1,0:T(8,128)(2,1)} %constant.32.clone.low_ref.fl_ref, bf16[512,1024]{1,0:T(8,128)(2,1)} %constant.33.clone.bt_ref.twice_ref, ...), custom_call_target="tpu_custom_call" | custom-call | flops 3221225472 | bytes 8388608 | tf_op jit(solution)/shard_map/potential/pallas_call | solution.py:936
  214.4 5.1 %all-to-all-start.2 = ((f32[16,4,32,256]{3,2,1,0:T(8,128)}), f32[16,4,32,256]{3,2,1,0:T(8,128)S(1)}, u32[]{:S(2)}, u32[]{:S(2)}) async-start(f32[16,4,32,256]{3,2,1,0:T(8,128)} %get-tuple-element.55), calls=%async_computation.2 | async-start | bytes 4194304 | tf_op jit(solution)/shard_map/all_to_all | solution.py:1116
  224.3 25.1 %collective-permute-done.14.refs_1_ = f32[4,512,128]{2,1,0:T(8,128)S(1)} collective-permute-done((f32[4,512,128]{2,1,0:T(8,128)}, f32[4,512,128]{2,1,0:T(8,128)S(1)}, u32[]{:S(2)}, u32[]{:S(2)}) %collective-permute-start.14) | collective-permute-done | bytes 1048608 | tf_op jit(solution)/shard_map/ppermute | solution.py:507
  250.4 5.4 %last_x_inverse.1._ = f32[16,2,4,32,128]{4,3,2,1,0:T(8,128)} custom-call(s32[2]{0:T(128)} %pad_add_fusion.place_ref, bf16[512,1024]{1,0:T(8,128)(2,1)} %constant.33.clone.bt_ref.twice_ref, bf16[512,512]{1,0:T(8,128)(2,1)} %constant.34.clone.bl_ref.low_ref, f32[4,512,128]{2,1,0:T(8,128)} %get-tuple-element.57.refs_0_, f32[4,512,128]{2,1,0:T(8,128)} %copy-done.17), custom_call_target="tpu_custom_call" | custom-call | flops 1610612736 | bytes 4194304 | tf_op jit(solution)/shard_map/last_x_inverse/pallas_call | solution.py:1003
  255.9 10.9 %all-to-all-done.2 = f32[16,4,32,256]{3,2,1,0:T(8,128)S(1)} async-done(((f32[16,4,32,256]{3,2,1,0:T(8,128)}), f32[16,4,32,256]{3,2,1,0:T(8,128)S(1)}, u32[]{:S(2)}, u32[]{:S(2)}) %all-to-all-start.2) | async-done | bytes 2097184 | tf_op jit(solution)/shard_map/all_to_all | solution.py:1116
  268.0 7.5 %pair_y_inverse.1 = (f32[2,64,32,128]{3,2,1,0:T(8,128)}, f32[2,64,32,128]{3,2,1,0:T(8,128)}, f32[16,2,4,32,128]{4,3,2,1,0:T(8,128)}) custom-call(s32[2]{0:T(128)} %pad_add_fusion.place_ref, bf16[2,2,256,128]{3,2,1,0:T(8,128)(2,1)} %constant.35.clone.table_ref, f32[64,32,256]{2,1,0:T(8,128)} %bitcast.11, ...), custom_call_target="tpu_custom_call", output_to_operand_aliasing={{2}: (3, {})} | custom-call | flops 1610612736 | bytes 6291456 | tf_op jit(solution)/shard_map/pair_y_inverse/pallas_call | solution.py:1033
  275.8 5.1 %all-to-all-start.3 = ((f32[16,2,4,32,128]{4,3,2,1,0:T(8,128)}), f32[16,2,4,32,128]{4,3,2,1,0:T(8,128)}, u32[]{:S(2)}, u32[]{:S(2)}) async-start(f32[16,2,4,32,128]{4,3,2,1,0:T(8,128)} %get-tuple-element.63), calls=%async_computation.3 | async-start | bytes 4194304 | tf_op jit(solution)/shard_map/all_to_all | solution.py:1116
  280.9 42.7 %collective-permute-done.15 = f32[2,64,32,128]{3,2,1,0:T(8,128)S(1)} collective-permute-done((f32[2,64,32,128]{3,2,1,0:T(8,128)}, f32[2,64,32,128]{3,2,1,0:T(8,128)S(1)}, u32[]{:S(2)}, u32[]{:S(2)}) %collective-permute-start.15) | collective-permute-done | bytes 2097184 | tf_op jit(solution)/shard_map/ppermute | solution.py:507
  324.9 9.5 %image_part.2 = (f32[32,128,128]{2,1,0:T(8,128)}, f32[32,128,128]{2,1,0:T(8,128)}) custom-call(s32[2]{0:T(128)} %pad_add_fusion.place_ref, bf16[2,2,2,64,128]{4,3,2,1,0:T(8,128)(2,1)} %constant.36.clone.table_ref, f32[3,32,128,128]{3,2,1,0:T(8,128)} %stencil_ends.3.refs_0_.refs_1_, f32[3,32,128,128]{3,2,1,0:T(8,128)} %stencil_ends.3.refs_0_.refs_1_, ...), custom_call_target="tpu_custom_call" | custom-call | flops 805306368000 | bytes 16777216000 | tf_op jit(solution)/shard_map/image_part/pallas_call | solution.py:1092
  334.5 7.8 %image_part.3 = (f32[32,128,128]{2,1,0:T(8,128)}, f32[32,128,128]{2,1,0:T(8,128)}) custom-call(s32[2]{0:T(128)} %pad_add_fusion.place_ref, bf16[1,2,1,128,128]{4,3,2,1,0:T(8,128)(2,1)} %constant.37.clone.table_ref, f32[3,32,128,128]{3,2,1,0:T(8,128)} %stencil_ends.3.refs_0_.refs_1_, bf16[3,32,128,128]{3,2,1,0:T(8,128)(2,1)} %refs_1_.7, ...), custom_call_target="tpu_custom_call" | custom-call | flops 402653184 | bytes 10485760 | tf_op jit(solution)/shard_map/image_part/pallas_call | solution.py:1092
  (69 shorter events, 60.1 us)
Async XLA Ops:
  3.9 30.7 %collective-permute-start.2 = (f32[6,128,128]{2,1,0:T(8,128)}, f32[6,128,128]{2,1,0:T(8,128)S(1)}, u32[]{:S(2)}, u32[]{:S(2)}) collective-permute-start(f32[6,128,128]{2,1,0:T(8,128)} %get-tuple-element.35), channel_id=1, source_target_pairs={{0,2},{2,4},{4,6},{6,8},{8,10},{10,12},{12,14},{14,16},{16,18},{18... | collective-permute-start | bytes 1179656 | tf_op jit(solution)/shard_map/ppermute | solution.py:20
  5.8 28.8 %collective-permute-start.3 = (f32[6,128,128]{2,1,0:T(8,128)}, f32[6,128,128]{2,1,0:T(8,128)S(1)}, u32[]{:S(2)}, u32[]{:S(2)}) collective-permute-start(f32[6,128,128]{2,1,0:T(8,128)} %get-tuple-element.36), channel_id=1, source_target_pairs={{2,0},{4,2},{6,4},{8,6},{10,8},{12,10},{14,12},{16,14},{18,16},{20... | collective-permute-start | bytes 1179656 | tf_op jit(solution)/shard_map/ppermute | solution.py:20
  9.5 8.2 %collective-permute-start = (f32[6,32,128]{2,1,0:T(8,128)}, f32[6,32,128]{2,1,0:T(8,128)S(1)}, u32[]{:S(2)}, u32[]{:S(2)}) collective-permute-start(f32[6,32,128]{2,1,0:T(8,128)} %get-tuple-element.33), channel_id=1, source_target_pairs={{0,1},{2,3},{4,5},{6,7},{8,9},{10,11},{12,13},{14,15},{16,17},{18,... | collective-permute-start | bytes 294920 | tf_op jit(solution)/shard_map/ppermute | solution.py:20
  12.9 6.7 %collective-permute-start.1 = (f32[6,32,128]{2,1,0:T(8,128)}, f32[6,32,128]{2,1,0:T(8,128)S(1)}, u32[]{:S(2)}, u32[]{:S(2)}) collective-permute-start(f32[6,32,128]{2,1,0:T(8,128)} %get-tuple-element.34), channel_id=1, source_target_pairs={{1,0},{3,2},{5,4},{7,6},{9,8},{11,10},{13,12},{15,14},{17,16},{19,... | collective-permute-start | bytes 294920 | tf_op jit(solution)/shard_map/ppermute | solution.py:20
  14.2 20.4 %collective-permute-start.4 = (f32[1,128]{1,0:T(1,128)}, f32[1,128]{1,0:T(1,128)S(1)}, u32[]{:S(2)}, u32[]{:S(2)}) collective-permute-start(f32[1,128]{1,0:T(1,128)} %get-tuple-element.37), channel_id=1, source_target_pairs={{2,1},{4,3},{6,5},{8,7},{10,9},{12,11},{14,13},{16,15},{18,17},{20... | collective-permute-start | bytes 1544 | tf_op jit(solution)/shard_map/ppermute | solution.py:31
  17.6 2.0 copy-start.4
  17.6 17.0 %collective-permute-start.5 = (f32[1,128]{1,0:T(1,128)}, f32[1,128]{1,0:T(1,128)S(1)}, u32[]{:S(2)}, u32[]{:S(2)}) collective-permute-start(f32[1,128]{1,0:T(1,128)} %get-tuple-element.38), channel_id=1, source_target_pairs={{1,2},{3,4},{5,6},{7,8},{9,10},{11,12},{13,14},{15,16},{17,18},{19... | collective-permute-start | bytes 1544 | tf_op jit(solution)/shard_map/ppermute | solution.py:31
  42.3 30.6 %collective-permute-start.8 = (f32[5,128,128]{2,1,0:T(8,128)}, f32[5,128,128]{2,1,0:T(8,128)S(1)}, u32[]{:S(2)}, u32[]{:S(2)}) collective-permute-start(f32[5,128,128]{2,1,0:T(8,128)} %get-tuple-element.47), channel_id=1, source_target_pairs={{0,2},{2,4},{4,6},{6,8},{8,10},{10,12},{12,14},{14,16},{16,18},{18... | collective-permute-start | bytes 983048 | tf_op jit(solution)/shard_map/ppermute | solution.py:20
  44.9 28.1 %collective-permute-start.9 = (f32[4,128,128]{2,1,0:T(8,128)}, f32[4,128,128]{2,1,0:T(8,128)S(1)}, u32[]{:S(2)}, u32[]{:S(2)}) collective-permute-start(f32[4,128,128]{2,1,0:T(8,128)} %get-tuple-element.48), channel_id=1, source_target_pairs={{2,0},{4,2},{6,4},{8,6},{10,8},{12,10},{14,12},{16,14},{18,16},{20... | collective-permute-start | bytes 786440 | tf_op jit(solution)/shard_map/ppermute | solution.py:20
  47.9 12.7 %collective-permute-start.6 = (f32[5,32,128]{2,1,0:T(8,128)}, f32[5,32,128]{2,1,0:T(8,128)S(1)}, u32[]{:S(2)}, u32[]{:S(2)}) collective-permute-start(f32[5,32,128]{2,1,0:T(8,128)} %get-tuple-element.45), channel_id=1, source_target_pairs={{0,1},{2,3},{4,5},{6,7},{8,9},{10,11},{12,13},{14,15},{16,17},{18,... | collective-permute-start | bytes 245768 | tf_op jit(solution)/shard_map/ppermute | solution.py:20
  52.7 6.6 %collective-permute-start.7 = (f32[4,32,128]{2,1,0:T(8,128)}, f32[4,32,128]{2,1,0:T(8,128)S(1)}, u32[]{:S(2)}, u32[]{:S(2)}) collective-permute-start(f32[4,32,128]{2,1,0:T(8,128)} %get-tuple-element.46), channel_id=1, source_target_pairs={{1,0},{3,2},{5,4},{7,6},{9,8},{11,10},{13,12},{15,14},{17,16},{19,... | collective-permute-start | bytes 196616 | tf_op jit(solution)/shard_map/ppermute | solution.py:20
  54.6 18.3 %collective-permute-start.10 = (f32[1,128]{1,0:T(1,128)}, f32[1,128]{1,0:T(1,128)S(1)}, u32[]{:S(2)}, u32[]{:S(2)}) collective-permute-start(f32[1,128]{1,0:T(1,128)} %get-tuple-element.49), channel_id=1, source_target_pairs={{2,1},{4,3},{6,5},{8,7},{10,9},{12,11},{14,13},{16,15},{18,17},{20... | collective-permute-start | bytes 1544 | tf_op jit(solution)/shard_map/ppermute | solution.py:31
  59.3 13.6 %collective-permute-start.11 = (f32[1,128]{1,0:T(1,128)}, f32[1,128]{1,0:T(1,128)S(1)}, u32[]{:S(2)}, u32[]{:S(2)}) collective-permute-start(f32[1,128]{1,0:T(1,128)} %get-tuple-element.50), channel_id=1, source_target_pairs={{1,2},{3,4},{5,6},{7,8},{9,10},{11,12},{13,14},{15,16},{17,18},{19... | collective-permute-start | bytes 1544 | tf_op jit(solution)/shard_map/ppermute | solution.py:31
  87.6 46.6 %collective-permute-start.13 = (f32[2,64,32,128]{3,2,1,0:T(8,128)}, f32[2,64,32,128]{3,2,1,0:T(8,128)S(1)}, u32[]{:S(2)}, u32[]{:S(2)}) collective-permute-start(f32[2,64,32,128]{3,2,1,0:T(8,128)} %bitcast.16), channel_id=1, source_target_pairs={{0,1},{1,0},{2,3},{3,2},{4,5},{5,4},{6,7},{7,6},{8,9},{9,8},{10,11... | collective-permute-start | bytes 6291464 | tf_op jit(solution)/shard_map/ppermute | solution.py:507
  95.2 54.9 %all-to-all-start = ((f32[16,2,4,32,128]{4,3,2,1,0:T(8,128)}), f32[16,2,4,32,128]{4,3,2,1,0:T(8,128)}, u32[]{:S(2)}, u32[]{:S(2)}) async-start(f32[16,2,4,32,128]{4,3,2,1,0:T(8,128)} %bitcast.10), calls=%async_computation | async-start | bytes 4194304 | tf_op jit(solution)/shard_map/all_to_all | solution.py:1116
  134.2 1.3 copy-start.16
  150.1 52.3 %all-to-all-start.1 = ((f32[16,4,32,256]{3,2,1,0:T(8,128)}), f32[16,4,32,256]{3,2,1,0:T(8,128)S(1)}, u32[]{:S(2)}, u32[]{:S(2)}) async-start(f32[16,4,32,256]{3,2,1,0:T(8,128)} %bitcast.12), calls=%async_computation.1 | async-start | bytes 4194304 | tf_op jit(solution)/shard_map/all_to_all | solution.py:1116
  160.6 25.4 %collective-permute-start.12 = (f32[4,512,128]{2,1,0:T(8,128)}, f32[4,512,128]{2,1,0:T(8,128)S(1)}, u32[]{:S(2)}, u32[]{:S(2)}) collective-permute-start(f32[4,512,128]{2,1,0:T(8,128)} %get-tuple-element.53), channel_id=1, source_target_pairs={{0,1},{1,0},{2,3},{3,2},{4,5},{5,4},{6,7},{7,6},{8,9},{9,8},{10,11... | collective-permute-start | bytes 3145736 | tf_op jit(solution)/shard_map/ppermute | solution.py:507
  202.4 1.3 copy-start.1
  214.4 52.3 %all-to-all-start.2 = ((f32[16,4,32,256]{3,2,1,0:T(8,128)}), f32[16,4,32,256]{3,2,1,0:T(8,128)S(1)}, u32[]{:S(2)}, u32[]{:S(2)}) async-start(f32[16,4,32,256]{3,2,1,0:T(8,128)} %get-tuple-element.55), calls=%async_computation.2 | async-start | bytes 4194304 | tf_op jit(solution)/shard_map/all_to_all | solution.py:1116
  224.0 25.4 %collective-permute-start.14 = (f32[4,512,128]{2,1,0:T(8,128)}, f32[4,512,128]{2,1,0:T(8,128)S(1)}, u32[]{:S(2)}, u32[]{:S(2)}) collective-permute-start(f32[4,512,128]{2,1,0:T(8,128)} %get-tuple-element.58), channel_id=1, source_target_pairs={{0,1},{1,0},{2,3},{3,2},{4,5},{5,4},{6,7},{7,6},{8,9},{9,8},{10,11... | collective-permute-start | bytes 3145736 | tf_op jit(solution)/shard_map/ppermute | solution.py:507
  266.7 1.3 copy-start
  275.6 48.0 %collective-permute-start.15 = (f32[2,64,32,128]{3,2,1,0:T(8,128)}, f32[2,64,32,128]{3,2,1,0:T(8,128)S(1)}, u32[]{:S(2)}, u32[]{:S(2)}) collective-permute-start(f32[2,64,32,128]{3,2,1,0:T(8,128)} %get-tuple-element.60), channel_id=1, source_target_pairs={{0,1},{1,0},{2,3},{3,2},{4,5},{5,4},{6,7},{7,6},{8,9},{9,8},{10,11... | collective-permute-start | bytes 6291464 | tf_op jit(solution)/shard_map/ppermute | solution.py:507
  275.8 58.6 %all-to-all-start.3 = ((f32[16,2,4,32,128]{4,3,2,1,0:T(8,128)}), f32[16,2,4,32,128]{4,3,2,1,0:T(8,128)}, u32[]{:S(2)}, u32[]{:S(2)}) async-start(f32[16,2,4,32,128]{4,3,2,1,0:T(8,128)} %get-tuple-element.63), calls=%async_computation.3 | async-start | bytes 4194304 | tf_op jit(solution)/shard_map/all_to_all | solution.py:1116
  (14 other events, 11.2 us)

commit v4 on v3

--- a/solution.py
+++ b/solution.py
@@ -9,7 +9,13 @@
 
 STEPS = 2
 MOST_CHUNKS = 1
-VMEM_BYTES = 56 * 2**20
+VMEM_BYTES = 63 * 2**20
+STENCIL_BYTES = 22 * 2**20
+Y_DEEP = 32
+Z_GROUP = 16
+X_GROUP = 4
+Y_TILE = 32
+WEIGHT = 1000
 
 time_step = 0.2
 
@@ -99,8 +105,9 @@
 def stencil(brick, state, rims, medium, x_rims, x_medium, done, last):
     x, y, z = brick
     velocity, stress, lame, shear, buoyancy = state
-    group = fit(x, 4)
+    group = fit(x, X_GROUP)
     groups = x // group
+    tall = fit(y, Y_TILE)
     ends = x_rims is not None
     if ends:
         count, of = min(groups, 2), lambda i: i * (groups - 1)
@@ -130,29 +137,29 @@
             s_out, y_last, y_first = take(3)
             if ends:
                 x_last, x_first, corner_y, corner_x = take(4)
-        carried = take(1)[0]
+        carried, xx_after = take(2)
+        s_new = take(1)[0] if last else s_out
         turn = pl.program_id(0)
         here_group = of(turn)
         at = here_group * group
         start, end = here_group == 0, here_group == groups - 1
         row = lax.broadcasted_iota(jnp.int32, (y, z), 0)
         lane = lax.broadcasted_iota(jnp.int32, (y, z), 1)
-        first_row, last_row = row == 0, row == y - 1
-        first_lane, last_lane = lane == 0, lane == z - 1
 
         def next_z(field):
-            edge = last_lane if field.shape[0] == y else last_lane[:1]
+            edge = lane[: field.shape[0]] == z - 1
             return jnp.where(edge, 0.0, pltpu.roll(field, z - 1, 1))
 
         def prior_z(field):
-            edge = first_lane if field.shape[0] == y else first_lane[:1]
+            edge = lane[: field.shape[0]] == 0
             return jnp.where(edge, 0.0, pltpu.roll(field, 1, 1))
 
         def next_y(field, rim):
-            return jnp.where(last_row, rim, pltpu.roll(field, y - 1, 0))
+            rows = field.shape[0]
+            return jnp.where(row[:rows] == rows - 1, rim, pltpu.roll(field, rows - 1, 0))
 
         def prior_y(field, rim):
-            return jnp.where(first_row, rim, pltpu.roll(field, 1, 0))
+            return jnp.where(row[: field.shape[0]] == 0, rim, pltpu.roll(field, 1, 0))
 
         def wide(value):
             return value.astype(f32)
@@ -197,102 +204,133 @@
                 y_last[...] = given[2][...]
                 y_first[...] = given[3][...]
 
-        after = [finish(v_next_ref[i, 0], lambda: xr[i]) for i in range(3)]
-        stresses = []
-        vx_prior = carried[0]
+        def after(i, rows):
+            return finish(v_next_ref[i, 0, rows], lambda: xr[i, rows])
+
+        spans = [slice(top, top + tall) for top in range(0, y, tall)]
+
+        def row_before(span, field, rim):
+            return rim() if span.start == 0 else field[span.start - 1 : span.start]
+
+        def row_after(span, field, rim):
+            return rim() if span.stop == y else field[span.stop : span.stop + 1]
+
         for k in range(group):
-            vx, vy, vz = v_ref[0, k], v_ref[1, k], v_ref[2, k]
-            vy_next = after[1] if k == group - 1 else v_ref[1, k + 1]
-            vz_next = after[2] if k == group - 1 else v_ref[2, k + 1]
-            lame_value, shear_value = wide(lame_ref[k]), wide(shear_ref[k])
-            ex = vx - vx_prior
-            ey = vy - prior_y(vy, line(yl, 1, at + k))
+            here = at + k
+            v_here = [v_ref.at[i, k] for i in range(3)]
+            for span in spans:
+                vx, vy, vz = (field[span] for field in v_here)
+                vx_prior = carried[0, span] if k == 0 else v_ref[0, k - 1, span]
+                vy_next = after(1, span) if k == group - 1 else v_ref[1, k + 1, span]
+                vz_next = after(2, span) if k == group - 1 else v_ref[2, k + 1, span]
+                vy_rim = row_before(span, v_here[1], lambda: line(yl, 1, here))
+                vx_rim = row_after(span, v_here[0], lambda: line(yr, 0, here))
+                vz_rim = row_after(span, v_here[2], lambda: line(yr, 2, here))
+                lame_value, shear_value = wide(lame_ref[k, span]), wide(shear_ref[k, span])
+                ex = vx - vx_prior
+                ey = vy - prior_y(vy, vy_rim)
+                ez = vz - prior_z(vz)
+                swell = lame_value * (ex + ey + ez)
+                double = 2.0 * shear_value
+                pull = time_step * shear_value
+                found = (
+                    s_ref[0, k, span] + time_step * (swell + double * ex),
+                    s_ref[1, k, span] + time_step * (swell + double * ey),
+                    s_ref[2, k, span] + time_step * (swell + double * ez),
+                    s_ref[3, k, span] + pull * ((next_y(vx, vx_rim) - vx) + (vy_next - vy)),
+                    s_ref[4, k, span] + pull * ((next_z(vx) - vx) + (vz_next - vz)),
+                    s_ref[5, k, span] + pull * ((next_z(vy) - vy) + (next_y(vz, vz_rim) - vz)),
+                )
+                for i, value in enumerate(found):
+                    s_new[i, k, span] = value
+
+        for span in spans:
+            vx, vy, vz = (after(i, span) for i in range(3))
+            vy_rim = (
+                line_after(at + group)
+                if span.start == 0
+                else after(1, slice(span.start - 1, span.start))
+            )
+            ex = vx - v_ref[0, group - 1, span]
+            ey = vy - prior_y(vy, vy_rim)
             ez = vz - prior_z(vz)
-            swell = lame_value * (ex + ey + ez)
-            double = 2.0 * shear_value
-            xx = s_ref[0, k] + time_step * (swell + double * ex)
-            yy = s_ref[1, k] + time_step * (swell + double * ey)
-            zz = s_ref[2, k] + time_step * (swell + double * ez)
-            pull = time_step * shear_value
-            xy = s_ref[3, k] + pull * ((next_y(vx, line(yr, 0, at + k)) - vx) + (vy_next - vy))
-            xz = s_ref[4, k] + pull * ((next_z(vx) - vx) + (vz_next - vz))
-            yz = s_ref[5, k] + pull * (
-                (next_z(vy) - vy) + (next_y(vz, line(yr, 2, at + k)) - vz)
+            lame_value = finish(wide(lame_next_ref[0, span]), lambda: xr_medium[4, span])
+            shear_value = finish(wide(shear_next_ref[0, span]), lambda: xr_medium[5, span])
+            xx_after[span] = finish(xx_next_ref[0, 0, span], lambda: xr[3, span]) + time_step * (
+                lame_value * (ex + ey + ez) + 2.0 * shear_value * ex
             )
-            stresses.append((xx, yy, zz, xy, xz, yz))
-            vx_prior = vx
-
-        ex = after[0] - vx_prior
-        ey = after[1] - prior_y(after[1], line_after(at + group))
-        ez = after[2] - prior_z(after[2])
-        lame_value = finish(wide(lame_next_ref[0]), lambda: xr_medium[4])
-        shear_value = finish(wide(shear_next_ref[0]), lambda: xr_medium[5])
-        xx_after = finish(xx_next_ref[0, 0], lambda: xr[3]) + time_step * (
-            lame_value * (ex + ey + ez) + 2.0 * shear_value * ex
-        )
-
-        xy_prior, xz_prior = carried[1], carried[2]
+
         for k in range(group):
-            xx, yy, zz, xy, xz, yz = stresses[k]
-            xx_next = xx_after if k == group - 1 else stresses[k + 1][0]
             here = at + k
-            vx, vy, vz = v_ref[0, k], v_ref[1, k], v_ref[2, k]
+            v_here = [v_ref.at[i, k] for i in range(3)]
+            vx_edge, vy_edge, vz_edge = v_here[0][:1], v_here[1][y - 1 :], v_here[2][:1]
             pull = time_step * line(yl_medium, 5, here)
             vy_rim, vz_rim = line(yl, 1, here), line(yl, 2, here)
             xy_rim = line(yl, 3, here) + pull * (
-                (vx[:1] - line(yl, 0, here)) + (line_after(here + 1) - vy_rim)
+                (vx_edge - line(yl, 0, here)) + (line_after(here + 1) - vy_rim)
             )
-            yz_rim = line(yl, 4, here) + pull * ((next_z(vy_rim) - vy_rim) + (vz[:1] - vz_rim))
+            yz_rim = line(yl, 4, here) + pull * ((next_z(vy_rim) - vy_rim) + (vz_edge - vz_rim))
             vx_rim, vz_rim = line(yr, 0, here), line(yr, 2, here)
             ex = vx_rim - line_before(here - 1)
-            ey = line(yr, 1, here) - vy[-1:]
+            ey = line(yr, 1, here) - vy_edge
             ez = vz_rim - prior_z(vz_rim)
             yy_rim = line(yr, 3, here) + time_step * (
                 line(yr_medium, 4, here) * (ex + ey + ez) + 2.0 * line(yr_medium, 5, here) * ey
             )
-            push = time_step * wide(buoy_ref[k])
-            vx = vx + push * (
-                (xx_next - xx) + (xy - prior_y(xy, xy_rim)) + (xz - prior_z(xz))
-            )
-            vy = vy + push * ((xy - xy_prior) + (next_y(yy, yy_rim) - yy) + (yz - prior_z(yz)))
-            vz = vz + push * ((xz - xz_prior) + (yz - prior_y(yz, yz_rim)) + (next_z(zz) - zz))
-            xy_prior, xz_prior = xy, xz
-            for i, value in enumerate((vx, vy, vz)):
-                new[i, k] = value
+            s_here = [s_new.at[i, k] for i in range(6)]
+            for span in spans:
+                xx, yy, zz, xy, xz, yz = (field[span] for field in s_here)
+                xx_next = xx_after[span] if k == group - 1 else s_new[0, k + 1, span]
+                xy_prior = carried[1, span] if k == 0 else s_new[3, k - 1, span]
+                xz_prior = carried[2, span] if k == 0 else s_new[4, k - 1, span]
+                xy_before = row_before(span, s_here[3], lambda: xy_rim)
+                yz_before = row_before(span, s_here[5], lambda: yz_rim)
+                yy_after = row_after(span, s_here[1], lambda: yy_rim)
+                push = time_step * wide(buoy_ref[k, span])
+                new[0, k, span] = v_ref[0, k, span] + push * (
+                    (xx_next - xx) + (xy - prior_y(xy, xy_before)) + (xz - prior_z(xz))
+                )
+                new[1, k, span] = v_ref[1, k, span] + push * (
+                    (xy - xy_prior) + (next_y(yy, yy_after) - yy) + (yz - prior_z(yz))
+                )
+                new[2, k, span] = v_ref[2, k, span] + push * (
+                    (xz - xz_prior) + (yz - prior_y(yz, yz_before)) + (next_z(zz) - zz)
+                )
             if last:
                 continue
-            for i, value in enumerate((xx, yy, zz, xy, xz, yz)):
-                s_out[i, k] = value
-            for i, value in enumerate((vx, vy, vz, xy, yz)):
-                y_last[i, pl.ds(here, 1), :] = value[-1:]
-            for i, value in enumerate((vx, vy, vz, yy)):
-                y_first[i, pl.ds(here, 1), :] = value[:1]
-            if ends and k == 0:
-
-                @pl.when(start)
-                def _():
-                    for i, value in enumerate((vx, vy, vz, xx)):
-                        x_first[i] = value
-                    corner_y[...] = vy[-1:]
-
-            if ends and k == group - 1:
-
-                @pl.when(end)
-                def _():
-                    for i, value in enumerate((vx, vy, vz, xy, xz)):
-                        x_last[i] = value
-                    corner_x[...] = vx[:1]
+            for i in range(3):
+                y_last[i, pl.ds(here, 1), :] = new[i, k, y - 1 :]
+                y_first[i, pl.ds(here, 1), :] = new[i, k, :1]
+            y_last[3, pl.ds(here, 1), :] = s_new[3, k, y - 1 :]
+            y_last[4, pl.ds(here, 1), :] = s_new[5, k, y - 1 :]
+            y_first[3, pl.ds(here, 1), :] = s_new[1, k, :1]
+
+        if ends and not last:
+
+            @pl.when(start)
+            def _():
+                for i in range(3):
+                    x_first[i] = new[i, 0]
+                x_first[3] = s_new[0, 0]
+                corner_y[...] = new[1, 0, y - 1 :]
+
+            @pl.when(end)
+            def _():
+                for i in range(3):
+                    x_last[i] = new[i, group - 1]
+                x_last[3], x_last[4] = s_new[3, group - 1], s_new[4, group - 1]
+                corner_x[...] = new[0, group - 1, :1]
 
         if not ends:
             carried[0] = v_ref[0, group - 1]
-            carried[1] = stresses[-1][3]
-            carried[2] = stresses[-1][4]
+            carried[1] = s_new[3, group - 1]
+            carried[2] = s_new[4, group - 1]
 
     def next_plane(i):
         return jnp.minimum((of(i) + 1) * group, x - 1)
 
     def prior_plane(i):
-        return jnp.maximum(of(i) * group - 1, 0)
+        return jnp.maximum(of(i) * group - 1, 0) if ends else group - 1
 
     def planes(number):
         return pl.BlockSpec((number, group, y, z), lambda i: (0, of(i), 0, 0))
@@ -329,16 +367,17 @@
         if ends:
             out_shape += [(5, y, z), (4, y, z), (1, z), (1, z)]
         out_specs += [whole_block(shape) for shape in out_shape[2:]]
-    part = count * group * y * z
+    part = (1 if ends else WEIGHT) * count * group * y * z
     return pl.pallas_call(
         kernel,
         grid=(count,),
         in_specs=in_specs,
         out_specs=out_specs,
         out_shape=[jax.ShapeDtypeStruct(shape, f32) for shape in out_shape],
-        scratch_shapes=[pltpu.VMEM((3, y, z), f32)],
+        scratch_shapes=[pltpu.VMEM((3, y, z), f32), pltpu.VMEM((y, z), f32)]
+        + ([pltpu.VMEM((6, group, y, z), f32)] if last else []),
         input_output_aliases=aliases,
-        compiler_params=params(),
+        compiler_params=params(STENCIL_BYTES),
         cost_estimate=pl.CostEstimate(
             flops=80 * part, bytes_accessed=(54 if last else 78) * part, transcendentals=0
         ),
@@ -348,7 +387,7 @@
 
 def propagate(velocity, stress, lame, shear, buoyancy):
     brick = velocity.shape[1:]
-    between = brick[0] // fit(brick[0], 4) > 2
+    between = brick[0] // fit(brick[0], X_GROUP) > 2
     rims, x_rims = exchange(*first_rims(brick, velocity, stress, lame, shear))
     held, medium, x_medium = (rims, x_rims[:2]), (), ()
     for step_index in range(STEPS):
@@ -420,8 +459,8 @@
     return size
 
 
-def params():
-    return pltpu.CompilerParams(vmem_limit_bytes=VMEM_BYTES)
+def params(limit=VMEM_BYTES):
+    return pltpu.CompilerParams(vmem_limit_bytes=limit)
 
 
 def whole_block(shape):
@@ -457,7 +496,7 @@
     table = table.reshape(2, 2, plan.chunks, plan.gy, kz, z)
     count = plan.chunks * plan.gy
 
-    group = fit(x, 8)
+    group = fit(x, Z_GROUP)
     deep = fit(group, 2)
 
     def kernel(place_ref, table_ref, v_ref, *outs):
@@ -670,7 +709,7 @@
     table = table.reshape(2, 2, plan.chunks, plan.gy, kz, z)
     blocks = [block.reshape(3, kz * x, y) for group in blocks for block in group]
 
-    group = fit(x, 8)
+    group = fit(x, Z_GROUP)
     deep = fit(group, 2)
 
     def kernel(place_ref, table_ref, v_ref, p_ref, s_ref, *refs):
@@ -748,9 +787,6 @@
     return pl.CostEstimate(flops=6 * flops, bytes_accessed=4 * values, transcendentals=0)
 
 
-WEIGHT = 1000
-
-
 def crossed(table, plan):
     shape = (plan.gy, plan.gx, plan.per, table.shape[-1])
     return table.reshape(shape).transpose(1, 0, 2, 3).reshape(table.shape)
@@ -763,7 +799,7 @@
 def along_z(plan, place, velocity, comps, tables, outs, ahead=()):
     x, y, z = plan.x, plan.y, plan.z
     table = np.stack([halves(table) for table in tables]).reshape(len(comps), 2, outs, z // outs, z)
-    group = fit(x, 8)
+    group = fit(x, Z_GROUP)
     deep = fit(group, 2)
     rows = z // outs
 
@@ -796,7 +832,7 @@
         + [unread()] * len(ahead),
         out_specs=[whole_block(shape)] * outs,
         out_shape=[jax.ShapeDtypeStruct(shape, jnp.float32)] * outs,
-        compiler_params=params(),
+        compiler_params=params(STENCIL_BYTES),
         cost_estimate=cost(len(comps) * x * y * z * z, 2 * len(comps) * x * y * z),
         name="along_z",
     )(place, jnp.asarray(table), *[velocity] * len(comps), *ahead)
@@ -821,7 +857,7 @@
     x, y, ny = plan.x, plan.y, plan.ny
     count = blocks[0].shape[1]
     table = halves(basis(ny).T).reshape(2, plan.gy, y, ny)
-    deep = fit(count, 8)
+    deep = fit(count, Y_DEEP)
     rows = deep * x
     half = ny // 2
 
@@ -1017,7 +1053,7 @@
     x, y, ny = plan.x, plan.y, plan.ny
     count = planes.shape[0]
     table = halves(np.stack(np.split(inverse_basis(ny), plan.gy, axis=1)))
-    deep = fit(count, 8)
+    deep = fit(count, Y_DEEP)
     rows = deep * x
     half = ny // 2
 
@@ -1054,7 +1090,7 @@
     outs = len(blocks)
     rows = z // outs
     table = np.stack([halves(table) for table in tables]).reshape(len(comps), 2, outs, rows, z)
-    group = fit(x, 8)
+    group = fit(x, Z_GROUP)
     deep = fit(group, 2)
 
     def kernel(place_ref, table_ref, *refs):

time: 344 us -> 317 us (0.922)
  Pallas kernels: 118 us -> 89.8 us
  waiting for transfers between devices: 155 us -> 160 us
  local copies, waits for them, and re-layouts: 10.7 us -> 6.49 us
    pallas_call x4, Pallas kernels: 38.5 us -> 22.2 us  [stencil(): pl.pallas_call(kernel, grid=(count,), in_specs=in_specs, out_specs=out_sp...]
    pallas_call x2, Pallas kernels: 12.8 us -> 8.28 us  [along_z(): pl.pallas_call(kernel, grid=(x // group,), in_specs=[scalars(), whole_blo...]
    unnamed x36 -> x20, local copies, waits for them, and re-layouts: 10.7 us -> 6.49 us
    all_to_all x4, waiting for transfers between devices: 28.9 us -> 33 us  [over_gx(): return lax.all_to_all(blocks, 'gx', 0, 0, tiled=True)]
  transfers between devices with their start and end apart: 20 -> 20, of which waited for: 9 -> 7; matrix products, arithmetic and copies ran while one was open for 0% -> 0% of each run, Pallas kernels for 20% -> 17%
where the time goes in v4:
time: 317 us; the launch traced here: 316 us
  waiting for transfers between devices  160 us (50%)
  Pallas kernels  89.8 us (28%)
  starting transfers between devices  58.8 us (19%)
  local copies, waits for them, and re-layouts  6.49 us (2%)
    ppermute x4, waiting for transfers between devices, swap_gy(): moved.append(lax.ppermute(blocks[step], 'gy', route))  127 us
    all_to_all x4, waiting for transfers between devices, over_gx(): return lax.all_to_all(blocks, 'gx', 0, 0, tiled=True)  33 us
    all_to_all x4, starting transfers between devices, over_gx(): return lax.all_to_all(blocks, 'gx', 0, 0, tiled=True)  22.3 us
    pallas_call x4, Pallas kernels, stencil(): pl.pallas_call(kernel, grid=(count,), in_specs=in_specs, out_specs=out_sp...  22.2 us
    ppermute x8, starting transfers between devices, passed_along(): return lax.ppermute(block, axis, route)  21.9 us
    pallas_call x2, Pallas kernels, image_part(): pl.pallas_call(kernel, grid=(x // group,), in_specs=[scalars(), whole_blo...  16.3 us
    pallas_call x1, Pallas kernels, potential(): pl.pallas_call(kernel, grid=(plan.per,), in_specs=[scalars()] + [whole_bl...  10.6 us
    ppermute x4, starting transfers between devices, across_corner(): return lax.ppermute(row, ('gx', 'gy'), route)  10.6 us
  transfers between devices with their start and end apart: 20, of which 7 were waited for; matrix products, arithmetic and copies ran while one was open for 0% of the time, Pallas kernels for 17%

profile of v4, /device:TPU:12, one launch (start us, length us, event | category | flops | bytes accessed | tf_op | source)
XLA Modules:
  0.0 315.8 jit_solution(13360974943475747085)
XLA Ops:
  26.0 9.0 %stencil_middle.2 = (f32[3,32,128,128]{3,2,1,0:T(8,128)S(1)}, f32[6,32,128,128]{3,2,1,0:T(8,128)S(1)}, f32[5,32,128]{2,1,0:T(8,128)S(1)}, f32[4,32,128]{2,1,0:T(8,128)S(1)}) custom-call(f32[3,32,128,128]{3,2,1,0:T(8,128)S(1)} %copy-done, f32[6,32,128,128]{3,2,1,0:T(8,128)} %refs_11_.5, bf16[32,128,128]{2,1,0:T(8,128)(2,1)S(1)} %copy-done.4, ...), custom_call_target="tpu_custom_call" | custom-call | flops 31457280000 | bytes 30670848000 | tf_op jit(solution)/shard_map/stencil_middle/pallas_call | solution.py:371
  39.1 4.8 %collective-permute-start.6 = (f32[5,32,128]{2,1,0:T(8,128)S(1)}, f32[5,32,128]{2,1,0:T(8,128)S(1)}, u32[]{:S(2)}, u32[]{:S(2)}) collective-permute-start(f32[5,32,128]{2,1,0:T(8,128)S(1)} %get-tuple-element.45), channel_id=1, source_target_pairs={{0,1},{2,3},{4,5},{6,7},{8,9},{10,11},{12,13},{14,15},{16,17},{18,... | collective-permute-start | bytes 245768 | tf_op jit(solution)/shard_map/ppermute | solution.py:26
  56.2 6.7 %stencil_middle.3.refs_23_ = f32[3,32,128,128]{3,2,1,0:T(8,128)S(1)} custom-call(f32[3,32,128,128]{3,2,1,0:T(8,128)S(1)} %get-tuple-element.43.refs_0_.refs_5_.refs_9_, f32[6,32,128,128]{3,2,1,0:T(8,128)S(1)} %get-tuple-element.44.refs_1_.refs_6_.refs_10_.refs_11_, bf16[32,128,128]{2,1,0:T(8,128)(2,1)S(1)} %copy-done.4, bf16[32,128,128]{2,1,0:T(8,128)(2,1)S(1)} %copy-done.3, ...), custom_call_target="tpu_custom_call" | custom-call | flops 31457280000 | bytes 21233664000 | tf_op jit(solution)/shard_map/stencil_middle/pallas_call | solution.py:371
  65.5 4.4 %along_z.2 = (f32[2,2048,128]{2,1,0:T(8,128)S(1)}, f32[2,2048,128]{2,1,0:T(8,128)S(1)}) custom-call(s32[2]{0:T(128)S(1)} %pad_add_fusion.place_ref, bf16[2,2,2,64,128]{4,3,2,1,0:T(8,128)(2,1)S(1)} %copy-done.7, f32[3,32,128,128]{3,2,1,0:T(8,128)S(1)} %stencil_ends.3.refs_0_.refs_1_, f32[3,32,128,128]{3,2,1,0:T(8,128)S(1)} %stencil_ends.3.refs_0_.refs_1_), custom_call_target="tpu_custom_call" | custom-call | flops 805306368 | bytes 8388608 | tf_op jit(solution)/shard_map/along_z/pallas_call | solution.py:827
  76.7 7.1 %all-to-all-start = ((f32[16,2,4,32,128]{4,3,2,1,0:T(8,128)}), f32[16,2,4,32,128]{4,3,2,1,0:T(8,128)}, u32[]{:S(2)}, u32[]{:S(2)}) async-start(f32[16,2,4,32,128]{4,3,2,1,0:T(8,128)} %bitcast.3), calls=%async_computation | async-start | bytes 4194304 | tf_op jit(solution)/shard_map/all_to_all | solution.py:1152
  83.9 33.5 %collective-permute-done.13.refs_1_ = f32[2,64,32,128]{3,2,1,0:T(8,128)} collective-permute-done((f32[2,64,32,128]{3,2,1,0:T(8,128)S(1)}, f32[2,64,32,128]{3,2,1,0:T(8,128)}, u32[]{:S(2)}, u32[]{:S(2)}) %collective-permute-start.13) | collective-permute-done | bytes 2097184 | tf_op jit(solution)/shard_map/ppermute | solution.py:546
  117.4 4.6 %pair_y_forward.1 = f32[64,32,256]{2,1,0:T(8,128)} custom-call(s32[2]{0:T(128)} %copy-done.9, bf16[2,2,128,256]{3,2,1,0:T(8,128)(2,1)} %constant.30.clone.table_ref, f32[2,64,32,128]{3,2,1,0:T(8,128)} %bitcast.11, f32[2,64,32,128]{3,2,1,0:T(8,128)} %collective-permute-done.13.refs_1_), custom_call_target="tpu_custom_call" | custom-call | flops 1610612736000 | bytes 6291456000 | tf_op jit(solution)/shard_map/pair_y_forward/pallas_call | solution.py:875
  122.0 9.3 %all-to-all-done.in_ref = f32[16,2,4,32,128]{4,3,2,1,0:T(8,128)} async-done(((f32[16,2,4,32,128]{4,3,2,1,0:T(8,128)}), f32[16,2,4,32,128]{4,3,2,1,0:T(8,128)}, u32[]{:S(2)}, u32[]{:S(2)}) %all-to-all-start) | async-done | bytes 2097184 | tf_op jit(solution)/shard_map/all_to_all | solution.py:1152
  131.3 5.1 %all-to-all-start.1 = ((f32[16,4,32,256]{3,2,1,0:T(8,128)}), f32[16,4,32,256]{3,2,1,0:T(8,128)}, u32[]{:S(2)}, u32[]{:S(2)}) async-start(f32[16,4,32,256]{3,2,1,0:T(8,128)} %bitcast.13), calls=%async_computation.1 | async-start | bytes 4194304 | tf_op jit(solution)/shard_map/all_to_all | solution.py:1152
  136.3 5.4 %first_x_forward.1 = (f32[4,512,128]{2,1,0:T(8,128)}, f32[4,512,128]{2,1,0:T(8,128)}) custom-call(s32[2]{0:T(128)} %copy-done.9, bf16[512,1024]{1,0:T(8,128)(2,1)} %constant.31.clone.twice_ref.ft_ref, bf16[512,512]{1,0:T(8,128)(2,1)} %constant.32.clone.low_ref.fl_ref, f32[16,2,4,32,128]{4,3,2,1,0:T(8,128)} %all-to-all-done.in_ref), custom_call_target="tpu_custom_call" | custom-call | flops 1610612736 | bytes 4194304 | tf_op jit(solution)/shard_map/first_x_forward/pallas_call | solution.py:899
  142.1 25.2 %collective-permute-done.12.refs_1_ = f32[4,512,128]{2,1,0:T(8,128)} collective-permute-done((f32[4,512,128]{2,1,0:T(8,128)}, f32[4,512,128]{2,1,0:T(8,128)}, u32[]{:S(2)}, u32[]{:S(2)}) %collective-permute-start.12) | collective-permute-done | bytes 1048608 | tf_op jit(solution)/shard_map/ppermute | solution.py:546
  167.3 4.6 %first_y_forward.1.first_ref = f32[4,512,256]{2,1,0:T(8,128)} custom-call(s32[2]{0:T(128)} %copy-done.9, bf16[2,2,128,256]{3,2,1,0:T(8,128)(2,1)} %constant.30.clone.table_ref, f32[4,512,128]{2,1,0:T(8,128)} %get-tuple-element.52.refs_0_, f32[4,512,128]{2,1,0:T(8,128)} %collective-permute-done.12.refs_1_), custom_call_target="tpu_custom_call" | custom-call | flops 805306368 | bytes 4194304 | tf_op jit(solution)/shard_map/first_y_forward/pallas_call | solution.py:935
  171.8 11.9 %all-to-all-done.1.in_ref = f32[16,4,32,256]{3,2,1,0:T(8,128)} async-done(((f32[16,4,32,256]{3,2,1,0:T(8,128)}), f32[16,4,32,256]{3,2,1,0:T(8,128)}, u32[]{:S(2)}, u32[]{:S(2)}) %all-to-all-start.1) | async-done | bytes 2097184 | tf_op jit(solution)/shard_map/all_to_all | solution.py:1152
  183.7 10.6 %potential.1 = (f32[16,4,32,256]{3,2,1,0:T(8,128)}, f32[4,512,256]{2,1,0:T(8,128)}) custom-call(s32[2]{0:T(128)} %copy-done.9, bf16[512,1024]{1,0:T(8,128)(2,1)} %constant.31.clone.twice_ref.ft_ref, bf16[512,512]{1,0:T(8,128)(2,1)} %constant.32.clone.low_ref.fl_ref, bf16[512,1024]{1,0:T(8,128)(2,1)} %constant.33.clone.bt_ref.twice_ref, ...), custom_call_target="tpu_custom_call" | custom-call | flops 3221225472 | bytes 8388608 | tf_op jit(solution)/shard_map/potential/pallas_call | solution.py:972
  194.3 5.1 %all-to-all-start.2 = ((f32[16,4,32,256]{3,2,1,0:T(8,128)}), f32[16,4,32,256]{3,2,1,0:T(8,128)}, u32[]{:S(2)}, u32[]{:S(2)}) async-start(f32[16,4,32,256]{3,2,1,0:T(8,128)} %get-tuple-element.55), calls=%async_computation.2 | async-start | bytes 4194304 | tf_op jit(solution)/shard_map/all_to_all | solution.py:1152
  199.4 4.6 %last_y_inverse.1 = (f32[4,512,128]{2,1,0:T(8,128)}, f32[4,512,128]{2,1,0:T(8,128)}) custom-call(s32[2]{0:T(128)} %copy-done.9, bf16[2,2,256,128]{3,2,1,0:T(8,128)(2,1)} %constant.35.clone.table_ref, f32[4,512,256]{2,1,0:T(8,128)} %get-tuple-element.56.in_ref), custom_call_target="tpu_custom_call" | custom-call | flops 805306368 | bytes 4194304 | tf_op jit(solution)/shard_map/last_y_inverse/pallas_call | solution.py:1012
  204.3 25.2 %collective-permute-done.14.refs_1_ = f32[4,512,128]{2,1,0:T(8,128)} collective-permute-done((f32[4,512,128]{2,1,0:T(8,128)}, f32[4,512,128]{2,1,0:T(8,128)}, u32[]{:S(2)}, u32[]{:S(2)}) %collective-permute-start.14) | collective-permute-done | bytes 1048608 | tf_op jit(solution)/shard_map/ppermute | solution.py:546
  229.5 5.4 %last_x_inverse.1._ = f32[16,2,4,32,128]{4,3,2,1,0:T(8,128)} custom-call(s32[2]{0:T(128)} %copy-done.9, bf16[512,1024]{1,0:T(8,128)(2,1)} %constant.33.clone.bt_ref.twice_ref, bf16[512,512]{1,0:T(8,128)(2,1)} %constant.34.clone.bl_ref.low_ref, f32[4,512,128]{2,1,0:T(8,128)} %get-tuple-element.57.refs_0_, f32[4,512,128]{2,1,0:T(8,128)} %collective-permute-done.14.refs_1_), custom_call_target="tpu_custom_call" | custom-call | flops 1610612736 | bytes 4194304 | tf_op jit(solution)/shard_map/last_x_inverse/pallas_call | solution.py:1039
  234.9 11.8 %all-to-all-done.2 = f32[16,4,32,256]{3,2,1,0:T(8,128)} async-done(((f32[16,4,32,256]{3,2,1,0:T(8,128)}), f32[16,4,32,256]{3,2,1,0:T(8,128)}, u32[]{:S(2)}, u32[]{:S(2)}) %all-to-all-start.2) | async-done | bytes 2097184 | tf_op jit(solution)/shard_map/all_to_all | solution.py:1152
  246.7 4.6 %pair_y_inverse.1 = (f32[2,64,32,128]{3,2,1,0:T(8,128)}, f32[2,64,32,128]{3,2,1,0:T(8,128)}, f32[16,2,4,32,128]{4,3,2,1,0:T(8,128)}) custom-call(s32[2]{0:T(128)} %copy-done.9, bf16[2,2,256,128]{3,2,1,0:T(8,128)(2,1)} %constant.35.clone.table_ref, f32[64,32,256]{2,1,0:T(8,128)} %bitcast.6.in_ref, ...), custom_call_target="tpu_custom_call", output_to_operand_aliasing={{2}: (3, {})} | custom-call | flops 1610612736 | bytes 6291456 | tf_op jit(solution)/shard_map/pair_y_inverse/pallas_call | solution.py:1069
  251.7 5.1 %all-to-all-start.3 = ((f32[16,2,4,32,128]{4,3,2,1,0:T(8,128)}), f32[16,2,4,32,128]{4,3,2,1,0:T(8,128)}, u32[]{:S(2)}, u32[]{:S(2)}) async-start(f32[16,2,4,32,128]{4,3,2,1,0:T(8,128)} %get-tuple-element.63), calls=%async_computation.3 | async-start | bytes 4194304 | tf_op jit(solution)/shard_map/all_to_all | solution.py:1152
  256.8 42.8 %collective-permute-done.15 = f32[2,64,32,128]{3,2,1,0:T(8,128)} collective-permute-done((f32[2,64,32,128]{3,2,1,0:T(8,128)}, f32[2,64,32,128]{3,2,1,0:T(8,128)}, u32[]{:S(2)}, u32[]{:S(2)}) %collective-permute-start.15) | collective-permute-done | bytes 2097184 | tf_op jit(solution)/shard_map/ppermute | solution.py:546
  299.5 9.5 %image_part.2 = (f32[32,128,128]{2,1,0:T(8,128)}, f32[32,128,128]{2,1,0:T(8,128)}) custom-call(s32[2]{0:T(128)} %copy-done.9, bf16[2,2,2,64,128]{4,3,2,1,0:T(8,128)(2,1)} %constant.36.clone.table_ref, f32[3,32,128,128]{3,2,1,0:T(8,128)} %copy-done.1, f32[3,32,128,128]{3,2,1,0:T(8,128)} %copy-done.1, bf16[3,32,128,128]{3,2,1,0:T(8,128)(2,1)} %refs_1_.7, ...), custom_call_target="tpu_custom_call" | custom-call | flops 805306368000 | bytes 16777216000 | tf_op jit(solution)/shard_map/image_part/pallas_call | solution.py:1128
  309.0 6.8 %image_part.3 = (f32[32,128,128]{2,1,0:T(8,128)}, f32[32,128,128]{2,1,0:T(8,128)}) custom-call(s32[2]{0:T(128)} %copy-done.9, bf16[1,2,1,128,128]{4,3,2,1,0:T(8,128)(2,1)} %constant.37.clone.table_ref, f32[3,32,128,128]{3,2,1,0:T(8,128)} %copy-done.1, bf16[3,32,128,128]{3,2,1,0:T(8,128)(2,1)} %refs_1_.7, bf16[3,32,128,128]{3,2,1,0:T(8,128)(2,1)} %refs_2_.13, ...), custom_call_target="tpu_custom_call" | custom-call | flops 402653184 | bytes 10485760 | tf_op jit(solution)/shard_map/image_part/pallas_call | solution.py:1128
  (53 shorter events, 51.9 us)
Async XLA Ops:
  3.9 14.3 %collective-permute-start = (f32[6,32,128]{2,1,0:T(8,128)}, f32[6,32,128]{2,1,0:T(8,128)S(1)}, u32[]{:S(2)}, u32[]{:S(2)}) collective-permute-start(f32[6,32,128]{2,1,0:T(8,128)} %get-tuple-element.33), channel_id=1, source_target_pairs={{0,1},{2,3},{4,5},{6,7},{8,9},{10,11},{12,13},{14,15},{16,17},{18,... | collective-permute-start | bytes 294920 | tf_op jit(solution)/shard_map/ppermute | solution.py:26
  7.3 12.2 %collective-permute-start.1 = (f32[6,32,128]{2,1,0:T(8,128)}, f32[6,32,128]{2,1,0:T(8,128)S(1)}, u32[]{:S(2)}, u32[]{:S(2)}) collective-permute-start(f32[6,32,128]{2,1,0:T(8,128)} %get-tuple-element.34), channel_id=1, source_target_pairs={{1,0},{3,2},{5,4},{7,6},{9,8},{11,10},{13,12},{15,14},{17,16},{19,... | collective-permute-start | bytes 294920 | tf_op jit(solution)/shard_map/ppermute | solution.py:26
  8.6 26.4 %collective-permute-start.2 = (f32[6,128,128]{2,1,0:T(8,128)}, f32[6,128,128]{2,1,0:T(8,128)S(1)}, u32[]{:S(2)}, u32[]{:S(2)}) collective-permute-start(f32[6,128,128]{2,1,0:T(8,128)} %get-tuple-element.35), channel_id=1, source_target_pairs={{0,2},{2,4},{4,6},{6,8},{8,10},{10,12},{12,14},{14,16},{16,18},{18... | collective-permute-start | bytes 1179656 | tf_op jit(solution)/shard_map/ppermute | solution.py:26
  10.5 24.5 %collective-permute-start.3 = (f32[6,128,128]{2,1,0:T(8,128)}, f32[6,128,128]{2,1,0:T(8,128)S(1)}, u32[]{:S(2)}, u32[]{:S(2)}) collective-permute-start(f32[6,128,128]{2,1,0:T(8,128)} %get-tuple-element.36), channel_id=1, source_target_pairs={{2,0},{4,2},{6,4},{8,6},{10,8},{12,10},{14,12},{16,14},{18,16},{20... | collective-permute-start | bytes 1179656 | tf_op jit(solution)/shard_map/ppermute | solution.py:26
  14.2 20.8 %collective-permute-start.4 = (f32[1,128]{1,0:T(1,128)}, f32[1,128]{1,0:T(1,128)S(1)}, u32[]{:S(2)}, u32[]{:S(2)}) collective-permute-start(f32[1,128]{1,0:T(1,128)} %get-tuple-element.37), channel_id=1, source_target_pairs={{2,1},{4,3},{6,5},{8,7},{10,9},{12,11},{14,13},{16,15},{18,17},{20... | collective-permute-start | bytes 1544 | tf_op jit(solution)/shard_map/ppermute | solution.py:37
  18.2 16.8 %collective-permute-start.5 = (f32[1,128]{1,0:T(1,128)}, f32[1,128]{1,0:T(1,128)S(1)}, u32[]{:S(2)}, u32[]{:S(2)}) collective-permute-start(f32[1,128]{1,0:T(1,128)} %get-tuple-element.38), channel_id=1, source_target_pairs={{1,2},{3,4},{5,6},{7,8},{9,10},{11,12},{13,14},{15,16},{17,18},{19... | collective-permute-start | bytes 1544 | tf_op jit(solution)/shard_map/ppermute | solution.py:37
  35.0 21.2 %copy-start.3 = (bf16[32,128,128]{2,1,0:T(8,128)(2,1)S(1)}, bf16[32,128,128]{2,1,0:T(8,128)(2,1)}, u32[]{:S(2)}) copy-start(bf16[32,128,128]{2,1,0:T(8,128)(2,1)} %refs_12_.9) | copy-start | bytes 3145732
  39.1 17.1 %collective-permute-start.6 = (f32[5,32,128]{2,1,0:T(8,128)S(1)}, f32[5,32,128]{2,1,0:T(8,128)S(1)}, u32[]{:S(2)}, u32[]{:S(2)}) collective-permute-start(f32[5,32,128]{2,1,0:T(8,128)S(1)} %get-tuple-element.45), channel_id=1, source_target_pairs={{0,1},{2,3},{4,5},{6,7},{8,9},{10,11},{12,13},{14,15},{16,17},{18,... | collective-permute-start | bytes 245768 | tf_op jit(solution)/shard_map/ppermute | solution.py:26
  43.9 11.0 %collective-permute-start.7 = (f32[4,32,128]{2,1,0:T(8,128)S(1)}, f32[4,32,128]{2,1,0:T(8,128)S(1)}, u32[]{:S(2)}, u32[]{:S(2)}) collective-permute-start(f32[4,32,128]{2,1,0:T(8,128)S(1)} %get-tuple-element.46), channel_id=1, source_target_pairs={{1,0},{3,2},{5,4},{7,6},{9,8},{11,10},{13,12},{15,14},{17,16},{19,... | collective-permute-start | bytes 196616 | tf_op jit(solution)/shard_map/ppermute | solution.py:26
  45.3 27.5 %copy-start.9 = (s32[2]{0:T(128)}, s32[2]{0:T(128)S(1)}, u32[]{:S(2)}) copy-start(s32[2]{0:T(128)S(1)} %pad_add_fusion.place_ref) | copy-start | bytes 28
  45.3 17.6 %collective-permute-start.8 = (f32[5,128,128]{2,1,0:T(8,128)S(1)}, f32[5,128,128]{2,1,0:T(8,128)S(1)}, u32[]{:S(2)}, u32[]{:S(2)}) collective-permute-start(f32[5,128,128]{2,1,0:T(8,128)S(1)} %get-tuple-element.47), channel_id=1, source_target_pairs={{0,2},{2,4},{4,6},{6,8},{8,10},{10,12},{12,14},{14,16},{16,18},{18... | collective-permute-start | bytes 983048 | tf_op jit(solution)/shard_map/ppermute | solution.py:26
  48.6 14.3 %collective-permute-start.9 = (f32[4,128,128]{2,1,0:T(8,128)S(1)}, f32[4,128,128]{2,1,0:T(8,128)S(1)}, u32[]{:S(2)}, u32[]{:S(2)}) collective-permute-start(f32[4,128,128]{2,1,0:T(8,128)S(1)} %get-tuple-element.48), channel_id=1, source_target_pairs={{2,0},{4,2},{6,4},{8,6},{10,8},{12,10},{14,12},{16,14},{18,16},{20... | collective-permute-start | bytes 786440 | tf_op jit(solution)/shard_map/ppermute | solution.py:26
  50.9 12.0 %collective-permute-start.10 = (f32[1,128]{1,0:T(1,128)S(1)}, f32[1,128]{1,0:T(1,128)S(1)}, u32[]{:S(2)}, u32[]{:S(2)}) collective-permute-start(f32[1,128]{1,0:T(1,128)S(1)} %get-tuple-element.49), channel_id=1, source_target_pairs={{2,1},{4,3},{6,5},{8,7},{10,9},{12,11},{14,13},{16,15},{18,17},{20... | collective-permute-start | bytes 1544 | tf_op jit(solution)/shard_map/ppermute | solution.py:37
  54.9 8.0 %collective-permute-start.11 = (f32[1,128]{1,0:T(1,128)S(1)}, f32[1,128]{1,0:T(1,128)S(1)}, u32[]{:S(2)}, u32[]{:S(2)}) collective-permute-start(f32[1,128]{1,0:T(1,128)S(1)} %get-tuple-element.50), channel_id=1, source_target_pairs={{1,2},{3,4},{5,6},{7,8},{9,10},{11,12},{13,14},{15,16},{17,18},{19... | collective-permute-start | bytes 1544 | tf_op jit(solution)/shard_map/ppermute | solution.py:37
  65.4 7.4 %copy-start.1 = (f32[3,32,128,128]{3,2,1,0:T(8,128)}, f32[3,32,128,128]{3,2,1,0:T(8,128)S(1)}, u32[]{:S(2)}) copy-start(f32[3,32,128,128]{3,2,1,0:T(8,128)S(1)} %stencil_ends.3.refs_0_.refs_1_) | copy-start | bytes 18874372
  65.4 7.4 %copy-start.8 = (bf16[1,2,1,128,128]{4,3,2,1,0:T(8,128)(2,1)S(1)}, bf16[1,2,1,128,128]{4,3,2,1,0:T(8,128)(2,1)}, u32[]{:S(2)}) copy-start(bf16[1,2,1,128,128]{4,3,2,1,0:T(8,128)(2,1)} %constant.29.clone.table_ref) | copy-start | bytes 196612
  69.8 47.6 %collective-permute-start.13 = (f32[2,64,32,128]{3,2,1,0:T(8,128)S(1)}, f32[2,64,32,128]{3,2,1,0:T(8,128)}, u32[]{:S(2)}, u32[]{:S(2)}) collective-permute-start(f32[2,64,32,128]{3,2,1,0:T(8,128)S(1)} %bitcast.12), channel_id=1, source_target_pairs={{0,1},{1,0},{2,3},{3,2},{4,5},{5,4},{6,7},{7,6},{8,9},{9,8},{10,11... | collective-permute-start | bytes 6291464 | tf_op jit(solution)/shard_map/ppermute | solution.py:546
  76.7 54.5 %all-to-all-start = ((f32[16,2,4,32,128]{4,3,2,1,0:T(8,128)}), f32[16,2,4,32,128]{4,3,2,1,0:T(8,128)}, u32[]{:S(2)}, u32[]{:S(2)}) async-start(f32[16,2,4,32,128]{4,3,2,1,0:T(8,128)} %bitcast.3), calls=%async_computation | async-start | bytes 4194304 | tf_op jit(solution)/shard_map/all_to_all | solution.py:1152
  131.3 52.4 %all-to-all-start.1 = ((f32[16,4,32,256]{3,2,1,0:T(8,128)}), f32[16,4,32,256]{3,2,1,0:T(8,128)}, u32[]{:S(2)}, u32[]{:S(2)}) async-start(f32[16,4,32,256]{3,2,1,0:T(8,128)} %bitcast.13), calls=%async_computation.1 | async-start | bytes 4194304 | tf_op jit(solution)/shard_map/all_to_all | solution.py:1152
  141.8 25.5 %collective-permute-start.12 = (f32[4,512,128]{2,1,0:T(8,128)}, f32[4,512,128]{2,1,0:T(8,128)}, u32[]{:S(2)}, u32[]{:S(2)}) collective-permute-start(f32[4,512,128]{2,1,0:T(8,128)} %get-tuple-element.53), channel_id=1, source_target_pairs={{0,1},{1,0},{2,3},{3,2},{4,5},{5,4},{6,7},{7,6},{8,9},{9,8},{10,11... | collective-permute-start | bytes 3145736 | tf_op jit(solution)/shard_map/ppermute | solution.py:546
  194.3 52.4 %all-to-all-start.2 = ((f32[16,4,32,256]{3,2,1,0:T(8,128)}), f32[16,4,32,256]{3,2,1,0:T(8,128)}, u32[]{:S(2)}, u32[]{:S(2)}) async-start(f32[16,4,32,256]{3,2,1,0:T(8,128)} %get-tuple-element.55), calls=%async_computation.2 | async-start | bytes 4194304 | tf_op jit(solution)/shard_map/all_to_all | solution.py:1152
  203.9 25.5 %collective-permute-start.14 = (f32[4,512,128]{2,1,0:T(8,128)}, f32[4,512,128]{2,1,0:T(8,128)}, u32[]{:S(2)}, u32[]{:S(2)}) collective-permute-start(f32[4,512,128]{2,1,0:T(8,128)} %get-tuple-element.58), channel_id=1, source_target_pairs={{0,1},{1,0},{2,3},{3,2},{4,5},{5,4},{6,7},{7,6},{8,9},{9,8},{10,11... | collective-permute-start | bytes 3145736 | tf_op jit(solution)/shard_map/ppermute | solution.py:546
  251.4 48.1 %collective-permute-start.15 = (f32[2,64,32,128]{3,2,1,0:T(8,128)}, f32[2,64,32,128]{3,2,1,0:T(8,128)}, u32[]{:S(2)}, u32[]{:S(2)}) collective-permute-start(f32[2,64,32,128]{3,2,1,0:T(8,128)} %get-tuple-element.60), channel_id=1, source_target_pairs={{0,1},{1,0},{2,3},{3,2},{4,5},{5,4},{6,7},{7,6},{8,9},{9,8},{10,11... | collective-permute-start | bytes 6291464 | tf_op jit(solution)/shard_map/ppermute | solution.py:546
  251.7 57.3 %all-to-all-start.3 = ((f32[16,2,4,32,128]{4,3,2,1,0:T(8,128)}), f32[16,2,4,32,128]{4,3,2,1,0:T(8,128)}, u32[]{:S(2)}, u32[]{:S(2)}) async-start(f32[16,2,4,32,128]{4,3,2,1,0:T(8,128)} %get-tuple-element.63), calls=%async_computation.3 | async-start | bytes 4194304 | tf_op jit(solution)/shard_map/all_to_all | solution.py:1152
  (6 other events, 15.9 us)

commit v5 on v4

--- a/solution.py
+++ b/solution.py
@@ -14,6 +14,7 @@
 Y_DEEP = 32
 Z_GROUP = 16
 X_GROUP = 4
+LINE_GROUP = 16
 Y_TILE = 32
 WEIGHT = 1000
 
@@ -775,11 +776,50 @@
     return dot(jnp.concatenate([high, low], axis=1), table[0]) + dot(high, table[1])
 
 
-def side_by_side(table, values):
+def odd_basis(length):
+    wave = 2 * np.arange(length // 4) + 1
+    angle = (wave[:, None] * np.arange(length // 2) % length) * (2.0 * np.pi / length)
+    return np.concatenate([np.cos(angle), np.sin(angle)])
+
+
+def x_tables(length, inverse):
+    even, odd = basis(length // 2), odd_basis(length)
+    if inverse:
+        even, odd = -inverse_basis(length // 2).T / 2.0, -odd.T * (2.0 / length)
+    return [*doubled(even, 1), *doubled(odd, 1)]
+
+
+def x_forward(tables, value):
+    half = value.shape[0] // 2
+    even = left_times(tables[:2], value[:half] + value[half:])
+    return jnp.concatenate([even, left_times(tables[2:], value[:half] - value[half:])], axis=0)
+
+
+def x_inverse(tables, value):
+    half = value.shape[0] // 2
+    even = left_times(tables[:2], value[:half])
+    odd = left_times(tables[2:], value[half:])
+    return jnp.concatenate([even + odd, even - odd], axis=0)
+
+
+def x_wave(length):
+    slot = lax.broadcasted_iota(jnp.int32, (length, 1), 0)
+    wave = 2 * lax.rem(slot, length // 4) + slot // (length // 2)
+    return wave.astype(jnp.float32)
+
+
+def slope_x(value):
+    part = value.shape[0] // 4
+    wave = x_wave(value.shape[0])
+    swapped = [value[part : 2 * part], -value[:part], value[3 * part :], -value[2 * part : 3 * part]]
+    return wave * jnp.concatenate(swapped, axis=0)
+
+
+def side_by_side(through, tables, values):
     width = values[0].shape[1]
     if width % 128:
-        return [left_times(table, value) for value in values]
-    both = left_times(table, joined(values, 1))
+        return [through(tables, value) for value in values]
+    both = through(tables, joined(values, 1))
     return [both[:, i * width : (i + 1) * width] for i in range(len(values))]
 
 
@@ -799,13 +839,13 @@
 def along_z(plan, place, velocity, comps, tables, outs, ahead=()):
     x, y, z = plan.x, plan.y, plan.z
     table = np.stack([halves(table) for table in tables]).reshape(len(comps), 2, outs, z // outs, z)
-    group = fit(x, Z_GROUP)
+    group = fit(x, LINE_GROUP)
     deep = fit(group, 2)
     rows = z // outs
 
     def kernel(place_ref, table_ref, *refs):
         fields, found = refs[: len(comps)], refs[len(comps) + len(ahead) :]
-        at = pl.program_id(0) * group
+        found = [out.reshape(len(comps), rows * group, y) for out in found]
         me = place_ref[1]
         order = [lax.rem(me + s, outs) if outs > 1 else 0 for s in range(outs)]
         for comp, field in enumerate(fields):
@@ -818,25 +858,24 @@
                 for i, out in enumerate(found):
                     for k in range(deep):
                         part = value[i * rows : (i + 1) * rows, k * y : (k + 1) * y]
-                        out[comp, pl.ds(at + plane + k, rows, stride=x), :] = part
+                        out[comp, pl.ds(plane + k, rows, stride=group), :] = part
 
     def block(comp):
         return pl.BlockSpec((1, group, y, z), lambda i: (comp, i, 0, 0))
 
-    shape = (len(comps), rows * x, y)
-    found = pl.pallas_call(
+    shape = (len(comps), rows, x, y)
+    return pl.pallas_call(
         kernel,
         grid=(x // group,),
         in_specs=[scalars(), whole_block(table.shape)]
         + [block(comp) for comp in comps]
         + [unread()] * len(ahead),
-        out_specs=[whole_block(shape)] * outs,
+        out_specs=[pl.BlockSpec((len(comps), rows, group, y), lambda i: (0, 0, i, 0))] * outs,
         out_shape=[jax.ShapeDtypeStruct(shape, jnp.float32)] * outs,
         compiler_params=params(STENCIL_BYTES),
         cost_estimate=cost(len(comps) * x * y * z * z, 2 * len(comps) * x * y * z),
         name="along_z",
     )(place, jnp.asarray(table), *[velocity] * len(comps), *ahead)
-    return [out.reshape(len(comps), rows, x, y) for out in found]
 
 
 def y_table(plan, table_ref, groups):
@@ -887,50 +926,39 @@
 
 def first_x_forward(plan, place, lines):
     x, y, nx = plan.x, plan.y, plan.nx
-    twice, low = doubled(basis(nx), 1)
-
-    def kernel(place_ref, twice_ref, low_ref, in_ref, *outs):
+    tables = x_tables(nx, False)
+
+    def kernel(place_ref, *refs):
+        table_refs, in_ref, outs = refs[:4], refs[4], refs[5:]
         me = place_ref[1]
         fields = [in_ref[:, lax.rem(me + s, plan.gy), 0].reshape(nx, y) for s in range(plan.gy)]
-        found = side_by_side((twice_ref[...], low_ref[...]), fields)
+        found = side_by_side(x_forward, [ref[...] for ref in table_refs], fields)
         for out, value in zip(outs, found):
             out[0] = value
 
     return pl.pallas_call(
         kernel,
         grid=(plan.per,),
-        in_specs=[
-            scalars(),
-            whole_block(twice.shape),
-            whole_block(low.shape),
-            pl.BlockSpec((plan.gx, plan.gy, 1, x, y), lambda i: (0, 0, i, 0, 0)),
-        ],
+        in_specs=[scalars()]
+        + [whole_block(table.shape) for table in tables]
+        + [pl.BlockSpec((plan.gx, plan.gy, 1, x, y), lambda i: (0, 0, i, 0, 0))],
         out_specs=[pl.BlockSpec((1, nx, y), lambda i: (i, 0, 0))] * plan.gy,
         out_shape=[jax.ShapeDtypeStruct((plan.per, nx, y), jnp.float32)] * plan.gy,
         compiler_params=params(),
         cost_estimate=cost(plan.per * plan.ny * nx * nx, 2 * plan.per * plan.ny * nx),
         name="first_x_forward",
-    )(place, jnp.asarray(twice), jnp.asarray(low), lines)
-
-
-def slope_x(value):
-    half = value.shape[0] // 2
-    wave = lax.broadcasted_iota(jnp.int32, (half, 1), 0).astype(jnp.float32)
-    return wave * value[half:], -wave * value[:half]
+    )(place, *[jnp.asarray(table) for table in tables], lines)
 
 
 def first_y_forward(plan, place, blocks):
     y, nx, ny = plan.y, plan.nx, plan.ny
     table = halves(basis(ny).T).reshape(2, plan.gy, y, ny)
-    half = nx // 2
 
     def kernel(place_ref, table_ref, *refs):
         ins, out = refs[:-1], refs[-1]
         me = place_ref[1]
         tables = y_table(plan, table_ref, [source(me, s, plan.gy) for s in range(plan.gy)])
-        cosine, sine = slope_x(over_y([ref[0] for ref in ins], tables))
-        out[0, :half] = cosine
-        out[0, half:] = sine
+        out[0] = slope_x(over_y([ref[0] for ref in ins], tables))
 
     return pl.pallas_call(
         kernel,
@@ -947,26 +975,23 @@
 
 def potential(plan, place, first, lines):
     x, nx, ny, gx = plan.x, plan.nx, plan.ny, plan.gx
-    forth_twice, forth_low = doubled(basis(nx), 1)
-    back_twice, back_low = doubled(-inverse_basis(nx).T, 1)
-    half = nx // 2
-
-    def kernel(place_ref, ft_ref, fl_ref, bt_ref, bl_ref, first_ref, in_ref, out_ref, slope_ref):
+    tables = x_tables(nx, False) + x_tables(nx, True)
+
+    def kernel(place_ref, *refs):
+        first_ref, in_ref, out_ref, slope_ref = refs[8:]
+        forth, back = ([ref[...] for ref in refs[i : i + 4]] for i in (0, 4))
         me_x, me_y = place_ref[0], place_ref[1]
-        total = left_times((ft_ref[...], fl_ref[...]), in_ref[:, 0].reshape(nx, ny))
-        wave_x = lax.broadcasted_iota(jnp.int32, (half, 1), 0).astype(jnp.float32)
+        total = x_forward(forth, in_ref[:, 0].reshape(nx, ny)) + first_ref[0]
+        wave_x = x_wave(nx)
         slot_y = lax.broadcasted_iota(jnp.int32, (1, ny), 1)
         wave_y = lax.rem(slot_y, ny // 2).astype(jnp.float32)
         slot_z = (me_y * gx + me_x) * plan.per + pl.program_id(0)
         wave_z = lax.rem(slot_z, plan.z // 2).astype(jnp.float32)
-        scale = 1.0 / jnp.maximum(wave_x * wave_x + (wave_y * wave_y + wave_z * wave_z), 1.0)
-        cosine = (total[:half] + first_ref[0, :half]) * scale
-        sine = (total[half:] + first_ref[0, half:]) * scale
-        found = jnp.concatenate([cosine, sine], axis=0)
-        out_ref[:, 0] = left_times((bt_ref[...], bl_ref[...]), found).reshape(gx, x, ny)
-        slope_ref[0, :half], slope_ref[0, half:] = slope_x(found)
-
-    tables = [forth_twice, forth_low, back_twice, back_low]
+        square = wave_x * wave_x + (wave_y * wave_y + wave_z * wave_z)
+        found = total / jnp.maximum(square, 1.0)
+        out_ref[:, 0] = x_inverse(back, found).reshape(gx, x, ny)
+        slope_ref[0] = slope_x(found)
+
     spectrum = pl.BlockSpec((1, nx, ny), lambda i: (i, 0, 0))
     block = pl.BlockSpec((gx, 1, x, ny), lambda i: (0, i, 0, 0))
     return pl.pallas_call(
@@ -1027,26 +1052,27 @@
 
 def last_x_inverse(plan, place, blocks):
     x, y, nx, gx = plan.x, plan.y, plan.nx, plan.gx
-    twice, low = doubled(-inverse_basis(nx).T, 1)
-
-    def kernel(place_ref, twice_ref, low_ref, *refs):
-        ins, out = refs[:-1], refs[-1]
+    tables = x_tables(nx, True)
+
+    def kernel(place_ref, *refs):
+        table_refs, ins, out = refs[:4], refs[4:-1], refs[-1]
         me = place_ref[1]
-        found = side_by_side((twice_ref[...], low_ref[...]), [ref[0] for ref in ins])
+        found = side_by_side(x_inverse, [ref[...] for ref in table_refs], [ref[0] for ref in ins])
         for s, value in enumerate(found):
             out[:, source(me, s, plan.gy), 0] = value.reshape(gx, x, y)
 
     return pl.pallas_call(
         kernel,
         grid=(plan.per,),
-        in_specs=[scalars(), whole_block(twice.shape), whole_block(low.shape)]
+        in_specs=[scalars()]
+        + [whole_block(table.shape) for table in tables]
         + [pl.BlockSpec((1, nx, y), lambda i: (i, 0, 0))] * plan.gy,
         out_specs=pl.BlockSpec((gx, plan.gy, 1, x, y), lambda i: (0, 0, i, 0, 0)),
         out_shape=jax.ShapeDtypeStruct((gx, plan.gy, plan.per, x, y), jnp.float32),
         compiler_params=params(),
         cost_estimate=cost(plan.per * plan.ny * nx * nx, 2 * plan.per * plan.ny * nx),
         name="last_x_inverse",
-    )(place, jnp.asarray(twice), jnp.asarray(low), *blocks)
+    )(place, *[jnp.asarray(table) for table in tables], *blocks)
 
 
 def pair_y_inverse(plan, place, planes, behind):
@@ -1090,7 +1116,7 @@
     outs = len(blocks)
     rows = z // outs
     table = np.stack([halves(table) for table in tables]).reshape(len(comps), 2, outs, rows, z)
-    group = fit(x, Z_GROUP)
+    group = fit(x, LINE_GROUP)
     deep = fit(group, 2)
 
     def kernel(place_ref, table_ref, *refs):
@@ -1098,7 +1124,7 @@
         inputs = [[refs.pop(0) for _ in comps] for _ in range(3)]
         started = [refs.pop(0) for _ in before]
         *ins, image_p, image_s = refs
-        at = pl.program_id(0) * group
+        ins = [ref.reshape(len(comps), rows * group, y) for ref in ins]
         order = [source(place_ref[1], s, outs) if outs > 1 else 0 for s in range(outs)]
         turned_tables = []
         for comp in range(len(comps)):
@@ -1112,7 +1138,7 @@
                 v_ref, p_ref, s_ref = (each[comp] for each in inputs)
                 columns = []
                 for k in range(deep):
-                    cut = pl.ds(at + plane + k, rows, stride=x)
+                    cut = pl.ds(plane + k, rows, stride=group)
                     columns.append(joined([ref[comp, cut, :] for ref in ins], 0))
                 field = left_times(table, joined(columns, 1)).T.reshape(deep, y, z)
                 total_p += p_ref[0, here].astype(jnp.float32) * field
@@ -1123,7 +1149,7 @@
     def block(comp):
         return pl.BlockSpec((1, group, y, z), lambda i: (comp, i, 0, 0))
 
-    blocks = [part.reshape(len(comps), rows * x, y) for part in blocks]
+    blocks = [part.reshape(len(comps), rows, x, y) for part in blocks]
     image = pl.BlockSpec((group, y, z), lambda i: (i, 0, 0))
     return pl.pallas_call(
         kernel,
@@ -1131,7 +1157,7 @@
         in_specs=[scalars(), whole_block(table.shape)]
         + [block(comp) for _ in fields for comp in comps]
         + [image] * len(before)
-        + [whole_block(part.shape) for part in blocks],
+        + [pl.BlockSpec((len(comps), rows, group, y), lambda i: (0, 0, i, 0))] * outs,
         out_specs=[image, image],
         out_shape=[jax.ShapeDtypeStruct((x, y, z), jnp.float32)] * 2,
         compiler_params=params(),

time: 317 us -> 309 us (0.975)
  Pallas kernels: 89.8 us -> 80.3 us
    pallas_call x1, Pallas kernels: 10.6 us -> 6.76 us  [potential(): pl.pallas_call(kernel, grid=(plan.per,), in_specs=[scalars()] + [whole_bl...]
  transfers between devices with their start and end apart: 20 -> 20, of which waited for: 7 -> 7; matrix products, arithmetic and copies ran while one was open for 0% -> 0% of each run, Pallas kernels for 17% -> 16%
where the time goes in v5:
time: 309 us; the launch traced here: 308 us
  waiting for transfers between devices  161 us (52%)
  Pallas kernels  80.3 us (26%)
  starting transfers between devices  58.7 us (19%)
  local copies, waits for them, and re-layouts  6.49 us (2%)
    ppermute x4, waiting for transfers between devices, swap_gy(): moved.append(lax.ppermute(blocks[step], 'gy', route))  128 us
    all_to_all x4, waiting for transfers between devices, over_gx(): return lax.all_to_all(blocks, 'gx', 0, 0, tiled=True)  33.4 us
    all_to_all x4, starting transfers between devices, over_gx(): return lax.all_to_all(blocks, 'gx', 0, 0, tiled=True)  22.3 us
    pallas_call x4, Pallas kernels, stencil(): pl.pallas_call(kernel, grid=(count,), in_specs=in_specs, out_specs=out_sp...  22.1 us
    ppermute x8, starting transfers between devices, passed_along(): return lax.ppermute(block, axis, route)  21.9 us
    pallas_call x2, Pallas kernels, image_part(): pl.pallas_call(kernel, grid=(x // group,), in_specs=[scalars(), whole_blo...  13.7 us
    ppermute x4, starting transfers between devices, across_corner(): return lax.ppermute(row, ('gx', 'gy'), route)  10.6 us
    pallas_call x1, Pallas kernels, potential(): pl.pallas_call(kernel, grid=(plan.per,), in_specs=[scalars()] + [whole_bl...  6.76 us
  transfers between devices with their start and end apart: 20, of which 7 were waited for; matrix products, arithmetic and copies ran while one was open for 0% of the time, Pallas kernels for 16%

profile of v5, /device:TPU:12, one launch (start us, length us, event | category | flops | bytes accessed | tf_op | source)
XLA Modules:
  0.0 307.6 jit_solution(16161068475990195362)
XLA Ops:
  26.0 9.0 %stencil_middle.2 = (f32[3,32,128,128]{3,2,1,0:T(8,128)S(1)}, f32[6,32,128,128]{3,2,1,0:T(8,128)S(1)}, f32[5,32,128]{2,1,0:T(8,128)S(1)}, f32[4,32,128]{2,1,0:T(8,128)S(1)}) custom-call(f32[3,32,128,128]{3,2,1,0:T(8,128)S(1)} %copy-done, f32[6,32,128,128]{3,2,1,0:T(8,128)} %refs_11_.5, bf16[32,128,128]{2,1,0:T(8,128)(2,1)S(1)} %copy-done.4, ...), custom_call_target="tpu_custom_call" | custom-call | flops 31457280000 | bytes 30670848000 | tf_op jit(solution)/shard_map/stencil_middle/pallas_call | solution.py:372
  35.0 4.0 %stencil_ends.2 = (f32[3,32,128,128]{3,2,1,0:T(8,128)S(1)}, f32[6,32,128,128]{3,2,1,0:T(8,128)S(1)}, f32[5,32,128]{2,1,0:T(8,128)S(1)}, f32[4,32,128]{2,1,0:T(8,...) custom-call(f32[3,32,128,128]{3,2,1,0:T(8,128)S(1)} %copy-done, ...), custom_call_target="tpu_custom_call", output_to_operand_aliasing={{0}: (19, {}), {1}: (20, {})} | custom-call | flops 10485760 | bytes 10223616 | tf_op jit(solution)/shard_map/stencil_ends/pallas_call | solution.py:372
  39.1 4.8 %collective-permute-start.6 = (f32[5,32,128]{2,1,0:T(8,128)S(1)}, f32[5,32,128]{2,1,0:T(8,128)S(1)}, u32[]{:S(2)}, u32[]{:S(2)}) collective-permute-start(f32[5,32,128]{2,1,0:T(8,128)S(1)} %get-tuple-element.45), channel_id=1, source_target_pairs={{0,1},{2,3},{4,5},{6,7},{8,9},{10,11},{12,13},{14,15},{16,17},{18,... | collective-permute-start | bytes 245768 | tf_op jit(solution)/shard_map/ppermute | solution.py:27
  56.2 6.7 %stencil_middle.3.refs_23_ = f32[3,32,128,128]{3,2,1,0:T(8,128)S(1)} custom-call(f32[3,32,128,128]{3,2,1,0:T(8,128)S(1)} %get-tuple-element.43.refs_0_.refs_5_.refs_9_, f32[6,32,128,128]{3,2,1,0:T(8,128)S(1)} %get-tuple-element.44.refs_1_.refs_6_.refs_10_.refs_11_, bf16[32,128,128]{2,1,0:T(8,128)(2,1)S(1)} %copy-done.4, bf16[32,128,128]{2,1,0:T(8,128)(2,1)S(1)} %copy-done.3, ...), custom_call_target="tpu_custom_call" | custom-call | flops 31457280000 | bytes 21233664000 | tf_op jit(solution)/shard_map/stencil_middle/pallas_call | solution.py:372
  74.9 7.1 %all-to-all-start = ((f32[16,2,4,32,128]{4,3,2,1,0:T(8,128)}), f32[16,2,4,32,128]{4,3,2,1,0:T(8,128)}, u32[]{:S(2)}, u32[]{:S(2)}) async-start(f32[16,2,4,32,128]{4,3,2,1,0:T(8,128)} %bitcast.2), calls=%async_computation | async-start | bytes 4194304 | tf_op jit(solution)/shard_map/all_to_all | solution.py:1178
  82.1 34.4 %collective-permute-done.13.refs_1_ = f32[2,64,32,128]{3,2,1,0:T(8,128)} collective-permute-done((f32[2,64,32,128]{3,2,1,0:T(8,128)S(1)}, f32[2,64,32,128]{3,2,1,0:T(8,128)}, u32[]{:S(2)}, u32[]{:S(2)}) %collective-permute-start.13) | collective-permute-done | bytes 2097184 | tf_op jit(solution)/shard_map/ppermute | solution.py:547
  116.5 4.6 %pair_y_forward.1 = f32[64,32,256]{2,1,0:T(8,128)} custom-call(s32[2]{0:T(128)} %copy-done.9, bf16[2,2,128,256]{3,2,1,0:T(8,128)(2,1)} %constant.38.clone.table_ref, f32[2,64,32,128]{3,2,1,0:T(8,128)} %copy-done.6, f32[2,64,32,128]{3,2,1,0:T(8,128)} %collective-permute-done.13.refs_1_), custom_call_target="tpu_custom_call" | custom-call | flops 1610612736000 | bytes 6291456000 | tf_op jit(solution)/shard_map/pair_y_forward/pallas_call | solution.py:914
  121.1 8.4 %all-to-all-done.refs_4_ = f32[16,2,4,32,128]{4,3,2,1,0:T(8,128)} async-done(((f32[16,2,4,32,128]{4,3,2,1,0:T(8,128)}), f32[16,2,4,32,128]{4,3,2,1,0:T(8,128)}, u32[]{:S(2)}, u32[]{:S(2)}) %all-to-all-start) | async-done | bytes 2097184 | tf_op jit(solution)/shard_map/all_to_all | solution.py:1178
  129.4 5.1 %all-to-all-start.1 = ((f32[16,4,32,256]{3,2,1,0:T(8,128)}), f32[16,4,32,256]{3,2,1,0:T(8,128)}, u32[]{:S(2)}, u32[]{:S(2)}) async-start(f32[16,4,32,256]{3,2,1,0:T(8,128)} %bitcast.6), calls=%async_computation.1 | async-start | bytes 4194304 | tf_op jit(solution)/shard_map/all_to_all | solution.py:1178
  134.5 4.7 %first_x_forward.1 = (f32[4,512,128]{2,1,0:T(8,128)}, f32[4,512,128]{2,1,0:T(8,128)}) custom-call(s32[2]{0:T(128)} %copy-done.9, bf16[256,512]{1,0:T(8,128)(2,1)} %constant.39.clone.refs_0_, bf16[256,256]{1,0:T(8,128)(2,1)} %constant.40.clone.refs_1_, bf16[256,512]{1,0:T(8,128)(2,1)} %constant.41.clone.refs_2_, bf16[256,256]{1,0:T(8,128)(2,1)} %constant.42.clone.refs_3_, ...), custom_call_target="tpu_custom_call" | custom-call | flops 1610612736 | bytes 4194304 | tf_op jit(solution)/shard_map/first_x_forward/pallas_call | solution.py:939
  139.6 25.2 %collective-permute-done.12.refs_1_ = f32[4,512,128]{2,1,0:T(8,128)} collective-permute-done((f32[4,512,128]{2,1,0:T(8,128)}, f32[4,512,128]{2,1,0:T(8,128)}, u32[]{:S(2)}, u32[]{:S(2)}) %collective-permute-start.12) | collective-permute-done | bytes 1048608 | tf_op jit(solution)/shard_map/ppermute | solution.py:547
  164.8 4.6 %first_y_forward.1.refs_8_ = f32[4,512,256]{2,1,0:T(8,128)} custom-call(s32[2]{0:T(128)} %copy-done.9, bf16[2,2,128,256]{3,2,1,0:T(8,128)(2,1)} %constant.38.clone.table_ref, f32[4,512,128]{2,1,0:T(8,128)} %get-tuple-element.52.refs_0_, f32[4,512,128]{2,1,0:T(8,128)} %collective-permute-done.12.refs_1_), custom_call_target="tpu_custom_call" | custom-call | flops 805306368 | bytes 4194304 | tf_op jit(solution)/shard_map/first_y_forward/pallas_call | solution.py:963
  169.3 12.5 %all-to-all-done.1.refs_9_ = f32[16,4,32,256]{3,2,1,0:T(8,128)} async-done(((f32[16,4,32,256]{3,2,1,0:T(8,128)}), f32[16,4,32,256]{3,2,1,0:T(8,128)}, u32[]{:S(2)}, u32[]{:S(2)}) %all-to-all-start.1) | async-done | bytes 2097184 | tf_op jit(solution)/shard_map/all_to_all | solution.py:1178
  181.9 6.8 %potential.1 = (f32[16,4,32,256]{3,2,1,0:T(8,128)}, f32[4,512,256]{2,1,0:T(8,128)}) custom-call(s32[2]{0:T(128)} %copy-done.9, bf16[256,512]{1,0:T(8,128)(2,1)} %constant.39.clone.refs_0_, bf16[256,256]{1,0:T(8,128)(2,1)} %constant.40.clone.refs_1_, bf16[256,512]{1,0:T(8,128)(2,1)} %constant.41.clone.refs_2_, bf16[256,256]{1,0:T(8,128)(2,1)} %constant.42.clone.refs_3_, ...), custom_call_target="tpu_custom_call" | custom-call | flops 3221225472 | bytes 8388608 | tf_op jit(solution)/shard_map/potential/pallas_call | solution.py:997
  188.6 5.1 %all-to-all-start.2 = ((f32[16,4,32,256]{3,2,1,0:T(8,128)}), f32[16,4,32,256]{3,2,1,0:T(8,128)}, u32[]{:S(2)}, u32[]{:S(2)}) async-start(f32[16,4,32,256]{3,2,1,0:T(8,128)} %get-tuple-element.55), calls=%async_computation.2 | async-start | bytes 4194304 | tf_op jit(solution)/shard_map/all_to_all | solution.py:1178
  193.7 4.6 %last_y_inverse.1 = (f32[4,512,128]{2,1,0:T(8,128)}, f32[4,512,128]{2,1,0:T(8,128)}) custom-call(s32[2]{0:T(128)} %copy-done.9, bf16[2,2,256,128]{3,2,1,0:T(8,128)(2,1)} %constant.47.clone.table_ref, f32[4,512,256]{2,1,0:T(8,128)} %get-tuple-element.56.in_ref), custom_call_target="tpu_custom_call" | custom-call | flops 805306368 | bytes 4194304 | tf_op jit(solution)/shard_map/last_y_inverse/pallas_call | solution.py:1037
  198.6 25.2 %collective-permute-done.14.refs_5_ = f32[4,512,128]{2,1,0:T(8,128)} collective-permute-done((f32[4,512,128]{2,1,0:T(8,128)}, f32[4,512,128]{2,1,0:T(8,128)}, u32[]{:S(2)}, u32[]{:S(2)}) %collective-permute-start.14) | collective-permute-done | bytes 1048608 | tf_op jit(solution)/shard_map/ppermute | solution.py:547
  223.8 4.7 %last_x_inverse.1._ = f32[16,2,4,32,128]{4,3,2,1,0:T(8,128)} custom-call(s32[2]{0:T(128)} %copy-done.9, bf16[256,512]{1,0:T(8,128)(2,1)} %constant.43.clone.refs_4_.refs_0_, bf16[256,256]{1,0:T(8,128)(2,1)} %constant.44.clone.refs_5_.refs_1_, bf16[256,512]{1,0:T(8,128)(2,1)} %constant.45.clone.refs_6_.refs_2_, ...), custom_call_target="tpu_custom_call" | custom-call | flops 1610612736 | bytes 4194304 | tf_op jit(solution)/shard_map/last_x_inverse/pallas_call | solution.py:1064
  228.5 12.5 %all-to-all-done.2 = f32[16,4,32,256]{3,2,1,0:T(8,128)} async-done(((f32[16,4,32,256]{3,2,1,0:T(8,128)}), f32[16,4,32,256]{3,2,1,0:T(8,128)}, u32[]{:S(2)}, u32[]{:S(2)}) %all-to-all-start.2) | async-done | bytes 2097184 | tf_op jit(solution)/shard_map/all_to_all | solution.py:1178
  241.1 4.6 %pair_y_inverse.1 = (f32[2,64,32,128]{3,2,1,0:T(8,128)}, f32[2,64,32,128]{3,2,1,0:T(8,128)}, f32[16,2,4,32,128]{4,3,2,1,0:T(8,128)}) custom-call(s32[2]{0:T(128)} %copy-done.9, bf16[2,2,256,128]{3,2,1,0:T(8,128)(2,1)} %constant.47.clone.table_ref, f32[64,32,256]{2,1,0:T(8,128)} %bitcast.4.in_ref, ...), custom_call_target="tpu_custom_call", output_to_operand_aliasing={{2}: (3, {})} | custom-call | flops 1610612736 | bytes 6291456 | tf_op jit(solution)/shard_map/pair_y_inverse/pallas_call | solution.py:1095
  246.0 5.1 %all-to-all-start.3 = ((f32[16,2,4,32,128]{4,3,2,1,0:T(8,128)}), f32[16,2,4,32,128]{4,3,2,1,0:T(8,128)}, u32[]{:S(2)}, u32[]{:S(2)}) async-start(f32[16,2,4,32,128]{4,3,2,1,0:T(8,128)} %get-tuple-element.63), calls=%async_computation.3 | async-start | bytes 4194304 | tf_op jit(solution)/shard_map/all_to_all | solution.py:1178
  251.1 42.8 %collective-permute-done.15.refs_7_ = f32[2,64,32,128]{3,2,1,0:T(8,128)} collective-permute-done((f32[2,64,32,128]{3,2,1,0:T(8,128)}, f32[2,64,32,128]{3,2,1,0:T(8,128)}, u32[]{:S(2)}, u32[]{:S(2)}) %collective-permute-start.15) | collective-permute-done | bytes 2097184 | tf_op jit(solution)/shard_map/ppermute | solution.py:547
  293.8 7.6 %image_part.2 = (f32[32,128,128]{2,1,0:T(8,128)}, f32[32,128,128]{2,1,0:T(8,128)}) custom-call(s32[2]{0:T(128)} %copy-done.9, bf16[2,2,2,64,128]{4,3,2,1,0:T(8,128)(2,1)} %constant.48.clone.table_ref, f32[3,32,128,128]{3,2,1,0:T(8,128)} %copy-done.1, f32[3,32,128,128]{3,2,1,0:T(8,128)} %copy-done.1, bf16[3,32,128,128]{3,2,1,0:T(8,128)(2,1)} %refs_1_.10, ...), custom_call_target="tpu_custom_call" | custom-call | flops 805306368000 | bytes 16777216000 | tf_op jit(solution)/shard_map/image_part/pallas_call | solution.py:1154
  301.4 6.1 %image_part.3 = (f32[32,128,128]{2,1,0:T(8,128)}, f32[32,128,128]{2,1,0:T(8,128)}) custom-call(s32[2]{0:T(128)} %copy-done.9, bf16[1,2,1,128,128]{4,3,2,1,0:T(8,128)(2,1)} %constant.49.clone.table_ref, f32[3,32,128,128]{3,2,1,0:T(8,128)} %copy-done.1, bf16[3,32,128,128]{3,2,1,0:T(8,128)(2,1)} %refs_1_.10, bf16[3,32,128,128]{3,2,1,0:T(8,128)(2,1)} %refs_2_.16, ...), custom_call_target="tpu_custom_call" | custom-call | flops 402653184 | bytes 10485760 | tf_op jit(solution)/shard_map/image_part/pallas_call | solution.py:1154
  (53 shorter events, 50.5 us)
Async XLA Ops:
  3.9 14.3 %collective-permute-start = (f32[6,32,128]{2,1,0:T(8,128)}, f32[6,32,128]{2,1,0:T(8,128)S(1)}, u32[]{:S(2)}, u32[]{:S(2)}) collective-permute-start(f32[6,32,128]{2,1,0:T(8,128)} %get-tuple-element.33), channel_id=1, source_target_pairs={{0,1},{2,3},{4,5},{6,7},{8,9},{10,11},{12,13},{14,15},{16,17},{18,... | collective-permute-start | bytes 294920 | tf_op jit(solution)/shard_map/ppermute | solution.py:27
  7.3 12.2 %collective-permute-start.1 = (f32[6,32,128]{2,1,0:T(8,128)}, f32[6,32,128]{2,1,0:T(8,128)S(1)}, u32[]{:S(2)}, u32[]{:S(2)}) collective-permute-start(f32[6,32,128]{2,1,0:T(8,128)} %get-tuple-element.34), channel_id=1, source_target_pairs={{1,0},{3,2},{5,4},{7,6},{9,8},{11,10},{13,12},{15,14},{17,16},{19,... | collective-permute-start | bytes 294920 | tf_op jit(solution)/shard_map/ppermute | solution.py:27
  8.6 26.4 %collective-permute-start.2 = (f32[6,128,128]{2,1,0:T(8,128)}, f32[6,128,128]{2,1,0:T(8,128)S(1)}, u32[]{:S(2)}, u32[]{:S(2)}) collective-permute-start(f32[6,128,128]{2,1,0:T(8,128)} %get-tuple-element.35), channel_id=1, source_target_pairs={{0,2},{2,4},{4,6},{6,8},{8,10},{10,12},{12,14},{14,16},{16,18},{18... | collective-permute-start | bytes 1179656 | tf_op jit(solution)/shard_map/ppermute | solution.py:27
  10.5 24.5 %collective-permute-start.3 = (f32[6,128,128]{2,1,0:T(8,128)}, f32[6,128,128]{2,1,0:T(8,128)S(1)}, u32[]{:S(2)}, u32[]{:S(2)}) collective-permute-start(f32[6,128,128]{2,1,0:T(8,128)} %get-tuple-element.36), channel_id=1, source_target_pairs={{2,0},{4,2},{6,4},{8,6},{10,8},{12,10},{14,12},{16,14},{18,16},{20... | collective-permute-start | bytes 1179656 | tf_op jit(solution)/shard_map/ppermute | solution.py:27
  14.2 20.8 %collective-permute-start.4 = (f32[1,128]{1,0:T(1,128)}, f32[1,128]{1,0:T(1,128)S(1)}, u32[]{:S(2)}, u32[]{:S(2)}) collective-permute-start(f32[1,128]{1,0:T(1,128)} %get-tuple-element.37), channel_id=1, source_target_pairs={{2,1},{4,3},{6,5},{8,7},{10,9},{12,11},{14,13},{16,15},{18,17},{20... | collective-permute-start | bytes 1544 | tf_op jit(solution)/shard_map/ppermute | solution.py:38
  18.2 16.8 %collective-permute-start.5 = (f32[1,128]{1,0:T(1,128)}, f32[1,128]{1,0:T(1,128)S(1)}, u32[]{:S(2)}, u32[]{:S(2)}) collective-permute-start(f32[1,128]{1,0:T(1,128)} %get-tuple-element.38), channel_id=1, source_target_pairs={{1,2},{3,4},{5,6},{7,8},{9,10},{11,12},{13,14},{15,16},{17,18},{19... | collective-permute-start | bytes 1544 | tf_op jit(solution)/shard_map/ppermute | solution.py:38
  35.0 21.1 %copy-start.3 = (bf16[32,128,128]{2,1,0:T(8,128)(2,1)S(1)}, bf16[32,128,128]{2,1,0:T(8,128)(2,1)}, u32[]{:S(2)}) copy-start(bf16[32,128,128]{2,1,0:T(8,128)(2,1)} %refs_12_.9) | copy-start | bytes 3145732
  39.1 17.1 %collective-permute-start.6 = (f32[5,32,128]{2,1,0:T(8,128)S(1)}, f32[5,32,128]{2,1,0:T(8,128)S(1)}, u32[]{:S(2)}, u32[]{:S(2)}) collective-permute-start(f32[5,32,128]{2,1,0:T(8,128)S(1)} %get-tuple-element.45), channel_id=1, source_target_pairs={{0,1},{2,3},{4,5},{6,7},{8,9},{10,11},{12,13},{14,15},{16,17},{18,... | collective-permute-start | bytes 245768 | tf_op jit(solution)/shard_map/ppermute | solution.py:27
  43.9 11.0 %collective-permute-start.7 = (f32[4,32,128]{2,1,0:T(8,128)S(1)}, f32[4,32,128]{2,1,0:T(8,128)S(1)}, u32[]{:S(2)}, u32[]{:S(2)}) collective-permute-start(f32[4,32,128]{2,1,0:T(8,128)S(1)} %get-tuple-element.46), channel_id=1, source_target_pairs={{1,0},{3,2},{5,4},{7,6},{9,8},{11,10},{13,12},{15,14},{17,16},{19,... | collective-permute-start | bytes 196616 | tf_op jit(solution)/shard_map/ppermute | solution.py:27
  45.3 26.6 %copy-start.9 = (s32[2]{0:T(128)}, s32[2]{0:T(128)S(1)}, u32[]{:S(2)}) copy-start(s32[2]{0:T(128)S(1)} %pad_add_fusion.place_ref) | copy-start | bytes 28
  45.3 17.6 %collective-permute-start.8 = (f32[5,128,128]{2,1,0:T(8,128)S(1)}, f32[5,128,128]{2,1,0:T(8,128)S(1)}, u32[]{:S(2)}, u32[]{:S(2)}) collective-permute-start(f32[5,128,128]{2,1,0:T(8,128)S(1)} %get-tuple-element.47), channel_id=1, source_target_pairs={{0,2},{2,4},{4,6},{6,8},{8,10},{10,12},{12,14},{14,16},{16,18},{18... | collective-permute-start | bytes 983048 | tf_op jit(solution)/shard_map/ppermute | solution.py:27
  48.6 14.3 %collective-permute-start.9 = (f32[4,128,128]{2,1,0:T(8,128)S(1)}, f32[4,128,128]{2,1,0:T(8,128)S(1)}, u32[]{:S(2)}, u32[]{:S(2)}) collective-permute-start(f32[4,128,128]{2,1,0:T(8,128)S(1)} %get-tuple-element.48), channel_id=1, source_target_pairs={{2,0},{4,2},{6,4},{8,6},{10,8},{12,10},{14,12},{16,14},{18,16},{20... | collective-permute-start | bytes 786440 | tf_op jit(solution)/shard_map/ppermute | solution.py:27
  50.8 12.0 %collective-permute-start.10 = (f32[1,128]{1,0:T(1,128)S(1)}, f32[1,128]{1,0:T(1,128)S(1)}, u32[]{:S(2)}, u32[]{:S(2)}) collective-permute-start(f32[1,128]{1,0:T(1,128)S(1)} %get-tuple-element.49), channel_id=1, source_target_pairs={{2,1},{4,3},{6,5},{8,7},{10,9},{12,11},{14,13},{16,15},{18,17},{20... | collective-permute-start | bytes 1544 | tf_op jit(solution)/shard_map/ppermute | solution.py:38
  54.8 8.0 %collective-permute-start.11 = (f32[1,128]{1,0:T(1,128)S(1)}, f32[1,128]{1,0:T(1,128)S(1)}, u32[]{:S(2)}, u32[]{:S(2)}) collective-permute-start(f32[1,128]{1,0:T(1,128)S(1)} %get-tuple-element.50), channel_id=1, source_target_pairs={{1,2},{3,4},{5,6},{7,8},{9,10},{11,12},{13,14},{15,16},{17,18},{19... | collective-permute-start | bytes 1544 | tf_op jit(solution)/shard_map/ppermute | solution.py:38
  65.3 6.6 %copy-start.1 = (f32[3,32,128,128]{3,2,1,0:T(8,128)}, f32[3,32,128,128]{3,2,1,0:T(8,128)S(1)}, u32[]{:S(2)}) copy-start(f32[3,32,128,128]{3,2,1,0:T(8,128)S(1)} %stencil_ends.3.refs_0_.refs_1_) | copy-start | bytes 18874372
  65.3 6.6 %copy-start.8 = (bf16[1,2,1,128,128]{4,3,2,1,0:T(8,128)(2,1)S(1)}, bf16[1,2,1,128,128]{4,3,2,1,0:T(8,128)(2,1)}, u32[]{:S(2)}) copy-start(bf16[1,2,1,128,128]{4,3,2,1,0:T(8,128)(2,1)} %constant.37.clone.table_ref) | copy-start | bytes 196612
  68.9 47.6 %collective-permute-start.13 = (f32[2,64,32,128]{3,2,1,0:T(8,128)S(1)}, f32[2,64,32,128]{3,2,1,0:T(8,128)}, u32[]{:S(2)}, u32[]{:S(2)}) collective-permute-start(f32[2,64,32,128]{3,2,1,0:T(8,128)S(1)} %get-tuple-element.54), channel_id=1, source_target_pairs={{0,1},{1,0},{2,3},{3,2},{4,5},{5,4},{6,7},{7,6},{8,9},{9,8},{10,11... | collective-permute-start | bytes 6291464 | tf_op jit(solution)/shard_map/ppermute | solution.py:547
  74.9 54.5 %all-to-all-start = ((f32[16,2,4,32,128]{4,3,2,1,0:T(8,128)}), f32[16,2,4,32,128]{4,3,2,1,0:T(8,128)}, u32[]{:S(2)}, u32[]{:S(2)}) async-start(f32[16,2,4,32,128]{4,3,2,1,0:T(8,128)} %bitcast.2), calls=%async_computation | async-start | bytes 4194304 | tf_op jit(solution)/shard_map/all_to_all | solution.py:1178
  129.4 52.4 %all-to-all-start.1 = ((f32[16,4,32,256]{3,2,1,0:T(8,128)}), f32[16,4,32,256]{3,2,1,0:T(8,128)}, u32[]{:S(2)}, u32[]{:S(2)}) async-start(f32[16,4,32,256]{3,2,1,0:T(8,128)} %bitcast.6), calls=%async_computation.1 | async-start | bytes 4194304 | tf_op jit(solution)/shard_map/all_to_all | solution.py:1178
  139.2 25.5 %collective-permute-start.12 = (f32[4,512,128]{2,1,0:T(8,128)}, f32[4,512,128]{2,1,0:T(8,128)}, u32[]{:S(2)}, u32[]{:S(2)}) collective-permute-start(f32[4,512,128]{2,1,0:T(8,128)} %get-tuple-element.53), channel_id=1, source_target_pairs={{0,1},{1,0},{2,3},{3,2},{4,5},{5,4},{6,7},{7,6},{8,9},{9,8},{10,11... | collective-permute-start | bytes 3145736 | tf_op jit(solution)/shard_map/ppermute | solution.py:547
  188.6 52.4 %all-to-all-start.2 = ((f32[16,4,32,256]{3,2,1,0:T(8,128)}), f32[16,4,32,256]{3,2,1,0:T(8,128)}, u32[]{:S(2)}, u32[]{:S(2)}) async-start(f32[16,4,32,256]{3,2,1,0:T(8,128)} %get-tuple-element.55), calls=%async_computation.2 | async-start | bytes 4194304 | tf_op jit(solution)/shard_map/all_to_all | solution.py:1178
  198.3 25.5 %collective-permute-start.14 = (f32[4,512,128]{2,1,0:T(8,128)}, f32[4,512,128]{2,1,0:T(8,128)}, u32[]{:S(2)}, u32[]{:S(2)}) collective-permute-start(f32[4,512,128]{2,1,0:T(8,128)} %get-tuple-element.58), channel_id=1, source_target_pairs={{0,1},{1,0},{2,3},{3,2},{4,5},{5,4},{6,7},{7,6},{8,9},{9,8},{10,11... | collective-permute-start | bytes 3145736 | tf_op jit(solution)/shard_map/ppermute | solution.py:547
  245.7 48.1 %collective-permute-start.15 = (f32[2,64,32,128]{3,2,1,0:T(8,128)}, f32[2,64,32,128]{3,2,1,0:T(8,128)}, u32[]{:S(2)}, u32[]{:S(2)}) collective-permute-start(f32[2,64,32,128]{3,2,1,0:T(8,128)} %get-tuple-element.60), channel_id=1, source_target_pairs={{0,1},{1,0},{2,3},{3,2},{4,5},{5,4},{6,7},{7,6},{8,9},{9,8},{10,11... | collective-permute-start | bytes 6291464 | tf_op jit(solution)/shard_map/ppermute | solution.py:547
  246.0 55.4 %all-to-all-start.3 = ((f32[16,2,4,32,128]{4,3,2,1,0:T(8,128)}), f32[16,2,4,32,128]{4,3,2,1,0:T(8,128)}, u32[]{:S(2)}, u32[]{:S(2)}) async-start(f32[16,2,4,32,128]{4,3,2,1,0:T(8,128)} %get-tuple-element.63), calls=%async_computation.3 | async-start | bytes 4194304 | tf_op jit(solution)/shard_map/all_to_all | solution.py:1178
  (6 other events, 15.0 us)

commit v6 on v5

--- a/solution.py
+++ b/solution.py
@@ -27,47 +27,82 @@
     return lax.ppermute(block, axis, route)
 
 
-def across_corner(row, x_way, y_way):
-    x_count, y_count = lax.axis_size("gx"), lax.axis_size("gy")
-    route = [
-        ((i - x_way) * y_count + j - y_way, i * y_count + j)
-        for i in range(x_count)
-        for j in range(y_count)
-        if 0 <= i - x_way < x_count and 0 <= j - y_way < y_count
-    ]
-    return lax.ppermute(row, ("gx", "gy"), route)
-
-
-def exchange(x_last, x_first, y_last, y_first, corner_y, corner_x):
-    yl, yr = passed_along(y_last, "gy", 1), passed_along(y_first, "gy", -1)
-    xl, xr = passed_along(x_last, "gx", 1), passed_along(x_first, "gx", -1)
-    return (yl, yr), (xl, xr, across_corner(corner_y, -1, 1), across_corner(corner_x, 1, -1))
-
-
-def first_rims(brick, velocity, stress, lame, shear):
+EDGE_ROWS = 8
+
+
+def with_edges(place, rims, x_last, x_first):
+    high, low = rims[-1], rims[0]
+    count, z = high.shape[1:]
+    some = fit(count, 8)
+    lone = len(rims) == 1
+
+    def kernel(place_ref, high_ref, low_ref, _, __, last_ref, first_ref):
+        row = lax.broadcasted_iota(jnp.int32, (EDGE_ROWS, z), 0)
+        me = place_ref[1]
+        keep_high, keep_low = (me == 0, me == 1) if lone else (True, True)
+        above = jnp.where(keep_high, high_ref[0, some - 1 :], 0.0)
+        below = jnp.where(keep_low, low_ref[0, :1], 0.0)
+        last_ref[...] = jnp.where(row == 0, above, 0.0)
+        first_ref[...] = jnp.where(row == 0, below, 0.0)
+
+    return pl.pallas_call(
+        kernel,
+        grid=(1,),
+        in_specs=[
+            scalars(),
+            pl.BlockSpec((1, some, z), lambda i: (0, count // some - 1, 0)),
+            pl.BlockSpec((1, some, z), lambda i: (1, 0, 0)),
+            unread(),
+            unread(),
+        ],
+        out_specs=[pl.BlockSpec((EDGE_ROWS, z), lambda i: (0, 0))] * 2,
+        out_shape=[jax.ShapeDtypeStruct(edge.shape, jnp.float32) for edge in (x_last, x_first)],
+        input_output_aliases={3: 0, 4: 1},
+        compiler_params=params(4 * 2**20),
+        name="with_edges",
+    )(place, high, low, x_last, x_first)
+
+
+def exchange(place, x_last, x_first, *y_outs):
+    if len(y_outs) == 1:
+        rims = (lax.ppermute(y_outs[0], "gy", [(0, 1), (1, 0)]),)
+    else:
+        rims = (passed_along(y_outs[0], "gy", 1), passed_along(y_outs[1], "gy", -1))
+    x_last, x_first = with_edges(place, rims, x_last, x_first)
+    return rims, (passed_along(x_last, "gx", 1), passed_along(x_first, "gx", -1))
+
+
+def first_rims(brick, place, velocity, stress, lame, shear):
     x, y, z = brick
     some = fit(y, 8)
     many = fit(y, 16)
-
-    def kernel(*refs):
+    swapped = lax.axis_size("gy") == 2
+
+    def kernel(place_ref, *refs):
         (v_first, v_last, s_first, s_last, lame_first, shear_first, shear_last) = refs[:7]
         (v_low, v_high, s_low, s_high, lame_low, shear_low, shear_high) = refs[7:14]
-        x_last, x_first, y_last, y_first, corner_y, corner_x = refs[14:]
+        x_last, x_first, *y_outs = refs[14:]
 
         def wide(value):
             return value.astype(jnp.float32)
 
-        for i in range(3):
-            x_last[i], x_first[i] = v_last[i, 0], v_first[i, 0]
-            y_last[i], y_first[i] = v_high[i, :, some - 1], v_low[i, :, 0]
-        x_last[3], x_last[4], x_last[5] = s_last[3, 0], s_last[4, 0], wide(shear_last[0])
-        x_first[3], x_first[4], x_first[5] = s_first[0, 0], wide(lame_first[0]), wide(shear_first[0])
-        y_last[3], y_last[4] = s_high[3, :, some - 1], s_high[5, :, some - 1]
-        y_last[5] = wide(shear_high[...])[:, many - 1]
-        y_first[3], y_first[4] = s_low[1, :, 0], wide(lame_low[...])[:, 0]
-        y_first[5] = wide(shear_low[...])[:, 0]
-        corner_y[...] = v_first[1, 0, y - 1 :]
-        corner_x[...] = v_last[0, 0, :1]
+        lasts = [v_last[0, 0], v_last[1, 0], v_last[2, 0], s_last[3, 0], s_last[4, 0]]
+        firsts = [v_first[0, 0], v_first[1, 0], v_first[2, 0], s_first[0, 0]]
+        lasts += [wide(shear_last[0])]
+        firsts += [wide(lame_first[0]), wide(shear_first[0])]
+        for ref, values in ((x_last, lasts), (x_first, firsts)):
+            ref[:EDGE_ROWS] = jnp.zeros((EDGE_ROWS, z), jnp.float32)
+            for i, value in enumerate(values):
+                ref[EDGE_ROWS + i * y : EDGE_ROWS + (i + 1) * y] = value
+        lasts = [v_high[i, :, some - 1] for i in range(3)]
+        firsts = [v_low[i, :, 0] for i in range(3)]
+        lasts += [s_high[3, :, some - 1], s_high[5, :, some - 1], wide(shear_high[...])[:, many - 1]]
+        firsts += [s_low[1, :, 0], wide(lame_low[...])[:, 0], wide(shear_low[...])[:, 0]]
+        for i, (low, high) in enumerate(zip(lasts, firsts)):
+            if swapped:
+                y_outs[0][i] = jnp.where(place_ref[1] == 0, low, high)
+            else:
+                y_outs[0][i], y_outs[1][i] = low, high
 
     def plane(count, at):
         return pl.BlockSpec((count, 1, y, z), lambda i: (0, at, 0, 0))
@@ -81,12 +116,12 @@
     def medium_rows(at):
         return pl.BlockSpec((x, many, z), lambda i: (0, at, 0))
 
-    shapes = [(6, y, z), (6, y, z), (6, x, z), (6, x, z), (1, z), (1, z)]
+    shapes = [(EDGE_ROWS + 6 * y, z)] * 2 + [(6, x, z)] * (1 if swapped else 2)
     ends, highs, most = x - 1, y // some - 1, y // many - 1
     return pl.pallas_call(
         kernel,
         grid=(1,),
-        in_specs=[plane(3, 0), plane(3, ends), plane(6, 0), plane(6, ends)]
+        in_specs=[scalars(), plane(3, 0), plane(3, ends), plane(6, 0), plane(6, ends)]
         + [medium_plane(0), medium_plane(0), medium_plane(ends)]
         + [rows(3, 0), rows(3, highs), rows(6, 0), rows(6, highs)]
         + [medium_rows(0), medium_rows(0), medium_rows(most)],
@@ -98,12 +133,13 @@
         ),
         name="first_rims",
     )(
+        place,
         *(velocity, velocity, stress, stress, lame, shear, shear),
         *(velocity, velocity, stress, stress, lame, shear, shear),
     )
 
 
-def stencil(brick, state, rims, medium, x_rims, x_medium, done, last):
+def stencil(brick, place, state, rims, medium, x_rims, x_medium, done, last):
     x, y, z = brick
     velocity, stress, lame, shear, buoyancy = state
     group = fit(x, X_GROUP)
@@ -115,9 +151,11 @@
     else:
         count, of = groups - 2, lambda i: i + 1
     f32 = jnp.float32
-
-    def kernel(*refs):
+    swapped = len(rims) == 1
+
+    def kernel(place_ref, *refs):
         refs = list(refs)
+        me = place_ref[1]
 
         def take(number):
             taken = refs[:number]
@@ -127,17 +165,18 @@
         v_ref, s_ref, lame_ref, shear_ref, buoy_ref = take(5)
         v_next_ref, xx_next_ref, lame_next_ref, shear_next_ref = take(4)
         v_prior_ref, xy_prior_ref, xz_prior_ref, shear_prior_ref = take(4)
-        yl, yr = take(2)
-        yl_medium, yr_medium = take(2) if medium else (yl, yr)
+        y_rims = take(len(rims))
+        y_medium = take(len(rims)) if medium else y_rims
         if ends:
-            xl, xr, edge_y, edge_x = take(4)
+            xl, xr = take(2)
             xl_medium, xr_medium = take(2) if medium else (xl, xr)
         given = take(len(done))
         new = take(1)[0]
         if not last:
-            s_out, y_last, y_first = take(3)
+            s_out = take(1)[0]
+            y_outs = take(len(rims))
             if ends:
-                x_last, x_first, corner_y, corner_x = take(4)
+                x_last, x_first = take(2)
         carried, xx_after = take(2)
         s_new = take(1)[0] if last else s_out
         turn = pl.program_id(0)
@@ -165,18 +204,27 @@
         def wide(value):
             return value.astype(f32)
 
-        def line(ref, which, place):
-            return ref[which, pl.ds(place, 1), :]
-
-        def line_after(place):
+        def low(which, at, refs=y_rims):
+            value = refs[0][which, pl.ds(at, 1), :]
+            return jnp.where(me == 1, value, 0.0) if swapped else value
+
+        def high(which, at, refs=y_rims):
+            value = refs[-1][which, pl.ds(at, 1), :]
+            return jnp.where(me == 0, value, 0.0) if swapped else value
+
+        def low_after(at):
             if not ends:
-                return line(yl, 1, place)
-            return jnp.where(place == x, edge_y[...], line(yl, 1, jnp.minimum(place, x - 1)))
-
-        def line_before(place):
+                return low(1, at)
+            return jnp.where(at == x, xr[:1], low(1, jnp.minimum(at, x - 1)))
+
+        def high_before(at):
             if not ends:
-                return line(yr, 0, place)
-            return jnp.where(place < 0, edge_x[...], line(yr, 0, jnp.maximum(place, 0)))
+                return high(0, at)
+            return jnp.where(at < 0, xl[:1], high(0, jnp.maximum(at, 0)))
+
+        def rows_of(ref, i, span=slice(0, y)):
+            start = EDGE_ROWS + i * y
+            return ref[start + span.start : start + span.stop]
 
         def begin(value, rim):
             return jnp.where(start, rim(), value) if ends else value
@@ -185,13 +233,13 @@
             return jnp.where(end, rim(), value) if ends else value
 
         def fresh():
-            shear_rim = begin(wide(shear_prior_ref[0]), lambda: xl_medium[5])
-            vx, vy, vz = (begin(v_prior_ref[i, 0], lambda: xl[i]) for i in range(3))
-            xy = begin(xy_prior_ref[0, 0], lambda: xl[3])
-            xz = begin(xz_prior_ref[0, 0], lambda: xl[4])
+            shear_rim = begin(wide(shear_prior_ref[0]), lambda: rows_of(xl_medium, 5))
+            vx, vy, vz = (begin(v_prior_ref[i, 0], lambda: rows_of(xl, i)) for i in range(3))
+            xy = begin(xy_prior_ref[0, 0], lambda: rows_of(xl, 3))
+            xz = begin(xz_prior_ref[0, 0], lambda: rows_of(xl, 4))
             pull = time_step * shear_rim
             carried[0] = vx
-            carried[1] = xy + pull * ((next_y(vx, line_before(at - 1)) - vx) + (v_ref[1, 0] - vy))
+            carried[1] = xy + pull * ((next_y(vx, high_before(at - 1)) - vx) + (v_ref[1, 0] - vy))
             carried[2] = xz + pull * ((next_z(vx) - vx) + (v_ref[2, 0] - vz))
 
         if ends:
@@ -202,11 +250,11 @@
 
             @pl.when(turn == 0)
             def _():
-                y_last[...] = given[2][...]
-                y_first[...] = given[3][...]
+                for out, value in zip(y_outs, given[2:]):
+                    out[...] = value[...]
 
         def after(i, rows):
-            return finish(v_next_ref[i, 0, rows], lambda: xr[i, rows])
+            return finish(v_next_ref[i, 0, rows], lambda: rows_of(xr, i, rows))
 
         spans = [slice(top, top + tall) for top in range(0, y, tall)]
 
@@ -224,9 +272,9 @@
                 vx_prior = carried[0, span] if k == 0 else v_ref[0, k - 1, span]
                 vy_next = after(1, span) if k == group - 1 else v_ref[1, k + 1, span]
                 vz_next = after(2, span) if k == group - 1 else v_ref[2, k + 1, span]
-                vy_rim = row_before(span, v_here[1], lambda: line(yl, 1, here))
-                vx_rim = row_after(span, v_here[0], lambda: line(yr, 0, here))
-                vz_rim = row_after(span, v_here[2], lambda: line(yr, 2, here))
+                vy_rim = row_before(span, v_here[1], lambda: low(1, here))
+                vx_rim = row_after(span, v_here[0], lambda: high(0, here))
+                vz_rim = row_after(span, v_here[2], lambda: high(2, here))
                 lame_value, shear_value = wide(lame_ref[k, span]), wide(shear_ref[k, span])
                 ex = vx - vx_prior
                 ey = vy - prior_y(vy, vy_rim)
@@ -248,16 +296,16 @@
         for span in spans:
             vx, vy, vz = (after(i, span) for i in range(3))
             vy_rim = (
-                line_after(at + group)
+                low_after(at + group)
                 if span.start == 0
                 else after(1, slice(span.start - 1, span.start))
             )
             ex = vx - v_ref[0, group - 1, span]
             ey = vy - prior_y(vy, vy_rim)
             ez = vz - prior_z(vz)
-            lame_value = finish(wide(lame_next_ref[0, span]), lambda: xr_medium[4, span])
-            shear_value = finish(wide(shear_next_ref[0, span]), lambda: xr_medium[5, span])
-            xx_after[span] = finish(xx_next_ref[0, 0, span], lambda: xr[3, span]) + time_step * (
+            lame_value = finish(wide(lame_next_ref[0, span]), lambda: rows_of(xr_medium, 4, span))
+            shear_value = finish(wide(shear_next_ref[0, span]), lambda: rows_of(xr_medium, 5, span))
+            xx_after[span] = finish(xx_next_ref[0, 0, span], lambda: rows_of(xr, 3, span)) + time_step * (
                 lame_value * (ex + ey + ez) + 2.0 * shear_value * ex
             )
 
@@ -265,18 +313,18 @@
             here = at + k
             v_here = [v_ref.at[i, k] for i in range(3)]
             vx_edge, vy_edge, vz_edge = v_here[0][:1], v_here[1][y - 1 :], v_here[2][:1]
-            pull = time_step * line(yl_medium, 5, here)
-            vy_rim, vz_rim = line(yl, 1, here), line(yl, 2, here)
-            xy_rim = line(yl, 3, here) + pull * (
-                (vx_edge - line(yl, 0, here)) + (line_after(here + 1) - vy_rim)
+            pull = time_step * low(5, here, y_medium)
+            vy_rim, vz_rim = low(1, here), low(2, here)
+            xy_rim = low(3, here) + pull * (
+                (vx_edge - low(0, here)) + (low_after(here + 1) - vy_rim)
             )
-            yz_rim = line(yl, 4, here) + pull * ((next_z(vy_rim) - vy_rim) + (vz_edge - vz_rim))
-            vx_rim, vz_rim = line(yr, 0, here), line(yr, 2, here)
-            ex = vx_rim - line_before(here - 1)
-            ey = line(yr, 1, here) - vy_edge
+            yz_rim = low(4, here) + pull * ((next_z(vy_rim) - vy_rim) + (vz_edge - vz_rim))
+            vx_rim, vz_rim = high(0, here), high(2, here)
+            ex = vx_rim - high_before(here - 1)
+            ey = high(1, here) - vy_edge
             ez = vz_rim - prior_z(vz_rim)
-            yy_rim = line(yr, 3, here) + time_step * (
-                line(yr_medium, 4, here) * (ex + ey + ez) + 2.0 * line(yr_medium, 5, here) * ey
+            yy_rim = high(3, here) + time_step * (
+                high(4, here, y_medium) * (ex + ey + ez) + 2.0 * high(5, here, y_medium) * ey
             )
             s_here = [s_new.at[i, k] for i in range(6)]
             for span in spans:
@@ -299,28 +347,32 @@
                 )
             if last:
                 continue
-            for i in range(3):
-                y_last[i, pl.ds(here, 1), :] = new[i, k, y - 1 :]
-                y_first[i, pl.ds(here, 1), :] = new[i, k, :1]
-            y_last[3, pl.ds(here, 1), :] = s_new[3, k, y - 1 :]
-            y_last[4, pl.ds(here, 1), :] = s_new[5, k, y - 1 :]
-            y_first[3, pl.ds(here, 1), :] = s_new[1, k, :1]
+            lasts = [new[i, k, y - 1 :] for i in range(3)]
+            lasts += [s_new[3, k, y - 1 :], s_new[5, k, y - 1 :]]
+            firsts = [new[i, k, :1] for i in range(3)] + [s_new[1, k, :1]] * 2
+            for i in range(5):
+                spot = pl.ds(here, 1)
+                if swapped:
+                    y_outs[0][i, spot, :] = jnp.where(me == 0, lasts[i], firsts[i])
+                else:
+                    y_outs[0][i, spot, :], y_outs[1][i, spot, :] = lasts[i], firsts[i]
 
         if ends and not last:
+
+            def edge(out, values):
+                out[:EDGE_ROWS] = jnp.zeros((EDGE_ROWS, z), f32)
+                for i, value in enumerate(values):
+                    out[EDGE_ROWS + i * y : EDGE_ROWS + (i + 1) * y] = value
 
             @pl.when(start)
             def _():
-                for i in range(3):
-                    x_first[i] = new[i, 0]
-                x_first[3] = s_new[0, 0]
-                corner_y[...] = new[1, 0, y - 1 :]
+                edge(x_first, [new[0, 0], new[1, 0], new[2, 0], s_new[0, 0]])
 
             @pl.when(end)
             def _():
-                for i in range(3):
-                    x_last[i] = new[i, group - 1]
-                x_last[3], x_last[4] = s_new[3, group - 1], s_new[4, group - 1]
-                corner_x[...] = new[0, group - 1, :1]
+                most = group - 1
+                values = [new[i, most] for i in range(3)]
+                edge(x_last, values + [s_new[3, most], s_new[4, most]])
 
         if not ends:
             carried[0] = v_ref[0, group - 1]
@@ -343,9 +395,9 @@
         return pl.BlockSpec((1, y, z), lambda i: (place(i), 0, 0))
 
     medium_block = pl.BlockSpec((group, y, z), lambda i: (of(i), 0, 0))
-    args = [velocity, stress, lame, shear, buoyancy, velocity, stress, lame, shear]
+    args = [place, velocity, stress, lame, shear, buoyancy, velocity, stress, lame, shear]
     args += [velocity, stress, stress, shear, *rims, *medium]
-    in_specs = [planes(3), planes(6), medium_block, medium_block, medium_block]
+    in_specs = [scalars(), planes(3), planes(6), medium_block, medium_block, medium_block]
     in_specs += [one(3, 0, next_plane), one(1, 0, next_plane)]
     in_specs += [medium_one(next_plane), medium_one(next_plane)]
     in_specs += [one(3, 0, prior_plane), one(1, 3, prior_plane), one(1, 4, prior_plane)]
@@ -363,10 +415,10 @@
     out_shape = [(3, x, y, z)]
     out_specs = [planes(3)]
     if not last:
-        out_shape += [(6, x, y, z), (5, x, z), (4, x, z)]
+        out_shape += [(6, x, y, z)] + [(5, x, z)] * len(rims)
         out_specs += [planes(6)]
         if ends:
-            out_shape += [(5, y, z), (4, y, z), (1, z), (1, z)]
+            out_shape += [(EDGE_ROWS + 5 * y, z), (EDGE_ROWS + 4 * y, z)]
         out_specs += [whole_block(shape) for shape in out_shape[2:]]
     part = (1 if ends else WEIGHT) * count * group * y * z
     return pl.pallas_call(
@@ -386,22 +438,22 @@
     )(*args)
 
 
-def propagate(velocity, stress, lame, shear, buoyancy):
+def propagate(place, velocity, stress, lame, shear, buoyancy):
     brick = velocity.shape[1:]
     between = brick[0] // fit(brick[0], X_GROUP) > 2
-    rims, x_rims = exchange(*first_rims(brick, velocity, stress, lame, shear))
-    held, medium, x_medium = (rims, x_rims[:2]), (), ()
+    rims, x_rims = exchange(place, *first_rims(brick, place, velocity, stress, lame, shear))
+    held, medium, x_medium = (rims, x_rims), (), ()
     for step_index in range(STEPS):
         last = step_index == STEPS - 1
         state = (velocity, stress, lame, shear, buoyancy)
         done = []
         if between:
-            done = stencil(brick, state, rims, medium, None, None, done, last)
-        found = stencil(brick, state, rims, medium, x_rims, x_medium, done, last)
+            done = stencil(brick, place, state, rims, medium, None, None, done, last)
+        found = stencil(brick, place, state, rims, medium, x_rims, x_medium, done, last)
         velocity = found[0]
         if not last:
-            stress, y_last, y_first, x_last, x_first, corner_y, corner_x = found[1:]
-            rims, x_rims = exchange(x_last, x_first, y_last, y_first, corner_y, corner_x)
+            _, stress, *y_outs, x_last, x_first = found
+            rims, x_rims = exchange(place, x_last, x_first, *y_outs)
             medium, x_medium = held
     return velocity
 
@@ -1200,9 +1252,9 @@
 
 
 def shards(velocity, stress, lame_lambda, shear_modulus, buoyancy, source_p, source_s):
-    velocity = propagate(velocity, stress, lame_lambda, shear_modulus, buoyancy)
+    place = jnp.stack([lax.axis_index("gx"), lax.axis_index("gy")]).astype(jnp.int32)
+    velocity = propagate(place, velocity, stress, lame_lambda, shear_modulus, buoyancy)
     plan = Plan(velocity.shape[1:])
-    place = jnp.stack([lax.axis_index("gx"), lax.axis_index("gy")]).astype(jnp.int32)
     if plan.z % (plan.gx * plan.gy) == 0:
         return tuple(separated(plan, place, velocity, source_p, source_s))
     blocks = z_forward(plan, place, velocity)

time: 309 us -> 296 us (0.958)
  starting transfers between devices: 58.7 us -> 37.2 us
  waiting for transfers between devices: 161 us -> 167 us
    ppermute x8 -> x4, starting transfers between devices: 21.9 us -> 9.88 us  [passed_along(): return lax.ppermute(block, axis, route)]
    ppermute x4 -> x2, starting transfers between devices: 10.6 us -> 3.05 us  [exchange(): rims = (lax.ppermute(y_outs[0], 'gy', [(0, 1), (1, 0)]),)]
    ppermute x4 -> x2, waiting for transfers between devices: 0.01 us -> 6.29 us  [exchange(): rims = (lax.ppermute(y_outs[0], 'gy', [(0, 1), (1, 0)]),)]
    all_to_all x4, waiting for transfers between devices: 33.4 us -> 30.1 us  [over_gx(): return lax.all_to_all(blocks, 'gx', 0, 0, tiled=True)]
  transfers between devices with their start and end apart: 20 -> 14, of which waited for: 7 -> 10; matrix products, arithmetic and copies ran while one was open for 0% -> 0% of each run, Pallas kernels for 16% -> 17%
where the time goes in v6:
time: 296 us; the launch traced here: 295 us
  waiting for transfers between devices  167 us (56%)
  Pallas kernels  82.7 us (28%)
  starting transfers between devices  37.2 us (13%)
  local copies, waits for them, and re-layouts  6.49 us (2%)
    ppermute x4, waiting for transfers between devices, swap_gy(): moved.append(lax.ppermute(blocks[step], 'gy', route))  130 us
    all_to_all x4, waiting for transfers between devices, over_gx(): return lax.all_to_all(blocks, 'gx', 0, 0, tiled=True)  30.1 us
    pallas_call x4, Pallas kernels, stencil(): pl.pallas_call(kernel, grid=(count,), in_specs=in_specs, out_specs=out_sp...  23.1 us
    all_to_all x4, starting transfers between devices, over_gx(): return lax.all_to_all(blocks, 'gx', 0, 0, tiled=True)  21.2 us
    pallas_call x2, Pallas kernels, image_part(): pl.pallas_call(kernel, grid=(x // group,), in_specs=[scalars(), whole_blo...  13.7 us
    ppermute x4, starting transfers between devices, passed_along(): return lax.ppermute(block, axis, route)  9.88 us
    pallas_call x1, Pallas kernels, potential(): pl.pallas_call(kernel, grid=(plan.per,), in_specs=[scalars()] + [whole_bl...  6.78 us
    pallas_call x2, Pallas kernels, along_z(): pl.pallas_call(kernel, grid=(x // group,), in_specs=[scalars(), whole_blo...  6.52 us
  transfers between devices with their start and end apart: 14, of which 10 were waited for; matrix products, arithmetic and copies ran while one was open for 0% of the time, Pallas kernels for 17%

profile of v6, /device:TPU:12, one launch (start us, length us, event | category | flops | bytes accessed | tf_op | source)
XLA Modules:
  0.0 295.3 jit_solution(5445803416009574286)
XLA Ops:
  12.4 3.6 %collective-permute-start.2 = (f32[776,128]{1,0:T(8,128)}, f32[776,128]{1,0:T(8,128)S(1)}, u32[]{:S(2)}, u32[]{:S(2)}) collective-permute-start(f32[776,128]{1,0:T(8,128)} %get-tuple-element.34), channel_id=1, source_target_pairs={{2,0},{4,2},{6,4},{8,6},{10,8},{12,10},{14,12},{16,14},{18,16},{20... | collective-permute-start | bytes 1191944 | tf_op jit(solution)/shard_map/ppermute | solution.py:27
  22.5 9.0 %stencil_middle.2 = (f32[3,32,128,128]{3,2,1,0:T(8,128)S(1)}, f32[6,32,128,128]{3,2,1,0:T(8,128)S(1)}, f32[5,32,128]{2,1,0:T(8,128)S(1)}) custom-call(s32[2]{0:T(128)S(1)} %copy-done.9, f32[3,32,128,128]{3,2,1,0:T(8,128)S(1)} %copy-done, f32[6,32,128,128]{3,2,1,0:T(8,128)} %refs_11_.5, bf16[32,128,128]{2,1,0:T(8,128)(2,1)S(1)} %copy-done.4, ...), custom_call_target="tpu_custom_call" | custom-call | flops 31457280000 | bytes 30670848000 | tf_op jit(solution)/shard_map/stencil_middle/pallas_call | solution.py:424
  31.5 4.0 %stencil_ends.2 = (f32[3,32,128,128]{3,2,1,0:T(8,128)S(1)}, f32[6,32,128,128]{3,2,1,0:T(8,128)S(1)}, f32[5,32,128]{2,1,0:T(8,128)S(1)}, f32[648,128]{1,0:T(8,128)S(1)}, f32[520,128]{1,0:T(8,128)S(1)}) custom-call(s32[2]{0:T(128)S(1)} %copy-done.9, f32[3,32,128,128]{3,2,1,0:T(8,128)S(1)} %copy-done, ...), custom_call_target="tpu_custom_call", output_to_operand_aliasing={{0}: (17, {}), {1}: (18, {})} | custom-call | flops 10485760 | bytes 10223616 | tf_op jit(solution)/shard_map/stencil_ends/pallas_call | solution.py:424
  45.0 7.2 %stencil_middle.3.refs_19_ = f32[3,32,128,128]{3,2,1,0:T(8,128)S(1)} custom-call(s32[2]{0:T(128)S(1)} %copy-done.9, f32[3,32,128,128]{3,2,1,0:T(8,128)S(1)} %get-tuple-element.38.refs_0_.refs_5_.refs_9_, f32[6,32,128,128]{3,2,1,0:T(8,128)S(1)} %get-tuple-element.39.refs_1_.refs_6_.refs_10_.refs_11_, bf16[32,128,128]{2,1,0:T(8,128)(2,1)S(1)} %copy-done.4, ...), custom_call_target="tpu_custom_call" | custom-call | flops 31457280000 | bytes 21233664000 | tf_op jit(solution)/shard_map/stencil_middle/pallas_call | solution.py:424
  63.9 6.0 %all-to-all-start = ((f32[16,2,4,32,128]{4,3,2,1,0:T(8,128)}), f32[16,2,4,32,128]{4,3,2,1,0:T(8,128)}, u32[]{:S(2)}, u32[]{:S(2)}) async-start(f32[16,2,4,32,128]{4,3,2,1,0:T(8,128)} %bitcast.2), calls=%async_computation | async-start | bytes 4194304 | tf_op jit(solution)/shard_map/all_to_all | solution.py:1230
  69.8 37.8 %collective-permute-done.7.refs_1_ = f32[2,64,32,128]{3,2,1,0:T(8,128)} collective-permute-done((f32[2,64,32,128]{3,2,1,0:T(8,128)S(1)}, f32[2,64,32,128]{3,2,1,0:T(8,128)}, u32[]{:S(2)}, u32[]{:S(2)}) %collective-permute-start.7) | collective-permute-done | bytes 2097184 | tf_op jit(solution)/shard_map/ppermute | solution.py:599
  107.6 4.6 %pair_y_forward.1 = f32[64,32,256]{2,1,0:T(8,128)} custom-call(s32[2]{0:T(128)} %pad_add_fusion.place_ref, bf16[2,2,128,256]{3,2,1,0:T(8,128)(2,1)} %constant.38.clone.table_ref, f32[2,64,32,128]{3,2,1,0:T(8,128)} %copy-done.6, f32[2,64,32,128]{3,2,1,0:T(8,128)} %collective-permute-done.7.refs_1_), custom_call_target="tpu_custom_call" | custom-call | flops 1610612736000 | bytes 6291456000 | tf_op jit(solution)/shard_map/pair_y_forward/pallas_call | solution.py:966
  112.2 5.0 %all-to-all-done.refs_4_ = f32[16,2,4,32,128]{4,3,2,1,0:T(8,128)} async-done(((f32[16,2,4,32,128]{4,3,2,1,0:T(8,128)}), f32[16,2,4,32,128]{4,3,2,1,0:T(8,128)}, u32[]{:S(2)}, u32[]{:S(2)}) %all-to-all-start) | async-done | bytes 2097184 | tf_op jit(solution)/shard_map/all_to_all | solution.py:1230
  117.2 5.1 %all-to-all-start.1 = ((f32[16,4,32,256]{3,2,1,0:T(8,128)}), f32[16,4,32,256]{3,2,1,0:T(8,128)}, u32[]{:S(2)}, u32[]{:S(2)}) async-start(f32[16,4,32,256]{3,2,1,0:T(8,128)} %bitcast.6), calls=%async_computation.1 | async-start | bytes 4194304 | tf_op jit(solution)/shard_map/all_to_all | solution.py:1230
  122.3 4.7 %first_x_forward.1 = (f32[4,512,128]{2,1,0:T(8,128)}, f32[4,512,128]{2,1,0:T(8,128)}) custom-call(s32[2]{0:T(128)} %pad_add_fusion.place_ref, bf16[256,512]{1,0:T(8,128)(2,1)} %constant.39.clone.refs_0_, bf16[256,256]{1,0:T(8,128)(2,1)} %constant.40.clone.refs_1_, bf16[256,512]{1,0:T(8,128)(2,1)} %constant.41.clone.refs_2_, ...), custom_call_target="tpu_custom_call" | custom-call | flops 1610612736 | bytes 4194304 | tf_op jit(solution)/shard_map/first_x_forward/pallas_call | solution.py:991
  127.5 25.0 %collective-permute-done.6.refs_1_ = f32[4,512,128]{2,1,0:T(8,128)} collective-permute-done((f32[4,512,128]{2,1,0:T(8,128)}, f32[4,512,128]{2,1,0:T(8,128)}, u32[]{:S(2)}, u32[]{:S(2)}) %collective-permute-start.6) | collective-permute-done | bytes 1048608 | tf_op jit(solution)/shard_map/ppermute | solution.py:599
  152.5 4.6 %first_y_forward.1.refs_8_ = f32[4,512,256]{2,1,0:T(8,128)} custom-call(s32[2]{0:T(128)} %pad_add_fusion.place_ref, bf16[2,2,128,256]{3,2,1,0:T(8,128)(2,1)} %constant.38.clone.table_ref, f32[4,512,128]{2,1,0:T(8,128)} %get-tuple-element.46.refs_0_, f32[4,512,128]{2,1,0:T(8,128)} %collective-permute-done.6.refs_1_), custom_call_target="tpu_custom_call" | custom-call | flops 805306368 | bytes 4194304 | tf_op jit(solution)/shard_map/first_y_forward/pallas_call | solution.py:1015
  157.1 12.5 %all-to-all-done.1.refs_9_ = f32[16,4,32,256]{3,2,1,0:T(8,128)} async-done(((f32[16,4,32,256]{3,2,1,0:T(8,128)}), f32[16,4,32,256]{3,2,1,0:T(8,128)}, u32[]{:S(2)}, u32[]{:S(2)}) %all-to-all-start.1) | async-done | bytes 2097184 | tf_op jit(solution)/shard_map/all_to_all | solution.py:1230
  169.6 6.8 %potential.1 = (f32[16,4,32,256]{3,2,1,0:T(8,128)}, f32[4,512,256]{2,1,0:T(8,128)}) custom-call(s32[2]{0:T(128)} %pad_add_fusion.place_ref, bf16[256,512]{1,0:T(8,128)(2,1)} %constant.39.clone.refs_0_, bf16[256,256]{1,0:T(8,128)(2,1)} %constant.40.clone.refs_1_, bf16[256,512]{1,0:T(8,128)(2,1)} %constant.41.clone.refs_2_, ...), custom_call_target="tpu_custom_call" | custom-call | flops 3221225472 | bytes 8388608 | tf_op jit(solution)/shard_map/potential/pallas_call | solution.py:1049
  176.4 5.1 %all-to-all-start.2 = ((f32[16,4,32,256]{3,2,1,0:T(8,128)}), f32[16,4,32,256]{3,2,1,0:T(8,128)}, u32[]{:S(2)}, u32[]{:S(2)}) async-start(f32[16,4,32,256]{3,2,1,0:T(8,128)} %get-tuple-element.49), calls=%async_computation.2 | async-start | bytes 4194304 | tf_op jit(solution)/shard_map/all_to_all | solution.py:1230
  181.5 4.6 %last_y_inverse.1 = (f32[4,512,128]{2,1,0:T(8,128)}, f32[4,512,128]{2,1,0:T(8,128)}) custom-call(s32[2]{0:T(128)} %pad_add_fusion.place_ref, bf16[2,2,256,128]{3,2,1,0:T(8,128)(2,1)} %constant.47.clone.table_ref, f32[4,512,256]{2,1,0:T(8,128)} %get-tuple-element.50.in_ref), custom_call_target="tpu_custom_call" | custom-call | flops 805306368 | bytes 4194304 | tf_op jit(solution)/shard_map/last_y_inverse/pallas_call | solution.py:1089
  186.6 25.0 %collective-permute-done.8.refs_5_ = f32[4,512,128]{2,1,0:T(8,128)} collective-permute-done((f32[4,512,128]{2,1,0:T(8,128)}, f32[4,512,128]{2,1,0:T(8,128)}, u32[]{:S(2)}, u32[]{:S(2)}) %collective-permute-start.8) | collective-permute-done | bytes 1048608 | tf_op jit(solution)/shard_map/ppermute | solution.py:599
  211.6 4.7 %last_x_inverse.1._ = f32[16,2,4,32,128]{4,3,2,1,0:T(8,128)} custom-call(s32[2]{0:T(128)} %pad_add_fusion.place_ref, bf16[256,512]{1,0:T(8,128)(2,1)} %constant.43.clone.refs_4_.refs_0_, bf16[256,256]{1,0:T(8,128)(2,1)} %constant.44.clone.refs_5_.refs_1_, bf16[256,512]{1,0:T(8,128)(2,1)} %constant.45.clone.refs_6_.refs_2_, ...), custom_call_target="tpu_custom_call" | custom-call | flops 1610612736 | bytes 4194304 | tf_op jit(solution)/shard_map/last_x_inverse/pallas_call | solution.py:1116
  216.3 12.5 %all-to-all-done.2 = f32[16,4,32,256]{3,2,1,0:T(8,128)} async-done(((f32[16,4,32,256]{3,2,1,0:T(8,128)}), f32[16,4,32,256]{3,2,1,0:T(8,128)}, u32[]{:S(2)}, u32[]{:S(2)}) %all-to-all-start.2) | async-done | bytes 2097184 | tf_op jit(solution)/shard_map/all_to_all | solution.py:1230
  228.9 4.6 %pair_y_inverse.1 = (f32[2,64,32,128]{3,2,1,0:T(8,128)}, f32[2,64,32,128]{3,2,1,0:T(8,128)}, f32[16,2,4,32,128]{4,3,2,1,0:T(8,128)}) custom-call(s32[2]{0:T(128)} %pad_add_fusion.place_ref, bf16[2,2,256,128]{3,2,1,0:T(8,128)(2,1)} %constant.47.clone.table_ref, f32[64,32,256]{2,1,0:T(8,128)} %bitcast.4.in_ref, ...), custom_call_target="tpu_custom_call", output_to_operand_aliasing={{2}: (3, {})} | custom-call | flops 1610612736 | bytes 6291456 | tf_op jit(solution)/shard_map/pair_y_inverse/pallas_call | solution.py:1147
  234.0 5.1 %all-to-all-start.3 = ((f32[16,2,4,32,128]{4,3,2,1,0:T(8,128)}), f32[16,2,4,32,128]{4,3,2,1,0:T(8,128)}, u32[]{:S(2)}, u32[]{:S(2)}) async-start(f32[16,2,4,32,128]{4,3,2,1,0:T(8,128)} %get-tuple-element.57), calls=%async_computation.3 | async-start | bytes 4194304 | tf_op jit(solution)/shard_map/all_to_all | solution.py:1230
  239.1 42.5 %collective-permute-done.9.refs_7_ = f32[2,64,32,128]{3,2,1,0:T(8,128)} collective-permute-done((f32[2,64,32,128]{3,2,1,0:T(8,128)}, f32[2,64,32,128]{3,2,1,0:T(8,128)}, u32[]{:S(2)}, u32[]{:S(2)}) %collective-permute-start.9) | collective-permute-done | bytes 2097184 | tf_op jit(solution)/shard_map/ppermute | solution.py:599
  281.6 7.6 %image_part.2 = (f32[32,128,128]{2,1,0:T(8,128)}, f32[32,128,128]{2,1,0:T(8,128)}) custom-call(s32[2]{0:T(128)} %pad_add_fusion.place_ref, bf16[2,2,2,64,128]{4,3,2,1,0:T(8,128)(2,1)} %constant.48.clone.table_ref, f32[3,32,128,128]{3,2,1,0:T(8,128)} %copy-done.1, f32[3,32,128,128]{3,2,1,0:T(8,128)} %copy-done.1, bf16[3,32,128,128]{3,2,1,0:T(8,128)(2,1)} %refs_1_.10, ...), custom_call_target="tpu_custom_call" | custom-call | flops 805306368000 | bytes 16777216000 | tf_op jit(solution)/shard_map/image_part/pallas_call | solution.py:1206
  289.2 6.1 %image_part.3 = (f32[32,128,128]{2,1,0:T(8,128)}, f32[32,128,128]{2,1,0:T(8,128)}) custom-call(s32[2]{0:T(128)} %pad_add_fusion.place_ref, bf16[1,2,1,128,128]{4,3,2,1,0:T(8,128)(2,1)} %constant.49.clone.table_ref, f32[3,32,128,128]{3,2,1,0:T(8,128)} %copy-done.1, bf16[3,32,128,128]{3,2,1,0:T(8,128)(2,1)} %refs_1_.10, bf16[3,32,128,128]{3,2,1,0:T(8,128)(2,1)} %refs_2_.16, ...), custom_call_target="tpu_custom_call" | custom-call | flops 402653184 | bytes 10485760 | tf_op jit(solution)/shard_map/image_part/pallas_call | solution.py:1206
  (43 shorter events, 40.8 us)
Async XLA Ops:
  1.3 8.0 %copy-start.9 = (s32[2]{0:T(128)S(1)}, s32[2]{0:T(128)}, u32[]{:S(2)}) copy-start(s32[2]{0:T(128)} %pad_add_fusion.place_ref) | copy-start | bytes 28
  4.5 4.8 %collective-permute-start = (f32[6,32,128]{2,1,0:T(8,128)}, f32[6,32,128]{2,1,0:T(8,128)S(1)}, u32[]{:S(2)}, u32[]{:S(2)}) collective-permute-start(f32[6,32,128]{2,1,0:T(8,128)} %get-tuple-element.30), channel_id=1, source_target_pairs={{0,1},{1,0},{2,3},{3,2},{4,5},{5,4},{6,7},{7,6},{8,9},{9,8},{10,11... | collective-permute-start | bytes 294920 | tf_op jit(solution)/shard_map/ppermute | solution.py:68
  10.4 21.0 %collective-permute-start.1 = (f32[776,128]{1,0:T(8,128)}, f32[776,128]{1,0:T(8,128)S(1)}, u32[]{:S(2)}, u32[]{:S(2)}) collective-permute-start(f32[776,128]{1,0:T(8,128)} %get-tuple-element.33), channel_id=1, source_target_pairs={{0,2},{2,4},{4,6},{6,8},{8,10},{10,12},{12,14},{14,16},{16,18},{18... | collective-permute-start | bytes 1191944 | tf_op jit(solution)/shard_map/ppermute | solution.py:27
  12.4 19.1 %collective-permute-start.2 = (f32[776,128]{1,0:T(8,128)}, f32[776,128]{1,0:T(8,128)S(1)}, u32[]{:S(2)}, u32[]{:S(2)}) collective-permute-start(f32[776,128]{1,0:T(8,128)} %get-tuple-element.34), channel_id=1, source_target_pairs={{2,0},{4,2},{6,4},{8,6},{10,8},{12,10},{14,12},{16,14},{18,16},{20... | collective-permute-start | bytes 1191944 | tf_op jit(solution)/shard_map/ppermute | solution.py:27
  16.0 2.8 copy-start
  18.8 1.2 copy-start.2
  20.0 1.2 copy-start.4
  21.3 1.2 copy-start.5
  31.5 13.5 %copy-start.3 = (bf16[32,128,128]{2,1,0:T(8,128)(2,1)S(1)}, bf16[32,128,128]{2,1,0:T(8,128)(2,1)}, u32[]{:S(2)}) copy-start(bf16[32,128,128]{2,1,0:T(8,128)(2,1)} %refs_12_.9) | copy-start | bytes 3145732
  35.5 4.5 %collective-permute-start.3 = (f32[5,32,128]{2,1,0:T(8,128)S(1)}, f32[5,32,128]{2,1,0:T(8,128)S(1)}, u32[]{:S(2)}, u32[]{:S(2)}) collective-permute-start(f32[5,32,128]{2,1,0:T(8,128)S(1)} %get-tuple-element.40), channel_id=1, source_target_pairs={{0,1},{1,0},{2,3},{3,2},{4,5},{5,4},{6,7},{7,6},{8,9},{9,8},{10,11... | collective-permute-start | bytes 245768 | tf_op jit(solution)/shard_map/ppermute | solution.py:68
  40.6 11.6 %collective-permute-start.5 = (f32[520,128]{1,0:T(8,128)S(1)}, f32[520,128]{1,0:T(8,128)S(1)}, u32[]{:S(2)}, u32[]{:S(2)}) collective-permute-start(f32[520,128]{1,0:T(8,128)S(1)} %get-tuple-element.44), channel_id=1, source_target_pairs={{2,0},{4,2},{6,4},{8,6},{10,8},{12,10},{14,12},{16,14},{18,16},{20... | collective-permute-start | bytes 798728 | tf_op jit(solution)/shard_map/ppermute | solution.py:27
  42.5 10.3 %collective-permute-start.4 = (f32[648,128]{1,0:T(8,128)S(1)}, f32[648,128]{1,0:T(8,128)S(1)}, u32[]{:S(2)}, u32[]{:S(2)}) collective-permute-start(f32[648,128]{1,0:T(8,128)S(1)} %get-tuple-element.43), channel_id=1, source_target_pairs={{0,2},{2,4},{4,6},{6,8},{8,10},{10,12},{12,14},{14,16},{16,18},{18... | collective-permute-start | bytes 995336 | tf_op jit(solution)/shard_map/ppermute | solution.py:27
  52.2 3.6 %copy-start.7 = (bf16[2,2,2,64,128]{4,3,2,1,0:T(8,128)(2,1)S(1)}, bf16[2,2,2,64,128]{4,3,2,1,0:T(8,128)(2,1)}, u32[]{:S(2)}) copy-start(bf16[2,2,2,64,128]{4,3,2,1,0:T(8,128)(2,1)} %constant.36.clone.table_ref) | copy-start | bytes 393220
  55.7 5.1 %copy-start.1 = (f32[3,32,128,128]{3,2,1,0:T(8,128)}, f32[3,32,128,128]{3,2,1,0:T(8,128)S(1)}, u32[]{:S(2)}) copy-start(f32[3,32,128,128]{3,2,1,0:T(8,128)S(1)} %stencil_ends.3.refs_0_.refs_1_) | copy-start | bytes 18874372
  55.7 5.1 %copy-start.8 = (bf16[1,2,1,128,128]{4,3,2,1,0:T(8,128)(2,1)S(1)}, bf16[1,2,1,128,128]{4,3,2,1,0:T(8,128)(2,1)}, u32[]{:S(2)}) copy-start(bf16[1,2,1,128,128]{4,3,2,1,0:T(8,128)(2,1)} %constant.37.clone.table_ref) | copy-start | bytes 196612
  59.3 4.6 %copy-start.6 = (f32[2,64,32,128]{3,2,1,0:T(8,128)}, f32[2,64,32,128]{3,2,1,0:T(8,128)S(1)}, u32[]{:S(2)}) copy-start(f32[2,64,32,128]{3,2,1,0:T(8,128)S(1)} %get-tuple-element.45.refs_1_.refs_0_) | copy-start | bytes 6291460
  59.3 48.3 %collective-permute-start.7 = (f32[2,64,32,128]{3,2,1,0:T(8,128)S(1)}, f32[2,64,32,128]{3,2,1,0:T(8,128)}, u32[]{:S(2)}, u32[]{:S(2)}) collective-permute-start(f32[2,64,32,128]{3,2,1,0:T(8,128)S(1)} %get-tuple-element.48), channel_id=1, source_target_pairs={{0,1},{1,0},{2,3},{3,2},{4,5},{5,4},{6,7},{7,6},{8,9},{9,8},{10,11... | collective-permute-start | bytes 6291464 | tf_op jit(solution)/shard_map/ppermute | solution.py:599
  63.9 53.3 %all-to-all-start = ((f32[16,2,4,32,128]{4,3,2,1,0:T(8,128)}), f32[16,2,4,32,128]{4,3,2,1,0:T(8,128)}, u32[]{:S(2)}, u32[]{:S(2)}) async-start(f32[16,2,4,32,128]{4,3,2,1,0:T(8,128)} %bitcast.2), calls=%async_computation | async-start | bytes 4194304 | tf_op jit(solution)/shard_map/all_to_all | solution.py:1230
  117.2 52.4 %all-to-all-start.1 = ((f32[16,4,32,256]{3,2,1,0:T(8,128)}), f32[16,4,32,256]{3,2,1,0:T(8,128)}, u32[]{:S(2)}, u32[]{:S(2)}) async-start(f32[16,4,32,256]{3,2,1,0:T(8,128)} %bitcast.6), calls=%async_computation.1 | async-start | bytes 4194304 | tf_op jit(solution)/shard_map/all_to_all | solution.py:1230
  127.0 25.5 %collective-permute-start.6 = (f32[4,512,128]{2,1,0:T(8,128)}, f32[4,512,128]{2,1,0:T(8,128)}, u32[]{:S(2)}, u32[]{:S(2)}) collective-permute-start(f32[4,512,128]{2,1,0:T(8,128)} %get-tuple-element.47), channel_id=1, source_target_pairs={{0,1},{1,0},{2,3},{3,2},{4,5},{5,4},{6,7},{7,6},{8,9},{9,8},{10,11... | collective-permute-start | bytes 3145736 | tf_op jit(solution)/shard_map/ppermute | solution.py:599
  176.4 52.4 %all-to-all-start.2 = ((f32[16,4,32,256]{3,2,1,0:T(8,128)}), f32[16,4,32,256]{3,2,1,0:T(8,128)}, u32[]{:S(2)}, u32[]{:S(2)}) async-start(f32[16,4,32,256]{3,2,1,0:T(8,128)} %get-tuple-element.49), calls=%async_computation.2 | async-start | bytes 4194304 | tf_op jit(solution)/shard_map/all_to_all | solution.py:1230
  186.0 25.5 %collective-permute-start.8 = (f32[4,512,128]{2,1,0:T(8,128)}, f32[4,512,128]{2,1,0:T(8,128)}, u32[]{:S(2)}, u32[]{:S(2)}) collective-permute-start(f32[4,512,128]{2,1,0:T(8,128)} %get-tuple-element.52), channel_id=1, source_target_pairs={{0,1},{1,0},{2,3},{3,2},{4,5},{5,4},{6,7},{7,6},{8,9},{9,8},{10,11... | collective-permute-start | bytes 3145736 | tf_op jit(solution)/shard_map/ppermute | solution.py:599
  233.5 48.1 %collective-permute-start.9 = (f32[2,64,32,128]{3,2,1,0:T(8,128)}, f32[2,64,32,128]{3,2,1,0:T(8,128)}, u32[]{:S(2)}, u32[]{:S(2)}) collective-permute-start(f32[2,64,32,128]{3,2,1,0:T(8,128)} %get-tuple-element.54), channel_id=1, source_target_pairs={{0,1},{1,0},{2,3},{3,2},{4,5},{5,4},{6,7},{7,6},{8,9},{9,8},{10,11... | collective-permute-start | bytes 6291464 | tf_op jit(solution)/shard_map/ppermute | solution.py:599
  234.0 55.2 %all-to-all-start.3 = ((f32[16,2,4,32,128]{4,3,2,1,0:T(8,128)}), f32[16,2,4,32,128]{4,3,2,1,0:T(8,128)}, u32[]{:S(2)}, u32[]{:S(2)}) async-start(f32[16,2,4,32,128]{4,3,2,1,0:T(8,128)} %get-tuple-element.57), calls=%async_computation.3 | async-start | bytes 4194304 | tf_op jit(solution)/shard_map/all_to_all | solution.py:1230

commit v7 on v6

--- a/solution.py
+++ b/solution.py
@@ -1102,12 +1102,12 @@
     )(place, jnp.asarray(table), slope)
 
 
-def last_x_inverse(plan, place, blocks):
+def last_x_inverse(plan, place, blocks, ahead):
     x, y, nx, gx = plan.x, plan.y, plan.nx, plan.gx
     tables = x_tables(nx, True)
 
     def kernel(place_ref, *refs):
-        table_refs, ins, out = refs[:4], refs[4:-1], refs[-1]
+        table_refs, ins, out = refs[:4], refs[4:-2], refs[-1]
         me = place_ref[1]
         found = side_by_side(x_inverse, [ref[...] for ref in table_refs], [ref[0] for ref in ins])
         for s, value in enumerate(found):
@@ -1118,13 +1118,14 @@
         grid=(plan.per,),
         in_specs=[scalars()]
         + [whole_block(table.shape) for table in tables]
-        + [pl.BlockSpec((1, nx, y), lambda i: (i, 0, 0))] * plan.gy,
+        + [pl.BlockSpec((1, nx, y), lambda i: (i, 0, 0))] * plan.gy
+        + [unread()],
         out_specs=pl.BlockSpec((gx, plan.gy, 1, x, y), lambda i: (0, 0, i, 0, 0)),
         out_shape=jax.ShapeDtypeStruct((gx, plan.gy, plan.per, x, y), jnp.float32),
         compiler_params=params(),
         cost_estimate=cost(plan.per * plan.ny * nx * nx, 2 * plan.per * plan.ny * nx),
         name="last_x_inverse",
-    )(place, *[jnp.asarray(table) for table in tables], *blocks)
+    )(place, *[jnp.asarray(table) for table in tables], *blocks, ahead)
 
 
 def pair_y_inverse(plan, place, planes, behind):
@@ -1163,6 +1164,26 @@
     )(place, jnp.asarray(table), planes, behind)
 
 
+def source_sum(plan, velocity, source_s, ahead):
+    x, y, z = plan.x, plan.y, plan.z
+    group = fit(x, X_GROUP)
+
+    def kernel(v_ref, s_ref, _, out):
+        out[...] = sum(s_ref[i].astype(jnp.float32) * v_ref[i] for i in range(3))
+
+    block = pl.BlockSpec((3, group, y, z), lambda i: (0, i, 0, 0))
+    return pl.pallas_call(
+        kernel,
+        grid=(x // group,),
+        in_specs=[block, block, unread()],
+        out_specs=pl.BlockSpec((group, y, z), lambda i: (i, 0, 0)),
+        out_shape=jax.ShapeDtypeStruct((x, y, z), jnp.float32),
+        compiler_params=params(),
+        cost_estimate=cost(x * y * z, 6 * x * y * z),
+        name="source_sum",
+    )(velocity, source_s, ahead)
+
+
 def image_part(plan, place, comps, tables, blocks, fields, before, weight):
     x, y, z = plan.x, plan.y, plan.z
     outs = len(blocks)
@@ -1173,9 +1194,9 @@
 
     def kernel(place_ref, table_ref, *refs):
         refs = list(refs)
-        inputs = [[refs.pop(0) for _ in comps] for _ in range(3)]
+        inputs = [[refs.pop(0) for _ in comps] for _ in fields]
         started = [refs.pop(0) for _ in before]
-        *ins, image_p, image_s = refs
+        *ins, image_s, image_p = refs
         ins = [ref.reshape(len(comps), rows * group, y) for ref in ins]
         order = [source(place_ref[1], s, outs) if outs > 1 else 0 for s in range(outs)]
         turned_tables = []
@@ -1185,18 +1206,18 @@
             turned_tables.append((jnp.concatenate([high, high], axis=1), low))
         for plane in range(0, group, deep):
             here = slice(plane, plane + deep)
-            total_p, total_s = (ref[here] for ref in started) if before else (0.0, 0.0)
+            total_s, total_p = ([ref[here] for ref in started] + [0.0])[:2]
             for comp, table in enumerate(turned_tables):
-                v_ref, p_ref, s_ref = (each[comp] for each in inputs)
+                p_ref, s_ref = (each[comp] for each in inputs)
                 columns = []
                 for k in range(deep):
                     cut = pl.ds(plane + k, rows, stride=group)
                     columns.append(joined([ref[comp, cut, :] for ref in ins], 0))
                 field = left_times(table, joined(columns, 1)).T.reshape(deep, y, z)
                 total_p += p_ref[0, here].astype(jnp.float32) * field
-                total_s += s_ref[0, here].astype(jnp.float32) * (v_ref[0, here] - field)
+                total_s -= s_ref[0, here].astype(jnp.float32) * field
+            image_s[here] = total_s
             image_p[here] = total_p
-            image_s[here] = total_s
 
     def block(comp):
         return pl.BlockSpec((1, group, y, z), lambda i: (comp, i, 0, 0))
@@ -1241,14 +1262,16 @@
     first = first_y_forward(plan, place, swap_gy(first_x_forward(plan, place, first)))
     lines, slope = potential(plan, place, first, pair)
     pair = over_gx(lines)
-    last = last_x_inverse(plan, place, swap_gy(last_y_inverse(plan, place, slope)))
+    last = last_y_inverse(plan, place, slope)
+    whole = source_sum(plan, velocity, source_s, last[0])
+    last = last_x_inverse(plan, place, swap_gy(last), whole)
     *pair, last = pair_y_inverse(plan, place, pair.reshape(gx * per, x, plan.ny), last)
     pair = swap_gy(pair)
     last = over_gx(last)
     back = inverse_basis(z)
-    fields = (velocity, source_p, source_s)
-    found = image_part(plan, place, (1, 2), (back, -turned(back)), pair, fields, (), WEIGHT)
-    return image_part(plan, place, (0,), (crossed(back, plan),), [last], fields, found, 1)
+    fields = (source_p, source_s)
+    found = image_part(plan, place, (1, 2), (back, -turned(back)), pair, fields, (whole,), WEIGHT)
+    return image_part(plan, place, (0,), (crossed(back, plan),), [last], fields, found, 1)[::-1]
 
 
 def shards(velocity, stress, lame_lambda, shear_modulus, buoyancy, source_p, source_s):

time: 296 us -> 296 us (level)
  waiting for transfers between devices: 167 us -> 160 us
  Pallas kernels: 82.7 us -> 89.1 us
    ppermute x4, waiting for transfers between devices: 130 us -> 123 us  [swap_gy(): moved.append(lax.ppermute(blocks[step], 'gy', route))]
    pallas_call x0 -> x1, Pallas kernels: none -> 7.18 us  [source_sum(): pl.pallas_call(kernel, grid=(x // group,), in_specs=[block, block, unread...]
  transfers between devices with their start and end apart: 14 -> 14, of which waited for: 10 -> 10; matrix products, arithmetic and copies ran while one was open for 0% -> 0% of each run, Pallas kernels for 17% -> 19%
where the time goes in v7:
time: 296 us; the launch traced here: 294 us
  waiting for transfers between devices  160 us (54%)
  Pallas kernels  89.1 us (30%)
  starting transfers between devices  37.3 us (13%)
  local copies, waits for them, and re-layouts  6.49 us (2%)
    ppermute x4, waiting for transfers between devices, swap_gy(): moved.append(lax.ppermute(blocks[step], 'gy', route))  123 us
    all_to_all x4, waiting for transfers between devices, over_gx(): return lax.all_to_all(blocks, 'gx', 0, 0, tiled=True)  30 us
    pallas_call x4, Pallas kernels, stencil(): pl.pallas_call(kernel, grid=(count,), in_specs=in_specs, out_specs=out_sp...  23.2 us
    all_to_all x4, starting transfers between devices, over_gx(): return lax.all_to_all(blocks, 'gx', 0, 0, tiled=True)  21.2 us
    pallas_call x2, Pallas kernels, image_part(): pl.pallas_call(kernel, grid=(x // group,), in_specs=[scalars(), whole_blo...  12.6 us
    ppermute x4, starting transfers between devices, passed_along(): return lax.ppermute(block, axis, route)  9.88 us
    pallas_call x1, Pallas kernels, source_sum(): pl.pallas_call(kernel, grid=(x // group,), in_specs=[block, block, unread...  7.18 us
    pallas_call x1, Pallas kernels, potential(): pl.pallas_call(kernel, grid=(plan.per,), in_specs=[scalars()] + [whole_bl...  6.77 us
  transfers between devices with their start and end apart: 14, of which 10 were waited for; matrix products, arithmetic and copies ran while one was open for 0% of the time, Pallas kernels for 19%

profile of v7, /device:TPU:12, one launch (start us, length us, event | category | flops | bytes accessed | tf_op | source)
XLA Modules:
  0.0 294.3 jit_solution(6417130269263271814)
XLA Ops:
  22.4 9.0 %stencil_middle.2 = (f32[3,32,128,128]{3,2,1,0:T(8,128)S(1)}, f32[6,32,128,128]{3,2,1,0:T(8,128)S(1)}, f32[5,32,128]{2,1,0:T(8,128)S(1)}) custom-call(s32[2]{0:T(128)S(1)} %copy-done.9, f32[3,32,128,128]{3,2,1,0:T(8,128)S(1)} %copy-done, f32[6,32,128,128]{3,2,1,0:T(8,128)} %refs_11_.5, bf16[32,128,128]{2,1,0:T(8,128)(2,1)S(1)} %copy-done.4, ...), custom_call_target="tpu_custom_call" | custom-call | flops 31457280000 | bytes 30670848000 | tf_op jit(solution)/shard_map/stencil_middle/pallas_call | solution.py:424
  31.5 4.0 %stencil_ends.2 = (f32[3,32,128,128]{3,2,1,0:T(8,128)S(1)}, f32[6,32,128,128]{3,2,1,0:T(8,128)S(1)}, f32[5,32,128]{2,1,0:T(8,128)S(1)}, f32[648,128]{1,0:T(8,128)S(1)}, f32[520,128]{1,0:T(8,128)S(1)}) custom-call(s32[2]{0:T(128)S(1)} %copy-done.9, f32[3,32,128,128]{3,2,1,0:T(8,128)S(1)} %copy-done, ...), custom_call_target="tpu_custom_call", output_to_operand_aliasing={{0}: (17, {}), {1}: (18, {})} | custom-call | flops 10485760 | bytes 10223616 | tf_op jit(solution)/shard_map/stencil_ends/pallas_call | solution.py:424
  44.9 7.2 %stencil_middle.3.refs_19_ = f32[3,32,128,128]{3,2,1,0:T(8,128)S(1)} custom-call(s32[2]{0:T(128)S(1)} %copy-done.9, f32[3,32,128,128]{3,2,1,0:T(8,128)S(1)} %get-tuple-element.40.refs_0_.refs_5_.refs_9_, f32[6,32,128,128]{3,2,1,0:T(8,128)S(1)} %get-tuple-element.41.refs_1_.refs_6_.refs_10_.refs_11_, bf16[32,128,128]{2,1,0:T(8,128)(2,1)S(1)} %copy-done.4, ...), custom_call_target="tpu_custom_call" | custom-call | flops 31457280000 | bytes 21233664000 | tf_op jit(solution)/shard_map/stencil_middle/pallas_call | solution.py:424
  63.9 6.0 %all-to-all-start = ((f32[16,2,4,32,128]{4,3,2,1,0:T(8,128)}), f32[16,2,4,32,128]{4,3,2,1,0:T(8,128)}, u32[]{:S(2)}, u32[]{:S(2)}) async-start(f32[16,2,4,32,128]{4,3,2,1,0:T(8,128)} %bitcast.2), calls=%async_computation | async-start | bytes 4194304 | tf_op jit(solution)/shard_map/all_to_all | solution.py:1251
  69.9 37.7 %collective-permute-done.7.refs_1_ = f32[2,64,32,128]{3,2,1,0:T(8,128)} collective-permute-done((f32[2,64,32,128]{3,2,1,0:T(8,128)S(1)}, f32[2,64,32,128]{3,2,1,0:T(8,128)}, u32[]{:S(2)}, u32[]{:S(2)}) %collective-permute-start.7) | collective-permute-done | bytes 2097184 | tf_op jit(solution)/shard_map/ppermute | solution.py:599
  107.6 4.6 %pair_y_forward.1 = f32[64,32,256]{2,1,0:T(8,128)} custom-call(s32[2]{0:T(128)} %pad_add_fusion.place_ref, bf16[2,2,128,256]{3,2,1,0:T(8,128)(2,1)} %constant.38.clone.table_ref, f32[2,64,32,128]{3,2,1,0:T(8,128)} %copy-done.6, f32[2,64,32,128]{3,2,1,0:T(8,128)} %collective-permute-done.7.refs_1_), custom_call_target="tpu_custom_call" | custom-call | flops 1610612736000 | bytes 6291456000 | tf_op jit(solution)/shard_map/pair_y_forward/pallas_call | solution.py:966
  112.2 5.0 %all-to-all-done.refs_4_ = f32[16,2,4,32,128]{4,3,2,1,0:T(8,128)} async-done(((f32[16,2,4,32,128]{4,3,2,1,0:T(8,128)}), f32[16,2,4,32,128]{4,3,2,1,0:T(8,128)}, u32[]{:S(2)}, u32[]{:S(2)}) %all-to-all-start) | async-done | bytes 2097184 | tf_op jit(solution)/shard_map/all_to_all | solution.py:1251
  117.3 5.1 %all-to-all-start.1 = ((f32[16,4,32,256]{3,2,1,0:T(8,128)}), f32[16,4,32,256]{3,2,1,0:T(8,128)}, u32[]{:S(2)}, u32[]{:S(2)}) async-start(f32[16,4,32,256]{3,2,1,0:T(8,128)} %bitcast.6), calls=%async_computation.1 | async-start | bytes 4194304 | tf_op jit(solution)/shard_map/all_to_all | solution.py:1251
  122.3 4.7 %first_x_forward.1 = (f32[4,512,128]{2,1,0:T(8,128)}, f32[4,512,128]{2,1,0:T(8,128)}) custom-call(s32[2]{0:T(128)} %pad_add_fusion.place_ref, bf16[256,512]{1,0:T(8,128)(2,1)} %constant.39.clone.refs_0_, bf16[256,256]{1,0:T(8,128)(2,1)} %constant.40.clone.refs_1_, bf16[256,512]{1,0:T(8,128)(2,1)} %constant.41.clone.refs_2_, ...), custom_call_target="tpu_custom_call" | custom-call | flops 1610612736 | bytes 4194304 | tf_op jit(solution)/shard_map/first_x_forward/pallas_call | solution.py:991
  127.6 25.0 %collective-permute-done.6.refs_1_ = f32[4,512,128]{2,1,0:T(8,128)} collective-permute-done((f32[4,512,128]{2,1,0:T(8,128)}, f32[4,512,128]{2,1,0:T(8,128)}, u32[]{:S(2)}, u32[]{:S(2)}) %collective-permute-start.6) | collective-permute-done | bytes 1048608 | tf_op jit(solution)/shard_map/ppermute | solution.py:599
  152.6 4.6 %first_y_forward.1.refs_8_ = f32[4,512,256]{2,1,0:T(8,128)} custom-call(s32[2]{0:T(128)} %pad_add_fusion.place_ref, bf16[2,2,128,256]{3,2,1,0:T(8,128)(2,1)} %constant.38.clone.table_ref, f32[4,512,128]{2,1,0:T(8,128)} %get-tuple-element.48.refs_0_, f32[4,512,128]{2,1,0:T(8,128)} %collective-permute-done.6.refs_1_), custom_call_target="tpu_custom_call" | custom-call | flops 805306368 | bytes 4194304 | tf_op jit(solution)/shard_map/first_y_forward/pallas_call | solution.py:1015
  157.1 12.5 %all-to-all-done.1.refs_9_ = f32[16,4,32,256]{3,2,1,0:T(8,128)} async-done(((f32[16,4,32,256]{3,2,1,0:T(8,128)}), f32[16,4,32,256]{3,2,1,0:T(8,128)}, u32[]{:S(2)}, u32[]{:S(2)}) %all-to-all-start.1) | async-done | bytes 2097184 | tf_op jit(solution)/shard_map/all_to_all | solution.py:1251
  169.7 6.8 %potential.1 = (f32[16,4,32,256]{3,2,1,0:T(8,128)}, f32[4,512,256]{2,1,0:T(8,128)}) custom-call(s32[2]{0:T(128)} %pad_add_fusion.place_ref, bf16[256,512]{1,0:T(8,128)(2,1)} %constant.39.clone.refs_0_, bf16[256,256]{1,0:T(8,128)(2,1)} %constant.40.clone.refs_1_, bf16[256,512]{1,0:T(8,128)(2,1)} %constant.41.clone.refs_2_, ...), custom_call_target="tpu_custom_call" | custom-call | flops 3221225472 | bytes 8388608 | tf_op jit(solution)/shard_map/potential/pallas_call | solution.py:1049
  176.5 5.1 %all-to-all-start.2 = ((f32[16,4,32,256]{3,2,1,0:T(8,128)}), f32[16,4,32,256]{3,2,1,0:T(8,128)}, u32[]{:S(2)}, u32[]{:S(2)}) async-start(f32[16,4,32,256]{3,2,1,0:T(8,128)} %get-tuple-element.53), calls=%async_computation.2 | async-start | bytes 4194304 | tf_op jit(solution)/shard_map/all_to_all | solution.py:1251
  181.5 4.6 %last_y_inverse.1 = (f32[4,512,128]{2,1,0:T(8,128)}, f32[4,512,128]{2,1,0:T(8,128)}) custom-call(s32[2]{0:T(128)} %pad_add_fusion.place_ref, bf16[2,2,256,128]{3,2,1,0:T(8,128)(2,1)} %constant.47.clone.table_ref, f32[4,512,256]{2,1,0:T(8,128)} %get-tuple-element.51.in_ref), custom_call_target="tpu_custom_call" | custom-call | flops 805306368 | bytes 4194304 | tf_op jit(solution)/shard_map/last_y_inverse/pallas_call | solution.py:1089
  186.7 7.2 %source_sum.1.refs_6_.refs_4_ = f32[32,128,128]{2,1,0:T(8,128)} custom-call(f32[3,32,128,128]{3,2,1,0:T(8,128)} %copy-done.1, bf16[3,32,128,128]{3,2,1,0:T(8,128)(2,1)} %refs_1_.12, f32[4,512,128]{2,1,0:T(8,128)} %get-tuple-element.52._.refs_4_), custom_call_target="tpu_custom_call" | custom-call | flops 3145728 | bytes 12582912 | tf_op jit(solution)/shard_map/source_sum/pallas_call | solution.py:1175
  193.8 17.8 %collective-permute-done.8.refs_5_ = f32[4,512,128]{2,1,0:T(8,128)} collective-permute-done((f32[4,512,128]{2,1,0:T(8,128)}, f32[4,512,128]{2,1,0:T(8,128)}, u32[]{:S(2)}, u32[]{:S(2)}) %collective-permute-start.8) | collective-permute-done | bytes 1048608 | tf_op jit(solution)/shard_map/ppermute | solution.py:599
  211.6 4.8 %last_x_inverse.1._ = f32[16,2,4,32,128]{4,3,2,1,0:T(8,128)} custom-call(s32[2]{0:T(128)} %pad_add_fusion.place_ref, bf16[256,512]{1,0:T(8,128)(2,1)} %constant.43.clone.refs_4_.refs_0_, bf16[256,256]{1,0:T(8,128)(2,1)} %constant.44.clone.refs_5_.refs_1_, bf16[256,512]{1,0:T(8,128)(2,1)} %constant.45.clone.refs_6_.refs_2_, ...), custom_call_target="tpu_custom_call" | custom-call | flops 1610612736 | bytes 4194304 | tf_op jit(solution)/shard_map/last_x_inverse/pallas_call | solution.py:1116
  216.5 12.4 %all-to-all-done.2 = f32[16,4,32,256]{3,2,1,0:T(8,128)} async-done(((f32[16,4,32,256]{3,2,1,0:T(8,128)}), f32[16,4,32,256]{3,2,1,0:T(8,128)}, u32[]{:S(2)}, u32[]{:S(2)}) %all-to-all-start.2) | async-done | bytes 2097184 | tf_op jit(solution)/shard_map/all_to_all | solution.py:1251
  228.9 4.6 %pair_y_inverse.1 = (f32[2,64,32,128]{3,2,1,0:T(8,128)}, f32[2,64,32,128]{3,2,1,0:T(8,128)}, f32[16,2,4,32,128]{4,3,2,1,0:T(8,128)}) custom-call(s32[2]{0:T(128)} %pad_add_fusion.place_ref, bf16[2,2,256,128]{3,2,1,0:T(8,128)(2,1)} %constant.47.clone.table_ref, f32[64,32,256]{2,1,0:T(8,128)} %bitcast.4.in_ref, ...), custom_call_target="tpu_custom_call", output_to_operand_aliasing={{2}: (3, {})} | custom-call | flops 1610612736 | bytes 6291456 | tf_op jit(solution)/shard_map/pair_y_inverse/pallas_call | solution.py:1148
  234.1 5.1 %all-to-all-start.3 = ((f32[16,2,4,32,128]{4,3,2,1,0:T(8,128)}), f32[16,2,4,32,128]{4,3,2,1,0:T(8,128)}, u32[]{:S(2)}, u32[]{:S(2)}) async-start(f32[16,2,4,32,128]{4,3,2,1,0:T(8,128)} %get-tuple-element.59), calls=%async_computation.3 | async-start | bytes 4194304 | tf_op jit(solution)/shard_map/all_to_all | solution.py:1251
  239.2 42.5 %collective-permute-done.9.refs_6_ = f32[2,64,32,128]{3,2,1,0:T(8,128)} collective-permute-done((f32[2,64,32,128]{3,2,1,0:T(8,128)}, f32[2,64,32,128]{3,2,1,0:T(8,128)}, u32[]{:S(2)}, u32[]{:S(2)}) %collective-permute-start.9) | collective-permute-done | bytes 2097184 | tf_op jit(solution)/shard_map/ppermute | solution.py:599
  281.7 7.1 %image_part.2 = (f32[32,128,128]{2,1,0:T(8,128)}, f32[32,128,128]{2,1,0:T(8,128)}) custom-call(s32[2]{0:T(128)} %pad_add_fusion.place_ref, bf16[2,2,2,64,128]{4,3,2,1,0:T(8,128)(2,1)} %constant.48.clone.table_ref, bf16[3,32,128,128]{3,2,1,0:T(8,128)(2,1)} %refs_0_.12, bf16[3,32,128,128]{3,2,1,0:T(8,128)(2,1)} %refs_0_.12, ...), custom_call_target="tpu_custom_call" | custom-call | flops 805306368000 | bytes 16777216000 | tf_op jit(solution)/shard_map/image_part/pallas_call | solution.py:1227
  288.8 5.5 %image_part.3 = (f32[32,128,128]{2,1,0:T(8,128)}, f32[32,128,128]{2,1,0:T(8,128)}) custom-call(s32[2]{0:T(128)} %pad_add_fusion.place_ref, bf16[1,2,1,128,128]{4,3,2,1,0:T(8,128)(2,1)} %constant.49.clone.table_ref, bf16[3,32,128,128]{3,2,1,0:T(8,128)(2,1)} %refs_0_.12, bf16[3,32,128,128]{3,2,1,0:T(8,128)(2,1)} %refs_1_.12, ...), custom_call_target="tpu_custom_call" | custom-call | flops 402653184 | bytes 10485760 | tf_op jit(solution)/shard_map/image_part/pallas_call | solution.py:1227
  (44 shorter events, 44.4 us)
Async XLA Ops:
  1.2 8.0 %copy-start.9 = (s32[2]{0:T(128)S(1)}, s32[2]{0:T(128)}, u32[]{:S(2)}) copy-start(s32[2]{0:T(128)} %pad_add_fusion.place_ref) | copy-start | bytes 28
  4.4 4.8 %collective-permute-start = (f32[6,32,128]{2,1,0:T(8,128)}, f32[6,32,128]{2,1,0:T(8,128)S(1)}, u32[]{:S(2)}, u32[]{:S(2)}) collective-permute-start(f32[6,32,128]{2,1,0:T(8,128)} %get-tuple-element.32), channel_id=1, source_target_pairs={{0,1},{1,0},{2,3},{3,2},{4,5},{5,4},{6,7},{7,6},{8,9},{9,8},{10,11... | collective-permute-start | bytes 294920 | tf_op jit(solution)/shard_map/ppermute | solution.py:68
  10.4 21.1 %collective-permute-start.1 = (f32[776,128]{1,0:T(8,128)}, f32[776,128]{1,0:T(8,128)S(1)}, u32[]{:S(2)}, u32[]{:S(2)}) collective-permute-start(f32[776,128]{1,0:T(8,128)} %get-tuple-element.35), channel_id=1, source_target_pairs={{0,2},{2,4},{4,6},{6,8},{8,10},{10,12},{12,14},{14,16},{16,18},{18... | collective-permute-start | bytes 1191944 | tf_op jit(solution)/shard_map/ppermute | solution.py:27
  12.3 19.2 %collective-permute-start.2 = (f32[776,128]{1,0:T(8,128)}, f32[776,128]{1,0:T(8,128)S(1)}, u32[]{:S(2)}, u32[]{:S(2)}) collective-permute-start(f32[776,128]{1,0:T(8,128)} %get-tuple-element.36), channel_id=1, source_target_pairs={{2,0},{4,2},{6,4},{8,6},{10,8},{12,10},{14,12},{16,14},{18,16},{20... | collective-permute-start | bytes 1191944 | tf_op jit(solution)/shard_map/ppermute | solution.py:27
  15.9 2.8 copy-start
  18.7 1.2 copy-start.2
  19.9 1.2 copy-start.4
  21.2 1.2 copy-start.5
  31.5 13.5 %copy-start.3 = (bf16[32,128,128]{2,1,0:T(8,128)(2,1)S(1)}, bf16[32,128,128]{2,1,0:T(8,128)(2,1)}, u32[]{:S(2)}) copy-start(bf16[32,128,128]{2,1,0:T(8,128)(2,1)} %refs_12_.9) | copy-start | bytes 3145732
  35.5 4.5 %collective-permute-start.3 = (f32[5,32,128]{2,1,0:T(8,128)S(1)}, f32[5,32,128]{2,1,0:T(8,128)S(1)}, u32[]{:S(2)}, u32[]{:S(2)}) collective-permute-start(f32[5,32,128]{2,1,0:T(8,128)S(1)} %get-tuple-element.42), channel_id=1, source_target_pairs={{0,1},{1,0},{2,3},{3,2},{4,5},{5,4},{6,7},{7,6},{8,9},{9,8},{10,11... | collective-permute-start | bytes 245768 | tf_op jit(solution)/shard_map/ppermute | solution.py:68
  40.6 11.6 %collective-permute-start.5 = (f32[520,128]{1,0:T(8,128)S(1)}, f32[520,128]{1,0:T(8,128)S(1)}, u32[]{:S(2)}, u32[]{:S(2)}) collective-permute-start(f32[520,128]{1,0:T(8,128)S(1)} %get-tuple-element.46), channel_id=1, source_target_pairs={{2,0},{4,2},{6,4},{8,6},{10,8},{12,10},{14,12},{16,14},{18,16},{20... | collective-permute-start | bytes 798728 | tf_op jit(solution)/shard_map/ppermute | solution.py:27
  42.5 10.3 %collective-permute-start.4 = (f32[648,128]{1,0:T(8,128)S(1)}, f32[648,128]{1,0:T(8,128)S(1)}, u32[]{:S(2)}, u32[]{:S(2)}) collective-permute-start(f32[648,128]{1,0:T(8,128)S(1)} %get-tuple-element.45), channel_id=1, source_target_pairs={{0,2},{2,4},{4,6},{6,8},{8,10},{10,12},{12,14},{14,16},{16,18},{18... | collective-permute-start | bytes 995336 | tf_op jit(solution)/shard_map/ppermute | solution.py:27
  52.2 3.6 %copy-start.7 = (bf16[2,2,2,64,128]{4,3,2,1,0:T(8,128)(2,1)S(1)}, bf16[2,2,2,64,128]{4,3,2,1,0:T(8,128)(2,1)}, u32[]{:S(2)}) copy-start(bf16[2,2,2,64,128]{4,3,2,1,0:T(8,128)(2,1)} %constant.36.clone.table_ref) | copy-start | bytes 393220
  55.7 5.1 %copy-start.1 = (f32[3,32,128,128]{3,2,1,0:T(8,128)}, f32[3,32,128,128]{3,2,1,0:T(8,128)S(1)}, u32[]{:S(2)}) copy-start(f32[3,32,128,128]{3,2,1,0:T(8,128)S(1)} %stencil_ends.3.refs_0_.refs_1_.v_ref) | copy-start | bytes 18874372
  55.7 5.1 %copy-start.8 = (bf16[1,2,1,128,128]{4,3,2,1,0:T(8,128)(2,1)S(1)}, bf16[1,2,1,128,128]{4,3,2,1,0:T(8,128)(2,1)}, u32[]{:S(2)}) copy-start(bf16[1,2,1,128,128]{4,3,2,1,0:T(8,128)(2,1)} %constant.37.clone.table_ref) | copy-start | bytes 196612
  59.3 4.6 %copy-start.6 = (f32[2,64,32,128]{3,2,1,0:T(8,128)}, f32[2,64,32,128]{3,2,1,0:T(8,128)S(1)}, u32[]{:S(2)}) copy-start(f32[2,64,32,128]{3,2,1,0:T(8,128)S(1)} %get-tuple-element.47.refs_1_.refs_0_) | copy-start | bytes 6291460
  59.3 48.3 %collective-permute-start.7 = (f32[2,64,32,128]{3,2,1,0:T(8,128)S(1)}, f32[2,64,32,128]{3,2,1,0:T(8,128)}, u32[]{:S(2)}, u32[]{:S(2)}) collective-permute-start(f32[2,64,32,128]{3,2,1,0:T(8,128)S(1)} %get-tuple-element.50), channel_id=1, source_target_pairs={{0,1},{1,0},{2,3},{3,2},{4,5},{5,4},{6,7},{7,6},{8,9},{9,8},{10,11... | collective-permute-start | bytes 6291464 | tf_op jit(solution)/shard_map/ppermute | solution.py:599
  63.9 53.4 %all-to-all-start = ((f32[16,2,4,32,128]{4,3,2,1,0:T(8,128)}), f32[16,2,4,32,128]{4,3,2,1,0:T(8,128)}, u32[]{:S(2)}, u32[]{:S(2)}) async-start(f32[16,2,4,32,128]{4,3,2,1,0:T(8,128)} %bitcast.2), calls=%async_computation | async-start | bytes 4194304 | tf_op jit(solution)/shard_map/all_to_all | solution.py:1251
  117.3 52.4 %all-to-all-start.1 = ((f32[16,4,32,256]{3,2,1,0:T(8,128)}), f32[16,4,32,256]{3,2,1,0:T(8,128)}, u32[]{:S(2)}, u32[]{:S(2)}) async-start(f32[16,4,32,256]{3,2,1,0:T(8,128)} %bitcast.6), calls=%async_computation.1 | async-start | bytes 4194304 | tf_op jit(solution)/shard_map/all_to_all | solution.py:1251
  127.1 25.5 %collective-permute-start.6 = (f32[4,512,128]{2,1,0:T(8,128)}, f32[4,512,128]{2,1,0:T(8,128)}, u32[]{:S(2)}, u32[]{:S(2)}) collective-permute-start(f32[4,512,128]{2,1,0:T(8,128)} %get-tuple-element.49), channel_id=1, source_target_pairs={{0,1},{1,0},{2,3},{3,2},{4,5},{5,4},{6,7},{7,6},{8,9},{9,8},{10,11... | collective-permute-start | bytes 3145736 | tf_op jit(solution)/shard_map/ppermute | solution.py:599
  176.5 52.4 %all-to-all-start.2 = ((f32[16,4,32,256]{3,2,1,0:T(8,128)}), f32[16,4,32,256]{3,2,1,0:T(8,128)}, u32[]{:S(2)}, u32[]{:S(2)}) async-start(f32[16,4,32,256]{3,2,1,0:T(8,128)} %get-tuple-element.53), calls=%async_computation.2 | async-start | bytes 4194304 | tf_op jit(solution)/shard_map/all_to_all | solution.py:1251
  186.1 25.5 %collective-permute-start.8 = (f32[4,512,128]{2,1,0:T(8,128)}, f32[4,512,128]{2,1,0:T(8,128)}, u32[]{:S(2)}, u32[]{:S(2)}) collective-permute-start(f32[4,512,128]{2,1,0:T(8,128)} %get-tuple-element.54), channel_id=1, source_target_pairs={{0,1},{1,0},{2,3},{3,2},{4,5},{5,4},{6,7},{7,6},{8,9},{9,8},{10,11... | collective-permute-start | bytes 3145736 | tf_op jit(solution)/shard_map/ppermute | solution.py:599
  233.5 48.2 %collective-permute-start.9 = (f32[2,64,32,128]{3,2,1,0:T(8,128)}, f32[2,64,32,128]{3,2,1,0:T(8,128)}, u32[]{:S(2)}, u32[]{:S(2)}) collective-permute-start(f32[2,64,32,128]{3,2,1,0:T(8,128)} %get-tuple-element.56), channel_id=1, source_target_pairs={{0,1},{1,0},{2,3},{3,2},{4,5},{5,4},{6,7},{7,6},{8,9},{9,8},{10,11... | collective-permute-start | bytes 6291464 | tf_op jit(solution)/shard_map/ppermute | solution.py:599
  234.1 54.7 %all-to-all-start.3 = ((f32[16,2,4,32,128]{4,3,2,1,0:T(8,128)}), f32[16,2,4,32,128]{4,3,2,1,0:T(8,128)}, u32[]{:S(2)}, u32[]{:S(2)}) async-start(f32[16,2,4,32,128]{4,3,2,1,0:T(8,128)} %get-tuple-element.59), calls=%async_computation.3 | async-start | bytes 4194304 | tf_op jit(solution)/shard_map/all_to_all | solution.py:1251

commit v8 on v7

--- a/solution.py
+++ b/solution.py
@@ -127,7 +127,7 @@
         + [medium_rows(0), medium_rows(0), medium_rows(most)],
         out_specs=[whole_block(shape) for shape in shapes],
         out_shape=[jax.ShapeDtypeStruct(shape, jnp.float32) for shape in shapes],
-        compiler_params=params(),
+        compiler_params=params(40 * 2**20),
         cost_estimate=pl.CostEstimate(
             flops=0, bytes_accessed=80 * (y + 8 * x) * z, transcendentals=0
         ),

time: 296 us -> 292 us (0.986)
    unnamed x20 -> x22, local copies, waits for them, and re-layouts: 6.49 us -> 5.28 us
  transfers between devices with their start and end apart: 14 -> 14, of which waited for: 10 -> 10; matrix products, arithmetic and copies ran while one was open for 0% -> 0% of each run, Pallas kernels for 19% -> 20%
where the time goes in v8:
time: 292 us; the launch traced here: 291 us
  waiting for transfers between devices  160 us (55%)
  Pallas kernels  87.5 us (30%)
  starting transfers between devices  37.3 us (13%)
  local copies, waits for them, and re-layouts  5.28 us (2%)
    ppermute x4, waiting for transfers between devices, swap_gy(): moved.append(lax.ppermute(blocks[step], 'gy', route))  123 us
    all_to_all x4, waiting for transfers between devices, over_gx(): return lax.all_to_all(blocks, 'gx', 0, 0, tiled=True)  30 us
    pallas_call x4, Pallas kernels, stencil(): pl.pallas_call(kernel, grid=(count,), in_specs=in_specs, out_specs=out_sp...  23.3 us
    all_to_all x4, starting transfers between devices, over_gx(): return lax.all_to_all(blocks, 'gx', 0, 0, tiled=True)  21.2 us
    pallas_call x2, Pallas kernels, image_part(): pl.pallas_call(kernel, grid=(x // group,), in_specs=[scalars(), whole_blo...  12.6 us
    ppermute x4, starting transfers between devices, passed_along(): return lax.ppermute(block, axis, route)  9.89 us
    pallas_call x1, Pallas kernels, source_sum(): pl.pallas_call(kernel, grid=(x // group,), in_specs=[block, block, unread...  7.18 us
    pallas_call x1, Pallas kernels, potential(): pl.pallas_call(kernel, grid=(plan.per,), in_specs=[scalars()] + [whole_bl...  6.77 us
  transfers between devices with their start and end apart: 14, of which 10 were waited for; matrix products, arithmetic and copies ran while one was open for 0% of the time, Pallas kernels for 20%

profile of v8, /device:TPU:12, one launch (start us, length us, event | category | flops | bytes accessed | tf_op | source)
XLA Modules:
  0.0 290.8 jit_solution(9609335671951867436)
XLA Ops:
  18.7 9.1 %stencil_middle.2 = (f32[3,32,128,128]{3,2,1,0:T(8,128)S(1)}, f32[6,32,128,128]{3,2,1,0:T(8,128)S(1)}, f32[5,32,128]{2,1,0:T(8,128)S(1)}) custom-call(s32[2]{0:T(128)S(1)} %pad_add_fusion.place_ref, f32[3,32,128,128]{3,2,1,0:T(8,128)S(1)} %copy-done, f32[6,32,128,128]{3,2,1,0:T(8,128)} %refs_11_.5, bf16[32,128,128]{2,1,0:T(8,128)(2,1)S(1)} %copy-done.4, ...), custom_call_target="tpu_custom_call" | custom-call | flops 31457280000 | bytes 30670848000 | tf_op jit(solution)/shard_map/stencil_middle/pallas_call | solution.py:424
  27.8 4.1 %stencil_ends.2 = (f32[3,32,128,128]{3,2,1,0:T(8,128)S(1)}, f32[6,32,128,128]{3,2,1,0:T(8,128)S(1)}, f32[5,32,128]{2,1,0:T(8,128)S(1)}, f32[648,128]{1,0:T(8,128)S(1)}, f32[520,128]{1,0:T(8,128)S(1)}) custom-call(s32[2]{0:T(128)S(1)} %pad_add_fusion.place_ref, f32[3,32,128,128]{3,2,1,0:T(8,128)S(1)} %copy-done, ...), custom_call_target="tpu_custom_call", output_to_operand_aliasing={{0}: (17, {}), {1}: (18, {})} | custom-call | flops 10485760 | bytes 10223616 | tf_op jit(solution)/shard_map/stencil_ends/pallas_call | solution.py:424
  41.4 7.2 %stencil_middle.3.refs_19_ = f32[3,32,128,128]{3,2,1,0:T(8,128)S(1)} custom-call(s32[2]{0:T(128)S(1)} %pad_add_fusion.place_ref, f32[3,32,128,128]{3,2,1,0:T(8,128)S(1)} %get-tuple-element.40.refs_0_.refs_5_.refs_9_, f32[6,32,128,128]{3,2,1,0:T(8,128)S(1)} %get-tuple-element.41.refs_1_.refs_6_.refs_10_.refs_11_, bf16[32,128,128]{2,1,0:T(8,128)(2,1)S(1)} %copy-done.5, ...), custom_call_target="tpu_custom_call" | custom-call | flops 31457280000 | bytes 21233664000 | tf_op jit(solution)/shard_map/stencil_middle/pallas_call | solution.py:424
  60.3 6.0 %all-to-all-start = ((f32[16,2,4,32,128]{4,3,2,1,0:T(8,128)}), f32[16,2,4,32,128]{4,3,2,1,0:T(8,128)}, u32[]{:S(2)}, u32[]{:S(2)}) async-start(f32[16,2,4,32,128]{4,3,2,1,0:T(8,128)} %bitcast.2), calls=%async_computation | async-start | bytes 4194304 | tf_op jit(solution)/shard_map/all_to_all | solution.py:1251
  66.3 37.6 %collective-permute-done.7.refs_1_ = f32[2,64,32,128]{3,2,1,0:T(8,128)} collective-permute-done((f32[2,64,32,128]{3,2,1,0:T(8,128)S(1)}, f32[2,64,32,128]{3,2,1,0:T(8,128)}, u32[]{:S(2)}, u32[]{:S(2)}) %collective-permute-start.7) | collective-permute-done | bytes 2097184 | tf_op jit(solution)/shard_map/ppermute | solution.py:599
  104.0 4.6 %pair_y_forward.1 = f32[64,32,256]{2,1,0:T(8,128)} custom-call(s32[2]{0:T(128)} %copy-done.10, bf16[2,2,128,256]{3,2,1,0:T(8,128)(2,1)} %constant.38.clone.table_ref, f32[2,64,32,128]{3,2,1,0:T(8,128)} %copy-done.7, f32[2,64,32,128]{3,2,1,0:T(8,128)} %collective-permute-done.7.refs_1_), custom_call_target="tpu_custom_call" | custom-call | flops 1610612736000 | bytes 6291456000 | tf_op jit(solution)/shard_map/pair_y_forward/pallas_call | solution.py:966
  108.6 5.1 %all-to-all-done.refs_4_ = f32[16,2,4,32,128]{4,3,2,1,0:T(8,128)} async-done(((f32[16,2,4,32,128]{4,3,2,1,0:T(8,128)}), f32[16,2,4,32,128]{4,3,2,1,0:T(8,128)}, u32[]{:S(2)}, u32[]{:S(2)}) %all-to-all-start) | async-done | bytes 2097184 | tf_op jit(solution)/shard_map/all_to_all | solution.py:1251
  113.7 5.1 %all-to-all-start.1 = ((f32[16,4,32,256]{3,2,1,0:T(8,128)}), f32[16,4,32,256]{3,2,1,0:T(8,128)}, u32[]{:S(2)}, u32[]{:S(2)}) async-start(f32[16,4,32,256]{3,2,1,0:T(8,128)} %bitcast.6), calls=%async_computation.1 | async-start | bytes 4194304 | tf_op jit(solution)/shard_map/all_to_all | solution.py:1251
  118.8 4.8 %first_x_forward.1 = (f32[4,512,128]{2,1,0:T(8,128)}, f32[4,512,128]{2,1,0:T(8,128)}) custom-call(s32[2]{0:T(128)} %copy-done.10, bf16[256,512]{1,0:T(8,128)(2,1)} %constant.39.clone.refs_0_, bf16[256,256]{1,0:T(8,128)(2,1)} %constant.40.clone.refs_1_, bf16[256,512]{1,0:T(8,128)(2,1)} %constant.41.clone.refs_2_, bf16[256,256]{1,0:T(8,128)(2,1)} %constant.42.clone.refs_3_, ...), custom_call_target="tpu_custom_call" | custom-call | flops 1610612736 | bytes 4194304 | tf_op jit(solution)/shard_map/first_x_forward/pallas_call | solution.py:991
  124.1 25.0 %collective-permute-done.6.refs_1_ = f32[4,512,128]{2,1,0:T(8,128)} collective-permute-done((f32[4,512,128]{2,1,0:T(8,128)}, f32[4,512,128]{2,1,0:T(8,128)}, u32[]{:S(2)}, u32[]{:S(2)}) %collective-permute-start.6) | collective-permute-done | bytes 1048608 | tf_op jit(solution)/shard_map/ppermute | solution.py:599
  149.1 4.6 %first_y_forward.1.refs_8_ = f32[4,512,256]{2,1,0:T(8,128)} custom-call(s32[2]{0:T(128)} %copy-done.10, bf16[2,2,128,256]{3,2,1,0:T(8,128)(2,1)} %constant.38.clone.table_ref, f32[4,512,128]{2,1,0:T(8,128)} %get-tuple-element.48.refs_0_, f32[4,512,128]{2,1,0:T(8,128)} %collective-permute-done.6.refs_1_), custom_call_target="tpu_custom_call" | custom-call | flops 805306368 | bytes 4194304 | tf_op jit(solution)/shard_map/first_y_forward/pallas_call | solution.py:1015
  153.7 12.5 %all-to-all-done.1.refs_9_ = f32[16,4,32,256]{3,2,1,0:T(8,128)} async-done(((f32[16,4,32,256]{3,2,1,0:T(8,128)}), f32[16,4,32,256]{3,2,1,0:T(8,128)}, u32[]{:S(2)}, u32[]{:S(2)}) %all-to-all-start.1) | async-done | bytes 2097184 | tf_op jit(solution)/shard_map/all_to_all | solution.py:1251
  166.1 6.8 %potential.1 = (f32[16,4,32,256]{3,2,1,0:T(8,128)}, f32[4,512,256]{2,1,0:T(8,128)}) custom-call(s32[2]{0:T(128)} %copy-done.10, bf16[256,512]{1,0:T(8,128)(2,1)} %constant.39.clone.refs_0_, bf16[256,256]{1,0:T(8,128)(2,1)} %constant.40.clone.refs_1_, bf16[256,512]{1,0:T(8,128)(2,1)} %constant.41.clone.refs_2_, bf16[256,256]{1,0:T(8,128)(2,1)} %constant.42.clone.refs_3_, ...), custom_call_target="tpu_custom_call" | custom-call | flops 3221225472 | bytes 8388608 | tf_op jit(solution)/shard_map/potential/pallas_call | solution.py:1049
  172.9 5.1 %all-to-all-start.2 = ((f32[16,4,32,256]{3,2,1,0:T(8,128)}), f32[16,4,32,256]{3,2,1,0:T(8,128)}, u32[]{:S(2)}, u32[]{:S(2)}) async-start(f32[16,4,32,256]{3,2,1,0:T(8,128)} %get-tuple-element.53), calls=%async_computation.2 | async-start | bytes 4194304 | tf_op jit(solution)/shard_map/all_to_all | solution.py:1251
  178.0 4.6 %last_y_inverse.1 = (f32[4,512,128]{2,1,0:T(8,128)}, f32[4,512,128]{2,1,0:T(8,128)}) custom-call(s32[2]{0:T(128)} %copy-done.10, bf16[2,2,256,128]{3,2,1,0:T(8,128)(2,1)} %constant.47.clone.table_ref, f32[4,512,256]{2,1,0:T(8,128)} %get-tuple-element.51.in_ref), custom_call_target="tpu_custom_call" | custom-call | flops 805306368 | bytes 4194304 | tf_op jit(solution)/shard_map/last_y_inverse/pallas_call | solution.py:1089
  183.1 7.2 %source_sum.1.refs_6_.refs_4_ = f32[32,128,128]{2,1,0:T(8,128)} custom-call(f32[3,32,128,128]{3,2,1,0:T(8,128)} %copy-done.1, bf16[3,32,128,128]{3,2,1,0:T(8,128)(2,1)} %refs_1_.12, f32[4,512,128]{2,1,0:T(8,128)} %get-tuple-element.52._.refs_4_), custom_call_target="tpu_custom_call" | custom-call | flops 3145728 | bytes 12582912 | tf_op jit(solution)/shard_map/source_sum/pallas_call | solution.py:1175
  190.3 17.8 %collective-permute-done.8.refs_5_ = f32[4,512,128]{2,1,0:T(8,128)} collective-permute-done((f32[4,512,128]{2,1,0:T(8,128)}, f32[4,512,128]{2,1,0:T(8,128)}, u32[]{:S(2)}, u32[]{:S(2)}) %collective-permute-start.8) | collective-permute-done | bytes 1048608 | tf_op jit(solution)/shard_map/ppermute | solution.py:599
  208.1 4.9 %last_x_inverse.1._ = f32[16,2,4,32,128]{4,3,2,1,0:T(8,128)} custom-call(s32[2]{0:T(128)} %copy-done.10, bf16[256,512]{1,0:T(8,128)(2,1)} %constant.43.clone.refs_4_.refs_0_, bf16[256,256]{1,0:T(8,128)(2,1)} %constant.44.clone.refs_5_.refs_1_, bf16[256,512]{1,0:T(8,128)(2,1)} %constant.45.clone.refs_6_.refs_2_, ...), custom_call_target="tpu_custom_call" | custom-call | flops 1610612736 | bytes 4194304 | tf_op jit(solution)/shard_map/last_x_inverse/pallas_call | solution.py:1116
  213.0 12.4 %all-to-all-done.2 = f32[16,4,32,256]{3,2,1,0:T(8,128)} async-done(((f32[16,4,32,256]{3,2,1,0:T(8,128)}), f32[16,4,32,256]{3,2,1,0:T(8,128)}, u32[]{:S(2)}, u32[]{:S(2)}) %all-to-all-start.2) | async-done | bytes 2097184 | tf_op jit(solution)/shard_map/all_to_all | solution.py:1251
  225.4 4.7 %pair_y_inverse.1 = (f32[2,64,32,128]{3,2,1,0:T(8,128)}, f32[2,64,32,128]{3,2,1,0:T(8,128)}, f32[16,2,4,32,128]{4,3,2,1,0:T(8,128)}) custom-call(s32[2]{0:T(128)} %copy-done.10, bf16[2,2,256,128]{3,2,1,0:T(8,128)(2,1)} %constant.47.clone.table_ref, f32[64,32,256]{2,1,0:T(8,128)} %bitcast.4.in_ref, ...), custom_call_target="tpu_custom_call", output_to_operand_aliasing={{2}: (3, {})} | custom-call | flops 1610612736 | bytes 6291456 | tf_op jit(solution)/shard_map/pair_y_inverse/pallas_call | solution.py:1148
  230.5 5.1 %all-to-all-start.3 = ((f32[16,2,4,32,128]{4,3,2,1,0:T(8,128)}), f32[16,2,4,32,128]{4,3,2,1,0:T(8,128)}, u32[]{:S(2)}, u32[]{:S(2)}) async-start(f32[16,2,4,32,128]{4,3,2,1,0:T(8,128)} %get-tuple-element.59), calls=%async_computation.3 | async-start | bytes 4194304 | tf_op jit(solution)/shard_map/all_to_all | solution.py:1251
  235.6 42.5 %collective-permute-done.9.refs_6_ = f32[2,64,32,128]{3,2,1,0:T(8,128)} collective-permute-done((f32[2,64,32,128]{3,2,1,0:T(8,128)}, f32[2,64,32,128]{3,2,1,0:T(8,128)}, u32[]{:S(2)}, u32[]{:S(2)}) %collective-permute-start.9) | collective-permute-done | bytes 2097184 | tf_op jit(solution)/shard_map/ppermute | solution.py:599
  278.2 7.1 %image_part.2 = (f32[32,128,128]{2,1,0:T(8,128)}, f32[32,128,128]{2,1,0:T(8,128)}) custom-call(s32[2]{0:T(128)} %copy-done.10, bf16[2,2,2,64,128]{4,3,2,1,0:T(8,128)(2,1)} %constant.48.clone.table_ref, bf16[3,32,128,128]{3,2,1,0:T(8,128)(2,1)} %refs_0_.12, bf16[3,32,128,128]{3,2,1,0:T(8,128)(2,1)} %refs_0_.12, bf16[3,32,128,128]{3,2,1,0:T(8,128)(2,1)} %refs_1_.12, ...), custom_call_target="tpu_custom_call" | custom-call | flops 805306368000 | bytes 16777216000 | tf_op jit(solution)/shard_map/image_part/pallas_call | solution.py:1227
  285.2 5.5 %image_part.3 = (f32[32,128,128]{2,1,0:T(8,128)}, f32[32,128,128]{2,1,0:T(8,128)}) custom-call(s32[2]{0:T(128)} %copy-done.10, bf16[1,2,1,128,128]{4,3,2,1,0:T(8,128)(2,1)} %constant.49.clone.table_ref, bf16[3,32,128,128]{3,2,1,0:T(8,128)(2,1)} %refs_0_.12, bf16[3,32,128,128]{3,2,1,0:T(8,128)(2,1)} %refs_1_.12, f32[32,128,128]{2,1,0:T(8,128)} %get-tuple-element.57.refs_2_, ...), custom_call_target="tpu_custom_call" | custom-call | flops 402653184 | bytes 10485760 | tf_op jit(solution)/shard_map/image_part/pallas_call | solution.py:1227
  (46 shorter events, 40.6 us)
Async XLA Ops:
  0.7 2.8 copy-start
  3.5 1.2 copy-start.2
  5.9 51.3 %copy-start.10 = (s32[2]{0:T(128)}, s32[2]{0:T(128)S(1)}, u32[]{:S(2)}) copy-start(s32[2]{0:T(128)S(1)} %pad_add_fusion.place_ref) | copy-start | bytes 28
  5.9 12.7 %copy-start.6 = (bf16[32,128,128]{2,1,0:T(8,128)(2,1)S(1)}, bf16[32,128,128]{2,1,0:T(8,128)(2,1)}, u32[]{:S(2)}) copy-start(bf16[32,128,128]{2,1,0:T(8,128)(2,1)} %refs_4_.10) | copy-start | bytes 3145732
  7.8 4.7 %collective-permute-start = (f32[6,32,128]{2,1,0:T(8,128)S(1)}, f32[6,32,128]{2,1,0:T(8,128)S(1)}, u32[]{:S(2)}, u32[]{:S(2)}) collective-permute-start(f32[6,32,128]{2,1,0:T(8,128)S(1)} %get-tuple-element.32), channel_id=1, source_target_pairs={{0,1},{1,0},{2,3},{3,2},{4,5},{5,4},{6,7},{7,6},{8,9},{9,8},{10,11... | collective-permute-start | bytes 294920 | tf_op jit(solution)/shard_map/ppermute | solution.py:68
  13.1 14.7 %collective-permute-start.1 = (f32[776,128]{1,0:T(8,128)S(1)}, f32[776,128]{1,0:T(8,128)S(1)}, u32[]{:S(2)}, u32[]{:S(2)}) collective-permute-start(f32[776,128]{1,0:T(8,128)S(1)} %get-tuple-element.35), channel_id=1, source_target_pairs={{0,2},{2,4},{4,6},{6,8},{8,10},{10,12},{12,14},{14,16},{16,18},{18... | collective-permute-start | bytes 1191944 | tf_op jit(solution)/shard_map/ppermute | solution.py:27
  15.0 12.8 %collective-permute-start.2 = (f32[776,128]{1,0:T(8,128)S(1)}, f32[776,128]{1,0:T(8,128)S(1)}, u32[]{:S(2)}, u32[]{:S(2)}) collective-permute-start(f32[776,128]{1,0:T(8,128)S(1)} %get-tuple-element.36), channel_id=1, source_target_pairs={{2,0},{4,2},{6,4},{8,6},{10,8},{12,10},{14,12},{16,14},{18,16},{20... | collective-permute-start | bytes 1191944 | tf_op jit(solution)/shard_map/ppermute | solution.py:27
  27.8 13.6 %copy-start.3 = (bf16[32,128,128]{2,1,0:T(8,128)(2,1)S(1)}, bf16[32,128,128]{2,1,0:T(8,128)(2,1)}, u32[]{:S(2)}) copy-start(bf16[32,128,128]{2,1,0:T(8,128)(2,1)} %refs_12_.9) | copy-start | bytes 3145732
  27.8 13.6 %copy-start.5 = (bf16[32,128,128]{2,1,0:T(8,128)(2,1)S(1)}, bf16[32,128,128]{2,1,0:T(8,128)(2,1)}, u32[]{:S(2)}) copy-start(bf16[32,128,128]{2,1,0:T(8,128)(2,1)} %refs_7_.10) | copy-start | bytes 3145732
  31.9 4.5 %collective-permute-start.3 = (f32[5,32,128]{2,1,0:T(8,128)S(1)}, f32[5,32,128]{2,1,0:T(8,128)S(1)}, u32[]{:S(2)}, u32[]{:S(2)}) collective-permute-start(f32[5,32,128]{2,1,0:T(8,128)S(1)} %get-tuple-element.42), channel_id=1, source_target_pairs={{0,1},{1,0},{2,3},{3,2},{4,5},{5,4},{6,7},{7,6},{8,9},{9,8},{10,11... | collective-permute-start | bytes 245768 | tf_op jit(solution)/shard_map/ppermute | solution.py:68
  37.0 11.6 %collective-permute-start.5 = (f32[520,128]{1,0:T(8,128)S(1)}, f32[520,128]{1,0:T(8,128)S(1)}, u32[]{:S(2)}, u32[]{:S(2)}) collective-permute-start(f32[520,128]{1,0:T(8,128)S(1)} %get-tuple-element.46), channel_id=1, source_target_pairs={{2,0},{4,2},{6,4},{8,6},{10,8},{12,10},{14,12},{16,14},{18,16},{20... | collective-permute-start | bytes 798728 | tf_op jit(solution)/shard_map/ppermute | solution.py:27
  38.9 10.3 %collective-permute-start.4 = (f32[648,128]{1,0:T(8,128)S(1)}, f32[648,128]{1,0:T(8,128)S(1)}, u32[]{:S(2)}, u32[]{:S(2)}) collective-permute-start(f32[648,128]{1,0:T(8,128)S(1)} %get-tuple-element.45), channel_id=1, source_target_pairs={{0,2},{2,4},{4,6},{6,8},{8,10},{10,12},{12,14},{14,16},{16,18},{18... | collective-permute-start | bytes 995336 | tf_op jit(solution)/shard_map/ppermute | solution.py:27
  48.6 3.5 %copy-start.8 = (bf16[2,2,2,64,128]{4,3,2,1,0:T(8,128)(2,1)S(1)}, bf16[2,2,2,64,128]{4,3,2,1,0:T(8,128)(2,1)}, u32[]{:S(2)}) copy-start(bf16[2,2,2,64,128]{4,3,2,1,0:T(8,128)(2,1)} %constant.36.clone.table_ref) | copy-start | bytes 393220
  52.1 5.2 %copy-start.1 = (f32[3,32,128,128]{3,2,1,0:T(8,128)}, f32[3,32,128,128]{3,2,1,0:T(8,128)S(1)}, u32[]{:S(2)}) copy-start(f32[3,32,128,128]{3,2,1,0:T(8,128)S(1)} %stencil_ends.3.refs_0_.refs_1_.v_ref) | copy-start | bytes 18874372
  52.1 5.1 %copy-start.9 = (bf16[1,2,1,128,128]{4,3,2,1,0:T(8,128)(2,1)S(1)}, bf16[1,2,1,128,128]{4,3,2,1,0:T(8,128)(2,1)}, u32[]{:S(2)}) copy-start(bf16[1,2,1,128,128]{4,3,2,1,0:T(8,128)(2,1)} %constant.37.clone.table_ref) | copy-start | bytes 196612
  55.7 4.6 %copy-start.7 = (f32[2,64,32,128]{3,2,1,0:T(8,128)}, f32[2,64,32,128]{3,2,1,0:T(8,128)S(1)}, u32[]{:S(2)}) copy-start(f32[2,64,32,128]{3,2,1,0:T(8,128)S(1)} %get-tuple-element.47.refs_1_.refs_0_) | copy-start | bytes 6291460
  55.7 48.3 %collective-permute-start.7 = (f32[2,64,32,128]{3,2,1,0:T(8,128)S(1)}, f32[2,64,32,128]{3,2,1,0:T(8,128)}, u32[]{:S(2)}, u32[]{:S(2)}) collective-permute-start(f32[2,64,32,128]{3,2,1,0:T(8,128)S(1)} %get-tuple-element.50), channel_id=1, source_target_pairs={{0,1},{1,0},{2,3},{3,2},{4,5},{5,4},{6,7},{7,6},{8,9},{9,8},{10,11... | collective-permute-start | bytes 6291464 | tf_op jit(solution)/shard_map/ppermute | solution.py:599
  60.3 53.4 %all-to-all-start = ((f32[16,2,4,32,128]{4,3,2,1,0:T(8,128)}), f32[16,2,4,32,128]{4,3,2,1,0:T(8,128)}, u32[]{:S(2)}, u32[]{:S(2)}) async-start(f32[16,2,4,32,128]{4,3,2,1,0:T(8,128)} %bitcast.2), calls=%async_computation | async-start | bytes 4194304 | tf_op jit(solution)/shard_map/all_to_all | solution.py:1251
  113.7 52.4 %all-to-all-start.1 = ((f32[16,4,32,256]{3,2,1,0:T(8,128)}), f32[16,4,32,256]{3,2,1,0:T(8,128)}, u32[]{:S(2)}, u32[]{:S(2)}) async-start(f32[16,4,32,256]{3,2,1,0:T(8,128)} %bitcast.6), calls=%async_computation.1 | async-start | bytes 4194304 | tf_op jit(solution)/shard_map/all_to_all | solution.py:1251
  123.6 25.5 %collective-permute-start.6 = (f32[4,512,128]{2,1,0:T(8,128)}, f32[4,512,128]{2,1,0:T(8,128)}, u32[]{:S(2)}, u32[]{:S(2)}) collective-permute-start(f32[4,512,128]{2,1,0:T(8,128)} %get-tuple-element.49), channel_id=1, source_target_pairs={{0,1},{1,0},{2,3},{3,2},{4,5},{5,4},{6,7},{7,6},{8,9},{9,8},{10,11... | collective-permute-start | bytes 3145736 | tf_op jit(solution)/shard_map/ppermute | solution.py:599
  172.9 52.4 %all-to-all-start.2 = ((f32[16,4,32,256]{3,2,1,0:T(8,128)}), f32[16,4,32,256]{3,2,1,0:T(8,128)}, u32[]{:S(2)}, u32[]{:S(2)}) async-start(f32[16,4,32,256]{3,2,1,0:T(8,128)} %get-tuple-element.53), calls=%async_computation.2 | async-start | bytes 4194304 | tf_op jit(solution)/shard_map/all_to_all | solution.py:1251
  182.6 25.5 %collective-permute-start.8 = (f32[4,512,128]{2,1,0:T(8,128)}, f32[4,512,128]{2,1,0:T(8,128)}, u32[]{:S(2)}, u32[]{:S(2)}) collective-permute-start(f32[4,512,128]{2,1,0:T(8,128)} %get-tuple-element.54), channel_id=1, source_target_pairs={{0,1},{1,0},{2,3},{3,2},{4,5},{5,4},{6,7},{7,6},{8,9},{9,8},{10,11... | collective-permute-start | bytes 3145736 | tf_op jit(solution)/shard_map/ppermute | solution.py:599
  230.0 48.2 %collective-permute-start.9 = (f32[2,64,32,128]{3,2,1,0:T(8,128)}, f32[2,64,32,128]{3,2,1,0:T(8,128)}, u32[]{:S(2)}, u32[]{:S(2)}) collective-permute-start(f32[2,64,32,128]{3,2,1,0:T(8,128)} %get-tuple-element.56), channel_id=1, source_target_pairs={{0,1},{1,0},{2,3},{3,2},{4,5},{5,4},{6,7},{7,6},{8,9},{9,8},{10,11... | collective-permute-start | bytes 6291464 | tf_op jit(solution)/shard_map/ppermute | solution.py:599
  230.5 54.7 %all-to-all-start.3 = ((f32[16,2,4,32,128]{4,3,2,1,0:T(8,128)}), f32[16,2,4,32,128]{4,3,2,1,0:T(8,128)}, u32[]{:S(2)}, u32[]{:S(2)}) async-start(f32[16,2,4,32,128]{4,3,2,1,0:T(8,128)} %get-tuple-element.59), calls=%async_computation.3 | async-start | bytes 4194304 | tf_op jit(solution)/shard_map/all_to_all | solution.py:1251
  (1 other events, 1.2 us)
